TPU v7x, 32 devices: a whole 2x2x4 slice. The times are simulated.
32 devices in a mesh: rep: 2 (over y), pair: 8 (over z, x), samp: 2 (over core).
Axes of the slice: x: 2, y: 2, z: 4, core: 2. Of those that a mesh axis runs over, the one named last changes fastest.
Arguments:
- dosage: bfloat16 [128, 4096], P(('rep', 'pair', 'samp')), parts along dimension 0, may hold values from 0 to 2
- phenotype: bfloat16 [2, 128], P(None, ('rep', 'pair', 'samp')), parts along dimension 1, may hold values from -6 to 6
- perms: int32 [2, 64], replicated, may hold values from 0 to 63, each once within a row
- pairs: int32 [8, 2], replicated, may hold values from 0 to 7
Outputs:
- stat: bfloat16 [16, 4, 512, 512], P(('rep', 'pair'), None, None, 'samp'), parts along dimension 0
There are 2 independent parts, one for each index of `rep`. A program takes and returns all parts, laid end to end along the dimension named above; an argument that names none is the same for every part. Nothing has to cross between parts.
Inputs may be any that keep to these rules, and one draw needn't show every extreme that they name: `perms`: each row is a permutation of the samples. `pairs`: panel ids; a panel may appear in many blocks.
All inputs are finite; a program needn't handle non-finite values.
Results may differ from a plain program's by a relative error of at most 0.02.
Values may be sent and summed in bfloat16 or wider, within the bound.
No kernel may reach another device: no remote copies, remote signals or barrier semaphores. Data moves between devices by JAX's collectives and lax.ppermute only.
A program may use at most 64 MiB of HBM per device.

v0:
```python
import jax
import jax.numpy as jnp
from jax import lax
from jax.sharding import PartitionSpec as P

PANEL = 512


def finish(prod, ya, yb_half, marg_a, marg_b_half, ysum, count):
    value = prod - ya[:, :, None] * marg_b_half[None, None, :] / count
    value = value - marg_a[None, :, None] * yb_half[:, None, :] / count
    value = value + marg_a[None, :, None] * marg_b_half[None, None, :] * ysum[:, None, None] / (
        count * count
    )
    return (value / jnp.sqrt(count)).astype(jnp.bfloat16)[None]


def permuted(whole_y, perms, sample_ids):
    picked = whole_y[:, perms[:, sample_ids]]
    return picked.reshape(-1, sample_ids.shape[0])


def on_device(dosage, phenotype, perms, pairs):
    s_dev = dosage.shape[0]
    pair_count = lax.axis_size("pair")
    samp_count = lax.axis_size("samp")
    grouped = dosage.reshape(s_dev, -1, PANEL)
    picked = jnp.take(grouped, pairs.reshape(-1), axis=1).reshape(s_dev, pairs.shape[0], 2 * PANEL)
    whole_y = lax.all_gather(phenotype, ("pair", "samp"), axis=1, tiled=True).astype(jnp.float32)
    count = jnp.float32(whole_y.shape[1])
    received = lax.all_to_all(picked, "pair", split_axis=1, concat_axis=0, tiled=True).reshape(
        pair_count * s_dev, 2 * PANEL
    )
    geno_a = received[:, :PANEL]
    geno_b = received[:, PANEL:]
    full_a = lax.all_gather(geno_a, "samp", axis=0, tiled=True)
    part_b = lax.all_to_all(geno_b, "samp", split_axis=1, concat_axis=0, tiled=True)
    rows = jnp.arange(full_a.shape[0], dtype=jnp.int32)
    group = rows // received.shape[0]
    inner = rows % received.shape[0]
    sample_ids = inner // s_dev * samp_count * s_dev + group * s_dev + inner % s_dev
    yperm = permuted(whole_y, perms, sample_ids)
    scaled = (yperm[:, :, None] * full_a[None].astype(jnp.float32)).astype(jnp.bfloat16)
    prod_half = jnp.einsum("ksi,sj->kij", scaled, part_b, preferred_element_type=jnp.float32)
    ya = jnp.sum(scaled, axis=1, dtype=jnp.float32)
    yb_half = jnp.einsum(
        "ks,sj->kj", yperm, part_b.astype(jnp.float32), precision=lax.Precision.HIGHEST
    )
    marg_a = jnp.sum(full_a, axis=0, dtype=jnp.float32)
    marg_b_half = jnp.sum(part_b, axis=0, dtype=jnp.float32)
    ysum = jnp.sum(yperm, axis=1)
    return finish(prod_half, ya, yb_half, marg_a, marg_b_half, ysum, count)


def solution(mesh):
    placed = (P(("rep", "pair", "samp"), None), P(None, ("rep", "pair", "samp")), P(), P())
    return jax.shard_map(
        on_device,
        mesh=mesh,
        in_specs=placed,
        out_specs=P(("rep", "pair"), None, None, "samp"),
        check_vma=False,
    )
```

profile of v0, /device:TPU:0, one launch (start us, length us, event | category | flops | bytes accessed | tf_op | source)
XLA Modules:
  0.0 43.7 jit_solution(8418153733974152815)
XLA Ops:
  0.0 0.0 copy-start
  0.0 0.7 %compare_and_fusion = pred[8,2]{0,1:T(4,128)(4,1)S(1)} fusion(s32[8,2]{0,1:T(2,128)} %param.7), kind=kLoop, calls=%fused_computation.23 | loop fusion | flops 96 | bytes 80 | tf_op jit(solution)/shard_map/jit(_take)/and | solution.py:28
  0.7 0.8 %copy.24 = s32[8,2]{1,0:T(8,128)S(1)} copy(s32[8,2]{0,1:T(2,128)} %param.7) | data formatting | bytes 128 | tf_op args[3]
  1.4 0.1 reshape.239
  1.5 0.0 copy-done
  1.6 0.6 %gather_fusion.2 = bf16[16,4,512]{2,1,0:T(4,128)(2,1)S(1)} fusion(bf16[4,8,512]{2,0,1:T(4,128)(2,1)S(1)} %bitcast.49, s32[1024]{0:T(1024)S(1)} %pad_clamp_fusion), kind=kCustom, calls=%fused_computation.2 | custom fusion | bytes 131136 | tf_op jit(solution)/shard_map/jit(_take)/gather | solution.py:28
  2.2 0.1 broadcast_in_dim.16
  2.2 0.7 %broadcast_select_fusion = bf16[4,8,1024]{2,0,1:T(4,128)(2,1)} fusion(bf16[4,8,1024]{2,0,1:T(4,128)(2,1)S(1)} %bitcast.53, pred[8,1024]{1,0:T(8,128)(4,1)S(1)} %bitcast.61), kind=kLoop, calls=%fused_computation.12 | loop fusion | flops 32768 | bytes 139264 | tf_op jit(solution)/shard_map/jit(_take)/select_n | solution.py:28
  2.9 7.3 %all-to-all-start = ((bf16[4,8,1024]{2,0,1:T(4,128)(2,1)}), bf16[4,8,1024]{2,0,1:T(4,128)(2,1)S(1)}, u32[]{:S(2)}, u32[]{:S(2)}) async-start(bf16[4,8,1024]{2,0,1:T(4,128)(2,1)} %broadcast_select_fusion), calls=%async_computation | async-start | bytes 131072 | tf_op jit(solution)/shard_map/all_to_all | solution.py:31
  10.2 0.8 %copy.21 = s32[2,64]{0,1:T(8,128)S(1)} copy(s32[2,64]{1,0:T(2,128)} %param.6) | data formatting | bytes 1024 | tf_op args[2]
  11.0 0.6 %gather_fusion = s32[64,2]{1,0:T(8,128)S(1)} fusion(s32[2,64]{0,1:T(8,128)S(1)} %copy.21, s32[1024]{0:T(1024)S(1)} %pad_clamp_fusion.2), kind=kCustom, calls=%fused_computation | custom fusion | bytes 1280 | tf_op jit(solution)/shard_map/gather | solution.py:19
  11.6 0.1 copy.22
  11.7 0.1 reshape.252
  11.8 21.9 %all-gather = bf16[16,4,2]{1,2,0:T(2,128)(2,1)S(1)} all-gather(bf16[1,4,2]{1,2,0:T(2,128)(2,1)} %bitcast.65), channel_id=1, replica_groups=mesh['rep'=2,'pair'=8,'samp'=2] {'pair','samp'}, dimensions={0}, use_global_device_ids=true | all-gather | bytes 272 | tf_op jit(solution)/shard_map/all_gather | solution.py:29
  33.6 0.2 copy.27
  33.8 0.7 %gather_fusion.3 = bf16[128,2]{1,0:T(8,128)(2,1)S(1)} fusion(bf16[2,64]{0,1:T(8,128)(2,1)S(1)} %bitcast.57, s32[1024]{0:T(1024)S(1)} %pad_clamp_fusion.1), kind=kCustom, calls=%fused_computation.3 | custom fusion | bytes 1536 | tf_op jit(solution)/shard_map/gather | solution.py:19
  34.6 0.1 copy.26
  34.6 0.7 %gather_fusion.1 = f32[128,2]{1,0:T(8,128)S(1)} fusion(f32[2,64]{0,1:T(8,128)S(1)} %convert_element_type.22, s32[1024]{0:T(1024)S(1)} %pad_clamp_fusion.1), kind=kCustom, calls=%fused_computation.1 | custom fusion | bytes 2560 | tf_op jit(solution)/shard_map/gather | solution.py:19
  35.3 0.1 copy.23
  35.4 0.1 bitcast_reduce_fusion
  35.5 0.1 mul.115
  35.6 0.0 all-to-all-done
  35.6 1.9 %all_gather.7 = bf16[64,512]{1,0:T(8,128)(2,1)S(1)} all-gather(bf16[32,512]{1,0:T(8,128)(2,1)S(1)} %get-tuple-element.5), channel_id=1, replica_groups=mesh['rep'=2,'pair'=8,'samp'=2] {'samp'}, dimensions={0}, use_global_device_ids=true | all-gather | bytes 98304 | tf_op jit(solution)/shard_map/all_gather | solution.py:36
  37.5 3.7 %all_to_all.34 = bf16[32,2,256]{2,0,1:T(8,128)(2,1)S(1)} all-to-all(bf16[32,2,256]{2,0,1:T(8,128)(2,1)S(1)} %bitcast.54), channel_id=1, replica_groups=mesh['rep'=2,'pair'=8,'samp'=2] {'samp'}, dimensions={1} | all-to-all | bytes 65536 | tf_op jit(solution)/shard_map/all_to_all | solution.py:37
  41.3 0.1 fusion.9
  41.4 0.1 convert_reduce_fusion
  41.5 0.1 broadcast_multiply_fusion
  41.7 2.0 %fusion = bf16[1,4,512,256]{3,2,1,0:T(8,128)(2,1)} fusion(bf16[64,256,1]{1,0,2:T(8,128)(2,1)S(1)} %bitcast.51, f32[4]{0:T(128)S(1)} %mul.115, f32[512,256]{1,0:T(8,128)S(1)} %broadcast_multiply_fusion, f32[4,256]{1,0:T(4,128)S(1)} %fusion.9, f32[512]{0:T(512)S(1)} %convert_reduce_fusion.2, f32[256]{0:T(256)S(1)} %convert_reduce_fusion.1, ...), kind=kOutput, calls=%fused_computation.5 | convolution fusion | flops 73138176 | bytes 1753104 | tf_op jit(solution)/shard_map/ksi,sj->kij/dot_general | solution.py:44
  (13 shorter events, 0.2 us)
Async XLA Ops:
  0.0 1.5 %copy-start = (bf16[4,4096]{1,0:T(4,128)(2,1)S(1)}, bf16[4,4096]{1,0:T(4,128)(2,1)}, u32[]{:S(2)}) copy-start(bf16[4,4096]{1,0:T(4,128)(2,1)} %param.4) | copy-start | bytes 98308
  2.9 32.6 %all-to-all-start = ((bf16[4,8,1024]{2,0,1:T(4,128)(2,1)}), bf16[4,8,1024]{2,0,1:T(4,128)(2,1)S(1)}, u32[]{:S(2)}, u32[]{:S(2)}) async-start(bf16[4,8,1024]{2,0,1:T(4,128)(2,1)} %broadcast_select_fusion), calls=%async_computation | async-start | bytes 131072 | tf_op jit(solution)/shard_map/all_to_all | solution.py:31
where the time goes:
time: 44 us; the launch traced here: 43.7 us
  blocking collectives  27.5 us (62%)
  starting transfers between devices  7.25 us (16%)
  local copies, waits for them, and re-layouts  4.91 us (11%)
  matrix products  2.12 us (5%)
  other arithmetic  1.85 us (4%)
    all_gather x1, blocking collectives, on_device(): lax.all_gather(phenotype, ('pair', 'samp'), axis=1, tiled=True)  21.9 us
    all_to_all x1, starting transfers between devices, on_device(): lax.all_to_all(picked, 'pair', split_axis=1, concat_axis=0, tiled=True)  7.25 us
    all_to_all x1, blocking collectives, on_device(): lax.all_to_all(geno_b, 'samp', split_axis=1, concat_axis=0, tiled=True)  3.75 us
    gather x6, local copies, waits for them, and re-layouts, permuted(): picked = whole_y[:, perms[:, sample_ids]]  2.21 us
    dot_general x1, matrix products, on_device(): jnp.einsum('ksi,sj->kij', scaled, part_b, preferred_element_type=jnp.floa...  2 us
    all_gather x1, blocking collectives, on_device(): full_a = lax.all_gather(geno_a, 'samp', axis=0, tiled=True)  1.85 us
    unnamed x5, local copies, waits for them, and re-layouts  1.73 us
  transfers between devices with their start and end apart: 1, of which 0 were waited for; matrix products, arithmetic and copies ran while one was open for 8% of the time, Pallas kernels for 0%

commit v1 on v0

v1 whole, which is shorter than its diff:
```python
import functools
import math

import jax
import jax.numpy as jnp
from jax import lax
from jax.experimental import pallas as pl
from jax.experimental.pallas import tpu as pltpu
from jax.sharding import PartitionSpec as P

PANEL = 512
LANES = 128
TILE = 16


def pack_kernel(pairs_ref, pheno_ref, grid_ref, out_ref):
    genes, s_dev = pheno_ref.shape
    rows = TILE // 2
    pheno = pheno_ref[...].astype(jnp.float32)
    row = lax.broadcasted_iota(jnp.int32, (TILE, LANES), 0)
    lane = lax.broadcasted_iota(jnp.int32, (TILE, LANES), 1)
    block = jnp.zeros((TILE, LANES), jnp.float32)
    for g in range(genes):
        for s in range(s_dev):
            hit = (lane == g) & (lax.rem(row, rows) == s)
            block = jnp.where(hit, pheno[g : g + 1, s : s + 1], block)
    upper = row < rows

    @pl.loop(0, pairs_ref.shape[1], unroll=math.gcd(8, pairs_ref.shape[1]))
    def _(n):
        first = pl.multiple_of(pairs_ref[0, n] * TILE, TILE)
        second = pl.multiple_of(pairs_ref[1, n] * TILE, TILE)
        panel_a = grid_ref[pl.ds(first, TILE), :]
        panel_b = grid_ref[pl.ds(second, TILE), :].astype(jnp.float32)
        out_ref[2 * n, 0:TILE, :] = panel_a
        out_ref[2 * n + 1, 0:TILE, :] = panel_a
        out_ref[2 * n, TILE : 2 * TILE, :] = jnp.where(upper, panel_b, block).astype(out_ref.dtype)
        out_ref[2 * n + 1, TILE : 2 * TILE, :] = jnp.where(upper, block, panel_b).astype(out_ref.dtype)


def stat_kernel(genes, half_ref, perms_ref, got_ref, out_ref):
    sources = got_ref.shape[0]
    rperms, samples = perms_ref.shape
    s_dev = samples // sources
    first_half = half_ref[0] == 0

    def by_samples(tiles, group):
        return tiles[:, group * s_dev : (group + 1) * s_dev, :].reshape(samples, LANES)

    panel_a = got_ref[:, 0:TILE, :].astype(jnp.float32)
    mixed = got_ref[:, TILE : 2 * TILE, :].astype(jnp.float32)
    low, high = mixed[:, : TILE // 2], mixed[:, TILE // 2 :]
    tile_b = jnp.where(first_half, low, high)
    tile_y = jnp.where(first_half, high, low)

    count = jnp.float32(samples)
    geno_b = jnp.concatenate([by_samples(tile_b, q) for q in range(TILE // 2 // s_dev)], axis=1)
    marg_b = jnp.sum(geno_b, axis=0, keepdims=True)
    centred = (geno_b - marg_b / count) * (samples**-0.5)
    b_hi = centred.astype(jnp.bfloat16)
    b_lo = (centred - b_hi.astype(jnp.float32)).astype(jnp.bfloat16)
    b_both = jnp.concatenate([b_hi, b_lo], axis=0)

    pheno = by_samples(tile_y, 0)
    perms = perms_ref[...]
    twice = jnp.concatenate([perms, perms], axis=1)
    sample = lax.broadcasted_iota(jnp.int32, (samples, 2 * samples), 0)
    yrows = []
    for g in range(genes):
        column = pheno[:, g : g + 1]
        for r in range(rperms):
            chosen = jnp.where(sample == twice[r : r + 1, :], column, 0.0)
            yrows.append(jnp.sum(chosen, axis=0, keepdims=True))
    yall = jnp.concatenate(yrows, axis=0)
    tail = jnp.dot(yall.astype(jnp.bfloat16), b_both, preferred_element_type=jnp.float32) / count
    c_hi = tail.astype(jnp.bfloat16)
    c_lo = tail - c_hi.astype(jnp.float32)

    geno_a = jnp.concatenate([by_samples(panel_a, q) for q in range(TILE // s_dev)], axis=1)
    a_rows = jnp.concatenate([geno_a, geno_a], axis=0).T
    a_half = -a_rows.astype(jnp.bfloat16)
    for k in range(len(yrows)):
        scaled = (a_rows * yrows[k]).astype(jnp.bfloat16)
        left = jnp.concatenate([scaled, a_half], axis=1)
        right = jnp.concatenate(
            [
                b_both,
                jnp.broadcast_to(c_hi[k : k + 1, :].astype(jnp.float32), geno_b.shape).astype(jnp.bfloat16),
                jnp.broadcast_to(c_lo[k : k + 1, :], geno_b.shape).astype(jnp.bfloat16),
            ],
            axis=0,
        )
        out_ref[0, k] = jnp.dot(left, right, preferred_element_type=jnp.float32).astype(out_ref.dtype)


def on_device(dosage, phenotype, perms, pairs):
    s_dev, snps = dosage.shape
    genes = phenotype.shape[0]
    devices = lax.axis_size("pair") * lax.axis_size("samp")
    half = PANEL // lax.axis_size("samp")
    grid = dosage.reshape(s_dev, snps // LANES, LANES).transpose(1, 0, 2).reshape(-1, LANES)
    vmem = pl.BlockSpec(memory_space=pltpu.VMEM)
    smem = pl.BlockSpec(memory_space=pltpu.SMEM)
    messages = pl.pallas_call(
        pack_kernel,
        out_shape=jax.ShapeDtypeStruct((devices, 2 * TILE, LANES), dosage.dtype),
        in_specs=[smem, vmem, vmem],
        out_specs=vmem,
        name="pack",
    )(pairs.T, phenotype, grid)
    got = lax.all_to_all(messages, ("pair", "samp"), split_axis=0, concat_axis=0, tiled=True)
    which = lax.axis_index("samp").reshape(1).astype(jnp.int32)
    return pl.pallas_call(
        functools.partial(stat_kernel, genes),
        out_shape=jax.ShapeDtypeStruct((1, genes * perms.shape[0], PANEL, half), jnp.bfloat16),
        in_specs=[smem, vmem, vmem],
        out_specs=vmem,
        compiler_params=pltpu.CompilerParams(vmem_limit_bytes=48 * 1024 * 1024),
        name="stat",
    )(which, perms, got)


def solution(mesh):
    placed = (P(("rep", "pair", "samp"), None), P(None, ("rep", "pair", "samp")), P(), P())
    return jax.shard_map(
        on_device,
        mesh=mesh,
        in_specs=placed,
        out_specs=P(("rep", "pair"), None, None, "samp"),
        check_vma=False,
    )
```

time: 44 us -> 18.7 us (0.42)
  blocking collectives: 27.5 us -> 0 us
  waiting for transfers between devices: 0.01 us -> 7.92 us
  local copies, waits for them, and re-layouts: 4.91 us -> 0.01 us
  Pallas kernels: 0 us -> 3.19 us
  matrix products: 2.12 us -> 0 us
  other arithmetic: 1.85 us -> 0 us
    all_gather x2 -> x0, blocking collectives: 23.7 us -> none  [the longest x1 21.9 us: on_device(): lax.all_gather(phenotype, ('pair', 'samp'), axis=1, tiled=True)]
    all_to_all x1, waiting for transfers between devices: 0.01 us -> 7.92 us  [on_device(): lax.all_to_all(messages, ('pair', 'samp'), split_axis=0, concat_axis=0, t...]
    all_to_all x1 -> x0, blocking collectives: 3.75 us -> none  [on_device(): lax.all_to_all(geno_b, 'samp', split_axis=1, concat_axis=0, tiled=True)]
    pallas_call x0 -> x2, Pallas kernels: none -> 3.19 us  [the longest x1 1.63 us: on_device(): pl.pallas_call(functools.partial(stat_kernel, genes), out_shape=jax.Shape...]
    gather x7 -> x0, local copies, waits for them, and re-layouts: 2.82 us -> none  [the longest x6 2.21 us: permuted(): picked = whole_y[:, perms[:, sample_ids]]]
    dot_general x2 -> x0, matrix products: 2.12 us -> none  [the longest x1 2 us: on_device(): jnp.einsum('ksi,sj->kij', scaled, part_b, preferred_element_type=jnp.floa...]
    unnamed x5 -> x2, local copies, waits for them, and re-layouts: 1.73 us -> 0.01 us
    select_n x4 -> x0, other arithmetic: 0.72 us -> none  [the longest x2 0.7 us: on_device(): jnp.take(grouped, pairs.reshape(-1), axis=1)]
  transfers between devices with their start and end apart: 1 -> 1, of which waited for: 0 -> 1; matrix products, arithmetic and copies ran while one was open for 8% -> 0% of each run, Pallas kernels for 0% -> 0%
where the time goes in v1:
time: 18.7 us; the launch traced here: 18.5 us
  waiting for transfers between devices  7.92 us (42%)
  starting transfers between devices  7.36 us (39%)
  Pallas kernels  3.19 us (17%)
    all_to_all x1, waiting for transfers between devices, on_device(): lax.all_to_all(messages, ('pair', 'samp'), split_axis=0, concat_axis=0, t...  7.92 us
    all_to_all x1, starting transfers between devices, on_device(): lax.all_to_all(messages, ('pair', 'samp'), split_axis=0, concat_axis=0, t...  7.36 us
    pallas_call x1, Pallas kernels, on_device(): pl.pallas_call(functools.partial(stat_kernel, genes), out_shape=jax.Shape...  1.63 us
    pallas_call x1, Pallas kernels, on_device(): pl.pallas_call(pack_kernel, out_shape=jax.ShapeDtypeStruct((devices, 2 *...  1.55 us
  transfers between devices with their start and end apart: 1, of which 1 were waited for; matrix products, arithmetic and copies ran while one was open for 0% of the time, Pallas kernels for 0%

profile of v1, /device:TPU:0, one launch (start us, length us, event | category | flops | bytes accessed | tf_op | source)
XLA Modules:
  0.0 18.5 jit_solution(13806413767774248342)
XLA Ops:
  0.0 1.6 %pack.1 = bf16[16,32,128]{2,1,0:T(8,128)(2,1)} custom-call(s32[2,8]{1,0:T(2,128)} %bitcast.8, bf16[2,4]{1,0:T(2,128)(2,1)} %pheno_ref.1, bf16[128,128]{1,0:T(8,128)(2,1)} %bitcast.7), custom_call_target="tpu_custom_call" | custom-call | tf_op jit(solution)/shard_map/pack/pallas_call | solution.py:104
  1.6 7.4 %all-to-all-start = ((bf16[16,32,128]{2,1,0:T(8,128)(2,1)}), bf16[16,32,128]{2,1,0:T(8,128)(2,1)S(1)}, u32[]{:S(2)}, u32[]{:S(2)}) async-start(bf16[16,32,128]{2,1,0:T(8,128)(2,1)} %pack.1), calls=%async_computation | async-start | bytes 262144 | tf_op jit(solution)/shard_map/all_to_all | solution.py:111
  8.9 0.0 copy-start
  8.9 7.9 %all-to-all-done.got_ref = bf16[16,32,128]{2,1,0:T(8,128)(2,1)S(1)} async-done(((bf16[16,32,128]{2,1,0:T(8,128)(2,1)}), bf16[16,32,128]{2,1,0:T(8,128)(2,1)S(1)}, u32[]{:S(2)}, u32[]{:S(2)}) %all-to-all-start) | async-done | bytes 131104 | tf_op jit(solution)/shard_map/all_to_all | solution.py:111
  16.9 0.0 copy-done
  16.9 1.6 %stat.1 = bf16[1,4,512,256]{3,2,1,0:T(8,128)(2,1)} custom-call(s32[1]{0:T(128)} %bitcast.half_ref, s32[2,64]{1,0:T(2,128)S(1)} %copy-done, bf16[16,32,128]{2,1,0:T(8,128)(2,1)S(1)} %all-to-all-done.got_ref), custom_call_target="tpu_custom_call" | custom-call | tf_op jit(solution)/shard_map/stat/pallas_call | solution.py:113
Async XLA Ops:
  1.6 15.3 %all-to-all-start = ((bf16[16,32,128]{2,1,0:T(8,128)(2,1)}), bf16[16,32,128]{2,1,0:T(8,128)(2,1)S(1)}, u32[]{:S(2)}, u32[]{:S(2)}) async-start(bf16[16,32,128]{2,1,0:T(8,128)(2,1)} %pack.1), calls=%async_computation | async-start | bytes 262144 | tf_op jit(solution)/shard_map/all_to_all | solution.py:111
  8.9 7.9 %copy-start = (s32[2,64]{1,0:T(2,128)S(1)}, s32[2,64]{1,0:T(2,128)}, u32[]{:S(2)}) copy-start(s32[2,64]{1,0:T(2,128)} %perms_ref.1) | copy-start | bytes 1540

commit v2 on v1

--- a/solution.py
+++ b/solution.py
@@ -1,5 +1,4 @@
 import functools
-import math
 
 import jax
 import jax.numpy as jnp
@@ -13,7 +12,11 @@
 TILE = 16
 
 
-def pack_kernel(pairs_ref, pheno_ref, grid_ref, out_ref):
+def offsets(pair_count, samp_count):
+    return [(p, s) for p in range(pair_count) for s in range(samp_count)]
+
+
+def pack_kernel(counts, place_ref, pairs_ref, pheno_ref, grid_ref, *out_refs):
     genes, s_dev = pheno_ref.shape
     rows = TILE // 2
     pheno = pheno_ref[...].astype(jnp.float32)
@@ -24,25 +27,27 @@
         for s in range(s_dev):
             hit = (lane == g) & (lax.rem(row, rows) == s)
             block = jnp.where(hit, pheno[g : g + 1, s : s + 1], block)
-    upper = row < rows
-
-    @pl.loop(0, pairs_ref.shape[1], unroll=math.gcd(8, pairs_ref.shape[1]))
-    def _(n):
+    for out_ref, (p, s) in zip(out_refs, offsets(*counts)):
+        n = lax.rem(place_ref[0] + p, counts[0])
+        half = lax.rem(place_ref[1] + s, counts[1])
         first = pl.multiple_of(pairs_ref[0, n] * TILE, TILE)
         second = pl.multiple_of(pairs_ref[1, n] * TILE, TILE)
-        panel_a = grid_ref[pl.ds(first, TILE), :]
         panel_b = grid_ref[pl.ds(second, TILE), :].astype(jnp.float32)
-        out_ref[2 * n, 0:TILE, :] = panel_a
-        out_ref[2 * n + 1, 0:TILE, :] = panel_a
-        out_ref[2 * n, TILE : 2 * TILE, :] = jnp.where(upper, panel_b, block).astype(out_ref.dtype)
-        out_ref[2 * n + 1, TILE : 2 * TILE, :] = jnp.where(upper, block, panel_b).astype(out_ref.dtype)
+        mine = row // rows == half
+        out_ref[0:TILE, :] = grid_ref[pl.ds(first, TILE), :]
+        out_ref[TILE : 2 * TILE, :] = jnp.where(mine, panel_b, block).astype(out_ref.dtype)
 
 
-def stat_kernel(genes, half_ref, perms_ref, got_ref, out_ref):
+def stat_kernel(counts, genes, place_ref, perms_ref, *refs):
+    *message_refs, out_ref, got_ref = refs
+    for message_ref, (p, s) in zip(message_refs, offsets(*counts)):
+        source_pair = lax.rem(place_ref[0] + (counts[0] - p), counts[0])
+        source_samp = lax.rem(place_ref[1] + (counts[1] - s), counts[1])
+        got_ref[source_pair * counts[1] + source_samp] = message_ref[...]
     sources = got_ref.shape[0]
     rperms, samples = perms_ref.shape
     s_dev = samples // sources
-    first_half = half_ref[0] == 0
+    first_half = place_ref[1] == 0
 
     def by_samples(tiles, group):
         return tiles[:, group * s_dev : (group + 1) * s_dev, :].reshape(samples, LANES)
@@ -96,28 +101,38 @@
 def on_device(dosage, phenotype, perms, pairs):
     s_dev, snps = dosage.shape
     genes = phenotype.shape[0]
-    devices = lax.axis_size("pair") * lax.axis_size("samp")
-    half = PANEL // lax.axis_size("samp")
+    axes = ("pair", "samp")
+    counts = tuple(lax.axis_size(axis) for axis in axes)
+    devices = counts[0] * counts[1]
+    half = PANEL // counts[1]
     grid = dosage.reshape(s_dev, snps // LANES, LANES).transpose(1, 0, 2).reshape(-1, LANES)
+    place = jnp.stack([lax.axis_index(axis) for axis in axes]).astype(jnp.int32)
     vmem = pl.BlockSpec(memory_space=pltpu.VMEM)
     smem = pl.BlockSpec(memory_space=pltpu.SMEM)
+    message = jax.ShapeDtypeStruct((2 * TILE, LANES), dosage.dtype)
     messages = pl.pallas_call(
-        pack_kernel,
-        out_shape=jax.ShapeDtypeStruct((devices, 2 * TILE, LANES), dosage.dtype),
-        in_specs=[smem, vmem, vmem],
+        functools.partial(pack_kernel, counts),
+        out_shape=[message] * devices,
+        in_specs=[smem, smem, vmem, vmem],
+        out_specs=[vmem] * devices,
+        name="pack",
+    )(place, pairs.T, phenotype, grid)
+    got = []
+    for message, (p, s) in zip(messages, offsets(*counts)):
+        route = [
+            (i * counts[1] + j, (i + p) % counts[0] * counts[1] + (j + s) % counts[1])
+            for i, j in offsets(*counts)
+        ]
+        got.append(message if p == s == 0 else lax.ppermute(message, axes, route))
+    return pl.pallas_call(
+        functools.partial(stat_kernel, counts, genes),
+        out_shape=jax.ShapeDtypeStruct((1, genes * perms.shape[0], PANEL, half), jnp.bfloat16),
+        in_specs=[smem] + [vmem] * (1 + devices),
         out_specs=vmem,
-        name="pack",
-    )(pairs.T, phenotype, grid)
-    got = lax.all_to_all(messages, ("pair", "samp"), split_axis=0, concat_axis=0, tiled=True)
-    which = lax.axis_index("samp").reshape(1).astype(jnp.int32)
-    return pl.pallas_call(
-        functools.partial(stat_kernel, genes),
-        out_shape=jax.ShapeDtypeStruct((1, genes * perms.shape[0], PANEL, half), jnp.bfloat16),
-        in_specs=[smem, vmem, vmem],
-        out_specs=vmem,
+        scratch_shapes=[pltpu.VMEM((devices, 2 * TILE, LANES), dosage.dtype)],
         compiler_params=pltpu.CompilerParams(vmem_limit_bytes=48 * 1024 * 1024),
         name="stat",
-    )(which, perms, got)
+    )(place, perms, *got)
 
 
 def solution(mesh):

time: 18.7 us -> 28.5 us (1.52)
  starting transfers between devices: 7.36 us -> 21.6 us
  waiting for transfers between devices: 7.92 us -> 2.32 us
  Pallas kernels: 3.19 us -> 3.79 us
  other arithmetic: 0 us -> 0.58 us
    ppermute x0 -> x15, starting transfers between devices: none -> 21.6 us  [on_device(): got.append(message if p == s == 0 else lax.ppermute(message, axes, route))]
    all_to_all x1 -> x0, waiting for transfers between devices: 7.92 us -> none  [on_device(): lax.all_to_all(messages, ('pair', 'samp'), split_axis=0, concat_axis=0, t...]
    all_to_all x1 -> x0, starting transfers between devices: 7.36 us -> none  [on_device(): lax.all_to_all(messages, ('pair', 'samp'), split_axis=0, concat_axis=0, t...]
    ppermute x0 -> x15, waiting for transfers between devices: none -> 2.32 us  [on_device(): got.append(message if p == s == 0 else lax.ppermute(message, axes, route))]
    pallas_call x2, Pallas kernels: 3.19 us -> 3.79 us  [the longest x1 2.23 us: on_device(): pl.pallas_call(functools.partial(stat_kernel, counts, genes), out_shape=j...]
    another operation x0 -> x1, other arithmetic: none -> 0.58 us  [on_device(): place = jnp.stack([lax.axis_index(axis) for axis in axes]).astype(jnp.int32)]
  transfers between devices with their start and end apart: 1 -> 15, of which waited for: 1 -> 2; matrix products, arithmetic and copies ran while one was open for 0% -> 0% of each run, Pallas kernels for 0% -> 0%
where the time goes in v2:
time: 28.5 us; the launch traced here: 28.3 us
  starting transfers between devices  21.6 us (76%)
  Pallas kernels  3.79 us (13%)
  waiting for transfers between devices  2.32 us (8%)
  other arithmetic  0.58 us (2%)
    ppermute x15, starting transfers between devices, on_device(): got.append(message if p == s == 0 else lax.ppermute(message, axes, route))  21.6 us
    ppermute x15, waiting for transfers between devices, on_device(): got.append(message if p == s == 0 else lax.ppermute(message, axes, route))  2.32 us
    pallas_call x1, Pallas kernels, on_device(): pl.pallas_call(functools.partial(stat_kernel, counts, genes), out_shape=j...  2.23 us
    pallas_call x1, Pallas kernels, on_device(): pl.pallas_call(functools.partial(pack_kernel, counts), out_shape=[message...  1.56 us
    another operation x1, other arithmetic, on_device(): place = jnp.stack([lax.axis_index(axis) for axis in axes]).astype(jnp.int32)  0.58 us
  transfers between devices with their start and end apart: 15, of which 2 were waited for; matrix products, arithmetic and copies ran while one was open for 0% of the time, Pallas kernels for 0%

profile of v2, /device:TPU:0, one launch (start us, length us, event | category | flops | bytes accessed | tf_op | source)
XLA Modules:
  0.0 28.3 jit_solution(12651214607271443938)
XLA Ops:
  0.0 0.6 %pad_add_fusion.place_ref = s32[2]{0:T(128)} fusion(s32[1]{0:T(128)} %bitcast.1, s32[1]{0:T(128)} %bitcast), kind=kLoop, calls=%fused_computation | loop fusion | flops 2 | bytes 16 | tf_op jit(solution)/shard_map/stack | solution.py:109
  0.6 1.6 %pack.1 = (bf16[32,128]{1,0:T(8,128)(2,1)}, bf16[32,128]{1,0:T(8,128)(2,1)}, bf16[32,128]{1,0:T(8,128)(2,1)}, bf16[32,128]{1,0:T(8,128)(2,1)}, bf16[32,128]{1,0:...) custom-call(s32[2]{0:T(128)} %pad_add_fusion.place_ref, ...), custom_call_target="tpu_custom_call" | custom-call | tf_op jit(solution)/shard_map/pack/pallas_call | solution.py:113
  2.1 0.5 %collective-permute-start = (bf16[32,128]{1,0:T(8,128)(2,1)}, bf16[32,128]{1,0:T(8,128)(2,1)S(1)}, u32[]{:S(2)}, u32[]{:S(2)}) collective-permute-start(bf16[32,128]{1,0:T(8,128)(2,1)} %get-tuple-element.22), channel_id=1, source_target_pairs={{0,1},{1,0},{2,3},{3,2},{4,5},{5,4},{6,7},{7,6},{8,9},{9,8},{10,11... | collective-permute-start | bytes 24584 | tf_op jit(solution)/shard_map/ppermute | solution.py:126
  2.7 2.6 %collective-permute-start.1 = (bf16[32,128]{1,0:T(8,128)(2,1)}, bf16[32,128]{1,0:T(8,128)(2,1)S(1)}, u32[]{:S(2)}, u32[]{:S(2)}) collective-permute-start(bf16[32,128]{1,0:T(8,128)(2,1)} %get-tuple-element.23), channel_id=1, source_target_pairs={{0,2},{1,3},{2,4},{3,5},{4,6},{5,7},{6,8},{7,9},{8,10},{9,11},{10,... | collective-permute-start | bytes 24584 | tf_op jit(solution)/shard_map/ppermute | solution.py:126
  5.2 0.0 copy-start.4
  5.2 1.3 %collective-permute-start.2 = (bf16[32,128]{1,0:T(8,128)(2,1)}, bf16[32,128]{1,0:T(8,128)(2,1)S(1)}, u32[]{:S(2)}, u32[]{:S(2)}) collective-permute-start(bf16[32,128]{1,0:T(8,128)(2,1)} %get-tuple-element.24), channel_id=1, source_target_pairs={{0,3},{1,2},{2,5},{3,4},{4,7},{5,6},{6,9},{7,8},{8,11},{9,10},{10,... | collective-permute-start | bytes 24584 | tf_op jit(solution)/shard_map/ppermute | solution.py:126
  6.5 1.6 %collective-permute-start.3 = (bf16[32,128]{1,0:T(8,128)(2,1)}, bf16[32,128]{1,0:T(8,128)(2,1)S(1)}, u32[]{:S(2)}, u32[]{:S(2)}) collective-permute-start(bf16[32,128]{1,0:T(8,128)(2,1)} %get-tuple-element.25), channel_id=1, source_target_pairs={{0,4},{1,5},{2,6},{3,7},{4,8},{5,9},{6,10},{7,11},{8,12},{9,13},{1... | collective-permute-start | bytes 24584 | tf_op jit(solution)/shard_map/ppermute | solution.py:126
  8.1 1.2 %collective-permute-start.4 = (bf16[32,128]{1,0:T(8,128)(2,1)}, bf16[32,128]{1,0:T(8,128)(2,1)S(1)}, u32[]{:S(2)}, u32[]{:S(2)}) collective-permute-start(bf16[32,128]{1,0:T(8,128)(2,1)} %get-tuple-element.26), channel_id=1, source_target_pairs={{0,5},{1,4},{2,7},{3,6},{4,9},{5,8},{6,11},{7,10},{8,13},{9,12},{1... | collective-permute-start | bytes 24584 | tf_op jit(solution)/shard_map/ppermute | solution.py:126
  9.4 0.0 collective-permute-done.refs_1_
  9.4 1.3 %collective-permute-start.5 = (bf16[32,128]{1,0:T(8,128)(2,1)}, bf16[32,128]{1,0:T(8,128)(2,1)S(1)}, u32[]{:S(2)}, u32[]{:S(2)}) collective-permute-start(bf16[32,128]{1,0:T(8,128)(2,1)} %get-tuple-element.27), channel_id=1, source_target_pairs={{0,6},{1,7},{2,8},{3,9},{4,10},{5,11},{6,12},{7,13},{8,14},{9,15},... | collective-permute-start | bytes 24584 | tf_op jit(solution)/shard_map/ppermute | solution.py:126
  10.6 0.0 collective-permute-done.1.refs_2_
  10.6 0.0 copy-start.3
  10.6 2.2 %collective-permute-start.6 = (bf16[32,128]{1,0:T(8,128)(2,1)}, bf16[32,128]{1,0:T(8,128)(2,1)S(1)}, u32[]{:S(2)}, u32[]{:S(2)}) collective-permute-start(bf16[32,128]{1,0:T(8,128)(2,1)} %get-tuple-element.28), channel_id=1, source_target_pairs={{0,7},{1,6},{2,9},{3,8},{4,11},{5,10},{6,13},{7,12},{8,15},{9,14},... | collective-permute-start | bytes 24584 | tf_op jit(solution)/shard_map/ppermute | solution.py:126
  12.8 0.0 collective-permute-done.2.refs_3_
  12.8 0.0 copy-start
  12.8 0.5 %collective-permute-start.7 = (bf16[32,128]{1,0:T(8,128)(2,1)}, bf16[32,128]{1,0:T(8,128)(2,1)S(1)}, u32[]{:S(2)}, u32[]{:S(2)}) collective-permute-start(bf16[32,128]{1,0:T(8,128)(2,1)} %get-tuple-element.29), channel_id=1, source_target_pairs={{0,8},{1,9},{2,10},{3,11},{4,12},{5,13},{6,14},{7,15},{8,0},{9,1},... | collective-permute-start | bytes 24584 | tf_op jit(solution)/shard_map/ppermute | solution.py:126
  13.3 0.0 collective-permute-done.3.refs_4_
  13.3 2.1 %collective-permute-start.8 = (bf16[32,128]{1,0:T(8,128)(2,1)}, bf16[32,128]{1,0:T(8,128)(2,1)S(1)}, u32[]{:S(2)}, u32[]{:S(2)}) collective-permute-start(bf16[32,128]{1,0:T(8,128)(2,1)} %get-tuple-element.30), channel_id=1, source_target_pairs={{0,9},{1,8},{2,11},{3,10},{4,13},{5,12},{6,15},{7,14},{8,1},{9,0},... | collective-permute-start | bytes 24584 | tf_op jit(solution)/shard_map/ppermute | solution.py:126
  15.4 0.0 collective-permute-done.4.refs_5_
  15.5 1.4 %collective-permute-start.9 = (bf16[32,128]{1,0:T(8,128)(2,1)}, bf16[32,128]{1,0:T(8,128)(2,1)S(1)}, u32[]{:S(2)}, u32[]{:S(2)}) collective-permute-start(bf16[32,128]{1,0:T(8,128)(2,1)} %get-tuple-element.31), channel_id=1, source_target_pairs={{0,10},{1,11},{2,12},{3,13},{4,14},{5,15},{6,0},{7,1},{8,2},{9,3},... | collective-permute-start | bytes 24584 | tf_op jit(solution)/shard_map/ppermute | solution.py:126
  16.8 0.0 collective-permute-done.5.refs_6_
  16.8 1.4 %collective-permute-start.10 = (bf16[32,128]{1,0:T(8,128)(2,1)}, bf16[32,128]{1,0:T(8,128)(2,1)S(1)}, u32[]{:S(2)}, u32[]{:S(2)}) collective-permute-start(bf16[32,128]{1,0:T(8,128)(2,1)} %get-tuple-element.32), channel_id=1, source_target_pairs={{0,11},{1,10},{2,13},{3,12},{4,15},{5,14},{6,1},{7,0},{8,3},{9,2},... | collective-permute-start | bytes 24584 | tf_op jit(solution)/shard_map/ppermute | solution.py:126
  18.3 0.0 collective-permute-done.6.refs_7_
  18.3 2.2 %collective-permute-start.11 = (bf16[32,128]{1,0:T(8,128)(2,1)}, bf16[32,128]{1,0:T(8,128)(2,1)S(1)}, u32[]{:S(2)}, u32[]{:S(2)}) collective-permute-start(bf16[32,128]{1,0:T(8,128)(2,1)} %get-tuple-element.33), channel_id=1, source_target_pairs={{0,12},{1,13},{2,14},{3,15},{4,0},{5,1},{6,2},{7,3},{8,4},{9,5},{1... | collective-permute-start | bytes 24584 | tf_op jit(solution)/shard_map/ppermute | solution.py:126
  20.5 0.0 collective-permute-done.7.refs_8_
  20.5 1.9 %collective-permute-start.12 = (bf16[32,128]{1,0:T(8,128)(2,1)}, bf16[32,128]{1,0:T(8,128)(2,1)S(1)}, u32[]{:S(2)}, u32[]{:S(2)}) collective-permute-start(bf16[32,128]{1,0:T(8,128)(2,1)} %get-tuple-element.34), channel_id=1, source_target_pairs={{0,13},{1,12},{2,15},{3,14},{4,1},{5,0},{6,3},{7,2},{8,5},{9,4},{1... | collective-permute-start | bytes 24584 | tf_op jit(solution)/shard_map/ppermute | solution.py:126
  22.4 0.0 collective-permute-done.8.refs_9_
  22.4 0.0 copy-done.4
  22.4 0.0 collective-permute-start.13
  22.4 0.0 collective-permute-done.9.refs_10_
  22.5 0.0 copy-done.3
  22.5 0.0 copy-start.1
  22.5 0.0 copy-start.2
  22.5 1.3 %collective-permute-start.14 = (bf16[32,128]{1,0:T(8,128)(2,1)S(1)}, bf16[32,128]{1,0:T(8,128)(2,1)S(1)}, u32[]{:S(2)}, u32[]{:S(2)}) collective-permute-start(bf16[32,128]{1,0:T(8,128)(2,1)S(1)} %copy-done.3), channel_id=1, source_target_pairs={{0,15},{1,14},{2,1},{3,0},{4,3},{5,2},{6,5},{7,4},{8,7},{9,6},{10,... | collective-permute-start | bytes 24584 | tf_op jit(solution)/shard_map/ppermute | solution.py:126
  23.8 0.0 collective-permute-done.10.refs_11_
  23.8 0.0 collective-permute-done.11.refs_12_
  23.8 0.2 collective-permute-done.12.refs_13_
  24.0 2.1 %collective-permute-done.13.refs_14_ = bf16[32,128]{1,0:T(8,128)(2,1)S(1)} collective-permute-done((bf16[32,128]{1,0:T(8,128)(2,1)S(1)}, bf16[32,128]{1,0:T(8,128)(2,1)S(1)}, u32[]{:S(2)}, u32[]{:S(2)}) %collective-permute-start.13) | collective-permute-done | bytes 8224 | tf_op jit(solution)/shard_map/ppermute | solution.py:126
  26.1 0.0 collective-permute-done.14.refs_15_
  26.1 0.0 copy-done
  26.1 0.0 copy-done.1
  26.1 0.0 copy-done.2
  26.1 2.2 %stat.1 = bf16[1,4,512,256]{3,2,1,0:T(8,128)(2,1)} custom-call(s32[2]{0:T(128)S(1)} %copy-done.1, s32[2,64]{1,0:T(2,128)S(1)} %copy-done.2, bf16[32,128]{1,0:T(8,128)(2,1)S(1)} %copy-done, bf16[32,128]{1,0:T(8,128)(2,1)S(1)} %collective-permute-done.refs_1_, bf16[32,128]{1,0:T(8,128)(2,1)S(1)} %collective-permute-done.1.refs_2_, ...), custom_call_target="tpu_custom_call" | custom-call | tf_op jit(solution)/shard_map/stat/pallas_call | solution.py:127
Async XLA Ops:
  2.1 7.2 %collective-permute-start = (bf16[32,128]{1,0:T(8,128)(2,1)}, bf16[32,128]{1,0:T(8,128)(2,1)S(1)}, u32[]{:S(2)}, u32[]{:S(2)}) collective-permute-start(bf16[32,128]{1,0:T(8,128)(2,1)} %get-tuple-element.22), channel_id=1, source_target_pairs={{0,1},{1,0},{2,3},{3,2},{4,5},{5,4},{6,7},{7,6},{8,9},{9,8},{10,11... | collective-permute-start | bytes 24584 | tf_op jit(solution)/shard_map/ppermute | solution.py:126
  2.7 8.0 %collective-permute-start.1 = (bf16[32,128]{1,0:T(8,128)(2,1)}, bf16[32,128]{1,0:T(8,128)(2,1)S(1)}, u32[]{:S(2)}, u32[]{:S(2)}) collective-permute-start(bf16[32,128]{1,0:T(8,128)(2,1)} %get-tuple-element.23), channel_id=1, source_target_pairs={{0,2},{1,3},{2,4},{3,5},{4,6},{5,7},{6,8},{7,9},{8,10},{9,11},{10,... | collective-permute-start | bytes 24584 | tf_op jit(solution)/shard_map/ppermute | solution.py:126
  5.2 17.2 %copy-start.4 = (bf16[32,128]{1,0:T(8,128)(2,1)S(1)}, bf16[32,128]{1,0:T(8,128)(2,1)}, u32[]{:S(2)}) copy-start(bf16[32,128]{1,0:T(8,128)(2,1)} %get-tuple-element.35) | copy-start | bytes 24580
  5.2 7.6 %collective-permute-start.2 = (bf16[32,128]{1,0:T(8,128)(2,1)}, bf16[32,128]{1,0:T(8,128)(2,1)S(1)}, u32[]{:S(2)}, u32[]{:S(2)}) collective-permute-start(bf16[32,128]{1,0:T(8,128)(2,1)} %get-tuple-element.24), channel_id=1, source_target_pairs={{0,3},{1,2},{2,5},{3,4},{4,7},{5,6},{6,9},{7,8},{8,11},{9,10},{10,... | collective-permute-start | bytes 24584 | tf_op jit(solution)/shard_map/ppermute | solution.py:126
  6.5 6.8 %collective-permute-start.3 = (bf16[32,128]{1,0:T(8,128)(2,1)}, bf16[32,128]{1,0:T(8,128)(2,1)S(1)}, u32[]{:S(2)}, u32[]{:S(2)}) collective-permute-start(bf16[32,128]{1,0:T(8,128)(2,1)} %get-tuple-element.25), channel_id=1, source_target_pairs={{0,4},{1,5},{2,6},{3,7},{4,8},{5,9},{6,10},{7,11},{8,12},{9,13},{1... | collective-permute-start | bytes 24584 | tf_op jit(solution)/shard_map/ppermute | solution.py:126
  8.1 7.3 %collective-permute-start.4 = (bf16[32,128]{1,0:T(8,128)(2,1)}, bf16[32,128]{1,0:T(8,128)(2,1)S(1)}, u32[]{:S(2)}, u32[]{:S(2)}) collective-permute-start(bf16[32,128]{1,0:T(8,128)(2,1)} %get-tuple-element.26), channel_id=1, source_target_pairs={{0,5},{1,4},{2,7},{3,6},{4,9},{5,8},{6,11},{7,10},{8,13},{9,12},{1... | collective-permute-start | bytes 24584 | tf_op jit(solution)/shard_map/ppermute | solution.py:126
  9.4 7.5 %collective-permute-start.5 = (bf16[32,128]{1,0:T(8,128)(2,1)}, bf16[32,128]{1,0:T(8,128)(2,1)S(1)}, u32[]{:S(2)}, u32[]{:S(2)}) collective-permute-start(bf16[32,128]{1,0:T(8,128)(2,1)} %get-tuple-element.27), channel_id=1, source_target_pairs={{0,6},{1,7},{2,8},{3,9},{4,10},{5,11},{6,12},{7,13},{8,14},{9,15},... | collective-permute-start | bytes 24584 | tf_op jit(solution)/shard_map/ppermute | solution.py:126
  10.6 11.8 %copy-start.3 = (bf16[32,128]{1,0:T(8,128)(2,1)S(1)}, bf16[32,128]{1,0:T(8,128)(2,1)}, u32[]{:S(2)}) copy-start(bf16[32,128]{1,0:T(8,128)(2,1)} %get-tuple-element.36) | copy-start | bytes 24580
  10.6 7.6 %collective-permute-start.6 = (bf16[32,128]{1,0:T(8,128)(2,1)}, bf16[32,128]{1,0:T(8,128)(2,1)S(1)}, u32[]{:S(2)}, u32[]{:S(2)}) collective-permute-start(bf16[32,128]{1,0:T(8,128)(2,1)} %get-tuple-element.28), channel_id=1, source_target_pairs={{0,7},{1,6},{2,9},{3,8},{4,11},{5,10},{6,13},{7,12},{8,15},{9,14},... | collective-permute-start | bytes 24584 | tf_op jit(solution)/shard_map/ppermute | solution.py:126
  12.8 13.3 %copy-start = (bf16[32,128]{1,0:T(8,128)(2,1)S(1)}, bf16[32,128]{1,0:T(8,128)(2,1)}, u32[]{:S(2)}) copy-start(bf16[32,128]{1,0:T(8,128)(2,1)} %get-tuple-element.21.refs_0_) | copy-start | bytes 24580
  12.8 7.7 %collective-permute-start.7 = (bf16[32,128]{1,0:T(8,128)(2,1)}, bf16[32,128]{1,0:T(8,128)(2,1)S(1)}, u32[]{:S(2)}, u32[]{:S(2)}) collective-permute-start(bf16[32,128]{1,0:T(8,128)(2,1)} %get-tuple-element.29), channel_id=1, source_target_pairs={{0,8},{1,9},{2,10},{3,11},{4,12},{5,13},{6,14},{7,15},{8,0},{9,1},... | collective-permute-start | bytes 24584 | tf_op jit(solution)/shard_map/ppermute | solution.py:126
  13.3 9.1 %collective-permute-start.8 = (bf16[32,128]{1,0:T(8,128)(2,1)}, bf16[32,128]{1,0:T(8,128)(2,1)S(1)}, u32[]{:S(2)}, u32[]{:S(2)}) collective-permute-start(bf16[32,128]{1,0:T(8,128)(2,1)} %get-tuple-element.30), channel_id=1, source_target_pairs={{0,9},{1,8},{2,11},{3,10},{4,13},{5,12},{6,15},{7,14},{8,1},{9,0},... | collective-permute-start | bytes 24584 | tf_op jit(solution)/shard_map/ppermute | solution.py:126
  15.5 7.0 %collective-permute-start.9 = (bf16[32,128]{1,0:T(8,128)(2,1)}, bf16[32,128]{1,0:T(8,128)(2,1)S(1)}, u32[]{:S(2)}, u32[]{:S(2)}) collective-permute-start(bf16[32,128]{1,0:T(8,128)(2,1)} %get-tuple-element.31), channel_id=1, source_target_pairs={{0,10},{1,11},{2,12},{3,13},{4,14},{5,15},{6,0},{7,1},{8,2},{9,3},... | collective-permute-start | bytes 24584 | tf_op jit(solution)/shard_map/ppermute | solution.py:126
  16.8 7.0 %collective-permute-start.10 = (bf16[32,128]{1,0:T(8,128)(2,1)}, bf16[32,128]{1,0:T(8,128)(2,1)S(1)}, u32[]{:S(2)}, u32[]{:S(2)}) collective-permute-start(bf16[32,128]{1,0:T(8,128)(2,1)} %get-tuple-element.32), channel_id=1, source_target_pairs={{0,11},{1,10},{2,13},{3,12},{4,15},{5,14},{6,1},{7,0},{8,3},{9,2},... | collective-permute-start | bytes 24584 | tf_op jit(solution)/shard_map/ppermute | solution.py:126
  18.3 5.5 %collective-permute-start.11 = (bf16[32,128]{1,0:T(8,128)(2,1)}, bf16[32,128]{1,0:T(8,128)(2,1)S(1)}, u32[]{:S(2)}, u32[]{:S(2)}) collective-permute-start(bf16[32,128]{1,0:T(8,128)(2,1)} %get-tuple-element.33), channel_id=1, source_target_pairs={{0,12},{1,13},{2,14},{3,15},{4,0},{5,1},{6,2},{7,3},{8,4},{9,5},{1... | collective-permute-start | bytes 24584 | tf_op jit(solution)/shard_map/ppermute | solution.py:126
  20.5 3.5 %collective-permute-start.12 = (bf16[32,128]{1,0:T(8,128)(2,1)}, bf16[32,128]{1,0:T(8,128)(2,1)S(1)}, u32[]{:S(2)}, u32[]{:S(2)}) collective-permute-start(bf16[32,128]{1,0:T(8,128)(2,1)} %get-tuple-element.34), channel_id=1, source_target_pairs={{0,13},{1,12},{2,15},{3,14},{4,1},{5,0},{6,3},{7,2},{8,5},{9,4},{1... | collective-permute-start | bytes 24584 | tf_op jit(solution)/shard_map/ppermute | solution.py:126
  22.4 3.7 %collective-permute-start.13 = (bf16[32,128]{1,0:T(8,128)(2,1)S(1)}, bf16[32,128]{1,0:T(8,128)(2,1)S(1)}, u32[]{:S(2)}, u32[]{:S(2)}) collective-permute-start(bf16[32,128]{1,0:T(8,128)(2,1)S(1)} %copy-done.4), channel_id=1, source_target_pairs={{0,14},{1,15},{2,0},{3,1},{4,2},{5,3},{6,4},{7,5},{8,6},{9,7},{10,... | collective-permute-start | bytes 24584 | tf_op jit(solution)/shard_map/ppermute | solution.py:126
  22.5 3.6 %copy-start.1 = (s32[2]{0:T(128)S(1)}, s32[2]{0:T(128)}, u32[]{:S(2)}) copy-start(s32[2]{0:T(128)} %pad_add_fusion.place_ref) | copy-start | bytes 28
  22.5 3.6 %copy-start.2 = (s32[2,64]{1,0:T(2,128)S(1)}, s32[2,64]{1,0:T(2,128)}, u32[]{:S(2)}) copy-start(s32[2,64]{1,0:T(2,128)} %perms_ref.1) | copy-start | bytes 1540
  22.5 3.6 %collective-permute-start.14 = (bf16[32,128]{1,0:T(8,128)(2,1)S(1)}, bf16[32,128]{1,0:T(8,128)(2,1)S(1)}, u32[]{:S(2)}, u32[]{:S(2)}) collective-permute-start(bf16[32,128]{1,0:T(8,128)(2,1)S(1)} %copy-done.3), channel_id=1, source_target_pairs={{0,15},{1,14},{2,1},{3,0},{4,3},{5,2},{6,5},{7,4},{8,7},{9,6},{10,... | collective-permute-start | bytes 24584 | tf_op jit(solution)/shard_map/ppermute | solution.py:126

commit v3 on v1

v3 whole, which is shorter than its diff:
```python
import functools

import jax
import jax.numpy as jnp
from jax import lax
from jax.experimental import pallas as pl
from jax.experimental.pallas import tpu as pltpu
from jax.sharding import PartitionSpec as P

PANEL = 512
LANES = 128
TILE = 16
BLOCK = 2 * TILE


def steps(pair_count):
    far = [1 << bit for bit in range(1, pair_count.bit_length() - 1)]
    return ([1] if pair_count > 1 else []) + far[::-1]


def distance(index, hops):
    return sum(hop for t, hop in enumerate(reversed(hops)) if index >> t & 1)


def wave_rows(genes, samples):
    return -(-genes * -(-samples // LANES) // TILE) * TILE


def pack_kernel(hops, samps, me_ref, pairs_ref, pheno_ref, grid_ref, keep_ref, send_ref, wave_ref):
    genes, s_dev = pheno_ref.shape
    me = me_ref[0]
    pair = lax.div(me, samps)
    half = keep_ref.shape[0]

    rows = wave_ref.shape[0]
    tiles = -(-s_dev * samps * 2 * half // LANES)
    pheno = pheno_ref[...].astype(jnp.float32)
    row = lax.broadcasted_iota(jnp.int32, (rows, LANES), 0)
    lane = lax.broadcasted_iota(jnp.int32, (rows, LANES), 1)
    wave = jnp.zeros((rows, LANES), jnp.float32)
    first_lane = lax.rem(me * s_dev, LANES)
    tile = lax.div(me * s_dev, LANES)
    for g in range(genes):
        for s in range(s_dev):
            hit = (lane == first_lane + s) & (row == g * tiles + tile)
            wave = jnp.where(hit, pheno[g : g + 1, s : s + 1], wave)
    wave_ref[...] = wave.astype(wave_ref.dtype)

    for j in range(2 * half):
        n = lax.bitwise_xor(pair, distance(j, hops))
        first = pl.multiple_of(pairs_ref[0, n] * TILE, TILE)
        second = pl.multiple_of(pairs_ref[1, n] * TILE, TILE)
        panel_a = grid_ref[pl.ds(first, TILE), :]
        panel_b = grid_ref[pl.ds(second, TILE), :]
        if j < half:
            keep_ref[j, 0:TILE, :] = panel_a
            keep_ref[j, TILE:BLOCK, :] = panel_b
        else:
            start = (j - half) * BLOCK
            send_ref[start : start + TILE, :] = panel_a
            send_ref[start + TILE : start + BLOCK, :] = panel_b
    send_ref[half * BLOCK :, :] = wave.astype(send_ref.dtype)


def stat_kernel(hops, samps, genes, me_ref, perms_ref, own_ref, other_ref, out_ref, got_ref):
    me = me_ref[0]
    pair = lax.div(me, samps)
    samp = lax.rem(me, samps)
    sources = got_ref.shape[0]
    pair_count = sources // samps
    for i in range(pair_count):
        source = lax.bitwise_xor(pair, distance(i, hops[::-1])) * samps
        rows = slice(i * BLOCK, (i + 1) * BLOCK)
        got_ref[source + samp] = own_ref[rows, :]
        got_ref[source + (samps - 1 - samp)] = other_ref[rows, :]
    rperms, samples = perms_ref.shape
    s_dev = samples // sources

    def by_samples(tiles, group):
        return tiles[:, group * s_dev : (group + 1) * s_dev, :].reshape(samples, LANES)

    panel_a = got_ref[:, 0:TILE, :].astype(jnp.float32)
    panel_b = got_ref[:, TILE:BLOCK, :].astype(jnp.float32)
    tile_b = jnp.where(samp == 0, panel_b[:, : TILE // 2], panel_b[:, TILE // 2 :])

    count = jnp.float32(samples)
    geno_b = jnp.concatenate([by_samples(tile_b, q) for q in range(TILE // 2 // s_dev)], axis=1)
    marg_b = jnp.sum(geno_b, axis=0, keepdims=True)
    centred = (geno_b - marg_b / count) * (samples**-0.5)
    b_hi = centred.astype(jnp.bfloat16)
    b_lo = (centred - b_hi.astype(jnp.float32)).astype(jnp.bfloat16)
    b_both = jnp.concatenate([b_hi, b_lo], axis=0)

    wave = own_ref[pair_count * BLOCK :, :].astype(jnp.float32)
    wave = wave + other_ref[pair_count * BLOCK :, :].astype(jnp.float32)
    tiles = -(-samples // LANES)
    pheno = [
        jnp.concatenate([wave[g * tiles + t : g * tiles + t + 1] for t in range(tiles)], axis=1)[:, :samples]
        for g in range(genes)
    ]
    pheno = jnp.concatenate(pheno, axis=0).astype(jnp.bfloat16)
    perms = perms_ref[...]
    twice = jnp.concatenate([perms, perms], axis=1)
    sample = lax.broadcasted_iota(jnp.int32, (samples, 2 * samples), 0)
    permuted = []
    for r in range(rperms):
        chosen = jnp.where(sample == twice[r : r + 1, :], 1.0, 0.0).astype(jnp.bfloat16)
        permuted.append(jnp.dot(pheno, chosen, preferred_element_type=jnp.float32))
    yrows = [permuted[r][g : g + 1] for g in range(genes) for r in range(rperms)]
    yall = jnp.concatenate(yrows, axis=0)
    tail = jnp.dot(yall.astype(jnp.bfloat16), b_both, preferred_element_type=jnp.float32) / count
    c_hi = tail.astype(jnp.bfloat16).astype(jnp.float32)
    c_lo = tail - c_hi

    geno_a = jnp.concatenate([by_samples(panel_a, q) for q in range(TILE // s_dev)], axis=1)
    a_rows = jnp.concatenate([geno_a, geno_a], axis=0).T
    a_minus = -a_rows.astype(jnp.bfloat16)
    for k in range(len(yrows)):
        scaled = (a_rows * yrows[k]).astype(jnp.bfloat16)
        left = jnp.concatenate([scaled, a_minus], axis=1)
        tails = [jnp.broadcast_to(c[k : k + 1], geno_b.shape).astype(jnp.bfloat16) for c in (c_hi, c_lo)]
        right = jnp.concatenate([b_both] + tails, axis=0)
        out_ref[0, k] = jnp.dot(left, right, preferred_element_type=jnp.float32).astype(out_ref.dtype)


def on_device(dosage, phenotype, perms, pairs):
    s_dev, snps = dosage.shape
    genes = phenotype.shape[0]
    samples = perms.shape[1]
    axes = ("pair", "samp")
    pair_count, samps = (lax.axis_size(axis) for axis in axes)
    hops = steps(pair_count)
    half = pair_count // 2
    rows = wave_rows(genes, samples)
    me = lax.axis_index(axes).astype(jnp.int32).reshape(1)
    grid = dosage.reshape(s_dev, snps // LANES, LANES).transpose(1, 0, 2).reshape(-1, LANES)
    vmem = pl.BlockSpec(memory_space=pltpu.VMEM)
    smem = pl.BlockSpec(memory_space=pltpu.SMEM)

    def array(*shape):
        return jax.ShapeDtypeStruct(shape, dosage.dtype)

    keep, send, wave = pl.pallas_call(
        functools.partial(pack_kernel, hops, samps),
        out_shape=[array(half, BLOCK, LANES), array(half * BLOCK + rows, LANES), array(rows, LANES)],
        in_specs=[smem, smem, vmem, vmem],
        out_specs=[vmem, vmem, vmem],
        compiler_params=pltpu.CompilerParams(vmem_limit_bytes=8 * 1024 * 1024),
        name="pack",
    )(me, pairs.T, phenotype, grid)

    held = [keep]
    for t, hop in enumerate(hops):
        route = [(i, i ^ hop) for i in range(pair_count)]
        left = pair_count >> (t + 1)
        if t > 0:
            send = jnp.concatenate([h[left:].reshape(-1, LANES) for h in held] + [wave], axis=0)
            held = [h[:left] for h in held]
        got = lax.ppermute(send, "pair", route)
        blocks = got[: half * BLOCK].reshape(len(held), left, BLOCK, LANES)
        held = held + [blocks[i] for i in range(len(held))]
        wave = wave + got[half * BLOCK :]
    own = jnp.concatenate([h.reshape(-1, LANES) for h in held] + [wave], axis=0)
    other = lax.ppermute(own, "samp", [(i, samps - 1 - i) for i in range(samps)])
    return pl.pallas_call(
        functools.partial(stat_kernel, hops, samps, genes),
        out_shape=jax.ShapeDtypeStruct((1, genes * perms.shape[0], PANEL, PANEL // samps), jnp.bfloat16),
        in_specs=[smem, vmem, vmem, vmem],
        out_specs=vmem,
        scratch_shapes=[pltpu.VMEM((pair_count * samps, BLOCK, LANES), dosage.dtype)],
        compiler_params=pltpu.CompilerParams(vmem_limit_bytes=48 * 1024 * 1024),
        name="stat",
    )(me, perms, own, other)


def solution(mesh):
    placed = (P(("rep", "pair", "samp"), None), P(None, ("rep", "pair", "samp")), P(), P())
    return jax.shard_map(
        on_device,
        mesh=mesh,
        in_specs=placed,
        out_specs=P(("rep", "pair"), None, None, "samp"),
        check_vma=False,
    )
```

time: 18.7 us -> 19.5 us (1.043)
  local copies, waits for them, and re-layouts: 0.01 us -> 1.48 us
  starting transfers between devices: 7.36 us -> 8.23 us
  Pallas kernels: 3.19 us -> 2.38 us
  waiting for transfers between devices: 7.92 us -> 7.16 us
    ppermute x0 -> x4, starting transfers between devices: none -> 8.23 us  [the longest x3 8.15 us: on_device(): got = lax.ppermute(send, 'pair', route)]
    all_to_all x1 -> x0, waiting for transfers between devices: 7.92 us -> none  [on_device(): lax.all_to_all(messages, ('pair', 'samp'), split_axis=0, concat_axis=0, t...]
    all_to_all x1 -> x0, starting transfers between devices: 7.36 us -> none  [on_device(): lax.all_to_all(messages, ('pair', 'samp'), split_axis=0, concat_axis=0, t...]
    ppermute x0 -> x4, waiting for transfers between devices: none -> 7.16 us  [the longest x3 5.91 us: on_device(): got = lax.ppermute(send, 'pair', route)]
    unnamed x2 -> x13, local copies, waits for them, and re-layouts: 0.01 us -> 1.48 us
    pallas_call x2, Pallas kernels: 3.19 us -> 2.38 us  [the longest x1 1.72 us: on_device(): pl.pallas_call(functools.partial(stat_kernel, hops, samps, genes), out_sh...]
  transfers between devices with their start and end apart: 1 -> 4, of which waited for: 1 -> 4; matrix products, arithmetic and copies ran while one was open for 0% -> 0% of each run, Pallas kernels for 0% -> 0%
where the time goes in v3:
time: 19.5 us; the launch traced here: 19.3 us
  starting transfers between devices  8.23 us (42%)
  waiting for transfers between devices  7.16 us (37%)
  Pallas kernels  2.38 us (12%)
  local copies, waits for them, and re-layouts  1.48 us (8%)
    ppermute x3, starting transfers between devices, on_device(): got = lax.ppermute(send, 'pair', route)  8.15 us
    ppermute x3, waiting for transfers between devices, on_device(): got = lax.ppermute(send, 'pair', route)  5.91 us
    pallas_call x1, Pallas kernels, on_device(): pl.pallas_call(functools.partial(stat_kernel, hops, samps, genes), out_sh...  1.72 us
    unnamed x13, local copies, waits for them, and re-layouts  1.48 us
    ppermute x1, waiting for transfers between devices, on_device(): lax.ppermute(own, 'samp', [(i, samps - 1 - i) for i in range(samps)])  1.25 us
    pallas_call x1, Pallas kernels, on_device(): pl.pallas_call(functools.partial(pack_kernel, hops, samps), out_shape=[ar...  0.66 us
  transfers between devices with their start and end apart: 4, of which 4 were waited for; matrix products, arithmetic and copies ran while one was open for 0% of the time, Pallas kernels for 0%

profile of v3, /device:TPU:0, one launch (start us, length us, event | category | flops | bytes accessed | tf_op | source)
XLA Modules:
  0.0 19.3 jit_solution(7736645291862149496)
XLA Ops:
  0.0 0.0 copy-start.2
  0.0 0.0 copy-start.3
  0.0 0.7 %copy-done.2 = s32[8,2]{0,1:T(2,128)S(1)} copy-done((s32[8,2]{0,1:T(2,128)S(1)}, s32[8,2]{0,1:T(2,128)}, u32[]{:S(2)}) %copy-start.2) | copy-done | bytes 88
  0.7 0.0 copy-done.3
  0.7 0.0 copy-start
  0.7 0.8 %copy-done = bf16[4,4096]{1,0:T(4,128)(2,1)S(1)} copy-done((bf16[4,4096]{1,0:T(4,128)(2,1)S(1)}, bf16[4,4096]{1,0:T(4,128)(2,1)}, u32[]{:S(2)}) %copy-start) | copy-done | bytes 32792
  1.4 0.7 %pack.1 = (bf16[4,32,128]{2,1,0:T(8,128)(2,1)S(1)}, bf16[144,128]{1,0:T(8,128)(2,1)S(1)}, bf16[16,128]{1,0:T(8,128)(2,1)S(1)}) custom-call(s32[1]{0:T(128)} %bitcast.me_ref, s32[2,8]{1,0:T(2,128)S(1)} %bitcast.13, bf16[2,4]{1,0:T(2,128)(2,1)S(1)} %copy-done.3, bf16[128,128]{1,0:T(8,128)(2,1)S(1)} %bitcast.12), custom_call_target="tpu_custom_call" | custom-call | tf_op jit(solution)/shard_map/pack/pallas_call | solution.py:143
  2.1 3.0 %collective-permute-start = (bf16[144,128]{1,0:T(8,128)(2,1)S(1)}, bf16[144,128]{1,0:T(8,128)(2,1)S(1)}, u32[]{:S(2)}, u32[]{:S(2)}) collective-permute-start(bf16[144,128]{1,0:T(8,128)(2,1)S(1)} %get-tuple-element.9), channel_id=1, source_target_pairs={{0,2},{2,0},{4,6},{6,4},{8,10},{10,8},{12,14},{14,12},{1,3},{3,1},... | collective-permute-start | bytes 110600 | tf_op jit(solution)/shard_map/ppermute | solution.py:159
  5.1 1.9 %collective-permute-done = bf16[144,128]{1,0:T(8,128)(2,1)S(1)} collective-permute-done((bf16[144,128]{1,0:T(8,128)(2,1)S(1)}, bf16[144,128]{1,0:T(8,128)(2,1)S(1)}, u32[]{:S(2)}, u32[]{:S(2)}) %collective-permute-start) | collective-permute-done | bytes 36896 | tf_op jit(solution)/shard_map/ppermute | solution.py:159
  7.1 3.2 %collective-permute-start.1 = (bf16[144,128]{1,0:T(8,128)(2,1)S(1)}, bf16[144,128]{1,0:T(8,128)(2,1)S(1)}, u32[]{:S(2)}, u32[]{:S(2)}) collective-permute-start(bf16[144,128]{1,0:T(8,128)(2,1)S(1)} %pad_maximum_fusion), channel_id=1, source_target_pairs={{0,8},{2,10},{4,12},{6,14},{8,0},{10,2},{12,4},{14,6},{1,9},{3,11}... | collective-permute-start | bytes 110600 | tf_op jit(solution)/shard_map/ppermute | solution.py:159
  10.3 1.9 %collective-permute-done.1 = bf16[144,128]{1,0:T(8,128)(2,1)S(1)} collective-permute-done((bf16[144,128]{1,0:T(8,128)(2,1)S(1)}, bf16[144,128]{1,0:T(8,128)(2,1)S(1)}, u32[]{:S(2)}, u32[]{:S(2)}) %collective-permute-start.1) | collective-permute-done | bytes 36896 | tf_op jit(solution)/shard_map/ppermute | solution.py:159
  12.2 2.0 %collective-permute-start.2 = (bf16[144,128]{1,0:T(8,128)(2,1)S(1)}, bf16[144,128]{1,0:T(8,128)(2,1)S(1)}, u32[]{:S(2)}, u32[]{:S(2)}) collective-permute-start(bf16[144,128]{1,0:T(8,128)(2,1)S(1)} %constant_dynamic-update-slice_fusion), channel_id=1, source_target_pairs={{0,4},{2,6},{4,0},{6,2},{8,12},{10,14},{12,8},{14,10},{1,5},{3,7},... | collective-permute-start | bytes 110600 | tf_op jit(solution)/shard_map/ppermute | solution.py:159
  14.2 2.1 %collective-permute-done.2 = bf16[144,128]{1,0:T(8,128)(2,1)S(1)} collective-permute-done((bf16[144,128]{1,0:T(8,128)(2,1)S(1)}, bf16[144,128]{1,0:T(8,128)(2,1)S(1)}, u32[]{:S(2)}, u32[]{:S(2)}) %collective-permute-start.2) | collective-permute-done | bytes 36896 | tf_op jit(solution)/shard_map/ppermute | solution.py:159
  16.2 0.0 copy-start.1
  16.3 0.1 collective-permute-start.3
  16.3 1.2 %collective-permute-done.3.other_ref = bf16[272,128]{1,0:T(8,128)(2,1)S(1)} collective-permute-done((bf16[272,128]{1,0:T(8,128)(2,1)S(1)}, bf16[272,128]{1,0:T(8,128)(2,1)S(1)}, u32[]{:S(2)}, u32[]{:S(2)}) %collective-permute-start.3) | collective-permute-done | bytes 69664 | tf_op jit(solution)/shard_map/ppermute | solution.py:164
  17.6 0.0 copy-done.1
  17.6 1.7 %stat.1 = bf16[1,4,512,256]{3,2,1,0:T(8,128)(2,1)} custom-call(s32[1]{0:T(128)} %bitcast.me_ref, s32[2,64]{1,0:T(2,128)S(1)} %copy-done.1, bf16[272,128]{1,0:T(8,128)(2,1)S(1)} %constant_dynamic-update-slice_fusion.5.own_ref, bf16[272,128]{1,0:T(8,128)(2,1)S(1)} %collective-permute-done.3.other_ref), custom_call_target="tpu_custom_call" | custom-call | tf_op jit(solution)/shard_map/stat/pallas_call | solution.py:165
  (11 shorter events, 0.1 us)
Async XLA Ops:
  0.0 0.7 %copy-start.2 = (s32[8,2]{0,1:T(2,128)S(1)}, s32[8,2]{0,1:T(2,128)}, u32[]{:S(2)}) copy-start(s32[8,2]{0,1:T(2,128)} %param.7) | copy-start | bytes 196
  0.0 0.7 %copy-start.3 = (bf16[2,4]{1,0:T(2,128)(2,1)S(1)}, bf16[2,4]{1,0:T(2,128)(2,1)}, u32[]{:S(2)}) copy-start(bf16[2,4]{1,0:T(2,128)(2,1)} %pheno_ref.1) | copy-start | bytes 52
  0.7 0.8 %copy-start = (bf16[4,4096]{1,0:T(4,128)(2,1)S(1)}, bf16[4,4096]{1,0:T(4,128)(2,1)}, u32[]{:S(2)}) copy-start(bf16[4,4096]{1,0:T(4,128)(2,1)} %param.4) | copy-start | bytes 98308
  2.1 4.9 %collective-permute-start = (bf16[144,128]{1,0:T(8,128)(2,1)S(1)}, bf16[144,128]{1,0:T(8,128)(2,1)S(1)}, u32[]{:S(2)}, u32[]{:S(2)}) collective-permute-start(bf16[144,128]{1,0:T(8,128)(2,1)S(1)} %get-tuple-element.9), channel_id=1, source_target_pairs={{0,2},{2,0},{4,6},{6,4},{8,10},{10,8},{12,14},{14,12},{1,3},{3,1},... | collective-permute-start | bytes 110600 | tf_op jit(solution)/shard_map/ppermute | solution.py:159
  7.1 5.1 %collective-permute-start.1 = (bf16[144,128]{1,0:T(8,128)(2,1)S(1)}, bf16[144,128]{1,0:T(8,128)(2,1)S(1)}, u32[]{:S(2)}, u32[]{:S(2)}) collective-permute-start(bf16[144,128]{1,0:T(8,128)(2,1)S(1)} %pad_maximum_fusion), channel_id=1, source_target_pairs={{0,8},{2,10},{4,12},{6,14},{8,0},{10,2},{12,4},{14,6},{1,9},{3,11}... | collective-permute-start | bytes 110600 | tf_op jit(solution)/shard_map/ppermute | solution.py:159
  12.2 4.0 %collective-permute-start.2 = (bf16[144,128]{1,0:T(8,128)(2,1)S(1)}, bf16[144,128]{1,0:T(8,128)(2,1)S(1)}, u32[]{:S(2)}, u32[]{:S(2)}) collective-permute-start(bf16[144,128]{1,0:T(8,128)(2,1)S(1)} %constant_dynamic-update-slice_fusion), channel_id=1, source_target_pairs={{0,4},{2,6},{4,0},{6,2},{8,12},{10,14},{12,8},{14,10},{1,5},{3,7},... | collective-permute-start | bytes 110600 | tf_op jit(solution)/shard_map/ppermute | solution.py:159
  16.2 1.3 %copy-start.1 = (s32[2,64]{1,0:T(2,128)S(1)}, s32[2,64]{1,0:T(2,128)}, u32[]{:S(2)}) copy-start(s32[2,64]{1,0:T(2,128)} %perms_ref.1) | copy-start | bytes 1540
  16.3 1.3 %collective-permute-start.3 = (bf16[272,128]{1,0:T(8,128)(2,1)S(1)}, bf16[272,128]{1,0:T(8,128)(2,1)S(1)}, u32[]{:S(2)}, u32[]{:S(2)}) collective-permute-start(bf16[272,128]{1,0:T(8,128)(2,1)S(1)} %constant_dynamic-update-slice_fusion.5.own_ref), channel_id=1, source_target_pairs={{0,1},{1,0},{2,3},{3,2},{4,5},{5,4},{6,7},{7,6},{8,9},{9,8},{10,11... | collective-permute-start | bytes 208904 | tf_op jit(solution)/shard_map/ppermute | solution.py:164

commit v4 on v3

v4 whole, which is shorter than its diff:
```python
import functools

import jax
import jax.numpy as jnp
from jax import lax
from jax.experimental import pallas as pl
from jax.experimental.pallas import tpu as pltpu
from jax.sharding import PartitionSpec as P

PANEL = 512
LANES = 128
TILE = 16
BLOCK = 2 * TILE


def offset(pair_count, core, i):
    return pair_count - 2 - 2 * i + core


def wave_rows(genes, samples):
    return -(-genes * -(-samples // LANES) // TILE) * TILE


def pack_kernel(pair_count, samps, me_ref, pairs_ref, pheno_ref, mate_pheno_ref, grid_ref, mate_grid_ref, *out_refs):
    genes, s_dev = pheno_ref.shape
    me = me_ref[0]
    pair = lax.div(me, samps)
    samp = lax.rem(me, samps)

    rows = out_refs[0].shape[0] - samps * BLOCK
    tiles = -(-s_dev * samps * pair_count // LANES)
    row = lax.broadcasted_iota(jnp.int32, (rows, LANES), 0)
    lane = lax.broadcasted_iota(jnp.int32, (rows, LANES), 1)
    wave = jnp.zeros((rows, LANES), jnp.float32)
    for ref, core in ((pheno_ref, samp), (mate_pheno_ref, samps - 1 - samp)):
        pheno = ref[...].astype(jnp.float32)
        spot = (pair * samps + core) * s_dev
        first = lax.rem(spot, LANES)
        tile = lax.div(spot, LANES)
        for g in range(genes):
            for s in range(s_dev):
                hit = (lane == first + s) & (row == g * tiles + tile)
                wave = jnp.where(hit, pheno[g : g + 1, s : s + 1], wave)
    wave = wave.astype(out_refs[0].dtype)

    for i, out_ref in enumerate(out_refs):
        n = lax.bitwise_xor(pair, offset(pair_count, samp, i))
        first = pl.multiple_of(pairs_ref[0, n] * TILE, TILE)
        second = pl.multiple_of(pairs_ref[1, n] * TILE, TILE)
        for core, ref in enumerate((grid_ref, mate_grid_ref)):
            out_ref[core * BLOCK : core * BLOCK + TILE, :] = ref[pl.ds(first, TILE), :]
            out_ref[core * BLOCK + TILE : (core + 1) * BLOCK, :] = ref[pl.ds(second, TILE), :]
        out_ref[samps * BLOCK :, :] = wave


def stat_kernel(samps, genes, me_ref, perms_ref, own_ref, mate_ref, out_ref, got_ref):
    me = me_ref[0]
    pair = lax.div(me, samps)
    samp = lax.rem(me, samps)
    sources = got_ref.shape[0]
    pair_count = sources // samps
    size = samps * BLOCK
    for ref, core in ((own_ref, samp), (mate_ref, samps - 1 - samp)):
        for i in range(pair_count // samps):
            source = lax.bitwise_xor(pair, offset(pair_count, core, i)) * samps
            got_ref[source + core] = ref[i * size : i * size + BLOCK, :]
            got_ref[source + (samps - 1 - core)] = ref[i * size + BLOCK : (i + 1) * size, :]
    end = pair_count // samps * size
    rperms, samples = perms_ref.shape
    s_dev = samples // sources

    def by_samples(tiles, group):
        return tiles[:, group * s_dev : (group + 1) * s_dev, :].reshape(samples, LANES)

    panel_a = got_ref[:, 0:TILE, :].astype(jnp.float32)
    panel_b = got_ref[:, TILE:BLOCK, :].astype(jnp.float32)
    tile_b = jnp.where(samp == 0, panel_b[:, : TILE // 2], panel_b[:, TILE // 2 :])

    count = jnp.float32(samples)
    geno_b = jnp.concatenate([by_samples(tile_b, q) for q in range(TILE // 2 // s_dev)], axis=1)
    marg_b = jnp.sum(geno_b, axis=0, keepdims=True)
    centred = (geno_b - marg_b / count) * (samples**-0.5)
    b_hi = centred.astype(jnp.bfloat16)
    b_lo = (centred - b_hi.astype(jnp.float32)).astype(jnp.bfloat16)
    b_both = jnp.concatenate([b_hi, b_lo], axis=0)

    wave = own_ref[end:, :].astype(jnp.float32)
    wave = wave + mate_ref[end:, :].astype(jnp.float32)
    tiles = -(-samples // LANES)
    pheno = [
        jnp.concatenate([wave[g * tiles + t : g * tiles + t + 1] for t in range(tiles)], axis=1)[:, :samples]
        for g in range(genes)
    ]
    pheno = jnp.concatenate(pheno, axis=0).astype(jnp.bfloat16)
    perms = perms_ref[...]
    twice = jnp.concatenate([perms, perms], axis=1)
    sample = lax.broadcasted_iota(jnp.int32, (samples, 2 * samples), 0)
    permuted = []
    for r in range(rperms):
        chosen = jnp.where(sample == twice[r : r + 1, :], 1.0, 0.0).astype(jnp.bfloat16)
        permuted.append(jnp.dot(pheno, chosen, preferred_element_type=jnp.float32))
    yrows = [permuted[r][g : g + 1] for g in range(genes) for r in range(rperms)]
    yall = jnp.concatenate(yrows, axis=0)
    tail = jnp.dot(yall.astype(jnp.bfloat16), b_both, preferred_element_type=jnp.float32) / count
    c_hi = tail.astype(jnp.bfloat16).astype(jnp.float32)
    c_lo = tail - c_hi

    geno_a = jnp.concatenate([by_samples(panel_a, q) for q in range(TILE // s_dev)], axis=1)
    a_rows = jnp.concatenate([geno_a, geno_a], axis=0).T
    a_minus = -a_rows.astype(jnp.bfloat16)
    for k in range(len(yrows)):
        scaled = (a_rows * yrows[k]).astype(jnp.bfloat16)
        left = jnp.concatenate([scaled, a_minus], axis=1)
        tails = [jnp.broadcast_to(c[k : k + 1], geno_b.shape).astype(jnp.bfloat16) for c in (c_hi, c_lo)]
        right = jnp.concatenate([b_both] + tails, axis=0)
        out_ref[0, k] = jnp.dot(left, right, preferred_element_type=jnp.float32).astype(out_ref.dtype)


def on_device(dosage, phenotype, perms, pairs):
    s_dev, snps = dosage.shape
    genes = phenotype.shape[0]
    samples = perms.shape[1]
    axes = ("pair", "samp")
    pair_count, samps = (lax.axis_size(axis) for axis in axes)
    size = samps * BLOCK
    me = lax.axis_index(axes).astype(jnp.int32).reshape(1)
    swap = [(i, samps - 1 - i) for i in range(samps)]
    mate_dosage = lax.ppermute(dosage, "samp", swap)
    mate_pheno = lax.ppermute(phenotype, "samp", swap)

    def grid(x):
        return x.reshape(s_dev, snps // LANES, LANES).transpose(1, 0, 2).reshape(-1, LANES)

    vmem = pl.BlockSpec(memory_space=pltpu.VMEM)
    smem = pl.BlockSpec(memory_space=pltpu.SMEM)
    message = jax.ShapeDtypeStruct((size + wave_rows(genes, samples), LANES), dosage.dtype)
    messages = pl.pallas_call(
        functools.partial(pack_kernel, pair_count, samps),
        out_shape=[message] * (pair_count // samps),
        in_specs=[smem, smem, vmem, vmem, vmem, vmem],
        out_specs=[vmem] * (pair_count // samps),
        compiler_params=pltpu.CompilerParams(vmem_limit_bytes=8 * 1024 * 1024),
        name="pack",
    )(me, pairs.T, phenotype, mate_pheno, grid(dosage), grid(mate_dosage))

    got = []
    for i, message in enumerate(messages):
        route = [
            (p * samps + c, (p ^ offset(pair_count, c, i)) * samps + c)
            for p in range(pair_count)
            for c in range(samps)
        ]
        got.append(lax.ppermute(message, axes, route))
    own = jnp.concatenate([g[:size] for g in got] + [sum(g[size:] for g in got)], axis=0)
    mate = lax.ppermute(own, "samp", swap)
    return pl.pallas_call(
        functools.partial(stat_kernel, samps, genes),
        out_shape=jax.ShapeDtypeStruct((1, genes * perms.shape[0], PANEL, PANEL // samps), jnp.bfloat16),
        in_specs=[smem, vmem, vmem, vmem],
        out_specs=vmem,
        scratch_shapes=[pltpu.VMEM((pair_count * samps, BLOCK, LANES), dosage.dtype)],
        compiler_params=pltpu.CompilerParams(vmem_limit_bytes=48 * 1024 * 1024),
        name="stat",
    )(me, perms, own, mate)


def solution(mesh):
    placed = (P(("rep", "pair", "samp"), None), P(None, ("rep", "pair", "samp")), P(), P())
    return jax.shard_map(
        on_device,
        mesh=mesh,
        in_specs=placed,
        out_specs=P(("rep", "pair"), None, None, "samp"),
        check_vma=False,
    )
```

time: 19.5 us -> 18.2 us (0.933)
  waiting for transfers between devices: 7.16 us -> 5.66 us
  starting transfers between devices: 8.23 us -> 8.43 us
    ppermute x4 -> x7, waiting for transfers between devices: 7.16 us -> 5.66 us  [the longest x4 3.55 us: on_device(): got.append(lax.ppermute(message, axes, route))]
    ppermute x4 -> x7, starting transfers between devices: 8.23 us -> 8.43 us  [the longest x4 6.16 us: on_device(): got.append(lax.ppermute(message, axes, route))]
    unnamed x13 -> x12, local copies, waits for them, and re-layouts: 1.48 us -> 1.47 us
  transfers between devices with their start and end apart: 4 -> 7, of which waited for: 4 -> 4; matrix products, arithmetic and copies ran while one was open for 0% -> 0% of each run, Pallas kernels for 0% -> 0%
where the time goes in v4:
time: 18.2 us; the launch traced here: 18 us
  starting transfers between devices  8.43 us (46%)
  waiting for transfers between devices  5.66 us (31%)
  Pallas kernels  2.39 us (13%)
  local copies, waits for them, and re-layouts  1.47 us (8%)
    ppermute x4, starting transfers between devices, on_device(): got.append(lax.ppermute(message, axes, route))  6.16 us
    ppermute x4, waiting for transfers between devices, on_device(): got.append(lax.ppermute(message, axes, route))  3.55 us
    ppermute x1, starting transfers between devices, on_device(): mate = lax.ppermute(own, 'samp', swap)  1.76 us
    pallas_call x1, Pallas kernels, on_device(): pl.pallas_call(functools.partial(stat_kernel, samps, genes), out_shape=ja...  1.72 us
    unnamed x12, local copies, waits for them, and re-layouts  1.47 us
    ppermute x1, waiting for transfers between devices, on_device(): mate_pheno = lax.ppermute(phenotype, 'samp', swap)  1.2 us
    ppermute x1, waiting for transfers between devices, on_device(): mate = lax.ppermute(own, 'samp', swap)  0.91 us
    pallas_call x1, Pallas kernels, on_device(): pl.pallas_call(functools.partial(pack_kernel, pair_count, samps), out_sha...  0.67 us
  transfers between devices with their start and end apart: 7, of which 4 were waited for; matrix products, arithmetic and copies ran while one was open for 0% of the time, Pallas kernels for 0%

profile of v4, /device:TPU:0, one launch (start us, length us, event | category | flops | bytes accessed | tf_op | source)
XLA Modules:
  0.0 18.0 jit_solution(18429128036126670889)
XLA Ops:
  0.0 0.5 %collective-permute-start.1 = (bf16[4,4096]{1,0:T(4,128)(2,1)}, bf16[4,4096]{1,0:T(4,128)(2,1)S(1)}, u32[]{:S(2)}, u32[]{:S(2)}) collective-permute-start(bf16[4,4096]{1,0:T(4,128)(2,1)} %param.4), channel_id=1, source_target_pairs={{0,1},{1,0},{2,3},{3,2},{4,5},{5,4},{6,7},{7,6},{8,9},{9,8},{10,11... | collective-permute-start | bytes 98312 | tf_op jit(solution)/shard_map/ppermute | solution.py:128
  0.5 0.1 collective-permute-start
  0.5 1.2 %collective-permute-done.mate_pheno_ref = bf16[2,4]{1,0:T(2,128)(2,1)S(1)} collective-permute-done((bf16[2,4]{1,0:T(2,128)(2,1)}, bf16[2,4]{1,0:T(2,128)(2,1)S(1)}, u32[]{:S(2)}, u32[]{:S(2)}) %collective-permute-start) | collective-permute-done | bytes 48 | tf_op jit(solution)/shard_map/ppermute | solution.py:129
  1.7 0.0 collective-permute-done.1
  1.7 0.0 copy-start.1
  1.7 0.0 copy-start.3
  1.7 0.7 %copy-done.1 = s32[8,2]{0,1:T(2,128)S(1)} copy-done((s32[8,2]{0,1:T(2,128)S(1)}, s32[8,2]{0,1:T(2,128)}, u32[]{:S(2)}) %copy-start.1) | copy-done | bytes 88
  2.4 0.0 copy-done.3
  2.4 0.0 copy-start
  2.4 0.8 %copy-done = bf16[4,4096]{1,0:T(4,128)(2,1)S(1)} copy-done((bf16[4,4096]{1,0:T(4,128)(2,1)S(1)}, bf16[4,4096]{1,0:T(4,128)(2,1)}, u32[]{:S(2)}) %copy-start) | copy-done | bytes 32792
  3.2 0.7 %pack.1 = (bf16[80,128]{1,0:T(8,128)(2,1)S(1)}, bf16[80,128]{1,0:T(8,128)(2,1)S(1)}, bf16[80,128]{1,0:T(8,128)(2,1)S(1)}, bf16[80,128]{1,0:T(8,128)(2,1)S(1)}) custom-call(s32[1]{0:T(128)} %bitcast.me_ref, s32[2,8]{1,0:T(2,128)S(1)} %bitcast.14, bf16[2,4]{1,0:T(2,128)(2,1)S(1)} %copy-done.3, bf16[2,4]{1,0:T(2,128)(2,1)S(1)} %collective-permute-done.mate_pheno_ref, ...), custom_call_target="tpu_custom_call" | custom-call | tf_op jit(solution)/shard_map/pack/pallas_call | solution.py:137
  3.8 4.9 %collective-permute-start.2 = (bf16[80,128]{1,0:T(8,128)(2,1)S(1)}, bf16[80,128]{1,0:T(8,128)(2,1)S(1)}, u32[]{:S(2)}, u32[]{:S(2)}) collective-permute-start(bf16[80,128]{1,0:T(8,128)(2,1)S(1)} %get-tuple-element.9), channel_id=1, source_target_pairs={{0,12},{1,15},{2,14},{3,13},{4,8},{5,11},{6,10},{7,9},{8,4},{9,7},... | collective-permute-start | bytes 61448 | tf_op jit(solution)/shard_map/ppermute | solution.py:153
  8.7 0.0 collective-permute-start.3
  8.7 0.6 %collective-permute-start.4 = (bf16[80,128]{1,0:T(8,128)(2,1)S(1)}, bf16[80,128]{1,0:T(8,128)(2,1)S(1)}, u32[]{:S(2)}, u32[]{:S(2)}) collective-permute-start(bf16[80,128]{1,0:T(8,128)(2,1)S(1)} %get-tuple-element.11), channel_id=1, source_target_pairs={{0,4},{1,7},{2,6},{3,5},{4,0},{5,3},{6,2},{7,1},{8,12},{9,15},{10,... | collective-permute-start | bytes 61448 | tf_op jit(solution)/shard_map/ppermute | solution.py:153
  9.3 0.7 %collective-permute-start.5 = (bf16[80,128]{1,0:T(8,128)(2,1)S(1)}, bf16[80,128]{1,0:T(8,128)(2,1)S(1)}, u32[]{:S(2)}, u32[]{:S(2)}) collective-permute-start(bf16[80,128]{1,0:T(8,128)(2,1)S(1)} %get-tuple-element.12), channel_id=1, source_target_pairs={{0,0},{1,3},{2,2},{3,1},{4,4},{5,7},{6,6},{7,5},{8,8},{9,11},{10,1... | collective-permute-start | bytes 61448 | tf_op jit(solution)/shard_map/ppermute | solution.py:153
  10.0 0.5 %collective-permute-done.2 = bf16[80,128]{1,0:T(8,128)(2,1)S(1)} collective-permute-done((bf16[80,128]{1,0:T(8,128)(2,1)S(1)}, bf16[80,128]{1,0:T(8,128)(2,1)S(1)}, u32[]{:S(2)}, u32[]{:S(2)}) %collective-permute-start.2) | collective-permute-done | bytes 20512 | tf_op jit(solution)/shard_map/ppermute | solution.py:153
  10.5 3.1 %collective-permute-done.3 = bf16[80,128]{1,0:T(8,128)(2,1)S(1)} collective-permute-done((bf16[80,128]{1,0:T(8,128)(2,1)S(1)}, bf16[80,128]{1,0:T(8,128)(2,1)S(1)}, u32[]{:S(2)}, u32[]{:S(2)}) %collective-permute-start.3) | collective-permute-done | bytes 20512 | tf_op jit(solution)/shard_map/ppermute | solution.py:153
  13.6 0.0 collective-permute-done.4
  13.6 0.0 collective-permute-done.5
  13.6 0.0 copy-start.2
  13.6 1.8 %collective-permute-start.6 = (bf16[272,128]{1,0:T(8,128)(2,1)S(1)}, bf16[272,128]{1,0:T(8,128)(2,1)S(1)}, u32[]{:S(2)}, u32[]{:S(2)}) collective-permute-start(bf16[272,128]{1,0:T(8,128)(2,1)S(1)} %constant_dynamic-update-slice_fusion.own_ref), channel_id=1, source_target_pairs={{0,1},{1,0},{2,3},{3,2},{4,5},{5,4},{6,7},{7,6},{8,9},{9,8},{10,11... | collective-permute-start | bytes 208904 | tf_op jit(solution)/shard_map/ppermute | solution.py:155
  15.4 0.9 %collective-permute-done.6.mate_ref = bf16[272,128]{1,0:T(8,128)(2,1)S(1)} collective-permute-done((bf16[272,128]{1,0:T(8,128)(2,1)S(1)}, bf16[272,128]{1,0:T(8,128)(2,1)S(1)}, u32[]{:S(2)}, u32[]{:S(2)}) %collective-permute-start.6) | collective-permute-done | bytes 69664 | tf_op jit(solution)/shard_map/ppermute | solution.py:155
  16.3 0.0 copy-done.2
  16.3 1.7 %stat.1 = bf16[1,4,512,256]{3,2,1,0:T(8,128)(2,1)} custom-call(s32[1]{0:T(128)} %bitcast.me_ref, s32[2,64]{1,0:T(2,128)S(1)} %copy-done.2, bf16[272,128]{1,0:T(8,128)(2,1)S(1)} %constant_dynamic-update-slice_fusion.own_ref, bf16[272,128]{1,0:T(8,128)(2,1)S(1)} %collective-permute-done.6.mate_ref), custom_call_target="tpu_custom_call" | custom-call | tf_op jit(solution)/shard_map/stat/pallas_call | solution.py:156
  (5 shorter events, 0.0 us)
Async XLA Ops:
  0.0 1.7 %collective-permute-start.1 = (bf16[4,4096]{1,0:T(4,128)(2,1)}, bf16[4,4096]{1,0:T(4,128)(2,1)S(1)}, u32[]{:S(2)}, u32[]{:S(2)}) collective-permute-start(bf16[4,4096]{1,0:T(4,128)(2,1)} %param.4), channel_id=1, source_target_pairs={{0,1},{1,0},{2,3},{3,2},{4,5},{5,4},{6,7},{7,6},{8,9},{9,8},{10,11... | collective-permute-start | bytes 98312 | tf_op jit(solution)/shard_map/ppermute | solution.py:128
  0.5 1.3 %collective-permute-start = (bf16[2,4]{1,0:T(2,128)(2,1)}, bf16[2,4]{1,0:T(2,128)(2,1)S(1)}, u32[]{:S(2)}, u32[]{:S(2)}) collective-permute-start(bf16[2,4]{1,0:T(2,128)(2,1)} %pheno_ref.1), channel_id=1, source_target_pairs={{0,1},{1,0},{2,3},{3,2},{4,5},{5,4},{6,7},{7,6},{8,9},{9,8},{10,11... | collective-permute-start | bytes 56 | tf_op jit(solution)/shard_map/ppermute | solution.py:129
  1.7 0.7 %copy-start.1 = (s32[8,2]{0,1:T(2,128)S(1)}, s32[8,2]{0,1:T(2,128)}, u32[]{:S(2)}) copy-start(s32[8,2]{0,1:T(2,128)} %param.7) | copy-start | bytes 196
  1.7 0.7 %copy-start.3 = (bf16[2,4]{1,0:T(2,128)(2,1)S(1)}, bf16[2,4]{1,0:T(2,128)(2,1)}, u32[]{:S(2)}) copy-start(bf16[2,4]{1,0:T(2,128)(2,1)} %pheno_ref.1) | copy-start | bytes 52
  2.4 0.8 %copy-start = (bf16[4,4096]{1,0:T(4,128)(2,1)S(1)}, bf16[4,4096]{1,0:T(4,128)(2,1)}, u32[]{:S(2)}) copy-start(bf16[4,4096]{1,0:T(4,128)(2,1)} %param.4) | copy-start | bytes 98308
  3.8 6.6 %collective-permute-start.2 = (bf16[80,128]{1,0:T(8,128)(2,1)S(1)}, bf16[80,128]{1,0:T(8,128)(2,1)S(1)}, u32[]{:S(2)}, u32[]{:S(2)}) collective-permute-start(bf16[80,128]{1,0:T(8,128)(2,1)S(1)} %get-tuple-element.9), channel_id=1, source_target_pairs={{0,12},{1,15},{2,14},{3,13},{4,8},{5,11},{6,10},{7,9},{8,4},{9,7},... | collective-permute-start | bytes 61448 | tf_op jit(solution)/shard_map/ppermute | solution.py:153
  8.7 4.9 %collective-permute-start.3 = (bf16[80,128]{1,0:T(8,128)(2,1)S(1)}, bf16[80,128]{1,0:T(8,128)(2,1)S(1)}, u32[]{:S(2)}, u32[]{:S(2)}) collective-permute-start(bf16[80,128]{1,0:T(8,128)(2,1)S(1)} %get-tuple-element.10), channel_id=1, source_target_pairs={{0,8},{1,11},{2,10},{3,9},{4,12},{5,15},{6,14},{7,13},{8,0},{9,3},... | collective-permute-start | bytes 61448 | tf_op jit(solution)/shard_map/ppermute | solution.py:153
  8.7 4.9 %collective-permute-start.4 = (bf16[80,128]{1,0:T(8,128)(2,1)S(1)}, bf16[80,128]{1,0:T(8,128)(2,1)S(1)}, u32[]{:S(2)}, u32[]{:S(2)}) collective-permute-start(bf16[80,128]{1,0:T(8,128)(2,1)S(1)} %get-tuple-element.11), channel_id=1, source_target_pairs={{0,4},{1,7},{2,6},{3,5},{4,0},{5,3},{6,2},{7,1},{8,12},{9,15},{10,... | collective-permute-start | bytes 61448 | tf_op jit(solution)/shard_map/ppermute | solution.py:153
  9.3 4.2 %collective-permute-start.5 = (bf16[80,128]{1,0:T(8,128)(2,1)S(1)}, bf16[80,128]{1,0:T(8,128)(2,1)S(1)}, u32[]{:S(2)}, u32[]{:S(2)}) collective-permute-start(bf16[80,128]{1,0:T(8,128)(2,1)S(1)} %get-tuple-element.12), channel_id=1, source_target_pairs={{0,0},{1,3},{2,2},{3,1},{4,4},{5,7},{6,6},{7,5},{8,8},{9,11},{10,1... | collective-permute-start | bytes 61448 | tf_op jit(solution)/shard_map/ppermute | solution.py:153
  13.6 2.7 %copy-start.2 = (s32[2,64]{1,0:T(2,128)S(1)}, s32[2,64]{1,0:T(2,128)}, u32[]{:S(2)}) copy-start(s32[2,64]{1,0:T(2,128)} %perms_ref.1) | copy-start | bytes 1540
  13.6 2.7 %collective-permute-start.6 = (bf16[272,128]{1,0:T(8,128)(2,1)S(1)}, bf16[272,128]{1,0:T(8,128)(2,1)S(1)}, u32[]{:S(2)}, u32[]{:S(2)}) collective-permute-start(bf16[272,128]{1,0:T(8,128)(2,1)S(1)} %constant_dynamic-update-slice_fusion.own_ref), channel_id=1, source_target_pairs={{0,1},{1,0},{2,3},{3,2},{4,5},{5,4},{6,7},{7,6},{8,9},{9,8},{10,11... | collective-permute-start | bytes 208904 | tf_op jit(solution)/shard_map/ppermute | solution.py:155

commit v5 on v3

v5 whole, which is shorter than its diff:
```python
import functools

import jax
import jax.numpy as jnp
from jax import lax
from jax.experimental import pallas as pl
from jax.experimental.pallas import tpu as pltpu
from jax.sharding import PartitionSpec as P

PANEL = 512
LANES = 128
TILE = 16
BLOCK = 2 * TILE


def wave_rows(genes, samples):
    return -(-genes * -(-samples // LANES) // TILE) * TILE


def pack_kernel(samples, me_ref, pheno_ref, grid_ref, out_ref):
    genes, s_dev = pheno_ref.shape
    panels = grid_ref.shape[0]
    tiles = -(-samples // LANES)
    shape = (out_ref.shape[0] - panels, LANES)
    row = lax.broadcasted_iota(jnp.int32, shape, 0)
    lane = lax.broadcasted_iota(jnp.int32, shape, 1)
    wave = jnp.zeros(shape, jnp.float32)
    pheno = pheno_ref[...].astype(jnp.float32)
    first = lax.rem(me_ref[0] * s_dev, LANES)
    tile = lax.div(me_ref[0] * s_dev, LANES)
    for g in range(genes):
        for s in range(s_dev):
            hit = (lane == first + s) & (row == g * tiles + tile)
            wave = jnp.where(hit, pheno[g : g + 1, s : s + 1], wave)
    out_ref[:panels] = grid_ref[...]
    out_ref[panels:] = wave.astype(out_ref.dtype)


def stat_kernel(samps, genes, me_ref, pairs_ref, perms_ref, all_ref, out_ref, a_ref, b_ref, wave_ref, sems):
    me = me_ref[0]
    pair = lax.div(me, samps)
    samp = lax.rem(me, samps)
    sources, rows, _ = all_ref.shape
    tail = rows - wave_ref.shape[1]
    copies = []
    for i, ref in enumerate((a_ref, b_ref)):
        first = pl.multiple_of(pairs_ref[i, pair] * TILE, TILE)
        copies.append(pltpu.make_async_copy(all_ref.at[:, pl.ds(first, TILE)], ref, sems.at[i]))
    copies.append(pltpu.make_async_copy(all_ref.at[:, tail:], wave_ref, sems.at[2]))
    for copy in copies:
        copy.start()
    for copy in copies:
        copy.wait()
    rperms, samples = perms_ref.shape
    s_dev = samples // sources

    def by_samples(tiles, group):
        return tiles[:, group * s_dev : (group + 1) * s_dev, :].reshape(samples, LANES)

    panel_a = a_ref[...].astype(jnp.float32)
    panel_b = b_ref[...].astype(jnp.float32)
    tile_b = jnp.where(samp == 0, panel_b[:, : TILE // 2], panel_b[:, TILE // 2 :])

    count = jnp.float32(samples)
    geno_b = jnp.concatenate([by_samples(tile_b, q) for q in range(TILE // 2 // s_dev)], axis=1)
    marg_b = jnp.sum(geno_b, axis=0, keepdims=True)
    centred = (geno_b - marg_b / count) * (samples**-0.5)
    b_hi = centred.astype(jnp.bfloat16)
    b_lo = (centred - b_hi.astype(jnp.float32)).astype(jnp.bfloat16)
    b_both = jnp.concatenate([b_hi, b_lo], axis=0)

    wave = jnp.sum(wave_ref[...].astype(jnp.float32), axis=0)
    tiles = -(-samples // LANES)
    pheno = [
        jnp.concatenate([wave[g * tiles + t : g * tiles + t + 1] for t in range(tiles)], axis=1)[:, :samples]
        for g in range(genes)
    ]
    pheno = jnp.concatenate(pheno, axis=0).astype(jnp.bfloat16)
    perms = perms_ref[...]
    twice = jnp.concatenate([perms, perms], axis=1)
    sample = lax.broadcasted_iota(jnp.int32, (samples, 2 * samples), 0)
    permuted = []
    for r in range(rperms):
        chosen = jnp.where(sample == twice[r : r + 1, :], 1.0, 0.0).astype(jnp.bfloat16)
        permuted.append(jnp.dot(pheno, chosen, preferred_element_type=jnp.float32))
    yrows = [permuted[r][g : g + 1] for g in range(genes) for r in range(rperms)]
    yall = jnp.concatenate(yrows, axis=0)
    tail = jnp.dot(yall.astype(jnp.bfloat16), b_both, preferred_element_type=jnp.float32) / count
    c_hi = tail.astype(jnp.bfloat16).astype(jnp.float32)
    c_lo = tail - c_hi

    geno_a = jnp.concatenate([by_samples(panel_a, q) for q in range(TILE // s_dev)], axis=1)
    a_rows = jnp.concatenate([geno_a, geno_a], axis=0).T
    a_minus = -a_rows.astype(jnp.bfloat16)
    for k in range(len(yrows)):
        scaled = (a_rows * yrows[k]).astype(jnp.bfloat16)
        left = jnp.concatenate([scaled, a_minus], axis=1)
        tails = [jnp.broadcast_to(c[k : k + 1], geno_b.shape).astype(jnp.bfloat16) for c in (c_hi, c_lo)]
        right = jnp.concatenate([b_both] + tails, axis=0)
        out_ref[0, k] = jnp.dot(left, right, preferred_element_type=jnp.float32).astype(out_ref.dtype)


def on_device(dosage, phenotype, perms, pairs):
    s_dev, snps = dosage.shape
    genes = phenotype.shape[0]
    samples = perms.shape[1]
    axes = ("pair", "samp")
    pair_count, samps = (lax.axis_size(axis) for axis in axes)
    me = lax.axis_index(axes).astype(jnp.int32).reshape(1)
    grid = dosage.reshape(s_dev, snps // LANES, LANES).transpose(1, 0, 2).reshape(-1, LANES)
    vmem = pl.BlockSpec(memory_space=pltpu.VMEM)
    smem = pl.BlockSpec(memory_space=pltpu.SMEM)
    rows = wave_rows(genes, samples)
    own = pl.pallas_call(
        functools.partial(pack_kernel, samples),
        out_shape=jax.ShapeDtypeStruct((grid.shape[0] + rows, LANES), dosage.dtype),
        in_specs=[smem, vmem, vmem],
        out_specs=vmem,
        name="pack",
    )(me, phenotype, grid)
    everyone = lax.all_gather(own, axes, axis=0)
    sources = pair_count * samps
    return pl.pallas_call(
        functools.partial(stat_kernel, samps, genes),
        out_shape=jax.ShapeDtypeStruct((1, genes * perms.shape[0], PANEL, PANEL // samps), jnp.bfloat16),
        in_specs=[smem, smem, vmem, pl.BlockSpec(memory_space=pl.ANY)],
        out_specs=vmem,
        scratch_shapes=[
            pltpu.VMEM((sources, TILE, LANES), dosage.dtype),
            pltpu.VMEM((sources, TILE, LANES), dosage.dtype),
            pltpu.VMEM((sources, rows, LANES), dosage.dtype),
            pltpu.SemaphoreType.DMA((3,)),
        ],
        compiler_params=pltpu.CompilerParams(vmem_limit_bytes=48 * 1024 * 1024),
        name="stat",
    )(me, pairs.T, perms, everyone)


def solution(mesh):
    placed = (P(("rep", "pair", "samp"), None), P(None, ("rep", "pair", "samp")), P(), P())
    return jax.shard_map(
        on_device,
        mesh=mesh,
        in_specs=placed,
        out_specs=P(("rep", "pair"), None, None, "samp"),
        check_vma=False,
    )
```

time: 19.5 us -> 29.9 us (1.53)
  blocking collectives: 0 us -> 25.2 us
  starting transfers between devices: 8.23 us -> 0 us
  waiting for transfers between devices: 7.16 us -> 0 us
  Pallas kernels: 2.38 us -> 3.83 us
  local copies, waits for them, and re-layouts: 1.48 us -> 0.68 us
    all_gather x0 -> x1, blocking collectives: none -> 25.2 us  [on_device(): everyone = lax.all_gather(own, axes, axis=0)]
    ppermute x4 -> x0, starting transfers between devices: 8.23 us -> none  [the longest x3 8.15 us: on_device(): got = lax.ppermute(send, 'pair', route)]
    ppermute x4 -> x0, waiting for transfers between devices: 7.16 us -> none  [the longest x3 5.91 us: on_device(): got = lax.ppermute(send, 'pair', route)]
    pallas_call x2, Pallas kernels: 2.38 us -> 3.83 us  [the longest x1 2.32 us: on_device(): pl.pallas_call(functools.partial(stat_kernel, samps, genes), out_shape=ja...]
    unnamed x13 -> x4, local copies, waits for them, and re-layouts: 1.48 us -> 0.68 us
  transfers between devices with their start and end apart: 4 -> 0, of which waited for: 4 -> 0; matrix products, arithmetic and copies ran while one was open for 0% -> 0% of each run, Pallas kernels for 0% -> 0%
where the time goes in v5:
time: 29.9 us; the launch traced here: 29.7 us
  blocking collectives  25.2 us (84%)
  Pallas kernels  3.83 us (13%)
  local copies, waits for them, and re-layouts  0.68 us (2%)
    all_gather x1, blocking collectives, on_device(): everyone = lax.all_gather(own, axes, axis=0)  25.2 us
    pallas_call x1, Pallas kernels, on_device(): pl.pallas_call(functools.partial(stat_kernel, samps, genes), out_shape=ja...  2.32 us
    pallas_call x1, Pallas kernels, on_device(): pl.pallas_call(functools.partial(pack_kernel, samples), out_shape=jax.Sha...  1.5 us
    unnamed x4, local copies, waits for them, and re-layouts  0.68 us

profile of v5, /device:TPU:0, one launch (start us, length us, event | category | flops | bytes accessed | tf_op | source)
XLA Modules:
  0.0 29.7 jit_solution(6513070081229725338)
XLA Ops:
  0.0 1.5 %pack.1 = bf16[144,128]{1,0:T(8,128)(2,1)} custom-call(s32[1]{0:T(128)} %bitcast.me_ref, bf16[2,4]{1,0:T(2,128)(2,1)} %pheno_ref.1, bf16[128,128]{1,0:T(8,128)(2,1)} %bitcast.10), custom_call_target="tpu_custom_call" | custom-call | tf_op jit(solution)/shard_map/pack/pallas_call | solution.py:114
  1.5 0.0 copy-start.1
  1.5 25.2 %all-gather = bf16[2304,128]{1,0:T(8,128)(2,1)S(1)} all-gather(bf16[144,128]{1,0:T(8,128)(2,1)} %pack.1), channel_id=2, replica_groups=mesh['rep'=2,'pair'=8,'samp'=2] {'pair','samp'}, dimensions={0}, use_global_device_ids=true | all-gather | bytes 626688 | tf_op jit(solution)/shard_map/all_gather | solution.py:121
  26.7 0.0 copy-start
  26.7 0.0 copy-done.1
  26.7 0.7 %copy-done = s32[8,2]{0,1:T(2,128)S(1)} copy-done((s32[8,2]{0,1:T(2,128)S(1)}, s32[8,2]{0,1:T(2,128)}, u32[]{:S(2)}) %copy-start) | copy-done | bytes 88
  27.4 2.3 %stat.1 = bf16[1,4,512,256]{3,2,1,0:T(8,128)(2,1)} custom-call(s32[1]{0:T(128)} %bitcast.me_ref, s32[2,8]{1,0:T(2,128)S(1)} %bitcast.9, s32[2,64]{1,0:T(2,128)S(1)} %copy-done.1, bf16[16,144,128]{2,1,0:T(8,128)(2,1)S(1)} %bitcast.8), custom_call_target="tpu_custom_call" | custom-call | tf_op jit(solution)/shard_map/stat/pallas_call | solution.py:123
Async XLA Ops:
  1.5 25.2 %copy-start.1 = (s32[2,64]{1,0:T(2,128)S(1)}, s32[2,64]{1,0:T(2,128)}, u32[]{:S(2)}) copy-start(s32[2,64]{1,0:T(2,128)} %perms_ref.1) | copy-start | bytes 1540
  26.7 0.7 %copy-start = (s32[8,2]{0,1:T(2,128)S(1)}, s32[8,2]{0,1:T(2,128)}, u32[]{:S(2)}) copy-start(s32[8,2]{0,1:T(2,128)} %param.7) | copy-start | bytes 196

commit v6 on v4

--- a/solution.py
+++ b/solution.py
@@ -139,7 +139,6 @@
         out_shape=[message] * (pair_count // samps),
         in_specs=[smem, smem, vmem, vmem, vmem, vmem],
         out_specs=[vmem] * (pair_count // samps),
-        compiler_params=pltpu.CompilerParams(vmem_limit_bytes=8 * 1024 * 1024),
         name="pack",
     )(me, pairs.T, phenotype, mate_pheno, grid(dosage), grid(mate_dosage))
 

time: 18.2 us -> 18.5 us (1.016)
  Pallas kernels: 2.39 us -> 3.31 us
  local copies, waits for them, and re-layouts: 1.47 us -> 0.65 us
  starting transfers between devices: 8.43 us -> 9.05 us
  waiting for transfers between devices: 5.66 us -> 5.19 us
    pallas_call x1, Pallas kernels: 0.67 us -> 1.59 us  [on_device(): pl.pallas_call(functools.partial(pack_kernel, pair_count, samps), out_sha...]
    unnamed x12 -> x10, local copies, waits for them, and re-layouts: 1.47 us -> 0.65 us
    ppermute x4, starting transfers between devices: 6.16 us -> 6.79 us  [on_device(): got.append(lax.ppermute(message, axes, route))]
    ppermute x4, waiting for transfers between devices: 3.55 us -> 3.08 us  [on_device(): got.append(lax.ppermute(message, axes, route))]
  transfers between devices with their start and end apart: 7 -> 7, of which waited for: 4 -> 3; matrix products, arithmetic and copies ran while one was open for 0% -> 0% of each run, Pallas kernels for 0% -> 0%
where the time goes in v6:
time: 18.5 us; the launch traced here: 18.2 us
  starting transfers between devices  9.05 us (49%)
  waiting for transfers between devices  5.19 us (28%)
  Pallas kernels  3.31 us (18%)
  local copies, waits for them, and re-layouts  0.65 us (4%)
    ppermute x4, starting transfers between devices, on_device(): got.append(lax.ppermute(message, axes, route))  6.79 us
    ppermute x4, waiting for transfers between devices, on_device(): got.append(lax.ppermute(message, axes, route))  3.08 us
    ppermute x1, starting transfers between devices, on_device(): mate = lax.ppermute(own, 'samp', swap)  1.76 us
    pallas_call x1, Pallas kernels, on_device(): pl.pallas_call(functools.partial(stat_kernel, samps, genes), out_shape=ja...  1.72 us
    pallas_call x1, Pallas kernels, on_device(): pl.pallas_call(functools.partial(pack_kernel, pair_count, samps), out_sha...  1.59 us
    ppermute x1, waiting for transfers between devices, on_device(): mate_pheno = lax.ppermute(phenotype, 'samp', swap)  1.2 us
    ppermute x1, waiting for transfers between devices, on_device(): mate = lax.ppermute(own, 'samp', swap)  0.91 us
    unnamed x10, local copies, waits for them, and re-layouts  0.65 us
  transfers between devices with their start and end apart: 7, of which 3 were waited for; matrix products, arithmetic and copies ran while one was open for 0% of the time, Pallas kernels for 0%

profile of v6, /device:TPU:0, one launch (start us, length us, event | category | flops | bytes accessed | tf_op | source)
XLA Modules:
  0.0 18.2 jit_solution(11647341682360632357)
XLA Ops:
  0.0 0.5 %collective-permute-start.1 = (bf16[4,4096]{1,0:T(4,128)(2,1)}, bf16[4,4096]{1,0:T(4,128)(2,1)S(1)}, u32[]{:S(2)}, u32[]{:S(2)}) collective-permute-start(bf16[4,4096]{1,0:T(4,128)(2,1)} %param.4), channel_id=1, source_target_pairs={{0,1},{1,0},{2,3},{3,2},{4,5},{5,4},{6,7},{7,6},{8,9},{9,8},{10,11... | collective-permute-start | bytes 98312 | tf_op jit(solution)/shard_map/ppermute | solution.py:128
  0.5 0.1 collective-permute-start
  0.5 1.2 %collective-permute-done.mate_pheno_ref = bf16[2,4]{1,0:T(2,128)(2,1)S(1)} collective-permute-done((bf16[2,4]{1,0:T(2,128)(2,1)}, bf16[2,4]{1,0:T(2,128)(2,1)S(1)}, u32[]{:S(2)}, u32[]{:S(2)}) %collective-permute-start) | collective-permute-done | bytes 48 | tf_op jit(solution)/shard_map/ppermute | solution.py:129
  1.7 0.0 copy-start.2
  1.7 0.0 collective-permute-done.1
  1.7 0.0 copy-start.1
  1.7 0.6 %copy-done.2 = bf16[2,4]{1,0:T(2,128)(2,1)} copy-done((bf16[2,4]{1,0:T(2,128)(2,1)}, bf16[2,4]{1,0:T(2,128)(2,1)S(1)}, u32[]{:S(2)}) %copy-start.2) | copy-done | bytes 40
  2.3 0.0 copy-done.1
  2.3 1.6 %pack.1 = (bf16[80,128]{1,0:T(8,128)(2,1)}, bf16[80,128]{1,0:T(8,128)(2,1)}, bf16[80,128]{1,0:T(8,128)(2,1)}, bf16[80,128]{1,0:T(8,128)(2,1)}) custom-call(s32[1]{0:T(128)} %bitcast.me_ref, s32[2,8]{1,0:T(2,128)} %bitcast.14, bf16[2,4]{1,0:T(2,128)(2,1)} %pheno_ref.1, bf16[2,4]{1,0:T(2,128)(2,1)} %copy-done.2, bf16[128,128]{1,0:T(8,128)(2,1)} %bitcast.12, ...), custom_call_target="tpu_custom_call" | custom-call | tf_op jit(solution)/shard_map/pack/pallas_call | solution.py:137
  3.9 4.8 %collective-permute-start.2 = (bf16[80,128]{1,0:T(8,128)(2,1)}, bf16[80,128]{1,0:T(8,128)(2,1)S(1)}, u32[]{:S(2)}, u32[]{:S(2)}) collective-permute-start(bf16[80,128]{1,0:T(8,128)(2,1)} %get-tuple-element.9), channel_id=1, source_target_pairs={{0,12},{1,15},{2,14},{3,13},{4,8},{5,11},{6,10},{7,9},{8,4},{9,7},... | collective-permute-start | bytes 61448 | tf_op jit(solution)/shard_map/ppermute | solution.py:152
  8.7 0.0 collective-permute-start.3
  8.7 0.6 %collective-permute-start.4 = (bf16[80,128]{1,0:T(8,128)(2,1)}, bf16[80,128]{1,0:T(8,128)(2,1)S(1)}, u32[]{:S(2)}, u32[]{:S(2)}) collective-permute-start(bf16[80,128]{1,0:T(8,128)(2,1)} %get-tuple-element.11), channel_id=1, source_target_pairs={{0,4},{1,7},{2,6},{3,5},{4,0},{5,3},{6,2},{7,1},{8,12},{9,15},{10,... | collective-permute-start | bytes 61448 | tf_op jit(solution)/shard_map/ppermute | solution.py:152
  9.3 1.4 %collective-permute-start.5 = (bf16[80,128]{1,0:T(8,128)(2,1)}, bf16[80,128]{1,0:T(8,128)(2,1)S(1)}, u32[]{:S(2)}, u32[]{:S(2)}) collective-permute-start(bf16[80,128]{1,0:T(8,128)(2,1)} %get-tuple-element.12), channel_id=1, source_target_pairs={{0,0},{1,3},{2,2},{3,1},{4,4},{5,7},{6,6},{7,5},{8,8},{9,11},{10,1... | collective-permute-start | bytes 61448 | tf_op jit(solution)/shard_map/ppermute | solution.py:152
  10.7 0.0 collective-permute-done.2
  10.7 3.1 %collective-permute-done.3 = bf16[80,128]{1,0:T(8,128)(2,1)S(1)} collective-permute-done((bf16[80,128]{1,0:T(8,128)(2,1)}, bf16[80,128]{1,0:T(8,128)(2,1)S(1)}, u32[]{:S(2)}, u32[]{:S(2)}) %collective-permute-start.3) | collective-permute-done | bytes 20512 | tf_op jit(solution)/shard_map/ppermute | solution.py:152
  13.8 0.0 collective-permute-done.4
  13.8 0.0 collective-permute-done.5
  13.8 0.0 copy-start
  13.9 1.8 %collective-permute-start.6 = (bf16[272,128]{1,0:T(8,128)(2,1)S(1)}, bf16[272,128]{1,0:T(8,128)(2,1)S(1)}, u32[]{:S(2)}, u32[]{:S(2)}) collective-permute-start(bf16[272,128]{1,0:T(8,128)(2,1)S(1)} %constant_dynamic-update-slice_fusion.own_ref), channel_id=1, source_target_pairs={{0,1},{1,0},{2,3},{3,2},{4,5},{5,4},{6,7},{7,6},{8,9},{9,8},{10,11... | collective-permute-start | bytes 208904 | tf_op jit(solution)/shard_map/ppermute | solution.py:154
  15.6 0.9 %collective-permute-done.6.mate_ref = bf16[272,128]{1,0:T(8,128)(2,1)S(1)} collective-permute-done((bf16[272,128]{1,0:T(8,128)(2,1)S(1)}, bf16[272,128]{1,0:T(8,128)(2,1)S(1)}, u32[]{:S(2)}, u32[]{:S(2)}) %collective-permute-start.6) | collective-permute-done | bytes 69664 | tf_op jit(solution)/shard_map/ppermute | solution.py:154
  16.5 0.0 copy-done
  16.5 1.7 %stat.1 = bf16[1,4,512,256]{3,2,1,0:T(8,128)(2,1)} custom-call(s32[1]{0:T(128)} %bitcast.me_ref, s32[2,64]{1,0:T(2,128)S(1)} %copy-done, bf16[272,128]{1,0:T(8,128)(2,1)S(1)} %constant_dynamic-update-slice_fusion.own_ref, bf16[272,128]{1,0:T(8,128)(2,1)S(1)} %collective-permute-done.6.mate_ref), custom_call_target="tpu_custom_call" | custom-call | tf_op jit(solution)/shard_map/stat/pallas_call | solution.py:155
  (5 shorter events, 0.0 us)
Async XLA Ops:
  0.0 1.7 %collective-permute-start.1 = (bf16[4,4096]{1,0:T(4,128)(2,1)}, bf16[4,4096]{1,0:T(4,128)(2,1)S(1)}, u32[]{:S(2)}, u32[]{:S(2)}) collective-permute-start(bf16[4,4096]{1,0:T(4,128)(2,1)} %param.4), channel_id=1, source_target_pairs={{0,1},{1,0},{2,3},{3,2},{4,5},{5,4},{6,7},{7,6},{8,9},{9,8},{10,11... | collective-permute-start | bytes 98312 | tf_op jit(solution)/shard_map/ppermute | solution.py:128
  0.5 1.3 %collective-permute-start = (bf16[2,4]{1,0:T(2,128)(2,1)}, bf16[2,4]{1,0:T(2,128)(2,1)S(1)}, u32[]{:S(2)}, u32[]{:S(2)}) collective-permute-start(bf16[2,4]{1,0:T(2,128)(2,1)} %pheno_ref.1), channel_id=1, source_target_pairs={{0,1},{1,0},{2,3},{3,2},{4,5},{5,4},{6,7},{7,6},{8,9},{9,8},{10,11... | collective-permute-start | bytes 56 | tf_op jit(solution)/shard_map/ppermute | solution.py:129
  1.7 0.6 %copy-start.2 = (bf16[2,4]{1,0:T(2,128)(2,1)}, bf16[2,4]{1,0:T(2,128)(2,1)S(1)}, u32[]{:S(2)}) copy-start(bf16[2,4]{1,0:T(2,128)(2,1)S(1)} %collective-permute-done.mate_pheno_ref) | copy-start | bytes 52
  1.7 0.6 %copy-start.1 = (bf16[4,4096]{1,0:T(4,128)(2,1)}, bf16[4,4096]{1,0:T(4,128)(2,1)S(1)}, u32[]{:S(2)}) copy-start(bf16[4,4096]{1,0:T(4,128)(2,1)S(1)} %collective-permute-done.1) | copy-start | bytes 98308
  3.9 6.8 %collective-permute-start.2 = (bf16[80,128]{1,0:T(8,128)(2,1)}, bf16[80,128]{1,0:T(8,128)(2,1)S(1)}, u32[]{:S(2)}, u32[]{:S(2)}) collective-permute-start(bf16[80,128]{1,0:T(8,128)(2,1)} %get-tuple-element.9), channel_id=1, source_target_pairs={{0,12},{1,15},{2,14},{3,13},{4,8},{5,11},{6,10},{7,9},{8,4},{9,7},... | collective-permute-start | bytes 61448 | tf_op jit(solution)/shard_map/ppermute | solution.py:152
  8.7 5.1 %collective-permute-start.3 = (bf16[80,128]{1,0:T(8,128)(2,1)}, bf16[80,128]{1,0:T(8,128)(2,1)S(1)}, u32[]{:S(2)}, u32[]{:S(2)}) collective-permute-start(bf16[80,128]{1,0:T(8,128)(2,1)} %get-tuple-element.10), channel_id=1, source_target_pairs={{0,8},{1,11},{2,10},{3,9},{4,12},{5,15},{6,14},{7,13},{8,0},{9,3},... | collective-permute-start | bytes 61448 | tf_op jit(solution)/shard_map/ppermute | solution.py:152
  8.7 5.1 %collective-permute-start.4 = (bf16[80,128]{1,0:T(8,128)(2,1)}, bf16[80,128]{1,0:T(8,128)(2,1)S(1)}, u32[]{:S(2)}, u32[]{:S(2)}) collective-permute-start(bf16[80,128]{1,0:T(8,128)(2,1)} %get-tuple-element.11), channel_id=1, source_target_pairs={{0,4},{1,7},{2,6},{3,5},{4,0},{5,3},{6,2},{7,1},{8,12},{9,15},{10,... | collective-permute-start | bytes 61448 | tf_op jit(solution)/shard_map/ppermute | solution.py:152
  9.3 4.5 %collective-permute-start.5 = (bf16[80,128]{1,0:T(8,128)(2,1)}, bf16[80,128]{1,0:T(8,128)(2,1)S(1)}, u32[]{:S(2)}, u32[]{:S(2)}) collective-permute-start(bf16[80,128]{1,0:T(8,128)(2,1)} %get-tuple-element.12), channel_id=1, source_target_pairs={{0,0},{1,3},{2,2},{3,1},{4,4},{5,7},{6,6},{7,5},{8,8},{9,11},{10,1... | collective-permute-start | bytes 61448 | tf_op jit(solution)/shard_map/ppermute | solution.py:152
  13.8 2.7 %copy-start = (s32[2,64]{1,0:T(2,128)S(1)}, s32[2,64]{1,0:T(2,128)}, u32[]{:S(2)}) copy-start(s32[2,64]{1,0:T(2,128)} %perms_ref.1) | copy-start | bytes 1540
  13.9 2.7 %collective-permute-start.6 = (bf16[272,128]{1,0:T(8,128)(2,1)S(1)}, bf16[272,128]{1,0:T(8,128)(2,1)S(1)}, u32[]{:S(2)}, u32[]{:S(2)}) collective-permute-start(bf16[272,128]{1,0:T(8,128)(2,1)S(1)} %constant_dynamic-update-slice_fusion.own_ref), channel_id=1, source_target_pairs={{0,1},{1,0},{2,3},{3,2},{4,5},{5,4},{6,7},{7,6},{8,9},{9,8},{10,11... | collective-permute-start | bytes 208904 | tf_op jit(solution)/shard_map/ppermute | solution.py:154

commit v7 on v5

v7 whole, which is shorter than its diff:
```python
import functools

import jax
import jax.numpy as jnp
from jax import lax
from jax.experimental import pallas as pl
from jax.experimental.pallas import tpu as pltpu
from jax.sharding import PartitionSpec as P

PANEL = 512
LANES = 128
TILE = 16
BLOCK = 2 * TILE
AXES = ("pair", "samp")


def offsets(pair_count, core):
    return [2 * i + core for i in range(pair_count // 2 - 1, 0, -1)] + [1, 0]


def wave_rows(genes, samples):
    return -(-genes * -(-samples // LANES) // 8) * 8


def pack_kernel(pair_count, samps, pairs_hbm, pheno_hbm, grid_hbm, keep_ref, give_ref, wave_ref, pairs_ref, pheno_ref, grid_ref, sems):
    copies = [
        pltpu.make_async_copy(source, target, sems.at[i])
        for i, (source, target) in enumerate(((pairs_hbm, pairs_ref), (grid_hbm, grid_ref), (pheno_hbm, pheno_ref)))
    ]
    for copy in copies:
        copy.start()
    pair, samp = lax.axis_index("pair"), lax.axis_index("samp")
    genes, s_dev = pheno_ref.shape
    rows = wave_ref.shape[0]
    tiles = -(-s_dev * samps * pair_count // LANES)
    row = lax.broadcasted_iota(jnp.int32, (rows, LANES), 0)
    lane = lax.broadcasted_iota(jnp.int32, (rows, LANES), 1)
    spot = (pair * samps + samp) * s_dev
    first, tile = lax.rem(spot, LANES), lax.div(spot, LANES)
    for copy in copies:
        copy.wait()

    pheno = pheno_ref[...].astype(jnp.float32)
    wave = jnp.zeros((rows, LANES), jnp.float32)
    for g in range(genes):
        for s in range(s_dev):
            hit = (lane == first + s) & (row == g * tiles + tile)
            wave = jnp.where(hit, pheno[g : g + 1, s : s + 1], wave)
    wave = wave.astype(wave_ref.dtype)
    wave_ref[...] = wave

    own_side, far_side = offsets(pair_count, 0), offsets(pair_count, 1)
    for i, (even, odd) in enumerate(zip(own_side, far_side)):
        for ref, core in ((keep_ref, samp), (give_ref, samps - 1 - samp)):
            n = lax.bitwise_xor(pair, even + (odd - even) * core)
            for j in range(2):
                start = pl.multiple_of(pairs_ref[j, n] * TILE, TILE)
                place = i * BLOCK + j * TILE
                ref[place : place + TILE, :] = grid_ref[pl.ds(start, TILE), :]
    give_ref[len(own_side) * BLOCK :, :] = wave


def stat_kernel(
    pair_count, samps, perms_ref, keep_ref, give_ref, own_ref, mate_ref, near_ref, wave_ref, out_hbm, got_ref, out_ref, sems
):
    pair, samp = lax.axis_index("pair"), lax.axis_index("samp")
    other = samps - 1 - samp
    far = pair_count // 2 - 1

    def place(offset, core, block):
        got_ref[lax.bitwise_xor(pair, offset) * samps + core] = block

    for ref, core in ((own_ref, samp), (mate_ref, other)):
        for i in range(far):
            offset = 2 * (far - i) + core
            start = 2 * i * BLOCK
            place(offset, core, ref[start : start + BLOCK, :])
            place(offset, samps - 1 - core, ref[start + BLOCK : start + 2 * BLOCK, :])
    place(1, samp, near_ref[:BLOCK, :])
    place(1, other, near_ref[BLOCK : 2 * BLOCK, :])
    itself = (far + 1) * BLOCK
    place(0, samp, keep_ref[itself : itself + BLOCK, :])
    place(0, other, give_ref[itself : itself + BLOCK, :])

    sources = got_ref.shape[0]
    rperms, samples = perms_ref.shape
    s_dev = samples // sources

    def by_samples(tiles, group):
        return tiles[:, group * s_dev : (group + 1) * s_dev, :].reshape(samples, LANES)

    panel_a = got_ref[:, 0:TILE, :].astype(jnp.float32)
    panel_b = got_ref[:, TILE:BLOCK, :].astype(jnp.float32)
    tile_b = jnp.where(samp == 0, panel_b[:, : TILE // 2], panel_b[:, TILE // 2 :])

    count = jnp.float32(samples)
    geno_b = jnp.concatenate([by_samples(tile_b, q) for q in range(TILE // 2 // s_dev)], axis=1)
    marg_b = jnp.sum(geno_b, axis=0, keepdims=True)
    centred = (geno_b - marg_b / count) * (samples**-0.5)
    b_hi = centred.astype(jnp.bfloat16)
    b_lo = (centred - b_hi.astype(jnp.float32)).astype(jnp.bfloat16)
    b_both = jnp.concatenate([b_hi, b_lo], axis=0)

    wave = wave_ref[...].astype(jnp.float32)
    genes = out_ref.shape[0] // rperms
    tiles = -(-samples // LANES)
    pheno = [
        jnp.concatenate([wave[g * tiles + t : g * tiles + t + 1] for t in range(tiles)], axis=1)[:, :samples]
        for g in range(genes)
    ]
    pheno = jnp.concatenate(pheno, axis=0).astype(jnp.bfloat16)
    perms = perms_ref[...]
    twice = jnp.concatenate([perms, perms], axis=1)
    sample = lax.broadcasted_iota(jnp.int32, (samples, 2 * samples), 0)
    permuted = []
    for r in range(rperms):
        chosen = jnp.where(sample == twice[r : r + 1, :], 1.0, 0.0).astype(jnp.bfloat16)
        permuted.append(jnp.dot(pheno, chosen, preferred_element_type=jnp.float32))
    yrows = [permuted[r][g : g + 1] for g in range(genes) for r in range(rperms)]
    yall = jnp.concatenate(yrows, axis=0)
    tail = jnp.dot(yall.astype(jnp.bfloat16), b_both, preferred_element_type=jnp.float32) / count
    c_hi = tail.astype(jnp.bfloat16).astype(jnp.float32)
    c_lo = tail - c_hi

    geno_a = jnp.concatenate([by_samples(panel_a, q) for q in range(TILE // s_dev)], axis=1)
    a_rows = jnp.concatenate([geno_a, geno_a], axis=0).T
    a_minus = -a_rows.astype(jnp.bfloat16)
    copies = []
    for k in range(len(yrows)):
        scaled = (a_rows * yrows[k]).astype(jnp.bfloat16)
        left = jnp.concatenate([scaled, a_minus], axis=1)
        tails = [jnp.broadcast_to(c[k : k + 1], geno_b.shape).astype(jnp.bfloat16) for c in (c_hi, c_lo)]
        right = jnp.concatenate([b_both] + tails, axis=0)
        out_ref[k] = jnp.dot(left, right, preferred_element_type=jnp.float32).astype(out_ref.dtype)
        copies.append(pltpu.make_async_copy(out_ref.at[k], out_hbm.at[0, k], sems.at[k]))
        copies[-1].start()
    for copy in copies:
        copy.wait()


def on_device(dosage, phenotype, perms, pairs):
    s_dev, snps = dosage.shape
    genes = phenotype.shape[0]
    samples = perms.shape[1]
    pair_count, samps = (lax.axis_size(axis) for axis in AXES)
    rounds = pair_count // 2 + 1
    rows = wave_rows(genes, samples)
    grid = dosage.reshape(s_dev, snps // LANES, LANES).transpose(1, 0, 2).reshape(-1, LANES)
    vmem = pl.BlockSpec(memory_space=pltpu.VMEM)
    hbm = pl.BlockSpec(memory_space=pltpu.HBM)

    def array(*shape):
        return jax.ShapeDtypeStruct(shape, dosage.dtype)

    keep, give, wave = pl.pallas_call(
        functools.partial(pack_kernel, pair_count, samps),
        out_shape=[array(rounds * BLOCK, LANES), array(rounds * BLOCK + rows, LANES), array(rows, LANES)],
        in_specs=[hbm, hbm, hbm],
        out_specs=[vmem, vmem, vmem],
        scratch_shapes=[
            pltpu.SMEM(pairs.shape[::-1], pairs.dtype),
            pltpu.VMEM(phenotype.shape, phenotype.dtype),
            pltpu.VMEM(grid.shape, grid.dtype),
            pltpu.SemaphoreType.DMA((3,)),
        ],
        compiler_params=pltpu.CompilerParams(vmem_limit_bytes=8 * 1024 * 1024),
        name="pack",
    )(pairs.T, phenotype, grid)

    swap = [(i, samps - 1 - i) for i in range(samps)]
    got = lax.ppermute(give, "samp", swap)
    wave = wave + got[rounds * BLOCK :]
    arrived = []
    for i in range(rounds - 1):
        blocks = slice(i * BLOCK, (i + 1) * BLOCK)
        message = jnp.concatenate([keep[blocks], got[blocks], wave], axis=0)
        route = [
            (p * samps + c, (p ^ offsets(pair_count, c)[i]) * samps + c)
            for p in range(pair_count)
            for c in range(samps)
        ]
        arrived.append(lax.ppermute(message, AXES, route))
    *far, near = arrived
    own = jnp.concatenate([a[: 2 * BLOCK] for a in far] + [sum(a[2 * BLOCK :] for a in far)], axis=0)
    mate = lax.ppermute(own, "samp", swap)
    end = 2 * BLOCK * len(far)
    wave = wave + own[end:] + mate[end:] + near[2 * BLOCK :]
    stats = genes * perms.shape[0]
    half = PANEL // samps
    return pl.pallas_call(
        functools.partial(stat_kernel, pair_count, samps),
        out_shape=jax.ShapeDtypeStruct((1, stats, PANEL, half), jnp.bfloat16),
        in_specs=[vmem] * 7,
        out_specs=hbm,
        scratch_shapes=[
            pltpu.VMEM((pair_count * samps, BLOCK, LANES), dosage.dtype),
            pltpu.VMEM((stats, PANEL, half), jnp.bfloat16),
            pltpu.SemaphoreType.DMA((stats,)),
        ],
        compiler_params=pltpu.CompilerParams(vmem_limit_bytes=48 * 1024 * 1024),
        name="stat",
    )(perms, keep, got, own, mate, near, wave)


def solution(mesh):
    placed = (P(("rep", "pair", "samp"), None), P(None, ("rep", "pair", "samp")), P(), P())
    return jax.shard_map(
        on_device,
        mesh=mesh,
        in_specs=placed,
        out_specs=P(("rep", "pair"), None, None, "samp"),
        check_vma=False,
    )
```

time: 29.9 us -> 21.5 us (0.72)
  blocking collectives: 25.2 us -> 0 us
  waiting for transfers between devices: 0 us -> 8.69 us
  starting transfers between devices: 0 us -> 7.88 us
  Pallas kernels: 3.83 us -> 2.33 us
  local copies, waits for them, and re-layouts: 0.68 us -> 2.17 us
    all_gather x1 -> x0, blocking collectives: 25.2 us -> none  [on_device(): everyone = lax.all_gather(own, axes, axis=0)]
    ppermute x0 -> x6, waiting for transfers between devices: none -> 8.69 us  [the longest x4 7.82 us: on_device(): arrived.append(lax.ppermute(message, AXES, route))]
    ppermute x0 -> x6, starting transfers between devices: none -> 7.88 us  [the longest x4 7.07 us: on_device(): arrived.append(lax.ppermute(message, AXES, route))]
    pallas_call x2, Pallas kernels: 3.83 us -> 2.33 us  [the longest x1 1.61 us: on_device(): pl.pallas_call(functools.partial(stat_kernel, pair_count, samps), out_sha...]
    unnamed x4 -> x12, local copies, waits for them, and re-layouts: 0.68 us -> 1.45 us
    slice x0 -> x7, local copies, waits for them, and re-layouts: none -> 0.72 us  [the longest x5 0.71 us: on_device(): a[:2 * BLOCK]]
  transfers between devices with their start and end apart: 0 -> 6, of which waited for: 0 -> 5; matrix products, arithmetic and copies ran while one was open for 0% -> 0% of each run, Pallas kernels for 0% -> 0%
where the time goes in v7:
time: 21.5 us; the launch traced here: 21.2 us
  waiting for transfers between devices  8.69 us (40%)
  starting transfers between devices  7.88 us (37%)
  Pallas kernels  2.33 us (11%)
  local copies, waits for them, and re-layouts  2.17 us (10%)
    ppermute x4, waiting for transfers between devices, on_device(): arrived.append(lax.ppermute(message, AXES, route))  7.82 us
    ppermute x4, starting transfers between devices, on_device(): arrived.append(lax.ppermute(message, AXES, route))  7.07 us
    pallas_call x1, Pallas kernels, on_device(): pl.pallas_call(functools.partial(stat_kernel, pair_count, samps), out_sha...  1.61 us
    unnamed x12, local copies, waits for them, and re-layouts  1.45 us
    ppermute x1, waiting for transfers between devices, on_device(): got = lax.ppermute(give, 'samp', swap)  0.87 us
    pallas_call x1, Pallas kernels, on_device(): pl.pallas_call(functools.partial(pack_kernel, pair_count, samps), out_sha...  0.72 us
    slice x5, local copies, waits for them, and re-layouts, on_device(): a[:2 * BLOCK]  0.71 us
    ppermute x1, starting transfers between devices, on_device(): got = lax.ppermute(give, 'samp', swap)  0.52 us
  transfers between devices with their start and end apart: 6, of which 5 were waited for; matrix products, arithmetic and copies ran while one was open for 0% of the time, Pallas kernels for 0%

profile of v7, /device:TPU:0, one launch (start us, length us, event | category | flops | bytes accessed | tf_op | source)
XLA Modules:
  0.0 21.2 jit_solution(1940036174260926956)
XLA Ops:
  0.0 0.0 copy-start.1
  0.0 0.0 copy-start.3
  0.0 0.7 %copy-done.1 = s32[8,2]{0,1:T(2,128)S(1)} copy-done((s32[8,2]{0,1:T(2,128)S(1)}, s32[8,2]{0,1:T(2,128)}, u32[]{:S(2)}) %copy-start.1) | copy-done | bytes 88
  0.7 0.0 copy-done.3
  0.7 0.0 copy-start
  0.7 0.8 %copy-done = bf16[4,4096]{1,0:T(4,128)(2,1)S(1)} copy-done((bf16[4,4096]{1,0:T(4,128)(2,1)S(1)}, bf16[4,4096]{1,0:T(4,128)(2,1)}, u32[]{:S(2)}) %copy-start) | copy-done | bytes 32792
  1.4 0.7 %pack.1 = (bf16[160,128]{1,0:T(8,128)(2,1)S(1)}, bf16[168,128]{1,0:T(8,128)(2,1)S(1)}, bf16[8,128]{1,0:T(8,128)(2,1)S(1)}) custom-call(s32[2,8]{1,0:T(2,128)S(1)} %bitcast.7, bf16[2,4]{1,0:T(2,128)(2,1)S(1)} %copy-done.3, bf16[128,128]{1,0:T(8,128)(2,1)S(1)} %bitcast.6), custom_call_target="tpu_custom_call" | custom-call | tf_op jit(solution)/shard_map/pack/pallas_call | solution.py:155
  2.2 0.5 %collective-permute-start = (bf16[168,128]{1,0:T(8,128)(2,1)S(1)}, bf16[168,128]{1,0:T(8,128)(2,1)S(1)}, u32[]{:S(2)}, u32[]{:S(2)}) collective-permute-start(bf16[168,128]{1,0:T(8,128)(2,1)S(1)} %get-tuple-element.9), channel_id=1, source_target_pairs={{0,1},{1,0},{2,3},{3,2},{4,5},{5,4},{6,7},{7,6},{8,9},{9,8},{10,11... | collective-permute-start | bytes 129032 | tf_op jit(solution)/shard_map/ppermute | solution.py:171
  2.7 0.9 %collective-permute-done.give_ref = bf16[168,128]{1,0:T(8,128)(2,1)S(1)} collective-permute-done((bf16[168,128]{1,0:T(8,128)(2,1)S(1)}, bf16[168,128]{1,0:T(8,128)(2,1)S(1)}, u32[]{:S(2)}, u32[]{:S(2)}) %collective-permute-start) | collective-permute-done | bytes 43040 | tf_op jit(solution)/shard_map/ppermute | solution.py:171
  3.6 4.0 %collective-permute-start.2 = (bf16[72,128]{1,0:T(8,128)(2,1)S(1)}, bf16[72,128]{1,0:T(8,128)(2,1)S(1)}, u32[]{:S(2)}, u32[]{:S(2)}) collective-permute-start(bf16[72,128]{1,0:T(8,128)(2,1)S(1)} %get-tuple-element.20), channel_id=1, source_target_pairs={{0,8},{1,11},{2,10},{3,9},{4,12},{5,15},{6,14},{7,13},{8,0},{9,3},... | collective-permute-start | bytes 55304 | tf_op jit(solution)/shard_map/ppermute | solution.py:182
  7.6 1.6 %collective-permute-start.3 = (bf16[72,128]{1,0:T(8,128)(2,1)S(1)}, bf16[72,128]{1,0:T(8,128)(2,1)S(1)}, u32[]{:S(2)}, u32[]{:S(2)}) collective-permute-start(bf16[72,128]{1,0:T(8,128)(2,1)S(1)} %get-tuple-element.21), channel_id=1, source_target_pairs={{0,4},{1,7},{2,6},{3,5},{4,0},{5,3},{6,2},{7,1},{8,12},{9,15},{10,... | collective-permute-start | bytes 55304 | tf_op jit(solution)/shard_map/ppermute | solution.py:182
  9.2 0.0 collective-permute-start.1
  9.2 0.2 collective-permute-done.2
  9.3 0.0 copy-start.4
  9.3 2.0 %collective-permute-done.3 = bf16[72,128]{1,0:T(8,128)(2,1)S(1)} collective-permute-done((bf16[72,128]{1,0:T(8,128)(2,1)S(1)}, bf16[72,128]{1,0:T(8,128)(2,1)S(1)}, u32[]{:S(2)}, u32[]{:S(2)}) %collective-permute-start.3) | collective-permute-done | bytes 18464 | tf_op jit(solution)/shard_map/ppermute | solution.py:182
  11.4 0.0 copy-start.5
  11.4 3.4 %collective-permute-done.1 = bf16[72,128]{1,0:T(8,128)(2,1)S(1)} collective-permute-done((bf16[72,128]{1,0:T(8,128)(2,1)S(1)}, bf16[72,128]{1,0:T(8,128)(2,1)S(1)}, u32[]{:S(2)}, u32[]{:S(2)}) %collective-permute-start.1) | collective-permute-done | bytes 18464 | tf_op jit(solution)/shard_map/ppermute | solution.py:182
  14.7 0.0 copy-done.4
  14.7 0.0 copy-done.5
  14.7 0.0 slice-start
  14.8 0.0 slice-start.1
  14.8 0.7 %slice-done = bf16[64,128]{1,0:T(8,128)(2,1)S(1)} async-done(((bf16[72,128]{1,0:T(8,128)(2,1)}), bf16[64,128]{1,0:T(8,128)(2,1)S(1)}, s32[]{:S(2)}) %slice-start) | async-done | bytes 16408 | tf_op jit(solution)/shard_map/slice | solution.py:184
  15.5 0.0 slice-done.1
  15.5 0.3 %collective-permute-start.4 = (bf16[200,128]{1,0:T(8,128)(2,1)S(1)}, bf16[200,128]{1,0:T(8,128)(2,1)S(1)}, u32[]{:S(2)}, u32[]{:S(2)}) collective-permute-start(bf16[200,128]{1,0:T(8,128)(2,1)S(1)} %pad_maximum_fusion.own_ref), channel_id=1, source_target_pairs={{0,1},{1,0},{2,3},{3,2},{4,5},{5,4},{6,7},{7,6},{8,9},{9,8},{10,11... | collective-permute-start | bytes 153608 | tf_op jit(solution)/shard_map/ppermute | solution.py:185
  15.8 0.0 copy-start.2
  15.8 1.5 %collective-permute-start.5 = (bf16[72,128]{1,0:T(8,128)(2,1)S(1)}, bf16[72,128]{1,0:T(8,128)(2,1)S(1)}, u32[]{:S(2)}, u32[]{:S(2)}) collective-permute-start(bf16[72,128]{1,0:T(8,128)(2,1)S(1)} %get-tuple-element.19), channel_id=1, source_target_pairs={{0,2},{1,3},{2,0},{3,1},{4,6},{5,7},{6,4},{7,5},{8,10},{9,11},{10,... | collective-permute-start | bytes 55304 | tf_op jit(solution)/shard_map/ppermute | solution.py:182
  17.3 2.3 %collective-permute-done.5.near_ref = bf16[72,128]{1,0:T(8,128)(2,1)S(1)} collective-permute-done((bf16[72,128]{1,0:T(8,128)(2,1)S(1)}, bf16[72,128]{1,0:T(8,128)(2,1)S(1)}, u32[]{:S(2)}, u32[]{:S(2)}) %collective-permute-start.5) | collective-permute-done | bytes 18464 | tf_op jit(solution)/shard_map/ppermute | solution.py:182
  19.5 0.0 collective-permute-done.4.mate_ref
  19.5 0.0 copy-done.2
  19.6 1.6 %stat.1 = bf16[1,4,512,256]{3,2,1,0:T(8,128)(2,1)} custom-call(s32[2,64]{1,0:T(2,128)S(1)} %copy-done.2, bf16[160,128]{1,0:T(8,128)(2,1)S(1)} %get-tuple-element.8.keep_ref, bf16[168,128]{1,0:T(8,128)(2,1)S(1)} %collective-permute-done.give_ref, bf16[200,128]{1,0:T(8,128)(2,1)S(1)} %pad_maximum_fusion.own_ref, ...), custom_call_target="tpu_custom_call" | custom-call | tf_op jit(solution)/shard_map/stat/pallas_call | solution.py:190
  (8 shorter events, 0.0 us)
Async XLA Ops:
  0.0 0.7 %copy-start.1 = (s32[8,2]{0,1:T(2,128)S(1)}, s32[8,2]{0,1:T(2,128)}, u32[]{:S(2)}) copy-start(s32[8,2]{0,1:T(2,128)} %param.7) | copy-start | bytes 196
  0.0 0.7 %copy-start.3 = (bf16[2,4]{1,0:T(2,128)(2,1)S(1)}, bf16[2,4]{1,0:T(2,128)(2,1)}, u32[]{:S(2)}) copy-start(bf16[2,4]{1,0:T(2,128)(2,1)} %pheno_hbm.1) | copy-start | bytes 52
  0.7 0.8 %copy-start = (bf16[4,4096]{1,0:T(4,128)(2,1)S(1)}, bf16[4,4096]{1,0:T(4,128)(2,1)}, u32[]{:S(2)}) copy-start(bf16[4,4096]{1,0:T(4,128)(2,1)} %param.4) | copy-start | bytes 98308
  2.2 1.4 %collective-permute-start = (bf16[168,128]{1,0:T(8,128)(2,1)S(1)}, bf16[168,128]{1,0:T(8,128)(2,1)S(1)}, u32[]{:S(2)}, u32[]{:S(2)}) collective-permute-start(bf16[168,128]{1,0:T(8,128)(2,1)S(1)} %get-tuple-element.9), channel_id=1, source_target_pairs={{0,1},{1,0},{2,3},{3,2},{4,5},{5,4},{6,7},{7,6},{8,9},{9,8},{10,11... | collective-permute-start | bytes 129032 | tf_op jit(solution)/shard_map/ppermute | solution.py:171
  3.6 5.7 %collective-permute-start.2 = (bf16[72,128]{1,0:T(8,128)(2,1)S(1)}, bf16[72,128]{1,0:T(8,128)(2,1)S(1)}, u32[]{:S(2)}, u32[]{:S(2)}) collective-permute-start(bf16[72,128]{1,0:T(8,128)(2,1)S(1)} %get-tuple-element.20), channel_id=1, source_target_pairs={{0,8},{1,11},{2,10},{3,9},{4,12},{5,15},{6,14},{7,13},{8,0},{9,3},... | collective-permute-start | bytes 55304 | tf_op jit(solution)/shard_map/ppermute | solution.py:182
  7.6 3.8 %collective-permute-start.3 = (bf16[72,128]{1,0:T(8,128)(2,1)S(1)}, bf16[72,128]{1,0:T(8,128)(2,1)S(1)}, u32[]{:S(2)}, u32[]{:S(2)}) collective-permute-start(bf16[72,128]{1,0:T(8,128)(2,1)S(1)} %get-tuple-element.21), channel_id=1, source_target_pairs={{0,4},{1,7},{2,6},{3,5},{4,0},{5,3},{6,2},{7,1},{8,12},{9,15},{10,... | collective-permute-start | bytes 55304 | tf_op jit(solution)/shard_map/ppermute | solution.py:182
  9.2 5.6 %collective-permute-start.1 = (bf16[72,128]{1,0:T(8,128)(2,1)S(1)}, bf16[72,128]{1,0:T(8,128)(2,1)S(1)}, u32[]{:S(2)}, u32[]{:S(2)}) collective-permute-start(bf16[72,128]{1,0:T(8,128)(2,1)S(1)} %get-tuple-element.22), channel_id=1, source_target_pairs={{0,12},{1,15},{2,14},{3,13},{4,8},{5,11},{6,10},{7,9},{8,4},{9,7},... | collective-permute-start | bytes 55304 | tf_op jit(solution)/shard_map/ppermute | solution.py:182
  9.3 5.4 %copy-start.4 = (bf16[72,128]{1,0:T(8,128)(2,1)}, bf16[72,128]{1,0:T(8,128)(2,1)S(1)}, u32[]{:S(2)}) copy-start(bf16[72,128]{1,0:T(8,128)(2,1)S(1)} %collective-permute-done.2) | copy-start | bytes 55300
  11.4 3.4 %copy-start.5 = (bf16[72,128]{1,0:T(8,128)(2,1)}, bf16[72,128]{1,0:T(8,128)(2,1)S(1)}, u32[]{:S(2)}) copy-start(bf16[72,128]{1,0:T(8,128)(2,1)S(1)} %collective-permute-done.3) | copy-start | bytes 55300
  14.7 0.7 %slice-start = ((bf16[72,128]{1,0:T(8,128)(2,1)}), bf16[64,128]{1,0:T(8,128)(2,1)S(1)}, s32[]{:S(2)}) async-start(bf16[72,128]{1,0:T(8,128)(2,1)} %copy-done.4), calls=%async_computation | async-start | bytes 32768 | tf_op jit(solution)/shard_map/slice | solution.py:184
  14.8 0.7 %slice-start.1 = ((bf16[72,128]{1,0:T(8,128)(2,1)}), bf16[64,128]{1,0:T(8,128)(2,1)S(1)}, s32[]{:S(2)}) async-start(bf16[72,128]{1,0:T(8,128)(2,1)} %copy-done.5), calls=%async_computation.1 | async-start | bytes 32768 | tf_op jit(solution)/shard_map/slice | solution.py:184
  15.5 4.1 %collective-permute-start.4 = (bf16[200,128]{1,0:T(8,128)(2,1)S(1)}, bf16[200,128]{1,0:T(8,128)(2,1)S(1)}, u32[]{:S(2)}, u32[]{:S(2)}) collective-permute-start(bf16[200,128]{1,0:T(8,128)(2,1)S(1)} %pad_maximum_fusion.own_ref), channel_id=1, source_target_pairs={{0,1},{1,0},{2,3},{3,2},{4,5},{5,4},{6,7},{7,6},{8,9},{9,8},{10,11... | collective-permute-start | bytes 153608 | tf_op jit(solution)/shard_map/ppermute | solution.py:185
  15.8 3.8 %copy-start.2 = (s32[2,64]{1,0:T(2,128)S(1)}, s32[2,64]{1,0:T(2,128)}, u32[]{:S(2)}) copy-start(s32[2,64]{1,0:T(2,128)} %perms_ref.1) | copy-start | bytes 1540
  15.8 3.8 %collective-permute-start.5 = (bf16[72,128]{1,0:T(8,128)(2,1)S(1)}, bf16[72,128]{1,0:T(8,128)(2,1)S(1)}, u32[]{:S(2)}, u32[]{:S(2)}) collective-permute-start(bf16[72,128]{1,0:T(8,128)(2,1)S(1)} %get-tuple-element.19), channel_id=1, source_target_pairs={{0,2},{1,3},{2,0},{3,1},{4,6},{5,7},{6,4},{7,5},{8,10},{9,11},{10,... | collective-permute-start | bytes 55304 | tf_op jit(solution)/shard_map/ppermute | solution.py:182

commit v8 on v7

--- a/solution.py
+++ b/solution.py
@@ -60,22 +60,21 @@
     give_ref[len(own_side) * BLOCK :, :] = wave
 
 
-def stat_kernel(
-    pair_count, samps, perms_ref, keep_ref, give_ref, own_ref, mate_ref, near_ref, wave_ref, out_hbm, got_ref, out_ref, sems
-):
+def stat_kernel(pair_count, samps, perms_ref, wave_ref, keep_ref, give_ref, near_ref, *refs):
+    far = pair_count // 2 - 1
+    own_refs, mate_refs = refs[:far], refs[far : 2 * far]
+    out_hbm, got_ref, out_ref, sems = refs[2 * far :]
     pair, samp = lax.axis_index("pair"), lax.axis_index("samp")
     other = samps - 1 - samp
-    far = pair_count // 2 - 1
 
     def place(offset, core, block):
         got_ref[lax.bitwise_xor(pair, offset) * samps + core] = block
 
-    for ref, core in ((own_ref, samp), (mate_ref, other)):
-        for i in range(far):
+    for arrived, core in ((own_refs, samp), (mate_refs, other)):
+        for i, ref in enumerate(arrived):
             offset = 2 * (far - i) + core
-            start = 2 * i * BLOCK
-            place(offset, core, ref[start : start + BLOCK, :])
-            place(offset, samps - 1 - core, ref[start + BLOCK : start + 2 * BLOCK, :])
+            place(offset, core, ref[:BLOCK, :])
+            place(offset, samps - 1 - core, ref[BLOCK : 2 * BLOCK, :])
     place(1, samp, near_ref[:BLOCK, :])
     place(1, other, near_ref[BLOCK : 2 * BLOCK, :])
     itself = (far + 1) * BLOCK
@@ -102,6 +101,8 @@
     b_both = jnp.concatenate([b_hi, b_lo], axis=0)
 
     wave = wave_ref[...].astype(jnp.float32)
+    for ref in (*own_refs, *mate_refs, near_ref):
+        wave = wave + ref[2 * BLOCK :, :].astype(jnp.float32)
     genes = out_ref.shape[0] // rperms
     tiles = -(-samples // LANES)
     pheno = [
@@ -165,7 +166,7 @@
         ],
         compiler_params=pltpu.CompilerParams(vmem_limit_bytes=8 * 1024 * 1024),
         name="pack",
-    )(pairs.T, phenotype, grid)
+    )(*[pltpu.with_memory_space_constraint(x, pltpu.HBM) for x in (pairs.T, phenotype, grid)])
 
     swap = [(i, samps - 1 - i) for i in range(samps)]
     got = lax.ppermute(give, "samp", swap)
@@ -181,16 +182,13 @@
         ]
         arrived.append(lax.ppermute(message, AXES, route))
     *far, near = arrived
-    own = jnp.concatenate([a[: 2 * BLOCK] for a in far] + [sum(a[2 * BLOCK :] for a in far)], axis=0)
-    mate = lax.ppermute(own, "samp", swap)
-    end = 2 * BLOCK * len(far)
-    wave = wave + own[end:] + mate[end:] + near[2 * BLOCK :]
+    mates = [lax.ppermute(a, "samp", swap) for a in far]
     stats = genes * perms.shape[0]
     half = PANEL // samps
     return pl.pallas_call(
         functools.partial(stat_kernel, pair_count, samps),
         out_shape=jax.ShapeDtypeStruct((1, stats, PANEL, half), jnp.bfloat16),
-        in_specs=[vmem] * 7,
+        in_specs=[vmem] * (5 + 2 * len(far)),
         out_specs=hbm,
         scratch_shapes=[
             pltpu.VMEM((pair_count * samps, BLOCK, LANES), dosage.dtype),
@@ -199,7 +197,7 @@
         ],
         compiler_params=pltpu.CompilerParams(vmem_limit_bytes=48 * 1024 * 1024),
         name="stat",
-    )(perms, keep, got, own, mate, near, wave)
+    )(perms, wave, keep, got, near, *far, *mates)
 
 
 def solution(mesh):

time: 21.5 us -> 15.5 us (0.72)
  waiting for transfers between devices: 8.69 us -> 4.11 us
  local copies, waits for them, and re-layouts: 2.17 us -> 0.01 us
  starting transfers between devices: 7.88 us -> 8.6 us
    ppermute x4, waiting for transfers between devices: 7.82 us -> 2.3 us  [on_device(): arrived.append(lax.ppermute(message, AXES, route))]
    unnamed x12 -> x2, local copies, waits for them, and re-layouts: 1.45 us -> 0.01 us
    ppermute x1 -> x3, waiting for transfers between devices: 0.01 us -> 0.94 us  [on_device(): mates = [lax.ppermute(a, 'samp', swap) for a in far]]
    ppermute x1 -> x3, starting transfers between devices: 0.28 us -> 1.01 us  [on_device(): mates = [lax.ppermute(a, 'samp', swap) for a in far]]
    slice x5 -> x0, local copies, waits for them, and re-layouts: 0.71 us -> none  [on_device(): a[:2 * BLOCK]]
  transfers between devices with their start and end apart: 6 -> 8, of which waited for: 5 -> 4; matrix products, arithmetic and copies ran while one was open for 0% -> 0% of each run, Pallas kernels for 0% -> 0%
where the time goes in v8:
time: 15.5 us; the launch traced here: 15.3 us
  starting transfers between devices  8.6 us (55%)
  waiting for transfers between devices  4.11 us (27%)
  Pallas kernels  2.52 us (16%)
    ppermute x4, starting transfers between devices, on_device(): arrived.append(lax.ppermute(message, AXES, route))  7.08 us
    ppermute x4, waiting for transfers between devices, on_device(): arrived.append(lax.ppermute(message, AXES, route))  2.3 us
    pallas_call x1, Pallas kernels, on_device(): pl.pallas_call(functools.partial(stat_kernel, pair_count, samps), out_sha...  1.61 us
    ppermute x3, starting transfers between devices, on_device(): mates = [lax.ppermute(a, 'samp', swap) for a in far]  1.01 us
    ppermute x3, waiting for transfers between devices, on_device(): mates = [lax.ppermute(a, 'samp', swap) for a in far]  0.94 us
    pallas_call x1, Pallas kernels, on_device(): pl.pallas_call(functools.partial(pack_kernel, pair_count, samps), out_sha...  0.92 us
    ppermute x1, waiting for transfers between devices, on_device(): got = lax.ppermute(give, 'samp', swap)  0.87 us
    ppermute x1, starting transfers between devices, on_device(): got = lax.ppermute(give, 'samp', swap)  0.52 us
  transfers between devices with their start and end apart: 8, of which 4 were waited for; matrix products, arithmetic and copies ran while one was open for 0% of the time, Pallas kernels for 0%

profile of v8, /device:TPU:0, one launch (start us, length us, event | category | flops | bytes accessed | tf_op | source)
XLA Modules:
  0.0 15.3 jit_solution(15683100914900665058)
XLA Ops:
  0.0 0.9 %pack.1 = (bf16[160,128]{1,0:T(8,128)(2,1)S(1)}, bf16[168,128]{1,0:T(8,128)(2,1)S(1)}, bf16[8,128]{1,0:T(8,128)(2,1)S(1)}) custom-call(s32[2,8]{1,0:T(2,128)} %bitcast.7, bf16[2,4]{1,0:T(2,128)(2,1)} %pheno_hbm.1, bf16[128,128]{1,0:T(8,128)(2,1)} %bitcast.6), custom_call_target="tpu_custom_call" | custom-call | tf_op jit(solution)/shard_map/pack/pallas_call | solution.py:156
  0.9 0.5 %collective-permute-start = (bf16[168,128]{1,0:T(8,128)(2,1)S(1)}, bf16[168,128]{1,0:T(8,128)(2,1)S(1)}, u32[]{:S(2)}, u32[]{:S(2)}) collective-permute-start(bf16[168,128]{1,0:T(8,128)(2,1)S(1)} %get-tuple-element.9), channel_id=1, source_target_pairs={{0,1},{1,0},{2,3},{3,2},{4,5},{5,4},{6,7},{7,6},{8,9},{9,8},{10,11... | collective-permute-start | bytes 129032 | tf_op jit(solution)/shard_map/ppermute | solution.py:172
  1.4 0.9 %collective-permute-done.give_ref = bf16[168,128]{1,0:T(8,128)(2,1)S(1)} collective-permute-done((bf16[168,128]{1,0:T(8,128)(2,1)S(1)}, bf16[168,128]{1,0:T(8,128)(2,1)S(1)}, u32[]{:S(2)}, u32[]{:S(2)}) %collective-permute-start) | collective-permute-done | bytes 43040 | tf_op jit(solution)/shard_map/ppermute | solution.py:172
  2.3 3.0 %collective-permute-start.4 = (bf16[72,128]{1,0:T(8,128)(2,1)S(1)}, bf16[72,128]{1,0:T(8,128)(2,1)S(1)}, u32[]{:S(2)}, u32[]{:S(2)}) collective-permute-start(bf16[72,128]{1,0:T(8,128)(2,1)S(1)} %get-tuple-element.19), channel_id=1, source_target_pairs={{0,4},{1,7},{2,6},{3,5},{4,0},{5,3},{6,2},{7,1},{8,12},{9,15},{10,... | collective-permute-start | bytes 55304 | tf_op jit(solution)/shard_map/ppermute | solution.py:183
  5.3 2.5 %collective-permute-start.2 = (bf16[72,128]{1,0:T(8,128)(2,1)S(1)}, bf16[72,128]{1,0:T(8,128)(2,1)S(1)}, u32[]{:S(2)}, u32[]{:S(2)}) collective-permute-start(bf16[72,128]{1,0:T(8,128)(2,1)S(1)} %get-tuple-element.20), channel_id=1, source_target_pairs={{0,12},{1,15},{2,14},{3,13},{4,8},{5,11},{6,10},{7,9},{8,4},{9,7},... | collective-permute-start | bytes 55304 | tf_op jit(solution)/shard_map/ppermute | solution.py:183
  7.8 0.0 copy-start
  7.8 0.1 collective-permute-start.3
  7.9 1.5 %collective-permute-start.1 = (bf16[72,128]{1,0:T(8,128)(2,1)S(1)}, bf16[72,128]{1,0:T(8,128)(2,1)S(1)}, u32[]{:S(2)}, u32[]{:S(2)}) collective-permute-start(bf16[72,128]{1,0:T(8,128)(2,1)S(1)} %get-tuple-element.22), channel_id=1, source_target_pairs={{0,2},{1,3},{2,0},{3,1},{4,6},{5,7},{6,4},{7,5},{8,10},{9,11},{10,... | collective-permute-start | bytes 55304 | tf_op jit(solution)/shard_map/ppermute | solution.py:183
  9.4 0.0 collective-permute-done.4.refs_2_
  9.4 0.2 %collective-permute-start.7 = (bf16[72,128]{1,0:T(8,128)(2,1)S(1)}, bf16[72,128]{1,0:T(8,128)(2,1)S(1)}, u32[]{:S(2)}, u32[]{:S(2)}) collective-permute-start(bf16[72,128]{1,0:T(8,128)(2,1)S(1)} %collective-permute-done.4.refs_2_), channel_id=1, source_target_pairs={{0,1},{1,0},{2,3},{3,2},{4,5},{5,4},{6,7},{7,6},{8,9},{9,8},{10,11... | collective-permute-start | bytes 55304 | tf_op jit(solution)/shard_map/ppermute | solution.py:185
  9.6 1.3 %collective-permute-done.2.refs_0_ = bf16[72,128]{1,0:T(8,128)(2,1)S(1)} collective-permute-done((bf16[72,128]{1,0:T(8,128)(2,1)S(1)}, bf16[72,128]{1,0:T(8,128)(2,1)S(1)}, u32[]{:S(2)}, u32[]{:S(2)}) %collective-permute-start.2) | collective-permute-done | bytes 18464 | tf_op jit(solution)/shard_map/ppermute | solution.py:183
  10.9 0.6 %collective-permute-start.5 = (bf16[72,128]{1,0:T(8,128)(2,1)S(1)}, bf16[72,128]{1,0:T(8,128)(2,1)S(1)}, u32[]{:S(2)}, u32[]{:S(2)}) collective-permute-start(bf16[72,128]{1,0:T(8,128)(2,1)S(1)} %collective-permute-done.2.refs_0_), channel_id=1, source_target_pairs={{0,1},{1,0},{2,3},{3,2},{4,5},{5,4},{6,7},{7,6},{8,9},{9,8},{10,11... | collective-permute-start | bytes 55304 | tf_op jit(solution)/shard_map/ppermute | solution.py:185
  11.4 1.0 %collective-permute-done.3.refs_1_ = bf16[72,128]{1,0:T(8,128)(2,1)S(1)} collective-permute-done((bf16[72,128]{1,0:T(8,128)(2,1)S(1)}, bf16[72,128]{1,0:T(8,128)(2,1)S(1)}, u32[]{:S(2)}, u32[]{:S(2)}) %collective-permute-start.3) | collective-permute-done | bytes 18464 | tf_op jit(solution)/shard_map/ppermute | solution.py:183
  12.5 0.2 %collective-permute-start.6 = (bf16[72,128]{1,0:T(8,128)(2,1)S(1)}, bf16[72,128]{1,0:T(8,128)(2,1)S(1)}, u32[]{:S(2)}, u32[]{:S(2)}) collective-permute-start(bf16[72,128]{1,0:T(8,128)(2,1)S(1)} %collective-permute-done.3.refs_1_), channel_id=1, source_target_pairs={{0,1},{1,0},{2,3},{3,2},{4,5},{5,4},{6,7},{7,6},{8,9},{9,8},{10,11... | collective-permute-start | bytes 55304 | tf_op jit(solution)/shard_map/ppermute | solution.py:185
  12.7 0.0 collective-permute-done.1.near_ref
  12.7 0.0 collective-permute-done.7.refs_5_
  12.7 0.0 collective-permute-done.5.refs_3_
  12.7 0.9 %collective-permute-done.6.refs_4_ = bf16[72,128]{1,0:T(8,128)(2,1)S(1)} collective-permute-done((bf16[72,128]{1,0:T(8,128)(2,1)S(1)}, bf16[72,128]{1,0:T(8,128)(2,1)S(1)}, u32[]{:S(2)}, u32[]{:S(2)}) %collective-permute-start.6) | collective-permute-done | bytes 18464 | tf_op jit(solution)/shard_map/ppermute | solution.py:185
  13.7 0.0 copy-done
  13.7 1.6 %stat.1 = bf16[1,4,512,256]{3,2,1,0:T(8,128)(2,1)} custom-call(s32[2,64]{1,0:T(2,128)S(1)} %copy-done, bf16[8,128]{1,0:T(8,128)(2,1)S(1)} %slice_add_fusion.wave_ref, bf16[160,128]{1,0:T(8,128)(2,1)S(1)} %get-tuple-element.10.keep_ref, bf16[168,128]{1,0:T(8,128)(2,1)S(1)} %collective-permute-done.give_ref, ...), custom_call_target="tpu_custom_call" | custom-call | tf_op jit(solution)/shard_map/stat/pallas_call | solution.py:188
  (4 shorter events, 0.0 us)
Async XLA Ops:
  0.9 1.4 %collective-permute-start = (bf16[168,128]{1,0:T(8,128)(2,1)S(1)}, bf16[168,128]{1,0:T(8,128)(2,1)S(1)}, u32[]{:S(2)}, u32[]{:S(2)}) collective-permute-start(bf16[168,128]{1,0:T(8,128)(2,1)S(1)} %get-tuple-element.9), channel_id=1, source_target_pairs={{0,1},{1,0},{2,3},{3,2},{4,5},{5,4},{6,7},{7,6},{8,9},{9,8},{10,11... | collective-permute-start | bytes 129032 | tf_op jit(solution)/shard_map/ppermute | solution.py:172
  2.3 7.1 %collective-permute-start.4 = (bf16[72,128]{1,0:T(8,128)(2,1)S(1)}, bf16[72,128]{1,0:T(8,128)(2,1)S(1)}, u32[]{:S(2)}, u32[]{:S(2)}) collective-permute-start(bf16[72,128]{1,0:T(8,128)(2,1)S(1)} %get-tuple-element.19), channel_id=1, source_target_pairs={{0,4},{1,7},{2,6},{3,5},{4,0},{5,3},{6,2},{7,1},{8,12},{9,15},{10,... | collective-permute-start | bytes 55304 | tf_op jit(solution)/shard_map/ppermute | solution.py:183
  5.3 5.6 %collective-permute-start.2 = (bf16[72,128]{1,0:T(8,128)(2,1)S(1)}, bf16[72,128]{1,0:T(8,128)(2,1)S(1)}, u32[]{:S(2)}, u32[]{:S(2)}) collective-permute-start(bf16[72,128]{1,0:T(8,128)(2,1)S(1)} %get-tuple-element.20), channel_id=1, source_target_pairs={{0,12},{1,15},{2,14},{3,13},{4,8},{5,11},{6,10},{7,9},{8,4},{9,7},... | collective-permute-start | bytes 55304 | tf_op jit(solution)/shard_map/ppermute | solution.py:183
  7.8 5.9 %copy-start = (s32[2,64]{1,0:T(2,128)S(1)}, s32[2,64]{1,0:T(2,128)}, u32[]{:S(2)}) copy-start(s32[2,64]{1,0:T(2,128)} %perms_ref.1) | copy-start | bytes 1540
  7.8 4.7 %collective-permute-start.3 = (bf16[72,128]{1,0:T(8,128)(2,1)S(1)}, bf16[72,128]{1,0:T(8,128)(2,1)S(1)}, u32[]{:S(2)}, u32[]{:S(2)}) collective-permute-start(bf16[72,128]{1,0:T(8,128)(2,1)S(1)} %get-tuple-element.21), channel_id=1, source_target_pairs={{0,8},{1,11},{2,10},{3,9},{4,12},{5,15},{6,14},{7,13},{8,0},{9,3},... | collective-permute-start | bytes 55304 | tf_op jit(solution)/shard_map/ppermute | solution.py:183
  7.9 4.8 %collective-permute-start.1 = (bf16[72,128]{1,0:T(8,128)(2,1)S(1)}, bf16[72,128]{1,0:T(8,128)(2,1)S(1)}, u32[]{:S(2)}, u32[]{:S(2)}) collective-permute-start(bf16[72,128]{1,0:T(8,128)(2,1)S(1)} %get-tuple-element.22), channel_id=1, source_target_pairs={{0,2},{1,3},{2,0},{3,1},{4,6},{5,7},{6,4},{7,5},{8,10},{9,11},{10,... | collective-permute-start | bytes 55304 | tf_op jit(solution)/shard_map/ppermute | solution.py:183
  9.4 3.3 %collective-permute-start.7 = (bf16[72,128]{1,0:T(8,128)(2,1)S(1)}, bf16[72,128]{1,0:T(8,128)(2,1)S(1)}, u32[]{:S(2)}, u32[]{:S(2)}) collective-permute-start(bf16[72,128]{1,0:T(8,128)(2,1)S(1)} %collective-permute-done.4.refs_2_), channel_id=1, source_target_pairs={{0,1},{1,0},{2,3},{3,2},{4,5},{5,4},{6,7},{7,6},{8,9},{9,8},{10,11... | collective-permute-start | bytes 55304 | tf_op jit(solution)/shard_map/ppermute | solution.py:185
  10.9 1.8 %collective-permute-start.5 = (bf16[72,128]{1,0:T(8,128)(2,1)S(1)}, bf16[72,128]{1,0:T(8,128)(2,1)S(1)}, u32[]{:S(2)}, u32[]{:S(2)}) collective-permute-start(bf16[72,128]{1,0:T(8,128)(2,1)S(1)} %collective-permute-done.2.refs_0_), channel_id=1, source_target_pairs={{0,1},{1,0},{2,3},{3,2},{4,5},{5,4},{6,7},{7,6},{8,9},{9,8},{10,11... | collective-permute-start | bytes 55304 | tf_op jit(solution)/shard_map/ppermute | solution.py:185
  12.5 1.2 %collective-permute-start.6 = (bf16[72,128]{1,0:T(8,128)(2,1)S(1)}, bf16[72,128]{1,0:T(8,128)(2,1)S(1)}, u32[]{:S(2)}, u32[]{:S(2)}) collective-permute-start(bf16[72,128]{1,0:T(8,128)(2,1)S(1)} %collective-permute-done.3.refs_1_), channel_id=1, source_target_pairs={{0,1},{1,0},{2,3},{3,2},{4,5},{5,4},{6,7},{7,6},{8,9},{9,8},{10,11... | collective-permute-start | bytes 55304 | tf_op jit(solution)/shard_map/ppermute | solution.py:185

commit v9 on v8

--- a/solution.py
+++ b/solution.py
@@ -171,17 +171,28 @@
     swap = [(i, samps - 1 - i) for i in range(samps)]
     got = lax.ppermute(give, "samp", swap)
     wave = wave + got[rounds * BLOCK :]
-    arrived = []
+    messages = []
     for i in range(rounds - 1):
         blocks = slice(i * BLOCK, (i + 1) * BLOCK)
-        message = jnp.concatenate([keep[blocks], got[blocks], wave], axis=0)
-        route = [
+        messages.append(jnp.concatenate([keep[blocks], got[blocks], wave], axis=0))
+    *far_messages, near_message = messages
+
+    def exchange(i, side=None):
+        bit = 1 << (pair_count // 2 - 1 - i).bit_length()
+        return [
             (p * samps + c, (p ^ offsets(pair_count, c)[i]) * samps + c)
             for p in range(pair_count)
             for c in range(samps)
+            if side in (None, (p & bit > 0))
         ]
-        arrived.append(lax.ppermute(message, AXES, route))
-    *far, near = arrived
+
+    count = len(far_messages)
+    down = [lax.ppermute(far_messages[i], AXES, exchange(i, 1)) for i in range(count - 1)]
+    last = lax.ppermute(far_messages[-1], AXES, exchange(count - 1))
+    near = lax.ppermute(near_message, "pair", [(p, p ^ 1) for p in range(pair_count)])
+    *far_messages, _, _ = lax.optimization_barrier((*far_messages, *down))
+    up = [lax.ppermute(far_messages[i], AXES, exchange(i, 0)) for i in range(count - 1)]
+    far = [d + u for d, u in zip(down, up)] + [last]
     mates = [lax.ppermute(a, "samp", swap) for a in far]
     stats = genes * perms.shape[0]
     half = PANEL // samps

time: 15.5 us -> 21.2 us (1.37)
  starting transfers between devices: 8.6 us -> 12 us
  waiting for transfers between devices: 4.11 us -> 6.25 us
    ppermute x4 -> x6, starting transfers between devices: 7.08 us -> 10.9 us  [the longest x2 3.72 us: on_device(): lax.ppermute(far_messages[i], AXES, exchange(i, 0))]
    ppermute x4 -> x6, waiting for transfers between devices: 2.3 us -> 5.37 us  [the longest x2 3.81 us: on_device(): lax.ppermute(far_messages[i], AXES, exchange(i, 1))]
    ppermute x3, waiting for transfers between devices: 0.94 us -> 0.01 us  [on_device(): mates = [lax.ppermute(a, 'samp', swap) for a in far]]
    ppermute x3, starting transfers between devices: 1.01 us -> 0.66 us  [on_device(): mates = [lax.ppermute(a, 'samp', swap) for a in far]]
  transfers between devices with their start and end apart: 8 -> 10, of which waited for: 4 -> 4; matrix products, arithmetic and copies ran while one was open for 0% -> 0% of each run, Pallas kernels for 0% -> 0%
where the time goes in v9:
time: 21.2 us; the launch traced here: 20.9 us
  starting transfers between devices  12 us (57%)
  waiting for transfers between devices  6.25 us (29%)
  Pallas kernels  2.53 us (12%)
    ppermute x2, waiting for transfers between devices, on_device(): lax.ppermute(far_messages[i], AXES, exchange(i, 1))  3.81 us
    ppermute x2, starting transfers between devices, on_device(): lax.ppermute(far_messages[i], AXES, exchange(i, 0))  3.72 us
    ppermute x1, starting transfers between devices, on_device(): last = lax.ppermute(far_messages[-1], AXES, exchange(count - 1))  3 us
    ppermute x2, starting transfers between devices, on_device(): lax.ppermute(far_messages[i], AXES, exchange(i, 1))  2.58 us
    pallas_call x1, Pallas kernels, on_device(): pl.pallas_call(functools.partial(stat_kernel, pair_count, samps), out_sha...  1.61 us
    ppermute x1, starting transfers between devices, on_device(): lax.ppermute(near_message, 'pair', [(p, p ^ 1) for p in range(pair_count)])  1.56 us
    ppermute x1, waiting for transfers between devices, on_device(): lax.ppermute(near_message, 'pair', [(p, p ^ 1) for p in range(pair_count)])  1.55 us
    pallas_call x1, Pallas kernels, on_device(): pl.pallas_call(functools.partial(pack_kernel, pair_count, samps), out_sha...  0.92 us
  transfers between devices with their start and end apart: 10, of which 4 were waited for; matrix products, arithmetic and copies ran while one was open for 0% of the time, Pallas kernels for 0%

profile of v9, /device:TPU:0, one launch (start us, length us, event | category | flops | bytes accessed | tf_op | source)
XLA Modules:
  0.0 20.9 jit_solution(11538238155885617142)
XLA Ops:
  0.0 0.9 %pack.1 = (bf16[160,128]{1,0:T(8,128)(2,1)S(1)}, bf16[168,128]{1,0:T(8,128)(2,1)S(1)}, bf16[8,128]{1,0:T(8,128)(2,1)S(1)}) custom-call(s32[2,8]{1,0:T(2,128)} %bitcast.7, bf16[2,4]{1,0:T(2,128)(2,1)} %pheno_hbm.1, bf16[128,128]{1,0:T(8,128)(2,1)} %bitcast.6), custom_call_target="tpu_custom_call" | custom-call | tf_op jit(solution)/shard_map/pack/pallas_call | solution.py:156
  0.9 0.5 %collective-permute-start = (bf16[168,128]{1,0:T(8,128)(2,1)S(1)}, bf16[168,128]{1,0:T(8,128)(2,1)S(1)}, u32[]{:S(2)}, u32[]{:S(2)}) collective-permute-start(bf16[168,128]{1,0:T(8,128)(2,1)S(1)} %get-tuple-element.11), channel_id=1, source_target_pairs={{0,1},{1,0},{2,3},{3,2},{4,5},{5,4},{6,7},{7,6},{8,9},{9,8},{10,11... | collective-permute-start | bytes 129032 | tf_op jit(solution)/shard_map/ppermute | solution.py:172
  1.4 0.9 %collective-permute-done.give_ref = bf16[168,128]{1,0:T(8,128)(2,1)S(1)} collective-permute-done((bf16[168,128]{1,0:T(8,128)(2,1)S(1)}, bf16[168,128]{1,0:T(8,128)(2,1)S(1)}, u32[]{:S(2)}, u32[]{:S(2)}) %collective-permute-start) | collective-permute-done | bytes 43040 | tf_op jit(solution)/shard_map/ppermute | solution.py:172
  2.3 1.3 %collective-permute-start.2 = (bf16[72,128]{1,0:T(8,128)(2,1)S(1)}, bf16[72,128]{1,0:T(8,128)(2,1)S(1)}, u32[]{:S(2)}, u32[]{:S(2)}) collective-permute-start(bf16[72,128]{1,0:T(8,128)(2,1)S(1)} %get-tuple-element.13), channel_id=1, source_target_pairs={{8,4},{9,7},{10,6},{11,5},{12,0},{13,3},{14,2},{15,1},{24,20},{25,... | collective-permute-start | bytes 55304 | tf_op jit(solution)/shard_map/ppermute | solution.py:190
  3.6 1.3 %collective-permute-start.3 = (bf16[72,128]{1,0:T(8,128)(2,1)S(1)}, bf16[72,128]{1,0:T(8,128)(2,1)S(1)}, u32[]{:S(2)}, u32[]{:S(2)}) collective-permute-start(bf16[72,128]{1,0:T(8,128)(2,1)S(1)} %get-tuple-element.14), channel_id=1, source_target_pairs={{8,0},{9,3},{10,2},{11,1},{12,4},{13,7},{14,6},{15,5},{24,16},{25,... | collective-permute-start | bytes 55304 | tf_op jit(solution)/shard_map/ppermute | solution.py:190
  4.9 3.0 %collective-permute-start.6 = (bf16[72,128]{1,0:T(8,128)(2,1)S(1)}, bf16[72,128]{1,0:T(8,128)(2,1)S(1)}, u32[]{:S(2)}, u32[]{:S(2)}) collective-permute-start(bf16[72,128]{1,0:T(8,128)(2,1)S(1)} %get-tuple-element.23), channel_id=1, source_target_pairs={{0,4},{1,7},{2,6},{3,5},{4,0},{5,3},{6,2},{7,1},{8,12},{9,15},{10,... | collective-permute-start | bytes 55304 | tf_op jit(solution)/shard_map/ppermute | solution.py:191
  7.9 2.5 %collective-permute-done.2 = bf16[72,128]{1,0:T(8,128)(2,1)S(1)} collective-permute-done((bf16[72,128]{1,0:T(8,128)(2,1)S(1)}, bf16[72,128]{1,0:T(8,128)(2,1)S(1)}, u32[]{:S(2)}, u32[]{:S(2)}) %collective-permute-start.2) | collective-permute-done | bytes 18464 | tf_op jit(solution)/shard_map/ppermute | solution.py:190
  10.4 1.3 %collective-permute-done.3 = bf16[72,128]{1,0:T(8,128)(2,1)S(1)} collective-permute-done((bf16[72,128]{1,0:T(8,128)(2,1)S(1)}, bf16[72,128]{1,0:T(8,128)(2,1)S(1)}, u32[]{:S(2)}, u32[]{:S(2)}) %collective-permute-start.3) | collective-permute-done | bytes 18464 | tf_op jit(solution)/shard_map/ppermute | solution.py:190
  11.7 2.4 %collective-permute-start.4 = (bf16[72,128]{1,0:T(8,128)(2,1)S(1)}, bf16[72,128]{1,0:T(8,128)(2,1)S(1)}, u32[]{:S(2)}, u32[]{:S(2)}) collective-permute-start(bf16[72,128]{1,0:T(8,128)(2,1)S(1)} %get-tuple-element.13), channel_id=1, source_target_pairs={{0,12},{1,15},{2,14},{3,13},{4,8},{5,11},{6,10},{7,9},{16,28},{17,... | collective-permute-start | bytes 55304 | tf_op jit(solution)/shard_map/ppermute | solution.py:194
  14.2 1.3 %collective-permute-start.5 = (bf16[72,128]{1,0:T(8,128)(2,1)S(1)}, bf16[72,128]{1,0:T(8,128)(2,1)S(1)}, u32[]{:S(2)}, u32[]{:S(2)}) collective-permute-start(bf16[72,128]{1,0:T(8,128)(2,1)S(1)} %get-tuple-element.14), channel_id=1, source_target_pairs={{0,8},{1,11},{2,10},{3,9},{4,12},{5,15},{6,14},{7,13},{16,24},{17,... | collective-permute-start | bytes 55304 | tf_op jit(solution)/shard_map/ppermute | solution.py:194
  15.5 1.6 %collective-permute-start.1 = (bf16[72,128]{1,0:T(8,128)(2,1)S(1)}, bf16[72,128]{1,0:T(8,128)(2,1)S(1)}, u32[]{:S(2)}, u32[]{:S(2)}) collective-permute-start(bf16[72,128]{1,0:T(8,128)(2,1)S(1)} %get-tuple-element.26), channel_id=1, source_target_pairs={{0,2},{2,0},{4,6},{6,4},{8,10},{10,8},{12,14},{14,12},{1,3},{3,1},... | collective-permute-start | bytes 55304 | tf_op jit(solution)/shard_map/ppermute | solution.py:192
  17.0 0.0 collective-permute-done.6.refs_2_
  17.0 0.0 collective-permute-start.9
  17.0 0.0 collective-permute-done.4
  17.1 0.0 copy-start
  17.1 0.6 %collective-permute-start.7 = (bf16[72,128]{1,0:T(8,128)(2,1)S(1)}, bf16[72,128]{1,0:T(8,128)(2,1)S(1)}, u32[]{:S(2)}, u32[]{:S(2)}) collective-permute-start(bf16[72,128]{1,0:T(8,128)(2,1)S(1)} %add.10.refs_0_), channel_id=1, source_target_pairs={{0,1},{1,0},{2,3},{3,2},{4,5},{5,4},{6,7},{7,6},{8,9},{9,8},{10,11... | collective-permute-start | bytes 55304 | tf_op jit(solution)/shard_map/ppermute | solution.py:196
  17.6 0.0 collective-permute-done.5
  17.7 0.1 collective-permute-start.8
  17.8 1.6 %collective-permute-done.1.near_ref = bf16[72,128]{1,0:T(8,128)(2,1)S(1)} collective-permute-done((bf16[72,128]{1,0:T(8,128)(2,1)S(1)}, bf16[72,128]{1,0:T(8,128)(2,1)S(1)}, u32[]{:S(2)}, u32[]{:S(2)}) %collective-permute-start.1) | collective-permute-done | bytes 18464 | tf_op jit(solution)/shard_map/ppermute | solution.py:192
  19.3 0.0 collective-permute-done.9.refs_5_
  19.3 0.0 collective-permute-done.7.refs_3_
  19.3 0.0 collective-permute-done.8.refs_4_
  19.3 0.0 copy-done
  19.3 1.6 %stat.1 = bf16[1,4,512,256]{3,2,1,0:T(8,128)(2,1)} custom-call(s32[2,64]{1,0:T(2,128)S(1)} %copy-done, bf16[8,128]{1,0:T(8,128)(2,1)S(1)} %slice_add_fusion.wave_ref, bf16[160,128]{1,0:T(8,128)(2,1)S(1)} %get-tuple-element.12.keep_ref, bf16[168,128]{1,0:T(8,128)(2,1)S(1)} %collective-permute-done.give_ref, ...), custom_call_target="tpu_custom_call" | custom-call | tf_op jit(solution)/shard_map/stat/pallas_call | solution.py:199
  (6 shorter events, 0.0 us)
Async XLA Ops:
  0.9 1.4 %collective-permute-start = (bf16[168,128]{1,0:T(8,128)(2,1)S(1)}, bf16[168,128]{1,0:T(8,128)(2,1)S(1)}, u32[]{:S(2)}, u32[]{:S(2)}) collective-permute-start(bf16[168,128]{1,0:T(8,128)(2,1)S(1)} %get-tuple-element.11), channel_id=1, source_target_pairs={{0,1},{1,0},{2,3},{3,2},{4,5},{5,4},{6,7},{7,6},{8,9},{9,8},{10,11... | collective-permute-start | bytes 129032 | tf_op jit(solution)/shard_map/ppermute | solution.py:172
  2.3 8.1 %collective-permute-start.2 = (bf16[72,128]{1,0:T(8,128)(2,1)S(1)}, bf16[72,128]{1,0:T(8,128)(2,1)S(1)}, u32[]{:S(2)}, u32[]{:S(2)}) collective-permute-start(bf16[72,128]{1,0:T(8,128)(2,1)S(1)} %get-tuple-element.13), channel_id=1, source_target_pairs={{8,4},{9,7},{10,6},{11,5},{12,0},{13,3},{14,2},{15,1},{24,20},{25,... | collective-permute-start | bytes 55304 | tf_op jit(solution)/shard_map/ppermute | solution.py:190
  3.6 8.1 %collective-permute-start.3 = (bf16[72,128]{1,0:T(8,128)(2,1)S(1)}, bf16[72,128]{1,0:T(8,128)(2,1)S(1)}, u32[]{:S(2)}, u32[]{:S(2)}) collective-permute-start(bf16[72,128]{1,0:T(8,128)(2,1)S(1)} %get-tuple-element.14), channel_id=1, source_target_pairs={{8,0},{9,3},{10,2},{11,1},{12,4},{13,7},{14,6},{15,5},{24,16},{25,... | collective-permute-start | bytes 55304 | tf_op jit(solution)/shard_map/ppermute | solution.py:190
  4.9 12.1 %collective-permute-start.6 = (bf16[72,128]{1,0:T(8,128)(2,1)S(1)}, bf16[72,128]{1,0:T(8,128)(2,1)S(1)}, u32[]{:S(2)}, u32[]{:S(2)}) collective-permute-start(bf16[72,128]{1,0:T(8,128)(2,1)S(1)} %get-tuple-element.23), channel_id=1, source_target_pairs={{0,4},{1,7},{2,6},{3,5},{4,0},{5,3},{6,2},{7,1},{8,12},{9,15},{10,... | collective-permute-start | bytes 55304 | tf_op jit(solution)/shard_map/ppermute | solution.py:191
  11.7 5.3 %collective-permute-start.4 = (bf16[72,128]{1,0:T(8,128)(2,1)S(1)}, bf16[72,128]{1,0:T(8,128)(2,1)S(1)}, u32[]{:S(2)}, u32[]{:S(2)}) collective-permute-start(bf16[72,128]{1,0:T(8,128)(2,1)S(1)} %get-tuple-element.13), channel_id=1, source_target_pairs={{0,12},{1,15},{2,14},{3,13},{4,8},{5,11},{6,10},{7,9},{16,28},{17,... | collective-permute-start | bytes 55304 | tf_op jit(solution)/shard_map/ppermute | solution.py:194
  14.2 3.5 %collective-permute-start.5 = (bf16[72,128]{1,0:T(8,128)(2,1)S(1)}, bf16[72,128]{1,0:T(8,128)(2,1)S(1)}, u32[]{:S(2)}, u32[]{:S(2)}) collective-permute-start(bf16[72,128]{1,0:T(8,128)(2,1)S(1)} %get-tuple-element.14), channel_id=1, source_target_pairs={{0,8},{1,11},{2,10},{3,9},{4,12},{5,15},{6,14},{7,13},{16,24},{17,... | collective-permute-start | bytes 55304 | tf_op jit(solution)/shard_map/ppermute | solution.py:194
  15.5 3.8 %collective-permute-start.1 = (bf16[72,128]{1,0:T(8,128)(2,1)S(1)}, bf16[72,128]{1,0:T(8,128)(2,1)S(1)}, u32[]{:S(2)}, u32[]{:S(2)}) collective-permute-start(bf16[72,128]{1,0:T(8,128)(2,1)S(1)} %get-tuple-element.26), channel_id=1, source_target_pairs={{0,2},{2,0},{4,6},{6,4},{8,10},{10,8},{12,14},{14,12},{1,3},{3,1},... | collective-permute-start | bytes 55304 | tf_op jit(solution)/shard_map/ppermute | solution.py:192
  17.0 2.3 %collective-permute-start.9 = (bf16[72,128]{1,0:T(8,128)(2,1)S(1)}, bf16[72,128]{1,0:T(8,128)(2,1)S(1)}, u32[]{:S(2)}, u32[]{:S(2)}) collective-permute-start(bf16[72,128]{1,0:T(8,128)(2,1)S(1)} %collective-permute-done.6.refs_2_), channel_id=1, source_target_pairs={{0,1},{1,0},{2,3},{3,2},{4,5},{5,4},{6,7},{7,6},{8,9},{9,8},{10,11... | collective-permute-start | bytes 55304 | tf_op jit(solution)/shard_map/ppermute | solution.py:196
  17.1 2.3 %copy-start = (s32[2,64]{1,0:T(2,128)S(1)}, s32[2,64]{1,0:T(2,128)}, u32[]{:S(2)}) copy-start(s32[2,64]{1,0:T(2,128)} %perms_ref.1) | copy-start | bytes 1540
  17.1 2.2 %collective-permute-start.7 = (bf16[72,128]{1,0:T(8,128)(2,1)S(1)}, bf16[72,128]{1,0:T(8,128)(2,1)S(1)}, u32[]{:S(2)}, u32[]{:S(2)}) collective-permute-start(bf16[72,128]{1,0:T(8,128)(2,1)S(1)} %add.10.refs_0_), channel_id=1, source_target_pairs={{0,1},{1,0},{2,3},{3,2},{4,5},{5,4},{6,7},{7,6},{8,9},{9,8},{10,11... | collective-permute-start | bytes 55304 | tf_op jit(solution)/shard_map/ppermute | solution.py:196
  17.7 1.7 %collective-permute-start.8 = (bf16[72,128]{1,0:T(8,128)(2,1)S(1)}, bf16[72,128]{1,0:T(8,128)(2,1)S(1)}, u32[]{:S(2)}, u32[]{:S(2)}) collective-permute-start(bf16[72,128]{1,0:T(8,128)(2,1)S(1)} %add.11.refs_1_), channel_id=1, source_target_pairs={{0,1},{1,0},{2,3},{3,2},{4,5},{5,4},{6,7},{7,6},{8,9},{9,8},{10,11... | collective-permute-start | bytes 55304 | tf_op jit(solution)/shard_map/ppermute | solution.py:196

commit v10 on v8

--- a/solution.py
+++ b/solution.py
@@ -15,7 +15,17 @@
 
 
 def offsets(pair_count, core):
-    return [2 * i + core for i in range(pair_count // 2 - 1, 0, -1)] + [1, 0]
+    shared = pair_count - 2
+    rest = [e for e in range(1, pair_count) if e != shared]
+    mine = rest[: len(rest) // 2] if core == 0 else rest[len(rest) // 2 :]
+    if core == 0:
+        mine = mine[1:] + mine[:1]
+    return mine[1:] + mine[:1] + [shared, 0]
+
+
+def shifted(pair, offset, pair_count, sign=1):
+    high = (pair // 2 + sign * (offset // 2) + pair_count // 2) % (pair_count // 2)
+    return high * 2 + (pair + offset) % 2
 
 
 def wave_rows(genes, samples):
@@ -52,7 +62,7 @@
     own_side, far_side = offsets(pair_count, 0), offsets(pair_count, 1)
     for i, (even, odd) in enumerate(zip(own_side, far_side)):
         for ref, core in ((keep_ref, samp), (give_ref, samps - 1 - samp)):
-            n = lax.bitwise_xor(pair, even + (odd - even) * core)
+            n = shifted(pair, jnp.where(core == 0, even, odd), pair_count)
             for j in range(2):
                 start = pl.multiple_of(pairs_ref[j, n] * TILE, TILE)
                 place = i * BLOCK + j * TILE
@@ -68,15 +78,16 @@
     other = samps - 1 - samp
 
     def place(offset, core, block):
-        got_ref[lax.bitwise_xor(pair, offset) * samps + core] = block
-
+        got_ref[shifted(pair, offset, pair_count, -1) * samps + core] = block
+
+    even, odd = offsets(pair_count, 0), offsets(pair_count, 1)
     for arrived, core in ((own_refs, samp), (mate_refs, other)):
         for i, ref in enumerate(arrived):
-            offset = 2 * (far - i) + core
+            offset = jnp.where(core == 0, even[i], odd[i])
             place(offset, core, ref[:BLOCK, :])
             place(offset, samps - 1 - core, ref[BLOCK : 2 * BLOCK, :])
-    place(1, samp, near_ref[:BLOCK, :])
-    place(1, other, near_ref[BLOCK : 2 * BLOCK, :])
+    place(even[far], samp, near_ref[:BLOCK, :])
+    place(even[far], other, near_ref[BLOCK : 2 * BLOCK, :])
     itself = (far + 1) * BLOCK
     place(0, samp, keep_ref[itself : itself + BLOCK, :])
     place(0, other, give_ref[itself : itself + BLOCK, :])
@@ -123,18 +134,21 @@
     c_hi = tail.astype(jnp.bfloat16).astype(jnp.float32)
     c_lo = tail - c_hi
 
-    geno_a = jnp.concatenate([by_samples(panel_a, q) for q in range(TILE // s_dev)], axis=1)
-    a_rows = jnp.concatenate([geno_a, geno_a], axis=0).T
-    a_minus = -a_rows.astype(jnp.bfloat16)
+    rows = []
+    for q in range(TILE // s_dev):
+        geno_a = by_samples(panel_a, q)
+        rows.append(jnp.concatenate([geno_a, geno_a], axis=0).astype(jnp.bfloat16).T)
     copies = []
-    for k in range(len(yrows)):
-        scaled = (a_rows * yrows[k]).astype(jnp.bfloat16)
-        left = jnp.concatenate([scaled, a_minus], axis=1)
+    for k, yrow in enumerate(yrows):
+        yrow = yrow.astype(jnp.bfloat16)
         tails = [jnp.broadcast_to(c[k : k + 1], geno_b.shape).astype(jnp.bfloat16) for c in (c_hi, c_lo)]
         right = jnp.concatenate([b_both] + tails, axis=0)
-        out_ref[k] = jnp.dot(left, right, preferred_element_type=jnp.float32).astype(out_ref.dtype)
-        copies.append(pltpu.make_async_copy(out_ref.at[k], out_hbm.at[0, k], sems.at[k]))
-        copies[-1].start()
+        for q, part in enumerate(rows):
+            left = jnp.concatenate([part * yrow, -part], axis=1)
+            piece = slice(q * LANES, (q + 1) * LANES)
+            out_ref[k, piece, :] = jnp.dot(left, right, preferred_element_type=jnp.float32).astype(out_ref.dtype)
+            copies.append(pltpu.make_async_copy(out_ref.at[k, piece], out_hbm.at[0, k, piece], sems.at[k, q]))
+            copies[-1].start()
     for copy in copies:
         copy.wait()
 
@@ -176,7 +190,7 @@
         blocks = slice(i * BLOCK, (i + 1) * BLOCK)
         message = jnp.concatenate([keep[blocks], got[blocks], wave], axis=0)
         route = [
-            (p * samps + c, (p ^ offsets(pair_count, c)[i]) * samps + c)
+            (p * samps + c, shifted(p, offsets(pair_count, c)[i], pair_count) * samps + c)
             for p in range(pair_count)
             for c in range(samps)
         ]
@@ -193,7 +207,7 @@
         scratch_shapes=[
             pltpu.VMEM((pair_count * samps, BLOCK, LANES), dosage.dtype),
             pltpu.VMEM((stats, PANEL, half), jnp.bfloat16),
-            pltpu.SemaphoreType.DMA((stats,)),
+            pltpu.SemaphoreType.DMA((stats, PANEL // LANES)),
         ],
         compiler_params=pltpu.CompilerParams(vmem_limit_bytes=48 * 1024 * 1024),
         name="stat",

time: 15.5 us -> 15.1 us (0.974)
  waiting for transfers between devices: 4.11 us -> 3.03 us
  starting transfers between devices: 8.6 us -> 9.34 us
    ppermute x4, starting transfers between devices: 7.08 us -> 8.27 us  [on_device(): arrived.append(lax.ppermute(message, AXES, route))]
    ppermute x4, waiting for transfers between devices: 2.3 us -> 1.32 us  [on_device(): arrived.append(lax.ppermute(message, AXES, route))]
    ppermute x3, starting transfers between devices: 1.01 us -> 0.55 us  [on_device(): mates = [lax.ppermute(a, 'samp', swap) for a in far]]
where the time goes in v10:
time: 15.1 us; the launch traced here: 14.9 us
  starting transfers between devices  9.34 us (62%)
  waiting for transfers between devices  3.03 us (20%)
  Pallas kernels  2.5 us (17%)
    ppermute x4, starting transfers between devices, on_device(): arrived.append(lax.ppermute(message, AXES, route))  8.27 us
    pallas_call x1, Pallas kernels, on_device(): pl.pallas_call(functools.partial(stat_kernel, pair_count, samps), out_sha...  1.6 us
    ppermute x4, waiting for transfers between devices, on_device(): arrived.append(lax.ppermute(message, AXES, route))  1.32 us
    pallas_call x1, Pallas kernels, on_device(): pl.pallas_call(functools.partial(pack_kernel, pair_count, samps), out_sha...  0.9 us
    ppermute x1, waiting for transfers between devices, on_device(): got = lax.ppermute(give, 'samp', swap)  0.87 us
    ppermute x3, waiting for transfers between devices, on_device(): mates = [lax.ppermute(a, 'samp', swap) for a in far]  0.84 us
    ppermute x3, starting transfers between devices, on_device(): mates = [lax.ppermute(a, 'samp', swap) for a in far]  0.55 us
    ppermute x1, starting transfers between devices, on_device(): got = lax.ppermute(give, 'samp', swap)  0.52 us
  transfers between devices with their start and end apart: 8, of which 4 were waited for; matrix products, arithmetic and copies ran while one was open for 0% of the time, Pallas kernels for 0%

profile of v10, /device:TPU:0, one launch (start us, length us, event | category | flops | bytes accessed | tf_op | source)
XLA Modules:
  0.0 14.9 jit_solution(7676790633991532702)
XLA Ops:
  0.0 0.9 %pack.1 = (bf16[160,128]{1,0:T(8,128)(2,1)S(1)}, bf16[168,128]{1,0:T(8,128)(2,1)S(1)}, bf16[8,128]{1,0:T(8,128)(2,1)S(1)}) custom-call(s32[2,8]{1,0:T(2,128)} %bitcast.7, bf16[2,4]{1,0:T(2,128)(2,1)} %pheno_hbm.1, bf16[128,128]{1,0:T(8,128)(2,1)} %bitcast.6), custom_call_target="tpu_custom_call" | custom-call | tf_op jit(solution)/shard_map/pack/pallas_call | solution.py:170
  0.9 0.5 %collective-permute-start = (bf16[168,128]{1,0:T(8,128)(2,1)S(1)}, bf16[168,128]{1,0:T(8,128)(2,1)S(1)}, u32[]{:S(2)}, u32[]{:S(2)}) collective-permute-start(bf16[168,128]{1,0:T(8,128)(2,1)S(1)} %get-tuple-element.9), channel_id=1, source_target_pairs={{0,1},{1,0},{2,3},{3,2},{4,5},{5,4},{6,7},{7,6},{8,9},{9,8},{10,11... | collective-permute-start | bytes 129032 | tf_op jit(solution)/shard_map/ppermute | solution.py:186
  1.4 0.9 %collective-permute-done.give_ref = bf16[168,128]{1,0:T(8,128)(2,1)S(1)} collective-permute-done((bf16[168,128]{1,0:T(8,128)(2,1)S(1)}, bf16[168,128]{1,0:T(8,128)(2,1)S(1)}, u32[]{:S(2)}, u32[]{:S(2)}) %collective-permute-start) | collective-permute-done | bytes 43040 | tf_op jit(solution)/shard_map/ppermute | solution.py:186
  2.3 3.0 %collective-permute-start.4 = (bf16[72,128]{1,0:T(8,128)(2,1)S(1)}, bf16[72,128]{1,0:T(8,128)(2,1)S(1)}, u32[]{:S(2)}, u32[]{:S(2)}) collective-permute-start(bf16[72,128]{1,0:T(8,128)(2,1)S(1)} %get-tuple-element.19), channel_id=1, source_target_pairs={{0,4},{1,9},{2,6},{3,11},{4,8},{5,13},{6,10},{7,15},{8,12},{9,1},{... | collective-permute-start | bytes 55304 | tf_op jit(solution)/shard_map/ppermute | solution.py:197
  5.3 2.5 %collective-permute-start.2 = (bf16[72,128]{1,0:T(8,128)(2,1)S(1)}, bf16[72,128]{1,0:T(8,128)(2,1)S(1)}, u32[]{:S(2)}, u32[]{:S(2)}) collective-permute-start(bf16[72,128]{1,0:T(8,128)(2,1)S(1)} %get-tuple-element.20), channel_id=1, source_target_pairs={{0,6},{1,11},{2,4},{3,9},{4,10},{5,15},{6,8},{7,13},{8,14},{9,3},{... | collective-permute-start | bytes 55304 | tf_op jit(solution)/shard_map/ppermute | solution.py:197
  7.8 0.0 copy-start
  7.8 0.5 %collective-permute-start.3 = (bf16[72,128]{1,0:T(8,128)(2,1)S(1)}, bf16[72,128]{1,0:T(8,128)(2,1)S(1)}, u32[]{:S(2)}, u32[]{:S(2)}) collective-permute-start(bf16[72,128]{1,0:T(8,128)(2,1)S(1)} %get-tuple-element.21), channel_id=1, source_target_pairs={{0,2},{1,15},{2,0},{3,13},{4,6},{5,3},{6,4},{7,1},{8,10},{9,7},{10... | collective-permute-start | bytes 55304 | tf_op jit(solution)/shard_map/ppermute | solution.py:197
  8.3 2.2 %collective-permute-start.1 = (bf16[72,128]{1,0:T(8,128)(2,1)S(1)}, bf16[72,128]{1,0:T(8,128)(2,1)S(1)}, u32[]{:S(2)}, u32[]{:S(2)}) collective-permute-start(bf16[72,128]{1,0:T(8,128)(2,1)S(1)} %get-tuple-element.22), channel_id=1, source_target_pairs={{0,12},{1,13},{2,14},{3,15},{4,0},{5,1},{6,2},{7,3},{8,4},{9,5},{1... | collective-permute-start | bytes 55304 | tf_op jit(solution)/shard_map/ppermute | solution.py:197
  10.6 0.0 collective-permute-done.4.refs_2_
  10.6 0.0 collective-permute-start.7
  10.6 1.3 %collective-permute-done.2.refs_0_ = bf16[72,128]{1,0:T(8,128)(2,1)S(1)} collective-permute-done((bf16[72,128]{1,0:T(8,128)(2,1)S(1)}, bf16[72,128]{1,0:T(8,128)(2,1)S(1)}, u32[]{:S(2)}, u32[]{:S(2)}) %collective-permute-start.2) | collective-permute-done | bytes 18464 | tf_op jit(solution)/shard_map/ppermute | solution.py:197
  12.0 0.0 collective-permute-start.5
  12.0 0.0 collective-permute-done.3.refs_1_
  12.0 0.5 %collective-permute-start.6 = (bf16[72,128]{1,0:T(8,128)(2,1)S(1)}, bf16[72,128]{1,0:T(8,128)(2,1)S(1)}, u32[]{:S(2)}, u32[]{:S(2)}) collective-permute-start(bf16[72,128]{1,0:T(8,128)(2,1)S(1)} %collective-permute-done.3.refs_1_), channel_id=1, source_target_pairs={{0,1},{1,0},{2,3},{3,2},{4,5},{5,4},{6,7},{7,6},{8,9},{9,8},{10,11... | collective-permute-start | bytes 55304 | tf_op jit(solution)/shard_map/ppermute | solution.py:199
  12.5 0.0 collective-permute-done.1.near_ref
  12.5 0.0 collective-permute-done.7.refs_5_
  12.5 0.7 %collective-permute-done.5.refs_3_ = bf16[72,128]{1,0:T(8,128)(2,1)S(1)} collective-permute-done((bf16[72,128]{1,0:T(8,128)(2,1)S(1)}, bf16[72,128]{1,0:T(8,128)(2,1)S(1)}, u32[]{:S(2)}, u32[]{:S(2)}) %collective-permute-start.5) | collective-permute-done | bytes 18464 | tf_op jit(solution)/shard_map/ppermute | solution.py:199
  13.1 0.2 %collective-permute-done.6.refs_4_ = bf16[72,128]{1,0:T(8,128)(2,1)S(1)} collective-permute-done((bf16[72,128]{1,0:T(8,128)(2,1)S(1)}, bf16[72,128]{1,0:T(8,128)(2,1)S(1)}, u32[]{:S(2)}, u32[]{:S(2)}) %collective-permute-start.6) | collective-permute-done | bytes 18464 | tf_op jit(solution)/shard_map/ppermute | solution.py:199
  13.3 0.0 copy-done
  13.3 1.6 %stat.1 = bf16[1,4,512,256]{3,2,1,0:T(8,128)(2,1)} custom-call(s32[2,64]{1,0:T(2,128)S(1)} %copy-done, bf16[8,128]{1,0:T(8,128)(2,1)S(1)} %slice_add_fusion.wave_ref, bf16[160,128]{1,0:T(8,128)(2,1)S(1)} %get-tuple-element.10.keep_ref, bf16[168,128]{1,0:T(8,128)(2,1)S(1)} %collective-permute-done.give_ref, ...), custom_call_target="tpu_custom_call" | custom-call | tf_op jit(solution)/shard_map/stat/pallas_call | solution.py:202
  (4 shorter events, 0.0 us)
Async XLA Ops:
  0.9 1.4 %collective-permute-start = (bf16[168,128]{1,0:T(8,128)(2,1)S(1)}, bf16[168,128]{1,0:T(8,128)(2,1)S(1)}, u32[]{:S(2)}, u32[]{:S(2)}) collective-permute-start(bf16[168,128]{1,0:T(8,128)(2,1)S(1)} %get-tuple-element.9), channel_id=1, source_target_pairs={{0,1},{1,0},{2,3},{3,2},{4,5},{5,4},{6,7},{7,6},{8,9},{9,8},{10,11... | collective-permute-start | bytes 129032 | tf_op jit(solution)/shard_map/ppermute | solution.py:186
  2.3 8.3 %collective-permute-start.4 = (bf16[72,128]{1,0:T(8,128)(2,1)S(1)}, bf16[72,128]{1,0:T(8,128)(2,1)S(1)}, u32[]{:S(2)}, u32[]{:S(2)}) collective-permute-start(bf16[72,128]{1,0:T(8,128)(2,1)S(1)} %get-tuple-element.19), channel_id=1, source_target_pairs={{0,4},{1,9},{2,6},{3,11},{4,8},{5,13},{6,10},{7,15},{8,12},{9,1},{... | collective-permute-start | bytes 55304 | tf_op jit(solution)/shard_map/ppermute | solution.py:197
  5.3 6.7 %collective-permute-start.2 = (bf16[72,128]{1,0:T(8,128)(2,1)S(1)}, bf16[72,128]{1,0:T(8,128)(2,1)S(1)}, u32[]{:S(2)}, u32[]{:S(2)}) collective-permute-start(bf16[72,128]{1,0:T(8,128)(2,1)S(1)} %get-tuple-element.20), channel_id=1, source_target_pairs={{0,6},{1,11},{2,4},{3,9},{4,10},{5,15},{6,8},{7,13},{8,14},{9,3},{... | collective-permute-start | bytes 55304 | tf_op jit(solution)/shard_map/ppermute | solution.py:197
  7.8 5.5 %copy-start = (s32[2,64]{1,0:T(2,128)S(1)}, s32[2,64]{1,0:T(2,128)}, u32[]{:S(2)}) copy-start(s32[2,64]{1,0:T(2,128)} %perms_ref.1) | copy-start | bytes 1540
  7.8 4.2 %collective-permute-start.3 = (bf16[72,128]{1,0:T(8,128)(2,1)S(1)}, bf16[72,128]{1,0:T(8,128)(2,1)S(1)}, u32[]{:S(2)}, u32[]{:S(2)}) collective-permute-start(bf16[72,128]{1,0:T(8,128)(2,1)S(1)} %get-tuple-element.21), channel_id=1, source_target_pairs={{0,2},{1,15},{2,0},{3,13},{4,6},{5,3},{6,4},{7,1},{8,10},{9,7},{10... | collective-permute-start | bytes 55304 | tf_op jit(solution)/shard_map/ppermute | solution.py:197
  8.3 4.1 %collective-permute-start.1 = (bf16[72,128]{1,0:T(8,128)(2,1)S(1)}, bf16[72,128]{1,0:T(8,128)(2,1)S(1)}, u32[]{:S(2)}, u32[]{:S(2)}) collective-permute-start(bf16[72,128]{1,0:T(8,128)(2,1)S(1)} %get-tuple-element.22), channel_id=1, source_target_pairs={{0,12},{1,13},{2,14},{3,15},{4,0},{5,1},{6,2},{7,3},{8,4},{9,5},{1... | collective-permute-start | bytes 55304 | tf_op jit(solution)/shard_map/ppermute | solution.py:197
  10.6 1.9 %collective-permute-start.7 = (bf16[72,128]{1,0:T(8,128)(2,1)S(1)}, bf16[72,128]{1,0:T(8,128)(2,1)S(1)}, u32[]{:S(2)}, u32[]{:S(2)}) collective-permute-start(bf16[72,128]{1,0:T(8,128)(2,1)S(1)} %collective-permute-done.4.refs_2_), channel_id=1, source_target_pairs={{0,1},{1,0},{2,3},{3,2},{4,5},{5,4},{6,7},{7,6},{8,9},{9,8},{10,11... | collective-permute-start | bytes 55304 | tf_op jit(solution)/shard_map/ppermute | solution.py:199
  12.0 1.2 %collective-permute-start.5 = (bf16[72,128]{1,0:T(8,128)(2,1)S(1)}, bf16[72,128]{1,0:T(8,128)(2,1)S(1)}, u32[]{:S(2)}, u32[]{:S(2)}) collective-permute-start(bf16[72,128]{1,0:T(8,128)(2,1)S(1)} %collective-permute-done.2.refs_0_), channel_id=1, source_target_pairs={{0,1},{1,0},{2,3},{3,2},{4,5},{5,4},{6,7},{7,6},{8,9},{9,8},{10,11... | collective-permute-start | bytes 55304 | tf_op jit(solution)/shard_map/ppermute | solution.py:199
  12.0 1.4 %collective-permute-start.6 = (bf16[72,128]{1,0:T(8,128)(2,1)S(1)}, bf16[72,128]{1,0:T(8,128)(2,1)S(1)}, u32[]{:S(2)}, u32[]{:S(2)}) collective-permute-start(bf16[72,128]{1,0:T(8,128)(2,1)S(1)} %collective-permute-done.3.refs_1_), channel_id=1, source_target_pairs={{0,1},{1,0},{2,3},{3,2},{4,5},{5,4},{6,7},{7,6},{8,9},{9,8},{10,11... | collective-permute-start | bytes 55304 | tf_op jit(solution)/shard_map/ppermute | solution.py:199

commit v11 on v10

--- a/solution.py
+++ b/solution.py
@@ -28,35 +28,36 @@
     return high * 2 + (pair + offset) % 2
 
 
-def wave_rows(genes, samples):
-    return -(-genes * -(-samples // LANES) // 8) * 8
-
-
-def pack_kernel(pair_count, samps, pairs_hbm, pheno_hbm, grid_hbm, keep_ref, give_ref, wave_ref, pairs_ref, pheno_ref, grid_ref, sems):
-    copies = [
-        pltpu.make_async_copy(source, target, sems.at[i])
-        for i, (source, target) in enumerate(((pairs_hbm, pairs_ref), (grid_hbm, grid_ref), (pheno_hbm, pheno_ref)))
-    ]
+def wave_rows(stats, samples):
+    return -(-stats * 2 * samples // LANES // 8) * 8
+
+
+def pack_kernel(
+    pair_count, samps, pairs_hbm, pheno_hbm, perms_hbm, grid_hbm, keep_ref, give_ref, wave_ref, pairs_ref, pheno_ref, perms_ref, grid_ref, sems
+):
+    fetched = ((pairs_hbm, pairs_ref), (grid_hbm, grid_ref), (pheno_hbm, pheno_ref), (perms_hbm, perms_ref))
+    copies = [pltpu.make_async_copy(source, target, sems.at[i]) for i, (source, target) in enumerate(fetched)]
     for copy in copies:
         copy.start()
     pair, samp = lax.axis_index("pair"), lax.axis_index("samp")
     genes, s_dev = pheno_ref.shape
-    rows = wave_ref.shape[0]
-    tiles = -(-s_dev * samps * pair_count // LANES)
-    row = lax.broadcasted_iota(jnp.int32, (rows, LANES), 0)
-    lane = lax.broadcasted_iota(jnp.int32, (rows, LANES), 1)
+    rperms, samples = perms_ref.shape
     spot = (pair * samps + samp) * s_dev
-    first, tile = lax.rem(spot, LANES), lax.div(spot, LANES)
     for copy in copies:
         copy.wait()
 
     pheno = pheno_ref[...].astype(jnp.float32)
-    wave = jnp.zeros((rows, LANES), jnp.float32)
+    perms = perms_ref[...] - spot
+    perms = jnp.concatenate([perms, perms], axis=1)
+    rows = []
     for g in range(genes):
+        drawn = jnp.zeros(perms.shape, jnp.float32)
         for s in range(s_dev):
-            hit = (lane == first + s) & (row == g * tiles + tile)
-            wave = jnp.where(hit, pheno[g : g + 1, s : s + 1], wave)
-    wave = wave.astype(wave_ref.dtype)
+            drawn = jnp.where(perms == s, pheno[g : g + 1, s : s + 1], drawn)
+        rows += [drawn[r : r + 1, t : t + LANES] for r in range(rperms) for t in range(0, 2 * samples, LANES)]
+    if wave_ref.shape[0] > len(rows):
+        rows.append(jnp.zeros((wave_ref.shape[0] - len(rows), LANES), jnp.float32))
+    wave = jnp.concatenate(rows, axis=0).astype(wave_ref.dtype)
     wave_ref[...] = wave
 
     own_side, far_side = offsets(pair_count, 0), offsets(pair_count, 1)
@@ -70,7 +71,7 @@
     give_ref[len(own_side) * BLOCK :, :] = wave
 
 
-def stat_kernel(pair_count, samps, perms_ref, wave_ref, keep_ref, give_ref, near_ref, *refs):
+def stat_kernel(pair_count, samps, wave_ref, keep_ref, give_ref, near_ref, *refs):
     far = pair_count // 2 - 1
     own_refs, mate_refs = refs[:far], refs[far : 2 * far]
     out_hbm, got_ref, out_ref, sems = refs[2 * far :]
@@ -93,8 +94,8 @@
     place(0, other, give_ref[itself : itself + BLOCK, :])
 
     sources = got_ref.shape[0]
-    rperms, samples = perms_ref.shape
-    s_dev = samples // sources
+    s_dev = TILE * LANES // PANEL
+    samples = sources * s_dev
 
     def by_samples(tiles, group):
         return tiles[:, group * s_dev : (group + 1) * s_dev, :].reshape(samples, LANES)
@@ -114,21 +115,11 @@
     wave = wave_ref[...].astype(jnp.float32)
     for ref in (*own_refs, *mate_refs, near_ref):
         wave = wave + ref[2 * BLOCK :, :].astype(jnp.float32)
-    genes = out_ref.shape[0] // rperms
-    tiles = -(-samples // LANES)
-    pheno = [
-        jnp.concatenate([wave[g * tiles + t : g * tiles + t + 1] for t in range(tiles)], axis=1)[:, :samples]
-        for g in range(genes)
+    tiles = 2 * samples // LANES
+    yrows = [
+        jnp.concatenate([wave[k * tiles + t : k * tiles + t + 1] for t in range(tiles)], axis=1)
+        for k in range(out_ref.shape[0])
     ]
-    pheno = jnp.concatenate(pheno, axis=0).astype(jnp.bfloat16)
-    perms = perms_ref[...]
-    twice = jnp.concatenate([perms, perms], axis=1)
-    sample = lax.broadcasted_iota(jnp.int32, (samples, 2 * samples), 0)
-    permuted = []
-    for r in range(rperms):
-        chosen = jnp.where(sample == twice[r : r + 1, :], 1.0, 0.0).astype(jnp.bfloat16)
-        permuted.append(jnp.dot(pheno, chosen, preferred_element_type=jnp.float32))
-    yrows = [permuted[r][g : g + 1] for g in range(genes) for r in range(rperms)]
     yall = jnp.concatenate(yrows, axis=0)
     tail = jnp.dot(yall.astype(jnp.bfloat16), b_both, preferred_element_type=jnp.float32) / count
     c_hi = tail.astype(jnp.bfloat16).astype(jnp.float32)
@@ -159,7 +150,8 @@
     samples = perms.shape[1]
     pair_count, samps = (lax.axis_size(axis) for axis in AXES)
     rounds = pair_count // 2 + 1
-    rows = wave_rows(genes, samples)
+    stats = genes * perms.shape[0]
+    rows = wave_rows(stats, samples)
     grid = dosage.reshape(s_dev, snps // LANES, LANES).transpose(1, 0, 2).reshape(-1, LANES)
     vmem = pl.BlockSpec(memory_space=pltpu.VMEM)
     hbm = pl.BlockSpec(memory_space=pltpu.HBM)
@@ -170,17 +162,18 @@
     keep, give, wave = pl.pallas_call(
         functools.partial(pack_kernel, pair_count, samps),
         out_shape=[array(rounds * BLOCK, LANES), array(rounds * BLOCK + rows, LANES), array(rows, LANES)],
-        in_specs=[hbm, hbm, hbm],
+        in_specs=[hbm, hbm, hbm, hbm],
         out_specs=[vmem, vmem, vmem],
         scratch_shapes=[
             pltpu.SMEM(pairs.shape[::-1], pairs.dtype),
             pltpu.VMEM(phenotype.shape, phenotype.dtype),
+            pltpu.VMEM(perms.shape, perms.dtype),
             pltpu.VMEM(grid.shape, grid.dtype),
-            pltpu.SemaphoreType.DMA((3,)),
+            pltpu.SemaphoreType.DMA((4,)),
         ],
         compiler_params=pltpu.CompilerParams(vmem_limit_bytes=8 * 1024 * 1024),
         name="pack",
-    )(*[pltpu.with_memory_space_constraint(x, pltpu.HBM) for x in (pairs.T, phenotype, grid)])
+    )(*[pltpu.with_memory_space_constraint(x, pltpu.HBM) for x in (pairs.T, phenotype, perms, grid)])
 
     swap = [(i, samps - 1 - i) for i in range(samps)]
     got = lax.ppermute(give, "samp", swap)
@@ -197,12 +190,11 @@
         arrived.append(lax.ppermute(message, AXES, route))
     *far, near = arrived
     mates = [lax.ppermute(a, "samp", swap) for a in far]
-    stats = genes * perms.shape[0]
     half = PANEL // samps
     return pl.pallas_call(
         functools.partial(stat_kernel, pair_count, samps),
         out_shape=jax.ShapeDtypeStruct((1, stats, PANEL, half), jnp.bfloat16),
-        in_specs=[vmem] * (5 + 2 * len(far)),
+        in_specs=[vmem] * (4 + 2 * len(far)),
         out_specs=hbm,
         scratch_shapes=[
             pltpu.VMEM((pair_count * samps, BLOCK, LANES), dosage.dtype),
@@ -211,7 +203,7 @@
         ],
         compiler_params=pltpu.CompilerParams(vmem_limit_bytes=48 * 1024 * 1024),
         name="stat",
-    )(perms, wave, keep, got, near, *far, *mates)
+    )(wave, keep, got, near, *far, *mates)
 
 
 def solution(mesh):

time: 15.1 us -> 15 us (level)
  no operation moved by 1% of the time
where the time goes in v11:
time: 15 us; the launch traced here: 14.8 us
  starting transfers between devices  9.34 us (62%)
  waiting for transfers between devices  3.03 us (20%)
  Pallas kernels  2.41 us (16%)
    ppermute x4, starting transfers between devices, on_device(): arrived.append(lax.ppermute(message, AXES, route))  8.27 us
    pallas_call x1, Pallas kernels, on_device(): pl.pallas_call(functools.partial(stat_kernel, pair_count, samps), out_sha...  1.49 us
    ppermute x4, waiting for transfers between devices, on_device(): arrived.append(lax.ppermute(message, AXES, route))  1.32 us
    pallas_call x1, Pallas kernels, on_device(): pl.pallas_call(functools.partial(pack_kernel, pair_count, samps), out_sha...  0.91 us
    ppermute x1, waiting for transfers between devices, on_device(): got = lax.ppermute(give, 'samp', swap)  0.87 us
    ppermute x3, waiting for transfers between devices, on_device(): mates = [lax.ppermute(a, 'samp', swap) for a in far]  0.84 us
    ppermute x3, starting transfers between devices, on_device(): mates = [lax.ppermute(a, 'samp', swap) for a in far]  0.55 us
    ppermute x1, starting transfers between devices, on_device(): got = lax.ppermute(give, 'samp', swap)  0.52 us
  transfers between devices with their start and end apart: 8, of which 4 were waited for; matrix products, arithmetic and copies ran while one was open for 0% of the time, Pallas kernels for 0%

profile of v11, /device:TPU:0, one launch (start us, length us, event | category | flops | bytes accessed | tf_op | source)
XLA Modules:
  0.0 14.8 jit_solution(13212920389405819376)
XLA Ops:
  0.0 0.9 %pack.1 = (bf16[160,128]{1,0:T(8,128)(2,1)S(1)}, bf16[168,128]{1,0:T(8,128)(2,1)S(1)}, bf16[8,128]{1,0:T(8,128)(2,1)S(1)}) custom-call(s32[2,8]{1,0:T(2,128)} %bitcast.7, bf16[2,4]{1,0:T(2,128)(2,1)} %pheno_hbm.1, s32[2,64]{1,0:T(2,128)} %perms_hbm.1, bf16[128,128]{1,0:T(8,128)(2,1)} %bitcast.6), custom_call_target="tpu_custom_call" | custom-call | tf_op jit(solution)/shard_map/pack/pallas_call | solution.py:162
  0.9 0.5 %collective-permute-start = (bf16[168,128]{1,0:T(8,128)(2,1)S(1)}, bf16[168,128]{1,0:T(8,128)(2,1)S(1)}, u32[]{:S(2)}, u32[]{:S(2)}) collective-permute-start(bf16[168,128]{1,0:T(8,128)(2,1)S(1)} %get-tuple-element.9), channel_id=1, source_target_pairs={{0,1},{1,0},{2,3},{3,2},{4,5},{5,4},{6,7},{7,6},{8,9},{9,8},{10,11... | collective-permute-start | bytes 129032 | tf_op jit(solution)/shard_map/ppermute | solution.py:179
  1.4 0.9 %collective-permute-done.give_ref = bf16[168,128]{1,0:T(8,128)(2,1)S(1)} collective-permute-done((bf16[168,128]{1,0:T(8,128)(2,1)S(1)}, bf16[168,128]{1,0:T(8,128)(2,1)S(1)}, u32[]{:S(2)}, u32[]{:S(2)}) %collective-permute-start) | collective-permute-done | bytes 43040 | tf_op jit(solution)/shard_map/ppermute | solution.py:179
  2.3 3.0 %collective-permute-start.4 = (bf16[72,128]{1,0:T(8,128)(2,1)S(1)}, bf16[72,128]{1,0:T(8,128)(2,1)S(1)}, u32[]{:S(2)}, u32[]{:S(2)}) collective-permute-start(bf16[72,128]{1,0:T(8,128)(2,1)S(1)} %get-tuple-element.19), channel_id=1, source_target_pairs={{0,4},{1,9},{2,6},{3,11},{4,8},{5,13},{6,10},{7,15},{8,12},{9,1},{... | collective-permute-start | bytes 55304 | tf_op jit(solution)/shard_map/ppermute | solution.py:190
  5.3 2.5 %collective-permute-start.2 = (bf16[72,128]{1,0:T(8,128)(2,1)S(1)}, bf16[72,128]{1,0:T(8,128)(2,1)S(1)}, u32[]{:S(2)}, u32[]{:S(2)}) collective-permute-start(bf16[72,128]{1,0:T(8,128)(2,1)S(1)} %get-tuple-element.20), channel_id=1, source_target_pairs={{0,6},{1,11},{2,4},{3,9},{4,10},{5,15},{6,8},{7,13},{8,14},{9,3},{... | collective-permute-start | bytes 55304 | tf_op jit(solution)/shard_map/ppermute | solution.py:190
  7.8 0.5 %collective-permute-start.3 = (bf16[72,128]{1,0:T(8,128)(2,1)S(1)}, bf16[72,128]{1,0:T(8,128)(2,1)S(1)}, u32[]{:S(2)}, u32[]{:S(2)}) collective-permute-start(bf16[72,128]{1,0:T(8,128)(2,1)S(1)} %get-tuple-element.21), channel_id=1, source_target_pairs={{0,2},{1,15},{2,0},{3,13},{4,6},{5,3},{6,4},{7,1},{8,10},{9,7},{10... | collective-permute-start | bytes 55304 | tf_op jit(solution)/shard_map/ppermute | solution.py:190
  8.4 2.2 %collective-permute-start.1 = (bf16[72,128]{1,0:T(8,128)(2,1)S(1)}, bf16[72,128]{1,0:T(8,128)(2,1)S(1)}, u32[]{:S(2)}, u32[]{:S(2)}) collective-permute-start(bf16[72,128]{1,0:T(8,128)(2,1)S(1)} %get-tuple-element.22), channel_id=1, source_target_pairs={{0,12},{1,13},{2,14},{3,15},{4,0},{5,1},{6,2},{7,3},{8,4},{9,5},{1... | collective-permute-start | bytes 55304 | tf_op jit(solution)/shard_map/ppermute | solution.py:190
  10.6 0.0 collective-permute-done.4.refs_2_
  10.6 0.0 collective-permute-start.7
  10.7 1.3 %collective-permute-done.2.refs_0_ = bf16[72,128]{1,0:T(8,128)(2,1)S(1)} collective-permute-done((bf16[72,128]{1,0:T(8,128)(2,1)S(1)}, bf16[72,128]{1,0:T(8,128)(2,1)S(1)}, u32[]{:S(2)}, u32[]{:S(2)}) %collective-permute-start.2) | collective-permute-done | bytes 18464 | tf_op jit(solution)/shard_map/ppermute | solution.py:190
  12.0 0.0 collective-permute-start.5
  12.0 0.0 collective-permute-done.3.refs_1_
  12.0 0.5 %collective-permute-start.6 = (bf16[72,128]{1,0:T(8,128)(2,1)S(1)}, bf16[72,128]{1,0:T(8,128)(2,1)S(1)}, u32[]{:S(2)}, u32[]{:S(2)}) collective-permute-start(bf16[72,128]{1,0:T(8,128)(2,1)S(1)} %collective-permute-done.3.refs_1_), channel_id=1, source_target_pairs={{0,1},{1,0},{2,3},{3,2},{4,5},{5,4},{6,7},{7,6},{8,9},{9,8},{10,11... | collective-permute-start | bytes 55304 | tf_op jit(solution)/shard_map/ppermute | solution.py:192
  12.5 0.0 collective-permute-done.1.near_ref
  12.5 0.0 collective-permute-done.7.refs_5_
  12.5 0.7 %collective-permute-done.5.refs_3_ = bf16[72,128]{1,0:T(8,128)(2,1)S(1)} collective-permute-done((bf16[72,128]{1,0:T(8,128)(2,1)S(1)}, bf16[72,128]{1,0:T(8,128)(2,1)S(1)}, u32[]{:S(2)}, u32[]{:S(2)}) %collective-permute-start.5) | collective-permute-done | bytes 18464 | tf_op jit(solution)/shard_map/ppermute | solution.py:192
  13.2 0.2 %collective-permute-done.6.refs_4_ = bf16[72,128]{1,0:T(8,128)(2,1)S(1)} collective-permute-done((bf16[72,128]{1,0:T(8,128)(2,1)S(1)}, bf16[72,128]{1,0:T(8,128)(2,1)S(1)}, u32[]{:S(2)}, u32[]{:S(2)}) %collective-permute-start.6) | collective-permute-done | bytes 18464 | tf_op jit(solution)/shard_map/ppermute | solution.py:192
  13.3 1.5 %stat.1 = bf16[1,4,512,256]{3,2,1,0:T(8,128)(2,1)} custom-call(bf16[8,128]{1,0:T(8,128)(2,1)S(1)} %slice_add_fusion.wave_ref, bf16[160,128]{1,0:T(8,128)(2,1)S(1)} %get-tuple-element.10.keep_ref, bf16[168,128]{1,0:T(8,128)(2,1)S(1)} %collective-permute-done.give_ref, bf16[72,128]{1,0:T(8,128)(2,1)S(1)} %collective-permute-done.1.near_ref, ...), custom_call_target="tpu_custom_call" | custom-call | tf_op jit(solution)/shard_map/stat/pallas_call | solution.py:194
  (4 shorter events, 0.0 us)
Async XLA Ops:
  0.9 1.4 %collective-permute-start = (bf16[168,128]{1,0:T(8,128)(2,1)S(1)}, bf16[168,128]{1,0:T(8,128)(2,1)S(1)}, u32[]{:S(2)}, u32[]{:S(2)}) collective-permute-start(bf16[168,128]{1,0:T(8,128)(2,1)S(1)} %get-tuple-element.9), channel_id=1, source_target_pairs={{0,1},{1,0},{2,3},{3,2},{4,5},{5,4},{6,7},{7,6},{8,9},{9,8},{10,11... | collective-permute-start | bytes 129032 | tf_op jit(solution)/shard_map/ppermute | solution.py:179
  2.3 8.3 %collective-permute-start.4 = (bf16[72,128]{1,0:T(8,128)(2,1)S(1)}, bf16[72,128]{1,0:T(8,128)(2,1)S(1)}, u32[]{:S(2)}, u32[]{:S(2)}) collective-permute-start(bf16[72,128]{1,0:T(8,128)(2,1)S(1)} %get-tuple-element.19), channel_id=1, source_target_pairs={{0,4},{1,9},{2,6},{3,11},{4,8},{5,13},{6,10},{7,15},{8,12},{9,1},{... | collective-permute-start | bytes 55304 | tf_op jit(solution)/shard_map/ppermute | solution.py:190
  5.3 6.7 %collective-permute-start.2 = (bf16[72,128]{1,0:T(8,128)(2,1)S(1)}, bf16[72,128]{1,0:T(8,128)(2,1)S(1)}, u32[]{:S(2)}, u32[]{:S(2)}) collective-permute-start(bf16[72,128]{1,0:T(8,128)(2,1)S(1)} %get-tuple-element.20), channel_id=1, source_target_pairs={{0,6},{1,11},{2,4},{3,9},{4,10},{5,15},{6,8},{7,13},{8,14},{9,3},{... | collective-permute-start | bytes 55304 | tf_op jit(solution)/shard_map/ppermute | solution.py:190
  7.8 4.2 %collective-permute-start.3 = (bf16[72,128]{1,0:T(8,128)(2,1)S(1)}, bf16[72,128]{1,0:T(8,128)(2,1)S(1)}, u32[]{:S(2)}, u32[]{:S(2)}) collective-permute-start(bf16[72,128]{1,0:T(8,128)(2,1)S(1)} %get-tuple-element.21), channel_id=1, source_target_pairs={{0,2},{1,15},{2,0},{3,13},{4,6},{5,3},{6,4},{7,1},{8,10},{9,7},{10... | collective-permute-start | bytes 55304 | tf_op jit(solution)/shard_map/ppermute | solution.py:190
  8.4 4.1 %collective-permute-start.1 = (bf16[72,128]{1,0:T(8,128)(2,1)S(1)}, bf16[72,128]{1,0:T(8,128)(2,1)S(1)}, u32[]{:S(2)}, u32[]{:S(2)}) collective-permute-start(bf16[72,128]{1,0:T(8,128)(2,1)S(1)} %get-tuple-element.22), channel_id=1, source_target_pairs={{0,12},{1,13},{2,14},{3,15},{4,0},{5,1},{6,2},{7,3},{8,4},{9,5},{1... | collective-permute-start | bytes 55304 | tf_op jit(solution)/shard_map/ppermute | solution.py:190
  10.6 1.9 %collective-permute-start.7 = (bf16[72,128]{1,0:T(8,128)(2,1)S(1)}, bf16[72,128]{1,0:T(8,128)(2,1)S(1)}, u32[]{:S(2)}, u32[]{:S(2)}) collective-permute-start(bf16[72,128]{1,0:T(8,128)(2,1)S(1)} %collective-permute-done.4.refs_2_), channel_id=1, source_target_pairs={{0,1},{1,0},{2,3},{3,2},{4,5},{5,4},{6,7},{7,6},{8,9},{9,8},{10,11... | collective-permute-start | bytes 55304 | tf_op jit(solution)/shard_map/ppermute | solution.py:192
  12.0 1.2 %collective-permute-start.5 = (bf16[72,128]{1,0:T(8,128)(2,1)S(1)}, bf16[72,128]{1,0:T(8,128)(2,1)S(1)}, u32[]{:S(2)}, u32[]{:S(2)}) collective-permute-start(bf16[72,128]{1,0:T(8,128)(2,1)S(1)} %collective-permute-done.2.refs_0_), channel_id=1, source_target_pairs={{0,1},{1,0},{2,3},{3,2},{4,5},{5,4},{6,7},{7,6},{8,9},{9,8},{10,11... | collective-permute-start | bytes 55304 | tf_op jit(solution)/shard_map/ppermute | solution.py:192
  12.0 1.4 %collective-permute-start.6 = (bf16[72,128]{1,0:T(8,128)(2,1)S(1)}, bf16[72,128]{1,0:T(8,128)(2,1)S(1)}, u32[]{:S(2)}, u32[]{:S(2)}) collective-permute-start(bf16[72,128]{1,0:T(8,128)(2,1)S(1)} %collective-permute-done.3.refs_1_), channel_id=1, source_target_pairs={{0,1},{1,0},{2,3},{3,2},{4,5},{5,4},{6,7},{7,6},{8,9},{9,8},{10,11... | collective-permute-start | bytes 55304 | tf_op jit(solution)/shard_map/ppermute | solution.py:192

commit v12 on v11

--- a/solution.py
+++ b/solution.py
@@ -129,17 +129,16 @@
     for q in range(TILE // s_dev):
         geno_a = by_samples(panel_a, q)
         rows.append(jnp.concatenate([geno_a, geno_a], axis=0).astype(jnp.bfloat16).T)
+    rows = jnp.concatenate(rows, axis=0)
+    minus = -rows
     copies = []
     for k, yrow in enumerate(yrows):
-        yrow = yrow.astype(jnp.bfloat16)
         tails = [jnp.broadcast_to(c[k : k + 1], geno_b.shape).astype(jnp.bfloat16) for c in (c_hi, c_lo)]
         right = jnp.concatenate([b_both] + tails, axis=0)
-        for q, part in enumerate(rows):
-            left = jnp.concatenate([part * yrow, -part], axis=1)
-            piece = slice(q * LANES, (q + 1) * LANES)
-            out_ref[k, piece, :] = jnp.dot(left, right, preferred_element_type=jnp.float32).astype(out_ref.dtype)
-            copies.append(pltpu.make_async_copy(out_ref.at[k, piece], out_hbm.at[0, k, piece], sems.at[k, q]))
-            copies[-1].start()
+        left = jnp.concatenate([rows * yrow.astype(jnp.bfloat16), minus], axis=1)
+        out_ref[k] = jnp.dot(left, right, preferred_element_type=jnp.float32).astype(out_ref.dtype)
+        copies.append(pltpu.make_async_copy(out_ref.at[k], out_hbm.at[0, k], sems.at[k]))
+        copies[-1].start()
     for copy in copies:
         copy.wait()
 
@@ -199,7 +198,7 @@
         scratch_shapes=[
             pltpu.VMEM((pair_count * samps, BLOCK, LANES), dosage.dtype),
             pltpu.VMEM((stats, PANEL, half), jnp.bfloat16),
-            pltpu.SemaphoreType.DMA((stats, PANEL // LANES)),
+            pltpu.SemaphoreType.DMA((stats,)),
         ],
         compiler_params=pltpu.CompilerParams(vmem_limit_bytes=48 * 1024 * 1024),
         name="stat",

time: 15 us -> 15 us (level)
  no operation moved by 1% of the time
where the time goes in v12:
time: 15 us; the launch traced here: 14.8 us
  starting transfers between devices  9.34 us (62%)
  waiting for transfers between devices  3.03 us (20%)
  Pallas kernels  2.41 us (16%)
    ppermute x4, starting transfers between devices, on_device(): arrived.append(lax.ppermute(message, AXES, route))  8.27 us
    pallas_call x1, Pallas kernels, on_device(): pl.pallas_call(functools.partial(stat_kernel, pair_count, samps), out_sha...  1.5 us
    ppermute x4, waiting for transfers between devices, on_device(): arrived.append(lax.ppermute(message, AXES, route))  1.32 us
    pallas_call x1, Pallas kernels, on_device(): pl.pallas_call(functools.partial(pack_kernel, pair_count, samps), out_sha...  0.91 us
    ppermute x1, waiting for transfers between devices, on_device(): got = lax.ppermute(give, 'samp', swap)  0.87 us
    ppermute x3, waiting for transfers between devices, on_device(): mates = [lax.ppermute(a, 'samp', swap) for a in far]  0.84 us
    ppermute x3, starting transfers between devices, on_device(): mates = [lax.ppermute(a, 'samp', swap) for a in far]  0.55 us
    ppermute x1, starting transfers between devices, on_device(): got = lax.ppermute(give, 'samp', swap)  0.52 us
  transfers between devices with their start and end apart: 8, of which 4 were waited for; matrix products, arithmetic and copies ran while one was open for 0% of the time, Pallas kernels for 0%

profile of v12, /device:TPU:0, one launch (start us, length us, event | category | flops | bytes accessed | tf_op | source)
XLA Modules:
  0.0 14.8 jit_solution(9737049063297487569)
XLA Ops:
  0.0 0.9 %pack.1 = (bf16[160,128]{1,0:T(8,128)(2,1)S(1)}, bf16[168,128]{1,0:T(8,128)(2,1)S(1)}, bf16[8,128]{1,0:T(8,128)(2,1)S(1)}) custom-call(s32[2,8]{1,0:T(2,128)} %bitcast.7, bf16[2,4]{1,0:T(2,128)(2,1)} %pheno_hbm.1, s32[2,64]{1,0:T(2,128)} %perms_hbm.1, bf16[128,128]{1,0:T(8,128)(2,1)} %bitcast.6), custom_call_target="tpu_custom_call" | custom-call | tf_op jit(solution)/shard_map/pack/pallas_call | solution.py:161
  0.9 0.5 %collective-permute-start = (bf16[168,128]{1,0:T(8,128)(2,1)S(1)}, bf16[168,128]{1,0:T(8,128)(2,1)S(1)}, u32[]{:S(2)}, u32[]{:S(2)}) collective-permute-start(bf16[168,128]{1,0:T(8,128)(2,1)S(1)} %get-tuple-element.9), channel_id=1, source_target_pairs={{0,1},{1,0},{2,3},{3,2},{4,5},{5,4},{6,7},{7,6},{8,9},{9,8},{10,11... | collective-permute-start | bytes 129032 | tf_op jit(solution)/shard_map/ppermute | solution.py:178
  1.4 0.9 %collective-permute-done.give_ref = bf16[168,128]{1,0:T(8,128)(2,1)S(1)} collective-permute-done((bf16[168,128]{1,0:T(8,128)(2,1)S(1)}, bf16[168,128]{1,0:T(8,128)(2,1)S(1)}, u32[]{:S(2)}, u32[]{:S(2)}) %collective-permute-start) | collective-permute-done | bytes 43040 | tf_op jit(solution)/shard_map/ppermute | solution.py:178
  2.3 3.0 %collective-permute-start.4 = (bf16[72,128]{1,0:T(8,128)(2,1)S(1)}, bf16[72,128]{1,0:T(8,128)(2,1)S(1)}, u32[]{:S(2)}, u32[]{:S(2)}) collective-permute-start(bf16[72,128]{1,0:T(8,128)(2,1)S(1)} %get-tuple-element.19), channel_id=1, source_target_pairs={{0,4},{1,9},{2,6},{3,11},{4,8},{5,13},{6,10},{7,15},{8,12},{9,1},{... | collective-permute-start | bytes 55304 | tf_op jit(solution)/shard_map/ppermute | solution.py:189
  5.3 2.5 %collective-permute-start.2 = (bf16[72,128]{1,0:T(8,128)(2,1)S(1)}, bf16[72,128]{1,0:T(8,128)(2,1)S(1)}, u32[]{:S(2)}, u32[]{:S(2)}) collective-permute-start(bf16[72,128]{1,0:T(8,128)(2,1)S(1)} %get-tuple-element.20), channel_id=1, source_target_pairs={{0,6},{1,11},{2,4},{3,9},{4,10},{5,15},{6,8},{7,13},{8,14},{9,3},{... | collective-permute-start | bytes 55304 | tf_op jit(solution)/shard_map/ppermute | solution.py:189
  7.8 0.5 %collective-permute-start.3 = (bf16[72,128]{1,0:T(8,128)(2,1)S(1)}, bf16[72,128]{1,0:T(8,128)(2,1)S(1)}, u32[]{:S(2)}, u32[]{:S(2)}) collective-permute-start(bf16[72,128]{1,0:T(8,128)(2,1)S(1)} %get-tuple-element.21), channel_id=1, source_target_pairs={{0,2},{1,15},{2,0},{3,13},{4,6},{5,3},{6,4},{7,1},{8,10},{9,7},{10... | collective-permute-start | bytes 55304 | tf_op jit(solution)/shard_map/ppermute | solution.py:189
  8.4 2.2 %collective-permute-start.1 = (bf16[72,128]{1,0:T(8,128)(2,1)S(1)}, bf16[72,128]{1,0:T(8,128)(2,1)S(1)}, u32[]{:S(2)}, u32[]{:S(2)}) collective-permute-start(bf16[72,128]{1,0:T(8,128)(2,1)S(1)} %get-tuple-element.22), channel_id=1, source_target_pairs={{0,12},{1,13},{2,14},{3,15},{4,0},{5,1},{6,2},{7,3},{8,4},{9,5},{1... | collective-permute-start | bytes 55304 | tf_op jit(solution)/shard_map/ppermute | solution.py:189
  10.6 0.0 collective-permute-done.4.refs_2_
  10.6 0.0 collective-permute-start.7
  10.7 1.3 %collective-permute-done.2.refs_0_ = bf16[72,128]{1,0:T(8,128)(2,1)S(1)} collective-permute-done((bf16[72,128]{1,0:T(8,128)(2,1)S(1)}, bf16[72,128]{1,0:T(8,128)(2,1)S(1)}, u32[]{:S(2)}, u32[]{:S(2)}) %collective-permute-start.2) | collective-permute-done | bytes 18464 | tf_op jit(solution)/shard_map/ppermute | solution.py:189
  12.0 0.0 collective-permute-start.5
  12.0 0.0 collective-permute-done.3.refs_1_
  12.0 0.5 %collective-permute-start.6 = (bf16[72,128]{1,0:T(8,128)(2,1)S(1)}, bf16[72,128]{1,0:T(8,128)(2,1)S(1)}, u32[]{:S(2)}, u32[]{:S(2)}) collective-permute-start(bf16[72,128]{1,0:T(8,128)(2,1)S(1)} %collective-permute-done.3.refs_1_), channel_id=1, source_target_pairs={{0,1},{1,0},{2,3},{3,2},{4,5},{5,4},{6,7},{7,6},{8,9},{9,8},{10,11... | collective-permute-start | bytes 55304 | tf_op jit(solution)/shard_map/ppermute | solution.py:191
  12.5 0.0 collective-permute-done.1.near_ref
  12.5 0.0 collective-permute-done.7.refs_5_
  12.5 0.7 %collective-permute-done.5.refs_3_ = bf16[72,128]{1,0:T(8,128)(2,1)S(1)} collective-permute-done((bf16[72,128]{1,0:T(8,128)(2,1)S(1)}, bf16[72,128]{1,0:T(8,128)(2,1)S(1)}, u32[]{:S(2)}, u32[]{:S(2)}) %collective-permute-start.5) | collective-permute-done | bytes 18464 | tf_op jit(solution)/shard_map/ppermute | solution.py:191
  13.2 0.2 %collective-permute-done.6.refs_4_ = bf16[72,128]{1,0:T(8,128)(2,1)S(1)} collective-permute-done((bf16[72,128]{1,0:T(8,128)(2,1)S(1)}, bf16[72,128]{1,0:T(8,128)(2,1)S(1)}, u32[]{:S(2)}, u32[]{:S(2)}) %collective-permute-start.6) | collective-permute-done | bytes 18464 | tf_op jit(solution)/shard_map/ppermute | solution.py:191
  13.3 1.5 %stat.1 = bf16[1,4,512,256]{3,2,1,0:T(8,128)(2,1)} custom-call(bf16[8,128]{1,0:T(8,128)(2,1)S(1)} %slice_add_fusion.wave_ref, bf16[160,128]{1,0:T(8,128)(2,1)S(1)} %get-tuple-element.10.keep_ref, bf16[168,128]{1,0:T(8,128)(2,1)S(1)} %collective-permute-done.give_ref, bf16[72,128]{1,0:T(8,128)(2,1)S(1)} %collective-permute-done.1.near_ref, ...), custom_call_target="tpu_custom_call" | custom-call | tf_op jit(solution)/shard_map/stat/pallas_call | solution.py:193
  (4 shorter events, 0.0 us)
Async XLA Ops:
  0.9 1.4 %collective-permute-start = (bf16[168,128]{1,0:T(8,128)(2,1)S(1)}, bf16[168,128]{1,0:T(8,128)(2,1)S(1)}, u32[]{:S(2)}, u32[]{:S(2)}) collective-permute-start(bf16[168,128]{1,0:T(8,128)(2,1)S(1)} %get-tuple-element.9), channel_id=1, source_target_pairs={{0,1},{1,0},{2,3},{3,2},{4,5},{5,4},{6,7},{7,6},{8,9},{9,8},{10,11... | collective-permute-start | bytes 129032 | tf_op jit(solution)/shard_map/ppermute | solution.py:178
  2.3 8.3 %collective-permute-start.4 = (bf16[72,128]{1,0:T(8,128)(2,1)S(1)}, bf16[72,128]{1,0:T(8,128)(2,1)S(1)}, u32[]{:S(2)}, u32[]{:S(2)}) collective-permute-start(bf16[72,128]{1,0:T(8,128)(2,1)S(1)} %get-tuple-element.19), channel_id=1, source_target_pairs={{0,4},{1,9},{2,6},{3,11},{4,8},{5,13},{6,10},{7,15},{8,12},{9,1},{... | collective-permute-start | bytes 55304 | tf_op jit(solution)/shard_map/ppermute | solution.py:189
  5.3 6.7 %collective-permute-start.2 = (bf16[72,128]{1,0:T(8,128)(2,1)S(1)}, bf16[72,128]{1,0:T(8,128)(2,1)S(1)}, u32[]{:S(2)}, u32[]{:S(2)}) collective-permute-start(bf16[72,128]{1,0:T(8,128)(2,1)S(1)} %get-tuple-element.20), channel_id=1, source_target_pairs={{0,6},{1,11},{2,4},{3,9},{4,10},{5,15},{6,8},{7,13},{8,14},{9,3},{... | collective-permute-start | bytes 55304 | tf_op jit(solution)/shard_map/ppermute | solution.py:189
  7.8 4.2 %collective-permute-start.3 = (bf16[72,128]{1,0:T(8,128)(2,1)S(1)}, bf16[72,128]{1,0:T(8,128)(2,1)S(1)}, u32[]{:S(2)}, u32[]{:S(2)}) collective-permute-start(bf16[72,128]{1,0:T(8,128)(2,1)S(1)} %get-tuple-element.21), channel_id=1, source_target_pairs={{0,2},{1,15},{2,0},{3,13},{4,6},{5,3},{6,4},{7,1},{8,10},{9,7},{10... | collective-permute-start | bytes 55304 | tf_op jit(solution)/shard_map/ppermute | solution.py:189
  8.4 4.1 %collective-permute-start.1 = (bf16[72,128]{1,0:T(8,128)(2,1)S(1)}, bf16[72,128]{1,0:T(8,128)(2,1)S(1)}, u32[]{:S(2)}, u32[]{:S(2)}) collective-permute-start(bf16[72,128]{1,0:T(8,128)(2,1)S(1)} %get-tuple-element.22), channel_id=1, source_target_pairs={{0,12},{1,13},{2,14},{3,15},{4,0},{5,1},{6,2},{7,3},{8,4},{9,5},{1... | collective-permute-start | bytes 55304 | tf_op jit(solution)/shard_map/ppermute | solution.py:189
  10.6 1.9 %collective-permute-start.7 = (bf16[72,128]{1,0:T(8,128)(2,1)S(1)}, bf16[72,128]{1,0:T(8,128)(2,1)S(1)}, u32[]{:S(2)}, u32[]{:S(2)}) collective-permute-start(bf16[72,128]{1,0:T(8,128)(2,1)S(1)} %collective-permute-done.4.refs_2_), channel_id=1, source_target_pairs={{0,1},{1,0},{2,3},{3,2},{4,5},{5,4},{6,7},{7,6},{8,9},{9,8},{10,11... | collective-permute-start | bytes 55304 | tf_op jit(solution)/shard_map/ppermute | solution.py:191
  12.0 1.2 %collective-permute-start.5 = (bf16[72,128]{1,0:T(8,128)(2,1)S(1)}, bf16[72,128]{1,0:T(8,128)(2,1)S(1)}, u32[]{:S(2)}, u32[]{:S(2)}) collective-permute-start(bf16[72,128]{1,0:T(8,128)(2,1)S(1)} %collective-permute-done.2.refs_0_), channel_id=1, source_target_pairs={{0,1},{1,0},{2,3},{3,2},{4,5},{5,4},{6,7},{7,6},{8,9},{9,8},{10,11... | collective-permute-start | bytes 55304 | tf_op jit(solution)/shard_map/ppermute | solution.py:191
  12.0 1.4 %collective-permute-start.6 = (bf16[72,128]{1,0:T(8,128)(2,1)S(1)}, bf16[72,128]{1,0:T(8,128)(2,1)S(1)}, u32[]{:S(2)}, u32[]{:S(2)}) collective-permute-start(bf16[72,128]{1,0:T(8,128)(2,1)S(1)} %collective-permute-done.3.refs_1_), channel_id=1, source_target_pairs={{0,1},{1,0},{2,3},{3,2},{4,5},{5,4},{6,7},{7,6},{8,9},{9,8},{10,11... | collective-permute-start | bytes 55304 | tf_op jit(solution)/shard_map/ppermute | solution.py:191

commit v13 on v12

--- a/solution.py
+++ b/solution.py
@@ -137,8 +137,10 @@
         right = jnp.concatenate([b_both] + tails, axis=0)
         left = jnp.concatenate([rows * yrow.astype(jnp.bfloat16), minus], axis=1)
         out_ref[k] = jnp.dot(left, right, preferred_element_type=jnp.float32).astype(out_ref.dtype)
-        copies.append(pltpu.make_async_copy(out_ref.at[k], out_hbm.at[0, k], sems.at[k]))
-        copies[-1].start()
+        for part in range(2):
+            piece = slice(part * PANEL // 2, (part + 1) * PANEL // 2)
+            copies.append(pltpu.make_async_copy(out_ref.at[k, piece], out_hbm.at[0, k, piece], sems.at[k, part]))
+            copies[-1].start(priority=part)
     for copy in copies:
         copy.wait()
 
@@ -198,7 +200,7 @@
         scratch_shapes=[
             pltpu.VMEM((pair_count * samps, BLOCK, LANES), dosage.dtype),
             pltpu.VMEM((stats, PANEL, half), jnp.bfloat16),
-            pltpu.SemaphoreType.DMA((stats,)),
+            pltpu.SemaphoreType.DMA((stats, 2)),
         ],
         compiler_params=pltpu.CompilerParams(vmem_limit_bytes=48 * 1024 * 1024),
         name="stat",

time: 15 us -> 15 us (level)
  no operation moved by 1% of the time
where the time goes in v13:
time: 15 us; the launch traced here: 14.9 us
  starting transfers between devices  9.34 us (62%)
  waiting for transfers between devices  3.03 us (20%)
  Pallas kernels  2.44 us (16%)
    ppermute x4, starting transfers between devices, on_device(): arrived.append(lax.ppermute(message, AXES, route))  8.27 us
    pallas_call x1, Pallas kernels, on_device(): pl.pallas_call(functools.partial(stat_kernel, pair_count, samps), out_sha...  1.53 us
    ppermute x4, waiting for transfers between devices, on_device(): arrived.append(lax.ppermute(message, AXES, route))  1.32 us
    pallas_call x1, Pallas kernels, on_device(): pl.pallas_call(functools.partial(pack_kernel, pair_count, samps), out_sha...  0.91 us
    ppermute x1, waiting for transfers between devices, on_device(): got = lax.ppermute(give, 'samp', swap)  0.87 us
    ppermute x3, waiting for transfers between devices, on_device(): mates = [lax.ppermute(a, 'samp', swap) for a in far]  0.84 us
    ppermute x3, starting transfers between devices, on_device(): mates = [lax.ppermute(a, 'samp', swap) for a in far]  0.55 us
    ppermute x1, starting transfers between devices, on_device(): got = lax.ppermute(give, 'samp', swap)  0.52 us
  transfers between devices with their start and end apart: 8, of which 4 were waited for; matrix products, arithmetic and copies ran while one was open for 0% of the time, Pallas kernels for 0%

profile of v13, /device:TPU:0, one launch (start us, length us, event | category | flops | bytes accessed | tf_op | source)
XLA Modules:
  0.0 14.9 jit_solution(12647721900842913392)
XLA Ops:
  0.0 0.9 %pack.1 = (bf16[160,128]{1,0:T(8,128)(2,1)S(1)}, bf16[168,128]{1,0:T(8,128)(2,1)S(1)}, bf16[8,128]{1,0:T(8,128)(2,1)S(1)}) custom-call(s32[2,8]{1,0:T(2,128)} %bitcast.7, bf16[2,4]{1,0:T(2,128)(2,1)} %pheno_hbm.1, s32[2,64]{1,0:T(2,128)} %perms_hbm.1, bf16[128,128]{1,0:T(8,128)(2,1)} %bitcast.6), custom_call_target="tpu_custom_call" | custom-call | tf_op jit(solution)/shard_map/pack/pallas_call | solution.py:163
  0.9 0.5 %collective-permute-start = (bf16[168,128]{1,0:T(8,128)(2,1)S(1)}, bf16[168,128]{1,0:T(8,128)(2,1)S(1)}, u32[]{:S(2)}, u32[]{:S(2)}) collective-permute-start(bf16[168,128]{1,0:T(8,128)(2,1)S(1)} %get-tuple-element.9), channel_id=1, source_target_pairs={{0,1},{1,0},{2,3},{3,2},{4,5},{5,4},{6,7},{7,6},{8,9},{9,8},{10,11... | collective-permute-start | bytes 129032 | tf_op jit(solution)/shard_map/ppermute | solution.py:180
  1.4 0.9 %collective-permute-done.give_ref = bf16[168,128]{1,0:T(8,128)(2,1)S(1)} collective-permute-done((bf16[168,128]{1,0:T(8,128)(2,1)S(1)}, bf16[168,128]{1,0:T(8,128)(2,1)S(1)}, u32[]{:S(2)}, u32[]{:S(2)}) %collective-permute-start) | collective-permute-done | bytes 43040 | tf_op jit(solution)/shard_map/ppermute | solution.py:180
  2.3 3.0 %collective-permute-start.4 = (bf16[72,128]{1,0:T(8,128)(2,1)S(1)}, bf16[72,128]{1,0:T(8,128)(2,1)S(1)}, u32[]{:S(2)}, u32[]{:S(2)}) collective-permute-start(bf16[72,128]{1,0:T(8,128)(2,1)S(1)} %get-tuple-element.19), channel_id=1, source_target_pairs={{0,4},{1,9},{2,6},{3,11},{4,8},{5,13},{6,10},{7,15},{8,12},{9,1},{... | collective-permute-start | bytes 55304 | tf_op jit(solution)/shard_map/ppermute | solution.py:191
  5.3 2.5 %collective-permute-start.2 = (bf16[72,128]{1,0:T(8,128)(2,1)S(1)}, bf16[72,128]{1,0:T(8,128)(2,1)S(1)}, u32[]{:S(2)}, u32[]{:S(2)}) collective-permute-start(bf16[72,128]{1,0:T(8,128)(2,1)S(1)} %get-tuple-element.20), channel_id=1, source_target_pairs={{0,6},{1,11},{2,4},{3,9},{4,10},{5,15},{6,8},{7,13},{8,14},{9,3},{... | collective-permute-start | bytes 55304 | tf_op jit(solution)/shard_map/ppermute | solution.py:191
  7.8 0.5 %collective-permute-start.3 = (bf16[72,128]{1,0:T(8,128)(2,1)S(1)}, bf16[72,128]{1,0:T(8,128)(2,1)S(1)}, u32[]{:S(2)}, u32[]{:S(2)}) collective-permute-start(bf16[72,128]{1,0:T(8,128)(2,1)S(1)} %get-tuple-element.21), channel_id=1, source_target_pairs={{0,2},{1,15},{2,0},{3,13},{4,6},{5,3},{6,4},{7,1},{8,10},{9,7},{10... | collective-permute-start | bytes 55304 | tf_op jit(solution)/shard_map/ppermute | solution.py:191
  8.4 2.2 %collective-permute-start.1 = (bf16[72,128]{1,0:T(8,128)(2,1)S(1)}, bf16[72,128]{1,0:T(8,128)(2,1)S(1)}, u32[]{:S(2)}, u32[]{:S(2)}) collective-permute-start(bf16[72,128]{1,0:T(8,128)(2,1)S(1)} %get-tuple-element.22), channel_id=1, source_target_pairs={{0,12},{1,13},{2,14},{3,15},{4,0},{5,1},{6,2},{7,3},{8,4},{9,5},{1... | collective-permute-start | bytes 55304 | tf_op jit(solution)/shard_map/ppermute | solution.py:191
  10.6 0.0 collective-permute-done.4.refs_2_
  10.6 0.0 collective-permute-start.7
  10.7 1.3 %collective-permute-done.2.refs_0_ = bf16[72,128]{1,0:T(8,128)(2,1)S(1)} collective-permute-done((bf16[72,128]{1,0:T(8,128)(2,1)S(1)}, bf16[72,128]{1,0:T(8,128)(2,1)S(1)}, u32[]{:S(2)}, u32[]{:S(2)}) %collective-permute-start.2) | collective-permute-done | bytes 18464 | tf_op jit(solution)/shard_map/ppermute | solution.py:191
  12.0 0.0 collective-permute-start.5
  12.0 0.0 collective-permute-done.3.refs_1_
  12.0 0.5 %collective-permute-start.6 = (bf16[72,128]{1,0:T(8,128)(2,1)S(1)}, bf16[72,128]{1,0:T(8,128)(2,1)S(1)}, u32[]{:S(2)}, u32[]{:S(2)}) collective-permute-start(bf16[72,128]{1,0:T(8,128)(2,1)S(1)} %collective-permute-done.3.refs_1_), channel_id=1, source_target_pairs={{0,1},{1,0},{2,3},{3,2},{4,5},{5,4},{6,7},{7,6},{8,9},{9,8},{10,11... | collective-permute-start | bytes 55304 | tf_op jit(solution)/shard_map/ppermute | solution.py:193
  12.5 0.0 collective-permute-done.1.near_ref
  12.5 0.0 collective-permute-done.7.refs_5_
  12.5 0.7 %collective-permute-done.5.refs_3_ = bf16[72,128]{1,0:T(8,128)(2,1)S(1)} collective-permute-done((bf16[72,128]{1,0:T(8,128)(2,1)S(1)}, bf16[72,128]{1,0:T(8,128)(2,1)S(1)}, u32[]{:S(2)}, u32[]{:S(2)}) %collective-permute-start.5) | collective-permute-done | bytes 18464 | tf_op jit(solution)/shard_map/ppermute | solution.py:193
  13.2 0.2 %collective-permute-done.6.refs_4_ = bf16[72,128]{1,0:T(8,128)(2,1)S(1)} collective-permute-done((bf16[72,128]{1,0:T(8,128)(2,1)S(1)}, bf16[72,128]{1,0:T(8,128)(2,1)S(1)}, u32[]{:S(2)}, u32[]{:S(2)}) %collective-permute-start.6) | collective-permute-done | bytes 18464 | tf_op jit(solution)/shard_map/ppermute | solution.py:193
  13.3 1.5 %stat.1 = bf16[1,4,512,256]{3,2,1,0:T(8,128)(2,1)} custom-call(bf16[8,128]{1,0:T(8,128)(2,1)S(1)} %slice_add_fusion.wave_ref, bf16[160,128]{1,0:T(8,128)(2,1)S(1)} %get-tuple-element.10.keep_ref, bf16[168,128]{1,0:T(8,128)(2,1)S(1)} %collective-permute-done.give_ref, bf16[72,128]{1,0:T(8,128)(2,1)S(1)} %collective-permute-done.1.near_ref, ...), custom_call_target="tpu_custom_call" | custom-call | tf_op jit(solution)/shard_map/stat/pallas_call | solution.py:195
  (4 shorter events, 0.0 us)
Async XLA Ops:
  0.9 1.4 %collective-permute-start = (bf16[168,128]{1,0:T(8,128)(2,1)S(1)}, bf16[168,128]{1,0:T(8,128)(2,1)S(1)}, u32[]{:S(2)}, u32[]{:S(2)}) collective-permute-start(bf16[168,128]{1,0:T(8,128)(2,1)S(1)} %get-tuple-element.9), channel_id=1, source_target_pairs={{0,1},{1,0},{2,3},{3,2},{4,5},{5,4},{6,7},{7,6},{8,9},{9,8},{10,11... | collective-permute-start | bytes 129032 | tf_op jit(solution)/shard_map/ppermute | solution.py:180
  2.3 8.3 %collective-permute-start.4 = (bf16[72,128]{1,0:T(8,128)(2,1)S(1)}, bf16[72,128]{1,0:T(8,128)(2,1)S(1)}, u32[]{:S(2)}, u32[]{:S(2)}) collective-permute-start(bf16[72,128]{1,0:T(8,128)(2,1)S(1)} %get-tuple-element.19), channel_id=1, source_target_pairs={{0,4},{1,9},{2,6},{3,11},{4,8},{5,13},{6,10},{7,15},{8,12},{9,1},{... | collective-permute-start | bytes 55304 | tf_op jit(solution)/shard_map/ppermute | solution.py:191
  5.3 6.7 %collective-permute-start.2 = (bf16[72,128]{1,0:T(8,128)(2,1)S(1)}, bf16[72,128]{1,0:T(8,128)(2,1)S(1)}, u32[]{:S(2)}, u32[]{:S(2)}) collective-permute-start(bf16[72,128]{1,0:T(8,128)(2,1)S(1)} %get-tuple-element.20), channel_id=1, source_target_pairs={{0,6},{1,11},{2,4},{3,9},{4,10},{5,15},{6,8},{7,13},{8,14},{9,3},{... | collective-permute-start | bytes 55304 | tf_op jit(solution)/shard_map/ppermute | solution.py:191
  7.8 4.2 %collective-permute-start.3 = (bf16[72,128]{1,0:T(8,128)(2,1)S(1)}, bf16[72,128]{1,0:T(8,128)(2,1)S(1)}, u32[]{:S(2)}, u32[]{:S(2)}) collective-permute-start(bf16[72,128]{1,0:T(8,128)(2,1)S(1)} %get-tuple-element.21), channel_id=1, source_target_pairs={{0,2},{1,15},{2,0},{3,13},{4,6},{5,3},{6,4},{7,1},{8,10},{9,7},{10... | collective-permute-start | bytes 55304 | tf_op jit(solution)/shard_map/ppermute | solution.py:191
  8.4 4.1 %collective-permute-start.1 = (bf16[72,128]{1,0:T(8,128)(2,1)S(1)}, bf16[72,128]{1,0:T(8,128)(2,1)S(1)}, u32[]{:S(2)}, u32[]{:S(2)}) collective-permute-start(bf16[72,128]{1,0:T(8,128)(2,1)S(1)} %get-tuple-element.22), channel_id=1, source_target_pairs={{0,12},{1,13},{2,14},{3,15},{4,0},{5,1},{6,2},{7,3},{8,4},{9,5},{1... | collective-permute-start | bytes 55304 | tf_op jit(solution)/shard_map/ppermute | solution.py:191
  10.6 1.9 %collective-permute-start.7 = (bf16[72,128]{1,0:T(8,128)(2,1)S(1)}, bf16[72,128]{1,0:T(8,128)(2,1)S(1)}, u32[]{:S(2)}, u32[]{:S(2)}) collective-permute-start(bf16[72,128]{1,0:T(8,128)(2,1)S(1)} %collective-permute-done.4.refs_2_), channel_id=1, source_target_pairs={{0,1},{1,0},{2,3},{3,2},{4,5},{5,4},{6,7},{7,6},{8,9},{9,8},{10,11... | collective-permute-start | bytes 55304 | tf_op jit(solution)/shard_map/ppermute | solution.py:193
  12.0 1.2 %collective-permute-start.5 = (bf16[72,128]{1,0:T(8,128)(2,1)S(1)}, bf16[72,128]{1,0:T(8,128)(2,1)S(1)}, u32[]{:S(2)}, u32[]{:S(2)}) collective-permute-start(bf16[72,128]{1,0:T(8,128)(2,1)S(1)} %collective-permute-done.2.refs_0_), channel_id=1, source_target_pairs={{0,1},{1,0},{2,3},{3,2},{4,5},{5,4},{6,7},{7,6},{8,9},{9,8},{10,11... | collective-permute-start | bytes 55304 | tf_op jit(solution)/shard_map/ppermute | solution.py:193
  12.0 1.4 %collective-permute-start.6 = (bf16[72,128]{1,0:T(8,128)(2,1)S(1)}, bf16[72,128]{1,0:T(8,128)(2,1)S(1)}, u32[]{:S(2)}, u32[]{:S(2)}) collective-permute-start(bf16[72,128]{1,0:T(8,128)(2,1)S(1)} %collective-permute-done.3.refs_1_), channel_id=1, source_target_pairs={{0,1},{1,0},{2,3},{3,2},{4,5},{5,4},{6,7},{7,6},{8,9},{9,8},{10,11... | collective-permute-start | bytes 55304 | tf_op jit(solution)/shard_map/ppermute | solution.py:193

commit v14 on v12

--- a/solution.py
+++ b/solution.py
@@ -24,8 +24,10 @@
 
 
 def shifted(pair, offset, pair_count, sign=1):
-    high = (pair // 2 + sign * (offset // 2) + pair_count // 2) % (pair_count // 2)
-    return high * 2 + (pair + offset) % 2
+    turn = pair_count // 2
+    high = (pair >> 1) + sign * (offset >> 1)
+    high = high - turn * (high >= turn) + turn * (high < 0)
+    return high * 2 + ((pair ^ offset) & 1)
 
 
 def wave_rows(stats, samples):
@@ -43,9 +45,20 @@
     genes, s_dev = pheno_ref.shape
     rperms, samples = perms_ref.shape
     spot = (pair * samps + samp) * s_dev
-    for copy in copies:
+    for copy in copies[:2]:
         copy.wait()
 
+    own_side, far_side = offsets(pair_count, 0), offsets(pair_count, 1)
+    for i, (even, odd) in enumerate(zip(own_side, far_side)):
+        for ref, core in ((keep_ref, samp), (give_ref, samps - 1 - samp)):
+            n = shifted(pair, jnp.where(core == 0, even, odd), pair_count)
+            for j in range(2):
+                start = pl.multiple_of(pairs_ref[j, n] * TILE, TILE)
+                place = i * BLOCK + j * TILE
+                ref[place : place + TILE, :] = grid_ref[pl.ds(start, TILE), :]
+
+    for copy in copies[2:]:
+        copy.wait()
     pheno = pheno_ref[...].astype(jnp.float32)
     perms = perms_ref[...] - spot
     perms = jnp.concatenate([perms, perms], axis=1)
@@ -59,15 +72,6 @@
         rows.append(jnp.zeros((wave_ref.shape[0] - len(rows), LANES), jnp.float32))
     wave = jnp.concatenate(rows, axis=0).astype(wave_ref.dtype)
     wave_ref[...] = wave
-
-    own_side, far_side = offsets(pair_count, 0), offsets(pair_count, 1)
-    for i, (even, odd) in enumerate(zip(own_side, far_side)):
-        for ref, core in ((keep_ref, samp), (give_ref, samps - 1 - samp)):
-            n = shifted(pair, jnp.where(core == 0, even, odd), pair_count)
-            for j in range(2):
-                start = pl.multiple_of(pairs_ref[j, n] * TILE, TILE)
-                place = i * BLOCK + j * TILE
-                ref[place : place + TILE, :] = grid_ref[pl.ds(start, TILE), :]
     give_ref[len(own_side) * BLOCK :, :] = wave
 
 
@@ -97,15 +101,23 @@
     s_dev = TILE * LANES // PANEL
     samples = sources * s_dev
 
-    def by_samples(tiles, group):
-        return tiles[:, group * s_dev : (group + 1) * s_dev, :].reshape(samples, LANES)
+    def by_samples(tiles):
+        groups = tiles.shape[1] // s_dev
+        if groups * s_dev != 8 or groups != 2:
+            return [tiles[:, g * s_dev : (g + 1) * s_dev, :].reshape(samples, LANES) for g in range(groups)]
+        couples = tiles.reshape(sources // 2, 2, 8, LANES)
+        one, two = couples[:, 0], couples[:, 1]
+        upper = lax.broadcasted_iota(jnp.int32, one.shape, 1) < s_dev
+        first = jnp.where(upper, one, pltpu.roll(two, s_dev, 1))
+        second = jnp.where(upper, pltpu.roll(one, s_dev, 1), two)
+        return [x.reshape(samples, LANES) for x in (first, second)]
 
     panel_a = got_ref[:, 0:TILE, :].astype(jnp.float32)
     panel_b = got_ref[:, TILE:BLOCK, :].astype(jnp.float32)
     tile_b = jnp.where(samp == 0, panel_b[:, : TILE // 2], panel_b[:, TILE // 2 :])
 
     count = jnp.float32(samples)
-    geno_b = jnp.concatenate([by_samples(tile_b, q) for q in range(TILE // 2 // s_dev)], axis=1)
+    geno_b = jnp.concatenate(by_samples(tile_b), axis=1)
     marg_b = jnp.sum(geno_b, axis=0, keepdims=True)
     centred = (geno_b - marg_b / count) * (samples**-0.5)
     b_hi = centred.astype(jnp.bfloat16)
@@ -126,15 +138,14 @@
     c_lo = tail - c_hi
 
     rows = []
-    for q in range(TILE // s_dev):
-        geno_a = by_samples(panel_a, q)
+    for geno_a in by_samples(panel_a[:, : TILE // 2]) + by_samples(panel_a[:, TILE // 2 :]):
         rows.append(jnp.concatenate([geno_a, geno_a], axis=0).astype(jnp.bfloat16).T)
     rows = jnp.concatenate(rows, axis=0)
     minus = -rows
     copies = []
     for k, yrow in enumerate(yrows):
-        tails = [jnp.broadcast_to(c[k : k + 1], geno_b.shape).astype(jnp.bfloat16) for c in (c_hi, c_lo)]
-        right = jnp.concatenate([b_both] + tails, axis=0)
+        tails = [jnp.broadcast_to(c[k : k + 1], (TILE, c.shape[1])).astype(jnp.bfloat16) for c in (c_hi, c_lo)]
+        right = jnp.concatenate([b_both] + [t for t in tails for _ in range(samples // TILE)], axis=0)
         left = jnp.concatenate([rows * yrow.astype(jnp.bfloat16), minus], axis=1)
         out_ref[k] = jnp.dot(left, right, preferred_element_type=jnp.float32).astype(out_ref.dtype)
         copies.append(pltpu.make_async_copy(out_ref.at[k], out_hbm.at[0, k], sems.at[k]))

time: 15 us -> 15 us (level)
  no operation moved by 1% of the time
where the time goes in v14:
time: 15 us; the launch traced here: 14.8 us
  starting transfers between devices  9.34 us (62%)
  waiting for transfers between devices  3.03 us (20%)
  Pallas kernels  2.43 us (16%)
    ppermute x4, starting transfers between devices, on_device(): arrived.append(lax.ppermute(message, AXES, route))  8.27 us
    pallas_call x1, Pallas kernels, on_device(): pl.pallas_call(functools.partial(stat_kernel, pair_count, samps), out_sha...  1.48 us
    ppermute x4, waiting for transfers between devices, on_device(): arrived.append(lax.ppermute(message, AXES, route))  1.32 us
    pallas_call x1, Pallas kernels, on_device(): pl.pallas_call(functools.partial(pack_kernel, pair_count, samps), out_sha...  0.95 us
    ppermute x1, waiting for transfers between devices, on_device(): got = lax.ppermute(give, 'samp', swap)  0.87 us
    ppermute x3, waiting for transfers between devices, on_device(): mates = [lax.ppermute(a, 'samp', swap) for a in far]  0.84 us
    ppermute x3, starting transfers between devices, on_device(): mates = [lax.ppermute(a, 'samp', swap) for a in far]  0.55 us
    ppermute x1, starting transfers between devices, on_device(): got = lax.ppermute(give, 'samp', swap)  0.52 us
  transfers between devices with their start and end apart: 8, of which 4 were waited for; matrix products, arithmetic and copies ran while one was open for 0% of the time, Pallas kernels for 0%

profile of v14, /device:TPU:0, one launch (start us, length us, event | category | flops | bytes accessed | tf_op | source)
XLA Modules:
  0.0 14.8 jit_solution(3370756727303925548)
XLA Ops:
  0.0 0.9 %pack.1 = (bf16[160,128]{1,0:T(8,128)(2,1)S(1)}, bf16[168,128]{1,0:T(8,128)(2,1)S(1)}, bf16[8,128]{1,0:T(8,128)(2,1)S(1)}) custom-call(s32[2,8]{1,0:T(2,128)} %bitcast.7, bf16[2,4]{1,0:T(2,128)(2,1)} %pheno_hbm.1, s32[2,64]{1,0:T(2,128)} %perms_hbm.1, bf16[128,128]{1,0:T(8,128)(2,1)} %bitcast.6), custom_call_target="tpu_custom_call" | custom-call | tf_op jit(solution)/shard_map/pack/pallas_call | solution.py:172
  1.0 0.5 %collective-permute-start = (bf16[168,128]{1,0:T(8,128)(2,1)S(1)}, bf16[168,128]{1,0:T(8,128)(2,1)S(1)}, u32[]{:S(2)}, u32[]{:S(2)}) collective-permute-start(bf16[168,128]{1,0:T(8,128)(2,1)S(1)} %get-tuple-element.9), channel_id=1, source_target_pairs={{0,1},{1,0},{2,3},{3,2},{4,5},{5,4},{6,7},{7,6},{8,9},{9,8},{10,11... | collective-permute-start | bytes 129032 | tf_op jit(solution)/shard_map/ppermute | solution.py:189
  1.5 0.9 %collective-permute-done.give_ref = bf16[168,128]{1,0:T(8,128)(2,1)S(1)} collective-permute-done((bf16[168,128]{1,0:T(8,128)(2,1)S(1)}, bf16[168,128]{1,0:T(8,128)(2,1)S(1)}, u32[]{:S(2)}, u32[]{:S(2)}) %collective-permute-start) | collective-permute-done | bytes 43040 | tf_op jit(solution)/shard_map/ppermute | solution.py:189
  2.4 3.0 %collective-permute-start.4 = (bf16[72,128]{1,0:T(8,128)(2,1)S(1)}, bf16[72,128]{1,0:T(8,128)(2,1)S(1)}, u32[]{:S(2)}, u32[]{:S(2)}) collective-permute-start(bf16[72,128]{1,0:T(8,128)(2,1)S(1)} %get-tuple-element.19), channel_id=1, source_target_pairs={{0,4},{1,9},{2,6},{3,11},{4,8},{5,13},{6,10},{7,15},{8,12},{9,1},{... | collective-permute-start | bytes 55304 | tf_op jit(solution)/shard_map/ppermute | solution.py:200
  5.3 2.5 %collective-permute-start.2 = (bf16[72,128]{1,0:T(8,128)(2,1)S(1)}, bf16[72,128]{1,0:T(8,128)(2,1)S(1)}, u32[]{:S(2)}, u32[]{:S(2)}) collective-permute-start(bf16[72,128]{1,0:T(8,128)(2,1)S(1)} %get-tuple-element.20), channel_id=1, source_target_pairs={{0,6},{1,11},{2,4},{3,9},{4,10},{5,15},{6,8},{7,13},{8,14},{9,3},{... | collective-permute-start | bytes 55304 | tf_op jit(solution)/shard_map/ppermute | solution.py:200
  7.9 0.5 %collective-permute-start.3 = (bf16[72,128]{1,0:T(8,128)(2,1)S(1)}, bf16[72,128]{1,0:T(8,128)(2,1)S(1)}, u32[]{:S(2)}, u32[]{:S(2)}) collective-permute-start(bf16[72,128]{1,0:T(8,128)(2,1)S(1)} %get-tuple-element.21), channel_id=1, source_target_pairs={{0,2},{1,15},{2,0},{3,13},{4,6},{5,3},{6,4},{7,1},{8,10},{9,7},{10... | collective-permute-start | bytes 55304 | tf_op jit(solution)/shard_map/ppermute | solution.py:200
  8.4 2.2 %collective-permute-start.1 = (bf16[72,128]{1,0:T(8,128)(2,1)S(1)}, bf16[72,128]{1,0:T(8,128)(2,1)S(1)}, u32[]{:S(2)}, u32[]{:S(2)}) collective-permute-start(bf16[72,128]{1,0:T(8,128)(2,1)S(1)} %get-tuple-element.22), channel_id=1, source_target_pairs={{0,12},{1,13},{2,14},{3,15},{4,0},{5,1},{6,2},{7,3},{8,4},{9,5},{1... | collective-permute-start | bytes 55304 | tf_op jit(solution)/shard_map/ppermute | solution.py:200
  10.6 0.0 collective-permute-done.4.refs_2_
  10.6 0.0 collective-permute-start.7
  10.7 1.3 %collective-permute-done.2.refs_0_ = bf16[72,128]{1,0:T(8,128)(2,1)S(1)} collective-permute-done((bf16[72,128]{1,0:T(8,128)(2,1)S(1)}, bf16[72,128]{1,0:T(8,128)(2,1)S(1)}, u32[]{:S(2)}, u32[]{:S(2)}) %collective-permute-start.2) | collective-permute-done | bytes 18464 | tf_op jit(solution)/shard_map/ppermute | solution.py:200
  12.0 0.0 collective-permute-start.5
  12.0 0.0 collective-permute-done.3.refs_1_
  12.0 0.5 %collective-permute-start.6 = (bf16[72,128]{1,0:T(8,128)(2,1)S(1)}, bf16[72,128]{1,0:T(8,128)(2,1)S(1)}, u32[]{:S(2)}, u32[]{:S(2)}) collective-permute-start(bf16[72,128]{1,0:T(8,128)(2,1)S(1)} %collective-permute-done.3.refs_1_), channel_id=1, source_target_pairs={{0,1},{1,0},{2,3},{3,2},{4,5},{5,4},{6,7},{7,6},{8,9},{9,8},{10,11... | collective-permute-start | bytes 55304 | tf_op jit(solution)/shard_map/ppermute | solution.py:202
  12.5 0.0 collective-permute-done.1.near_ref
  12.5 0.0 collective-permute-done.7.refs_5_
  12.5 0.7 %collective-permute-done.5.refs_3_ = bf16[72,128]{1,0:T(8,128)(2,1)S(1)} collective-permute-done((bf16[72,128]{1,0:T(8,128)(2,1)S(1)}, bf16[72,128]{1,0:T(8,128)(2,1)S(1)}, u32[]{:S(2)}, u32[]{:S(2)}) %collective-permute-start.5) | collective-permute-done | bytes 18464 | tf_op jit(solution)/shard_map/ppermute | solution.py:202
  13.2 0.2 %collective-permute-done.6.refs_4_ = bf16[72,128]{1,0:T(8,128)(2,1)S(1)} collective-permute-done((bf16[72,128]{1,0:T(8,128)(2,1)S(1)}, bf16[72,128]{1,0:T(8,128)(2,1)S(1)}, u32[]{:S(2)}, u32[]{:S(2)}) %collective-permute-start.6) | collective-permute-done | bytes 18464 | tf_op jit(solution)/shard_map/ppermute | solution.py:202
  13.4 1.5 %stat.1 = bf16[1,4,512,256]{3,2,1,0:T(8,128)(2,1)} custom-call(bf16[8,128]{1,0:T(8,128)(2,1)S(1)} %slice_add_fusion.wave_ref, bf16[160,128]{1,0:T(8,128)(2,1)S(1)} %get-tuple-element.10.keep_ref, bf16[168,128]{1,0:T(8,128)(2,1)S(1)} %collective-permute-done.give_ref, bf16[72,128]{1,0:T(8,128)(2,1)S(1)} %collective-permute-done.1.near_ref, ...), custom_call_target="tpu_custom_call" | custom-call | tf_op jit(solution)/shard_map/stat/pallas_call | solution.py:204
  (4 shorter events, 0.0 us)
Async XLA Ops:
  1.0 1.4 %collective-permute-start = (bf16[168,128]{1,0:T(8,128)(2,1)S(1)}, bf16[168,128]{1,0:T(8,128)(2,1)S(1)}, u32[]{:S(2)}, u32[]{:S(2)}) collective-permute-start(bf16[168,128]{1,0:T(8,128)(2,1)S(1)} %get-tuple-element.9), channel_id=1, source_target_pairs={{0,1},{1,0},{2,3},{3,2},{4,5},{5,4},{6,7},{7,6},{8,9},{9,8},{10,11... | collective-permute-start | bytes 129032 | tf_op jit(solution)/shard_map/ppermute | solution.py:189
  2.4 8.3 %collective-permute-start.4 = (bf16[72,128]{1,0:T(8,128)(2,1)S(1)}, bf16[72,128]{1,0:T(8,128)(2,1)S(1)}, u32[]{:S(2)}, u32[]{:S(2)}) collective-permute-start(bf16[72,128]{1,0:T(8,128)(2,1)S(1)} %get-tuple-element.19), channel_id=1, source_target_pairs={{0,4},{1,9},{2,6},{3,11},{4,8},{5,13},{6,10},{7,15},{8,12},{9,1},{... | collective-permute-start | bytes 55304 | tf_op jit(solution)/shard_map/ppermute | solution.py:200
  5.3 6.7 %collective-permute-start.2 = (bf16[72,128]{1,0:T(8,128)(2,1)S(1)}, bf16[72,128]{1,0:T(8,128)(2,1)S(1)}, u32[]{:S(2)}, u32[]{:S(2)}) collective-permute-start(bf16[72,128]{1,0:T(8,128)(2,1)S(1)} %get-tuple-element.20), channel_id=1, source_target_pairs={{0,6},{1,11},{2,4},{3,9},{4,10},{5,15},{6,8},{7,13},{8,14},{9,3},{... | collective-permute-start | bytes 55304 | tf_op jit(solution)/shard_map/ppermute | solution.py:200
  7.9 4.2 %collective-permute-start.3 = (bf16[72,128]{1,0:T(8,128)(2,1)S(1)}, bf16[72,128]{1,0:T(8,128)(2,1)S(1)}, u32[]{:S(2)}, u32[]{:S(2)}) collective-permute-start(bf16[72,128]{1,0:T(8,128)(2,1)S(1)} %get-tuple-element.21), channel_id=1, source_target_pairs={{0,2},{1,15},{2,0},{3,13},{4,6},{5,3},{6,4},{7,1},{8,10},{9,7},{10... | collective-permute-start | bytes 55304 | tf_op jit(solution)/shard_map/ppermute | solution.py:200
  8.4 4.1 %collective-permute-start.1 = (bf16[72,128]{1,0:T(8,128)(2,1)S(1)}, bf16[72,128]{1,0:T(8,128)(2,1)S(1)}, u32[]{:S(2)}, u32[]{:S(2)}) collective-permute-start(bf16[72,128]{1,0:T(8,128)(2,1)S(1)} %get-tuple-element.22), channel_id=1, source_target_pairs={{0,12},{1,13},{2,14},{3,15},{4,0},{5,1},{6,2},{7,3},{8,4},{9,5},{1... | collective-permute-start | bytes 55304 | tf_op jit(solution)/shard_map/ppermute | solution.py:200
  10.6 1.9 %collective-permute-start.7 = (bf16[72,128]{1,0:T(8,128)(2,1)S(1)}, bf16[72,128]{1,0:T(8,128)(2,1)S(1)}, u32[]{:S(2)}, u32[]{:S(2)}) collective-permute-start(bf16[72,128]{1,0:T(8,128)(2,1)S(1)} %collective-permute-done.4.refs_2_), channel_id=1, source_target_pairs={{0,1},{1,0},{2,3},{3,2},{4,5},{5,4},{6,7},{7,6},{8,9},{9,8},{10,11... | collective-permute-start | bytes 55304 | tf_op jit(solution)/shard_map/ppermute | solution.py:202
  12.0 1.2 %collective-permute-start.5 = (bf16[72,128]{1,0:T(8,128)(2,1)S(1)}, bf16[72,128]{1,0:T(8,128)(2,1)S(1)}, u32[]{:S(2)}, u32[]{:S(2)}) collective-permute-start(bf16[72,128]{1,0:T(8,128)(2,1)S(1)} %collective-permute-done.2.refs_0_), channel_id=1, source_target_pairs={{0,1},{1,0},{2,3},{3,2},{4,5},{5,4},{6,7},{7,6},{8,9},{9,8},{10,11... | collective-permute-start | bytes 55304 | tf_op jit(solution)/shard_map/ppermute | solution.py:202
  12.0 1.4 %collective-permute-start.6 = (bf16[72,128]{1,0:T(8,128)(2,1)S(1)}, bf16[72,128]{1,0:T(8,128)(2,1)S(1)}, u32[]{:S(2)}, u32[]{:S(2)}) collective-permute-start(bf16[72,128]{1,0:T(8,128)(2,1)S(1)} %collective-permute-done.3.refs_1_), channel_id=1, source_target_pairs={{0,1},{1,0},{2,3},{3,2},{4,5},{5,4},{6,7},{7,6},{8,9},{9,8},{10,11... | collective-permute-start | bytes 55304 | tf_op jit(solution)/shard_map/ppermute | solution.py:202

commit v15 on v14

--- a/solution.py
+++ b/solution.py
@@ -20,7 +20,7 @@
     mine = rest[: len(rest) // 2] if core == 0 else rest[len(rest) // 2 :]
     if core == 0:
         mine = mine[1:] + mine[:1]
-    return mine[1:] + mine[:1] + [shared, 0]
+    return mine + [shared, 0]
 
 
 def shifted(pair, offset, pair_count, sign=1):
@@ -34,48 +34,62 @@
     return -(-stats * 2 * samples // LANES // 8) * 8
 
 
-def pack_kernel(
-    pair_count, samps, pairs_hbm, pheno_hbm, perms_hbm, grid_hbm, keep_ref, give_ref, wave_ref, pairs_ref, pheno_ref, perms_ref, grid_ref, sems
+def spread(pheno, perms, first, rows):
+    genes, s_dev = pheno.shape
+    samples = perms.shape[1]
+    pheno = pheno.astype(jnp.float32)
+    perms = perms - first
+    perms = jnp.concatenate([perms, perms], axis=1)
+    tiles = []
+    for g in range(genes):
+        drawn = jnp.zeros(perms.shape, jnp.float32)
+        for s in range(s_dev):
+            drawn = jnp.where(perms == s, pheno[g : g + 1, s : s + 1], drawn)
+        tiles += [drawn[r : r + 1, t : t + LANES] for r in range(perms.shape[0]) for t in range(0, 2 * samples, LANES)]
+    if rows > len(tiles):
+        tiles.append(jnp.zeros((rows - len(tiles), LANES), jnp.float32))
+    return jnp.concatenate(tiles, axis=0)
+
+
+def pick_kernel(
+    pair_count, samps, pairs_hbm, grid_hbm, pheno_hbm, perms_hbm, keep_ref, pick_ref, wave_ref, perms_ref, pairs_ref, grid_ref, pheno_ref, sems
 ):
     fetched = ((pairs_hbm, pairs_ref), (grid_hbm, grid_ref), (pheno_hbm, pheno_ref), (perms_hbm, perms_ref))
     copies = [pltpu.make_async_copy(source, target, sems.at[i]) for i, (source, target) in enumerate(fetched)]
     for copy in copies:
         copy.start()
     pair, samp = lax.axis_index("pair"), lax.axis_index("samp")
-    genes, s_dev = pheno_ref.shape
-    rperms, samples = perms_ref.shape
-    spot = (pair * samps + samp) * s_dev
-    for copy in copies[:2]:
+    shape = (TILE, pick_ref.shape[1])
+    ahead = lax.broadcasted_iota(jnp.int32, shape, 1) - lax.broadcasted_iota(jnp.int32, shape, 0)
+    for copy in copies:
         copy.wait()
-
-    own_side, far_side = offsets(pair_count, 0), offsets(pair_count, 1)
-    for i, (even, odd) in enumerate(zip(own_side, far_side)):
-        for ref, core in ((keep_ref, samp), (give_ref, samps - 1 - samp)):
-            n = shifted(pair, jnp.where(core == 0, even, odd), pair_count)
-            for j in range(2):
-                start = pl.multiple_of(pairs_ref[j, n] * TILE, TILE)
-                place = i * BLOCK + j * TILE
-                ref[place : place + TILE, :] = grid_ref[pl.ds(start, TILE), :]
-
-    for copy in copies[2:]:
-        copy.wait()
-    pheno = pheno_ref[...].astype(jnp.float32)
-    perms = perms_ref[...] - spot
-    perms = jnp.concatenate([perms, perms], axis=1)
-    rows = []
-    for g in range(genes):
-        drawn = jnp.zeros(perms.shape, jnp.float32)
-        for s in range(s_dev):
-            drawn = jnp.where(perms == s, pheno[g : g + 1, s : s + 1], drawn)
-        rows += [drawn[r : r + 1, t : t + LANES] for r in range(rperms) for t in range(0, 2 * samples, LANES)]
-    if wave_ref.shape[0] > len(rows):
-        rows.append(jnp.zeros((wave_ref.shape[0] - len(rows), LANES), jnp.float32))
-    wave = jnp.concatenate(rows, axis=0).astype(wave_ref.dtype)
-    wave_ref[...] = wave
-    give_ref[len(own_side) * BLOCK :, :] = wave
-
-
-def stat_kernel(pair_count, samps, wave_ref, keep_ref, give_ref, near_ref, *refs):
+    wave = spread(pheno_ref[...], perms_ref[...], (pair * samps + samp) * pheno_ref.shape[1], wave_ref.shape[0])
+    wave_ref[...] = wave.astype(wave_ref.dtype)
+    for i, (even, odd) in enumerate(zip(offsets(pair_count, 0), offsets(pair_count, 1))):
+        n = shifted(pair, jnp.where(samp == 0, even, odd), pair_count)
+        for j in range(2):
+            start = pl.multiple_of(pairs_ref[j, n] * TILE, TILE)
+            rows = slice(i * BLOCK + j * TILE, i * BLOCK + (j + 1) * TILE)
+            keep_ref[rows, :] = grid_ref[pl.ds(start, TILE), :]
+            pick_ref[rows, :] = jnp.where(ahead == start, 1.0, 0.0).astype(pick_ref.dtype)
+
+
+def join_kernel(pair_count, samps, keep_ref, pick_ref, wave_ref, perms_ref, grid_ref, pheno_ref, mate_ref, both_ref, *out_refs):
+    pair, samp = lax.axis_index("pair"), lax.axis_index("samp")
+    first = (pair * samps + samps - 1 - samp) * pheno_ref.shape[1]
+    wave = spread(pheno_ref[...], perms_ref[...], first, wave_ref.shape[0])
+    wave = (wave_ref[...].astype(jnp.float32) + wave).astype(wave_ref.dtype)
+    both_ref[...] = wave
+    picked = jnp.dot(pick_ref[...], grid_ref[...], preferred_element_type=jnp.float32).astype(mate_ref.dtype)
+    for i, ref in enumerate(out_refs):
+        rows = slice(i * BLOCK, (i + 1) * BLOCK)
+        ref[:BLOCK, :] = keep_ref[rows, :]
+        ref[BLOCK : 2 * BLOCK, :] = picked[rows]
+        ref[2 * BLOCK :, :] = wave
+    mate_ref[...] = picked[len(out_refs) * BLOCK :]
+
+
+def stat_kernel(pair_count, samps, wave_ref, keep_ref, mate_self_ref, near_ref, *refs):
     far = pair_count // 2 - 1
     own_refs, mate_refs = refs[:far], refs[far : 2 * far]
     out_hbm, got_ref, out_ref, sems = refs[2 * far :]
@@ -95,7 +109,7 @@
     place(even[far], other, near_ref[BLOCK : 2 * BLOCK, :])
     itself = (far + 1) * BLOCK
     place(0, samp, keep_ref[itself : itself + BLOCK, :])
-    place(0, other, give_ref[itself : itself + BLOCK, :])
+    place(0, other, mate_self_ref[...])
 
     sources = got_ref.shape[0]
     s_dev = TILE * LANES // PANEL
@@ -169,29 +183,44 @@
     def array(*shape):
         return jax.ShapeDtypeStruct(shape, dosage.dtype)
 
-    keep, give, wave = pl.pallas_call(
-        functools.partial(pack_kernel, pair_count, samps),
-        out_shape=[array(rounds * BLOCK, LANES), array(rounds * BLOCK + rows, LANES), array(rows, LANES)],
-        in_specs=[hbm, hbm, hbm, hbm],
-        out_specs=[vmem, vmem, vmem],
+    swap = [(i, samps - 1 - i) for i in range(samps)]
+    mate_dosage = lax.ppermute(dosage, "samp", swap)
+    mate_pheno = lax.ppermute(phenotype, "samp", swap)
+    params = pltpu.CompilerParams(vmem_limit_bytes=24 * 1024 * 1024)
+    blocks = rounds * BLOCK
+    keep, pick, wave, perms_near = pl.pallas_call(
+        functools.partial(pick_kernel, pair_count, samps),
+        out_shape=[
+            array(blocks, LANES),
+            array(blocks, grid.shape[0]),
+            array(rows, LANES),
+            jax.ShapeDtypeStruct(perms.shape, perms.dtype),
+        ],
+        in_specs=[hbm] * 4,
+        out_specs=[vmem] * 4,
         scratch_shapes=[
             pltpu.SMEM(pairs.shape[::-1], pairs.dtype),
+            pltpu.VMEM(grid.shape, grid.dtype),
             pltpu.VMEM(phenotype.shape, phenotype.dtype),
-            pltpu.VMEM(perms.shape, perms.dtype),
-            pltpu.VMEM(grid.shape, grid.dtype),
             pltpu.SemaphoreType.DMA((4,)),
         ],
-        compiler_params=pltpu.CompilerParams(vmem_limit_bytes=8 * 1024 * 1024),
-        name="pack",
-    )(*[pltpu.with_memory_space_constraint(x, pltpu.HBM) for x in (pairs.T, phenotype, perms, grid)])
-
-    swap = [(i, samps - 1 - i) for i in range(samps)]
-    got = lax.ppermute(give, "samp", swap)
-    wave = wave + got[rounds * BLOCK :]
+        compiler_params=params,
+        cost_estimate=pl.CostEstimate(flops=0, bytes_accessed=4 * blocks * LANES * 2, transcendentals=0),
+        name="pick",
+    )(*[pltpu.with_memory_space_constraint(x, pltpu.HBM) for x in (pairs.T, grid, phenotype, perms)])
+
+    mate_grid = mate_dosage.reshape(s_dev, snps // LANES, LANES).transpose(1, 0, 2).reshape(-1, LANES)
+    mate_self, wave, *messages = pl.pallas_call(
+        functools.partial(join_kernel, pair_count, samps),
+        out_shape=[array(BLOCK, LANES), array(rows, LANES)] + [array(2 * BLOCK + rows, LANES)] * (rounds - 1),
+        in_specs=[vmem] * 6,
+        out_specs=[vmem] * (rounds + 1),
+        compiler_params=params,
+        name="join",
+    )(keep, pick, wave, perms_near, mate_grid, mate_pheno)
+
     arrived = []
-    for i in range(rounds - 1):
-        blocks = slice(i * BLOCK, (i + 1) * BLOCK)
-        message = jnp.concatenate([keep[blocks], got[blocks], wave], axis=0)
+    for i, message in enumerate(messages):
         route = [
             (p * samps + c, shifted(p, offsets(pair_count, c)[i], pair_count) * samps + c)
             for p in range(pair_count)
@@ -213,7 +242,7 @@
         ],
         compiler_params=pltpu.CompilerParams(vmem_limit_bytes=48 * 1024 * 1024),
         name="stat",
-    )(wave, keep, got, near, *far, *mates)
+    )(wave, keep, mate_self, near, *far, *mates)
 
 
 def solution(mesh):

time: 15 us -> 14.2 us (0.947)
  waiting for transfers between devices: 3.03 us -> 2.11 us
    ppermute x1 -> x2, waiting for transfers between devices: 0.87 us -> 0.28 us  [the longest x1 0.28 us: on_device(): mate_pheno = lax.ppermute(phenotype, 'samp', swap)]
    ppermute x4, waiting for transfers between devices: 1.32 us -> 1 us  [on_device(): arrived.append(lax.ppermute(message, AXES, route))]
    ppermute x3, starting transfers between devices: 0.55 us -> 0.71 us  [on_device(): mates = [lax.ppermute(a, 'samp', swap) for a in far]]
    pallas_call x1 -> x2, Pallas kernels: 0.95 us -> 1.05 us  [the longest x1 0.91 us: on_device(): pl.pallas_call(functools.partial(pick_kernel, pair_count, samps), out_sha...]
    ppermute x1 -> x2, starting transfers between devices: 0.52 us -> 0.51 us  [the longest x1 0.45 us: on_device(): mate_dosage = lax.ppermute(dosage, 'samp', swap)]
  transfers between devices with their start and end apart: 8 -> 9, of which waited for: 4 -> 4; matrix products, arithmetic and copies ran while one was open for 0% -> 0% of each run, Pallas kernels for 0% -> 7%
where the time goes in v15:
time: 14.2 us; the launch traced here: 14 us
  starting transfers between devices  9.33 us (66%)
  Pallas kernels  2.54 us (18%)
  waiting for transfers between devices  2.11 us (15%)
    ppermute x4, starting transfers between devices, on_device(): arrived.append(lax.ppermute(message, AXES, route))  8.12 us
    pallas_call x1, Pallas kernels, on_device(): pl.pallas_call(functools.partial(stat_kernel, pair_count, samps), out_sha...  1.48 us
    ppermute x4, waiting for transfers between devices, on_device(): arrived.append(lax.ppermute(message, AXES, route))  1 us
    pallas_call x1, Pallas kernels, on_device(): pl.pallas_call(functools.partial(pick_kernel, pair_count, samps), out_sha...  0.91 us
    ppermute x3, waiting for transfers between devices, on_device(): mates = [lax.ppermute(a, 'samp', swap) for a in far]  0.84 us
    ppermute x3, starting transfers between devices, on_device(): mates = [lax.ppermute(a, 'samp', swap) for a in far]  0.71 us
    ppermute x1, starting transfers between devices, on_device(): mate_dosage = lax.ppermute(dosage, 'samp', swap)  0.45 us
  transfers between devices with their start and end apart: 9, of which 4 were waited for; matrix products, arithmetic and copies ran while one was open for 0% of the time, Pallas kernels for 7%

profile of v15, /device:TPU:0, one launch (start us, length us, event | category | flops | bytes accessed | tf_op | source)
XLA Modules:
  0.0 14.0 jit_solution(3488692279120691827)
XLA Ops:
  0.0 0.5 %collective-permute-start = (bf16[4,4096]{1,0:T(4,128)(2,1)}, bf16[4,4096]{1,0:T(4,128)(2,1)S(1)}, u32[]{:S(2)}, u32[]{:S(2)}) collective-permute-start(bf16[4,4096]{1,0:T(4,128)(2,1)} %param.4), channel_id=1, source_target_pairs={{0,1},{1,0},{2,3},{3,2},{4,5},{5,4},{6,7},{7,6},{8,9},{9,8},{10,11... | collective-permute-start | bytes 98312 | tf_op jit(solution)/shard_map/ppermute | solution.py:187
  0.5 0.1 collective-permute-start.1
  0.5 0.9 %pick.1 = (bf16[160,128]{1,0:T(8,128)(2,1)S(1)}, bf16[160,128]{1,0:T(8,128)(2,1)S(1)}, bf16[8,128]{1,0:T(8,128)(2,1)S(1)}, s32[2,64]{1,0:T(2,128)S(1)}) custom-call(s32[2,8]{1,0:T(2,128)} %bitcast.13, bf16[128,128]{1,0:T(8,128)(2,1)} %bitcast.12, bf16[2,4]{1,0:T(2,128)(2,1)} %pheno_hbm.1, s32[2,64]{1,0:T(2,128)} %perms_hbm.1), custom_call_target="tpu_custom_call" | custom-call | bytes 163840 | tf_op jit(solution)/shard_map/pick/pallas_call | solution.py:191
  1.4 0.3 %collective-permute-done.1.pheno_ref = bf16[2,4]{1,0:T(2,128)(2,1)S(1)} collective-permute-done((bf16[2,4]{1,0:T(2,128)(2,1)}, bf16[2,4]{1,0:T(2,128)(2,1)S(1)}, u32[]{:S(2)}, u32[]{:S(2)}) %collective-permute-start.1) | collective-permute-done | bytes 48 | tf_op jit(solution)/shard_map/ppermute | solution.py:188
  1.7 0.0 collective-permute-done
  1.7 0.1 %join.1 = (bf16[32,128]{1,0:T(8,128)(2,1)S(1)}, bf16[8,128]{1,0:T(8,128)(2,1)S(1)}, bf16[72,128]{1,0:T(8,128)(2,1)S(1)}, bf16[72,128]{1,0:T(8,128)(2,1)S(1)}, bf...) custom-call(bf16[160,128]{1,0:T(8,128)(2,1)S(1)} %get-tuple-element.15.keep_ref, ...), custom_call_target="tpu_custom_call" | custom-call | tf_op jit(solution)/shard_map/join/pallas_call | solution.py:213
  1.9 2.8 %collective-permute-start.3 = (bf16[72,128]{1,0:T(8,128)(2,1)S(1)}, bf16[72,128]{1,0:T(8,128)(2,1)S(1)}, u32[]{:S(2)}, u32[]{:S(2)}) collective-permute-start(bf16[72,128]{1,0:T(8,128)(2,1)S(1)} %get-tuple-element.22), channel_id=1, source_target_pairs={{0,4},{1,9},{2,6},{3,11},{4,8},{5,13},{6,10},{7,15},{8,12},{9,1},{... | collective-permute-start | bytes 55304 | tf_op jit(solution)/shard_map/ppermute | solution.py:229
  4.7 2.5 %collective-permute-start.4 = (bf16[72,128]{1,0:T(8,128)(2,1)S(1)}, bf16[72,128]{1,0:T(8,128)(2,1)S(1)}, u32[]{:S(2)}, u32[]{:S(2)}) collective-permute-start(bf16[72,128]{1,0:T(8,128)(2,1)S(1)} %get-tuple-element.23), channel_id=1, source_target_pairs={{0,6},{1,11},{2,4},{3,9},{4,10},{5,15},{6,8},{7,13},{8,14},{9,3},{... | collective-permute-start | bytes 55304 | tf_op jit(solution)/shard_map/ppermute | solution.py:229
  7.2 0.5 %collective-permute-start.5 = (bf16[72,128]{1,0:T(8,128)(2,1)S(1)}, bf16[72,128]{1,0:T(8,128)(2,1)S(1)}, u32[]{:S(2)}, u32[]{:S(2)}) collective-permute-start(bf16[72,128]{1,0:T(8,128)(2,1)S(1)} %get-tuple-element.24), channel_id=1, source_target_pairs={{0,2},{1,15},{2,0},{3,13},{4,6},{5,3},{6,4},{7,1},{8,10},{9,7},{10... | collective-permute-start | bytes 55304 | tf_op jit(solution)/shard_map/ppermute | solution.py:229
  7.7 2.2 %collective-permute-start.2 = (bf16[72,128]{1,0:T(8,128)(2,1)S(1)}, bf16[72,128]{1,0:T(8,128)(2,1)S(1)}, u32[]{:S(2)}, u32[]{:S(2)}) collective-permute-start(bf16[72,128]{1,0:T(8,128)(2,1)S(1)} %get-tuple-element.21), channel_id=1, source_target_pairs={{0,12},{1,13},{2,14},{3,15},{4,0},{5,1},{6,2},{7,3},{8,4},{9,5},{1... | collective-permute-start | bytes 55304 | tf_op jit(solution)/shard_map/ppermute | solution.py:229
  10.0 0.0 collective-permute-done.3.refs_0_
  10.0 0.2 %collective-permute-start.6 = (bf16[72,128]{1,0:T(8,128)(2,1)S(1)}, bf16[72,128]{1,0:T(8,128)(2,1)S(1)}, u32[]{:S(2)}, u32[]{:S(2)}) collective-permute-start(bf16[72,128]{1,0:T(8,128)(2,1)S(1)} %collective-permute-done.3.refs_0_), channel_id=1, source_target_pairs={{0,1},{1,0},{2,3},{3,2},{4,5},{5,4},{6,7},{7,6},{8,9},{9,8},{10,11... | collective-permute-start | bytes 55304 | tf_op jit(solution)/shard_map/ppermute | solution.py:231
  10.2 1.0 %collective-permute-done.4.refs_1_ = bf16[72,128]{1,0:T(8,128)(2,1)S(1)} collective-permute-done((bf16[72,128]{1,0:T(8,128)(2,1)S(1)}, bf16[72,128]{1,0:T(8,128)(2,1)S(1)}, u32[]{:S(2)}, u32[]{:S(2)}) %collective-permute-start.4) | collective-permute-done | bytes 18464 | tf_op jit(solution)/shard_map/ppermute | solution.py:229
  11.2 0.0 collective-permute-start.7
  11.2 0.0 collective-permute-done.5.refs_2_
  11.2 0.5 %collective-permute-start.8 = (bf16[72,128]{1,0:T(8,128)(2,1)S(1)}, bf16[72,128]{1,0:T(8,128)(2,1)S(1)}, u32[]{:S(2)}, u32[]{:S(2)}) collective-permute-start(bf16[72,128]{1,0:T(8,128)(2,1)S(1)} %collective-permute-done.5.refs_2_), channel_id=1, source_target_pairs={{0,1},{1,0},{2,3},{3,2},{4,5},{5,4},{6,7},{7,6},{8,9},{9,8},{10,11... | collective-permute-start | bytes 55304 | tf_op jit(solution)/shard_map/ppermute | solution.py:231
  11.7 0.0 collective-permute-done.2.near_ref
  11.7 0.0 collective-permute-done.6.refs_3_
  11.7 0.7 %collective-permute-done.7.refs_4_ = bf16[72,128]{1,0:T(8,128)(2,1)S(1)} collective-permute-done((bf16[72,128]{1,0:T(8,128)(2,1)S(1)}, bf16[72,128]{1,0:T(8,128)(2,1)S(1)}, u32[]{:S(2)}, u32[]{:S(2)}) %collective-permute-start.7) | collective-permute-done | bytes 18464 | tf_op jit(solution)/shard_map/ppermute | solution.py:231
  12.4 0.2 %collective-permute-done.8.refs_5_ = bf16[72,128]{1,0:T(8,128)(2,1)S(1)} collective-permute-done((bf16[72,128]{1,0:T(8,128)(2,1)S(1)}, bf16[72,128]{1,0:T(8,128)(2,1)S(1)}, u32[]{:S(2)}, u32[]{:S(2)}) %collective-permute-start.8) | collective-permute-done | bytes 18464 | tf_op jit(solution)/shard_map/ppermute | solution.py:231
  12.5 1.5 %stat.1 = bf16[1,4,512,256]{3,2,1,0:T(8,128)(2,1)} custom-call(bf16[8,128]{1,0:T(8,128)(2,1)S(1)} %get-tuple-element.19.wave_ref, bf16[160,128]{1,0:T(8,128)(2,1)S(1)} %get-tuple-element.15.keep_ref, bf16[32,128]{1,0:T(8,128)(2,1)S(1)} %get-tuple-element.20.mate_self_ref, bf16[72,128]{1,0:T(8,128)(2,1)S(1)} %collective-permute-done.2.near_ref, ...), custom_call_target="tpu_custom_call" | custom-call | tf_op jit(solution)/shard_map/stat/pallas_call | solution.py:233
Async XLA Ops:
  0.0 1.7 %collective-permute-start = (bf16[4,4096]{1,0:T(4,128)(2,1)}, bf16[4,4096]{1,0:T(4,128)(2,1)S(1)}, u32[]{:S(2)}, u32[]{:S(2)}) collective-permute-start(bf16[4,4096]{1,0:T(4,128)(2,1)} %param.4), channel_id=1, source_target_pairs={{0,1},{1,0},{2,3},{3,2},{4,5},{5,4},{6,7},{7,6},{8,9},{9,8},{10,11... | collective-permute-start | bytes 98312 | tf_op jit(solution)/shard_map/ppermute | solution.py:187
  0.5 1.3 %collective-permute-start.1 = (bf16[2,4]{1,0:T(2,128)(2,1)}, bf16[2,4]{1,0:T(2,128)(2,1)S(1)}, u32[]{:S(2)}, u32[]{:S(2)}) collective-permute-start(bf16[2,4]{1,0:T(2,128)(2,1)} %pheno_hbm.1), channel_id=1, source_target_pairs={{0,1},{1,0},{2,3},{3,2},{4,5},{5,4},{6,7},{7,6},{8,9},{9,8},{10,11... | collective-permute-start | bytes 56 | tf_op jit(solution)/shard_map/ppermute | solution.py:188
  1.9 8.1 %collective-permute-start.3 = (bf16[72,128]{1,0:T(8,128)(2,1)S(1)}, bf16[72,128]{1,0:T(8,128)(2,1)S(1)}, u32[]{:S(2)}, u32[]{:S(2)}) collective-permute-start(bf16[72,128]{1,0:T(8,128)(2,1)S(1)} %get-tuple-element.22), channel_id=1, source_target_pairs={{0,4},{1,9},{2,6},{3,11},{4,8},{5,13},{6,10},{7,15},{8,12},{9,1},{... | collective-permute-start | bytes 55304 | tf_op jit(solution)/shard_map/ppermute | solution.py:229
  4.7 6.5 %collective-permute-start.4 = (bf16[72,128]{1,0:T(8,128)(2,1)S(1)}, bf16[72,128]{1,0:T(8,128)(2,1)S(1)}, u32[]{:S(2)}, u32[]{:S(2)}) collective-permute-start(bf16[72,128]{1,0:T(8,128)(2,1)S(1)} %get-tuple-element.23), channel_id=1, source_target_pairs={{0,6},{1,11},{2,4},{3,9},{4,10},{5,15},{6,8},{7,13},{8,14},{9,3},{... | collective-permute-start | bytes 55304 | tf_op jit(solution)/shard_map/ppermute | solution.py:229
  7.2 4.0 %collective-permute-start.5 = (bf16[72,128]{1,0:T(8,128)(2,1)S(1)}, bf16[72,128]{1,0:T(8,128)(2,1)S(1)}, u32[]{:S(2)}, u32[]{:S(2)}) collective-permute-start(bf16[72,128]{1,0:T(8,128)(2,1)S(1)} %get-tuple-element.24), channel_id=1, source_target_pairs={{0,2},{1,15},{2,0},{3,13},{4,6},{5,3},{6,4},{7,1},{8,10},{9,7},{10... | collective-permute-start | bytes 55304 | tf_op jit(solution)/shard_map/ppermute | solution.py:229
  7.7 4.0 %collective-permute-start.2 = (bf16[72,128]{1,0:T(8,128)(2,1)S(1)}, bf16[72,128]{1,0:T(8,128)(2,1)S(1)}, u32[]{:S(2)}, u32[]{:S(2)}) collective-permute-start(bf16[72,128]{1,0:T(8,128)(2,1)S(1)} %get-tuple-element.21), channel_id=1, source_target_pairs={{0,12},{1,13},{2,14},{3,15},{4,0},{5,1},{6,2},{7,3},{8,4},{9,5},{1... | collective-permute-start | bytes 55304 | tf_op jit(solution)/shard_map/ppermute | solution.py:229
  10.0 1.7 %collective-permute-start.6 = (bf16[72,128]{1,0:T(8,128)(2,1)S(1)}, bf16[72,128]{1,0:T(8,128)(2,1)S(1)}, u32[]{:S(2)}, u32[]{:S(2)}) collective-permute-start(bf16[72,128]{1,0:T(8,128)(2,1)S(1)} %collective-permute-done.3.refs_0_), channel_id=1, source_target_pairs={{0,1},{1,0},{2,3},{3,2},{4,5},{5,4},{6,7},{7,6},{8,9},{9,8},{10,11... | collective-permute-start | bytes 55304 | tf_op jit(solution)/shard_map/ppermute | solution.py:231
  11.2 1.2 %collective-permute-start.7 = (bf16[72,128]{1,0:T(8,128)(2,1)S(1)}, bf16[72,128]{1,0:T(8,128)(2,1)S(1)}, u32[]{:S(2)}, u32[]{:S(2)}) collective-permute-start(bf16[72,128]{1,0:T(8,128)(2,1)S(1)} %collective-permute-done.4.refs_1_), channel_id=1, source_target_pairs={{0,1},{1,0},{2,3},{3,2},{4,5},{5,4},{6,7},{7,6},{8,9},{9,8},{10,11... | collective-permute-start | bytes 55304 | tf_op jit(solution)/shard_map/ppermute | solution.py:231
  11.2 1.4 %collective-permute-start.8 = (bf16[72,128]{1,0:T(8,128)(2,1)S(1)}, bf16[72,128]{1,0:T(8,128)(2,1)S(1)}, u32[]{:S(2)}, u32[]{:S(2)}) collective-permute-start(bf16[72,128]{1,0:T(8,128)(2,1)S(1)} %collective-permute-done.5.refs_2_), channel_id=1, source_target_pairs={{0,1},{1,0},{2,3},{3,2},{4,5},{5,4},{6,7},{7,6},{8,9},{9,8},{10,11... | collective-permute-start | bytes 55304 | tf_op jit(solution)/shard_map/ppermute | solution.py:231

commit v16 on v15

--- a/solution.py
+++ b/solution.py
@@ -17,9 +17,9 @@
 def offsets(pair_count, core):
     shared = pair_count - 2
     rest = [e for e in range(1, pair_count) if e != shared]
-    mine = rest[: len(rest) // 2] if core == 0 else rest[len(rest) // 2 :]
-    if core == 0:
-        mine = mine[1:] + mine[:1]
+    quarter = (len(rest) + 2) // 4
+    middle = rest[quarter : quarter + len(rest) // 2]
+    mine = [e for e in rest if e not in middle] if core == 0 else sorted(middle, key=lambda e: e % 2 == 0)
     return mine + [shared, 0]
 
 

time: 14.2 us -> 14.1 us (level)
  waiting for transfers between devices: 2.11 us -> 1.24 us
  starting transfers between devices: 9.33 us -> 10.1 us
    ppermute x3, starting transfers between devices: 0.71 us -> 1.26 us  [on_device(): mates = [lax.ppermute(a, 'samp', swap) for a in far]]
    ppermute x4, waiting for transfers between devices: 1 us -> 0.5 us  [on_device(): arrived.append(lax.ppermute(message, AXES, route))]
    ppermute x3, waiting for transfers between devices: 0.84 us -> 0.46 us  [on_device(): mates = [lax.ppermute(a, 'samp', swap) for a in far]]
    ppermute x4, starting transfers between devices: 8.12 us -> 8.34 us  [on_device(): arrived.append(lax.ppermute(message, AXES, route))]
where the time goes in v16:
time: 14.1 us; the launch traced here: 13.9 us
  starting transfers between devices  10.1 us (72%)
  Pallas kernels  2.54 us (18%)
  waiting for transfers between devices  1.24 us (9%)
    ppermute x4, starting transfers between devices, on_device(): arrived.append(lax.ppermute(message, AXES, route))  8.34 us
    pallas_call x1, Pallas kernels, on_device(): pl.pallas_call(functools.partial(stat_kernel, pair_count, samps), out_sha...  1.48 us
    ppermute x3, starting transfers between devices, on_device(): mates = [lax.ppermute(a, 'samp', swap) for a in far]  1.26 us
    pallas_call x1, Pallas kernels, on_device(): pl.pallas_call(functools.partial(pick_kernel, pair_count, samps), out_sha...  0.91 us
    ppermute x4, waiting for transfers between devices, on_device(): arrived.append(lax.ppermute(message, AXES, route))  0.5 us
    ppermute x3, waiting for transfers between devices, on_device(): mates = [lax.ppermute(a, 'samp', swap) for a in far]  0.46 us
    ppermute x1, starting transfers between devices, on_device(): mate_dosage = lax.ppermute(dosage, 'samp', swap)  0.45 us
  transfers between devices with their start and end apart: 9, of which 4 were waited for; matrix products, arithmetic and copies ran while one was open for 0% of the time, Pallas kernels for 7%

profile of v16, /device:TPU:0, one launch (start us, length us, event | category | flops | bytes accessed | tf_op | source)
XLA Modules:
  0.0 13.9 jit_solution(13221986748461200288)
XLA Ops:
  0.0 0.5 %collective-permute-start = (bf16[4,4096]{1,0:T(4,128)(2,1)}, bf16[4,4096]{1,0:T(4,128)(2,1)S(1)}, u32[]{:S(2)}, u32[]{:S(2)}) collective-permute-start(bf16[4,4096]{1,0:T(4,128)(2,1)} %param.4), channel_id=1, source_target_pairs={{0,1},{1,0},{2,3},{3,2},{4,5},{5,4},{6,7},{7,6},{8,9},{9,8},{10,11... | collective-permute-start | bytes 98312 | tf_op jit(solution)/shard_map/ppermute | solution.py:187
  0.5 0.1 collective-permute-start.1
  0.5 0.9 %pick.1 = (bf16[160,128]{1,0:T(8,128)(2,1)S(1)}, bf16[160,128]{1,0:T(8,128)(2,1)S(1)}, bf16[8,128]{1,0:T(8,128)(2,1)S(1)}, s32[2,64]{1,0:T(2,128)S(1)}) custom-call(s32[2,8]{1,0:T(2,128)} %bitcast.13, bf16[128,128]{1,0:T(8,128)(2,1)} %bitcast.12, bf16[2,4]{1,0:T(2,128)(2,1)} %pheno_hbm.1, s32[2,64]{1,0:T(2,128)} %perms_hbm.1), custom_call_target="tpu_custom_call" | custom-call | bytes 163840 | tf_op jit(solution)/shard_map/pick/pallas_call | solution.py:191
  1.4 0.3 %collective-permute-done.1.pheno_ref = bf16[2,4]{1,0:T(2,128)(2,1)S(1)} collective-permute-done((bf16[2,4]{1,0:T(2,128)(2,1)}, bf16[2,4]{1,0:T(2,128)(2,1)S(1)}, u32[]{:S(2)}, u32[]{:S(2)}) %collective-permute-start.1) | collective-permute-done | bytes 48 | tf_op jit(solution)/shard_map/ppermute | solution.py:188
  1.7 0.0 collective-permute-done
  1.7 0.1 %join.1 = (bf16[32,128]{1,0:T(8,128)(2,1)S(1)}, bf16[8,128]{1,0:T(8,128)(2,1)S(1)}, bf16[72,128]{1,0:T(8,128)(2,1)S(1)}, bf16[72,128]{1,0:T(8,128)(2,1)S(1)}, bf...) custom-call(bf16[160,128]{1,0:T(8,128)(2,1)S(1)} %get-tuple-element.15.keep_ref, ...), custom_call_target="tpu_custom_call" | custom-call | tf_op jit(solution)/shard_map/join/pallas_call | solution.py:213
  1.9 2.7 %collective-permute-start.3 = (bf16[72,128]{1,0:T(8,128)(2,1)S(1)}, bf16[72,128]{1,0:T(8,128)(2,1)S(1)}, u32[]{:S(2)}, u32[]{:S(2)}) collective-permute-start(bf16[72,128]{1,0:T(8,128)(2,1)S(1)} %get-tuple-element.22), channel_id=1, source_target_pairs={{0,2},{1,7},{2,0},{3,5},{4,6},{5,11},{6,4},{7,9},{8,10},{9,15},{10... | collective-permute-start | bytes 55304 | tf_op jit(solution)/shard_map/ppermute | solution.py:229
  4.6 1.6 %collective-permute-start.4 = (bf16[72,128]{1,0:T(8,128)(2,1)S(1)}, bf16[72,128]{1,0:T(8,128)(2,1)S(1)}, u32[]{:S(2)}, u32[]{:S(2)}) collective-permute-start(bf16[72,128]{1,0:T(8,128)(2,1)S(1)} %get-tuple-element.23), channel_id=1, source_target_pairs={{0,4},{1,11},{2,6},{3,9},{4,8},{5,15},{6,10},{7,13},{8,12},{9,3},{... | collective-permute-start | bytes 55304 | tf_op jit(solution)/shard_map/ppermute | solution.py:229
  6.2 2.0 %collective-permute-start.5 = (bf16[72,128]{1,0:T(8,128)(2,1)S(1)}, bf16[72,128]{1,0:T(8,128)(2,1)S(1)}, u32[]{:S(2)}, u32[]{:S(2)}) collective-permute-start(bf16[72,128]{1,0:T(8,128)(2,1)S(1)} %get-tuple-element.24), channel_id=1, source_target_pairs={{0,14},{1,9},{2,12},{3,11},{4,2},{5,13},{6,0},{7,15},{8,6},{9,1},{... | collective-permute-start | bytes 55304 | tf_op jit(solution)/shard_map/ppermute | solution.py:229
  8.2 2.0 %collective-permute-start.2 = (bf16[72,128]{1,0:T(8,128)(2,1)S(1)}, bf16[72,128]{1,0:T(8,128)(2,1)S(1)}, u32[]{:S(2)}, u32[]{:S(2)}) collective-permute-start(bf16[72,128]{1,0:T(8,128)(2,1)S(1)} %get-tuple-element.21), channel_id=1, source_target_pairs={{0,12},{1,13},{2,14},{3,15},{4,0},{5,1},{6,2},{7,3},{8,4},{9,5},{1... | collective-permute-start | bytes 55304 | tf_op jit(solution)/shard_map/ppermute | solution.py:229
  10.2 0.0 collective-permute-done.3.refs_0_
  10.2 0.0 collective-permute-start.6
  10.2 0.0 collective-permute-done.4.refs_1_
  10.2 0.5 %collective-permute-start.7 = (bf16[72,128]{1,0:T(8,128)(2,1)S(1)}, bf16[72,128]{1,0:T(8,128)(2,1)S(1)}, u32[]{:S(2)}, u32[]{:S(2)}) collective-permute-start(bf16[72,128]{1,0:T(8,128)(2,1)S(1)} %collective-permute-done.4.refs_1_), channel_id=1, source_target_pairs={{0,1},{1,0},{2,3},{3,2},{4,5},{5,4},{6,7},{7,6},{8,9},{9,8},{10,11... | collective-permute-start | bytes 55304 | tf_op jit(solution)/shard_map/ppermute | solution.py:231
  10.7 0.1 collective-permute-done.5.refs_2_
  10.8 0.8 %collective-permute-start.8 = (bf16[72,128]{1,0:T(8,128)(2,1)S(1)}, bf16[72,128]{1,0:T(8,128)(2,1)S(1)}, u32[]{:S(2)}, u32[]{:S(2)}) collective-permute-start(bf16[72,128]{1,0:T(8,128)(2,1)S(1)} %collective-permute-done.5.refs_2_), channel_id=1, source_target_pairs={{0,1},{1,0},{2,3},{3,2},{4,5},{5,4},{6,7},{7,6},{8,9},{9,8},{10,11... | collective-permute-start | bytes 55304 | tf_op jit(solution)/shard_map/ppermute | solution.py:231
  11.6 0.4 %collective-permute-done.2.near_ref = bf16[72,128]{1,0:T(8,128)(2,1)S(1)} collective-permute-done((bf16[72,128]{1,0:T(8,128)(2,1)S(1)}, bf16[72,128]{1,0:T(8,128)(2,1)S(1)}, u32[]{:S(2)}, u32[]{:S(2)}) %collective-permute-start.2) | collective-permute-done | bytes 18464 | tf_op jit(solution)/shard_map/ppermute | solution.py:229
  12.0 0.0 collective-permute-done.6.refs_3_
  12.0 0.0 collective-permute-done.7.refs_4_
  12.0 0.5 %collective-permute-done.8.refs_5_ = bf16[72,128]{1,0:T(8,128)(2,1)S(1)} collective-permute-done((bf16[72,128]{1,0:T(8,128)(2,1)S(1)}, bf16[72,128]{1,0:T(8,128)(2,1)S(1)}, u32[]{:S(2)}, u32[]{:S(2)}) %collective-permute-start.8) | collective-permute-done | bytes 18464 | tf_op jit(solution)/shard_map/ppermute | solution.py:231
  12.4 1.5 %stat.1 = bf16[1,4,512,256]{3,2,1,0:T(8,128)(2,1)} custom-call(bf16[8,128]{1,0:T(8,128)(2,1)S(1)} %get-tuple-element.19.wave_ref, bf16[160,128]{1,0:T(8,128)(2,1)S(1)} %get-tuple-element.15.keep_ref, bf16[32,128]{1,0:T(8,128)(2,1)S(1)} %get-tuple-element.20.mate_self_ref, bf16[72,128]{1,0:T(8,128)(2,1)S(1)} %collective-permute-done.2.near_ref, ...), custom_call_target="tpu_custom_call" | custom-call | tf_op jit(solution)/shard_map/stat/pallas_call | solution.py:233
Async XLA Ops:
  0.0 1.7 %collective-permute-start = (bf16[4,4096]{1,0:T(4,128)(2,1)}, bf16[4,4096]{1,0:T(4,128)(2,1)S(1)}, u32[]{:S(2)}, u32[]{:S(2)}) collective-permute-start(bf16[4,4096]{1,0:T(4,128)(2,1)} %param.4), channel_id=1, source_target_pairs={{0,1},{1,0},{2,3},{3,2},{4,5},{5,4},{6,7},{7,6},{8,9},{9,8},{10,11... | collective-permute-start | bytes 98312 | tf_op jit(solution)/shard_map/ppermute | solution.py:187
  0.5 1.3 %collective-permute-start.1 = (bf16[2,4]{1,0:T(2,128)(2,1)}, bf16[2,4]{1,0:T(2,128)(2,1)S(1)}, u32[]{:S(2)}, u32[]{:S(2)}) collective-permute-start(bf16[2,4]{1,0:T(2,128)(2,1)} %pheno_hbm.1), channel_id=1, source_target_pairs={{0,1},{1,0},{2,3},{3,2},{4,5},{5,4},{6,7},{7,6},{8,9},{9,8},{10,11... | collective-permute-start | bytes 56 | tf_op jit(solution)/shard_map/ppermute | solution.py:188
  1.9 8.3 %collective-permute-start.3 = (bf16[72,128]{1,0:T(8,128)(2,1)S(1)}, bf16[72,128]{1,0:T(8,128)(2,1)S(1)}, u32[]{:S(2)}, u32[]{:S(2)}) collective-permute-start(bf16[72,128]{1,0:T(8,128)(2,1)S(1)} %get-tuple-element.22), channel_id=1, source_target_pairs={{0,2},{1,7},{2,0},{3,5},{4,6},{5,11},{6,4},{7,9},{8,10},{9,15},{10... | collective-permute-start | bytes 55304 | tf_op jit(solution)/shard_map/ppermute | solution.py:229
  4.6 5.6 %collective-permute-start.4 = (bf16[72,128]{1,0:T(8,128)(2,1)S(1)}, bf16[72,128]{1,0:T(8,128)(2,1)S(1)}, u32[]{:S(2)}, u32[]{:S(2)}) collective-permute-start(bf16[72,128]{1,0:T(8,128)(2,1)S(1)} %get-tuple-element.23), channel_id=1, source_target_pairs={{0,4},{1,11},{2,6},{3,9},{4,8},{5,15},{6,10},{7,13},{8,12},{9,3},{... | collective-permute-start | bytes 55304 | tf_op jit(solution)/shard_map/ppermute | solution.py:229
  6.2 4.7 %collective-permute-start.5 = (bf16[72,128]{1,0:T(8,128)(2,1)S(1)}, bf16[72,128]{1,0:T(8,128)(2,1)S(1)}, u32[]{:S(2)}, u32[]{:S(2)}) collective-permute-start(bf16[72,128]{1,0:T(8,128)(2,1)S(1)} %get-tuple-element.24), channel_id=1, source_target_pairs={{0,14},{1,9},{2,12},{3,11},{4,2},{5,13},{6,0},{7,15},{8,6},{9,1},{... | collective-permute-start | bytes 55304 | tf_op jit(solution)/shard_map/ppermute | solution.py:229
  8.2 3.8 %collective-permute-start.2 = (bf16[72,128]{1,0:T(8,128)(2,1)S(1)}, bf16[72,128]{1,0:T(8,128)(2,1)S(1)}, u32[]{:S(2)}, u32[]{:S(2)}) collective-permute-start(bf16[72,128]{1,0:T(8,128)(2,1)S(1)} %get-tuple-element.21), channel_id=1, source_target_pairs={{0,12},{1,13},{2,14},{3,15},{4,0},{5,1},{6,2},{7,3},{8,4},{9,5},{1... | collective-permute-start | bytes 55304 | tf_op jit(solution)/shard_map/ppermute | solution.py:229
  10.2 1.8 %collective-permute-start.6 = (bf16[72,128]{1,0:T(8,128)(2,1)S(1)}, bf16[72,128]{1,0:T(8,128)(2,1)S(1)}, u32[]{:S(2)}, u32[]{:S(2)}) collective-permute-start(bf16[72,128]{1,0:T(8,128)(2,1)S(1)} %collective-permute-done.3.refs_0_), channel_id=1, source_target_pairs={{0,1},{1,0},{2,3},{3,2},{4,5},{5,4},{6,7},{7,6},{8,9},{9,8},{10,11... | collective-permute-start | bytes 55304 | tf_op jit(solution)/shard_map/ppermute | solution.py:231
  10.2 1.8 %collective-permute-start.7 = (bf16[72,128]{1,0:T(8,128)(2,1)S(1)}, bf16[72,128]{1,0:T(8,128)(2,1)S(1)}, u32[]{:S(2)}, u32[]{:S(2)}) collective-permute-start(bf16[72,128]{1,0:T(8,128)(2,1)S(1)} %collective-permute-done.4.refs_1_), channel_id=1, source_target_pairs={{0,1},{1,0},{2,3},{3,2},{4,5},{5,4},{6,7},{7,6},{8,9},{9,8},{10,11... | collective-permute-start | bytes 55304 | tf_op jit(solution)/shard_map/ppermute | solution.py:231
  10.8 1.6 %collective-permute-start.8 = (bf16[72,128]{1,0:T(8,128)(2,1)S(1)}, bf16[72,128]{1,0:T(8,128)(2,1)S(1)}, u32[]{:S(2)}, u32[]{:S(2)}) collective-permute-start(bf16[72,128]{1,0:T(8,128)(2,1)S(1)} %collective-permute-done.5.refs_2_), channel_id=1, source_target_pairs={{0,1},{1,0},{2,3},{3,2},{4,5},{5,4},{6,7},{7,6},{8,9},{9,8},{10,11... | collective-permute-start | bytes 55304 | tf_op jit(solution)/shard_map/ppermute | solution.py:231

commit v17 on v15

--- a/solution.py
+++ b/solution.py
@@ -134,36 +134,36 @@
     geno_b = jnp.concatenate(by_samples(tile_b), axis=1)
     marg_b = jnp.sum(geno_b, axis=0, keepdims=True)
     centred = (geno_b - marg_b / count) * (samples**-0.5)
-    b_hi = centred.astype(jnp.bfloat16)
-    b_lo = (centred - b_hi.astype(jnp.float32)).astype(jnp.bfloat16)
-    b_both = jnp.concatenate([b_hi, b_lo], axis=0)
-
     wave = wave_ref[...].astype(jnp.float32)
     for ref in (*own_refs, *mate_refs, near_ref):
         wave = wave + ref[2 * BLOCK :, :].astype(jnp.float32)
     tiles = 2 * samples // LANES
+    stats = out_ref.shape[0]
     yrows = [
-        jnp.concatenate([wave[k * tiles + t : k * tiles + t + 1] for t in range(tiles)], axis=1)
-        for k in range(out_ref.shape[0])
+        jnp.concatenate([wave[k * tiles + t : k * tiles + t + 1] for t in range(tiles)], axis=1) for k in range(stats)
     ]
-    yall = jnp.concatenate(yrows, axis=0)
-    tail = jnp.dot(yall.astype(jnp.bfloat16), b_both, preferred_element_type=jnp.float32) / count
-    c_hi = tail.astype(jnp.bfloat16).astype(jnp.float32)
-    c_lo = tail - c_hi
-
+    yrows.append(jnp.zeros((8 * -(-stats // 8) - stats, 2 * samples), jnp.float32))
+    ycolumns = jnp.concatenate(yrows, axis=0).T
+    rights = []
+    for k in range(stats):
+        products = ycolumns[:samples, k : k + 1] * centred
+        products = products - jnp.sum(products, axis=0, keepdims=True) / count
+        high = products.astype(jnp.bfloat16)
+        low = (products - high.astype(jnp.float32)).astype(jnp.bfloat16)
+        rights.append(jnp.concatenate([high, low], axis=0))
     rows = []
     for geno_a in by_samples(panel_a[:, : TILE // 2]) + by_samples(panel_a[:, TILE // 2 :]):
         rows.append(jnp.concatenate([geno_a, geno_a], axis=0).astype(jnp.bfloat16).T)
-    rows = jnp.concatenate(rows, axis=0)
-    minus = -rows
+    left = jnp.concatenate(rows, axis=0)
+    half = out_ref.shape[2]
     copies = []
-    for k, yrow in enumerate(yrows):
-        tails = [jnp.broadcast_to(c[k : k + 1], (TILE, c.shape[1])).astype(jnp.bfloat16) for c in (c_hi, c_lo)]
-        right = jnp.concatenate([b_both] + [t for t in tails for _ in range(samples // TILE)], axis=0)
-        left = jnp.concatenate([rows * yrow.astype(jnp.bfloat16), minus], axis=1)
-        out_ref[k] = jnp.dot(left, right, preferred_element_type=jnp.float32).astype(out_ref.dtype)
-        copies.append(pltpu.make_async_copy(out_ref.at[k], out_hbm.at[0, k], sems.at[k]))
-        copies[-1].start()
+    for k in range(0, stats, 2):
+        right = jnp.concatenate(rights[k : k + 2], axis=1)
+        both = jnp.dot(left, right, preferred_element_type=jnp.float32).astype(out_ref.dtype)
+        for j in range(len(rights[k : k + 2])):
+            out_ref[k + j] = both[:, j * half : (j + 1) * half]
+            copies.append(pltpu.make_async_copy(out_ref.at[k + j], out_hbm.at[0, k + j], sems.at[k + j]))
+            copies[-1].start()
     for copy in copies:
         copy.wait()
 

time: 14.2 us -> 14.2 us (level)
  no operation moved by 1% of the time
where the time goes in v17:
time: 14.2 us; the launch traced here: 14 us
  starting transfers between devices  9.33 us (66%)
  Pallas kernels  2.53 us (18%)
  waiting for transfers between devices  2.11 us (15%)
    ppermute x4, starting transfers between devices, on_device(): arrived.append(lax.ppermute(message, AXES, route))  8.12 us
    pallas_call x1, Pallas kernels, on_device(): pl.pallas_call(functools.partial(stat_kernel, pair_count, samps), out_sha...  1.48 us
    ppermute x4, waiting for transfers between devices, on_device(): arrived.append(lax.ppermute(message, AXES, route))  1 us
    pallas_call x1, Pallas kernels, on_device(): pl.pallas_call(functools.partial(pick_kernel, pair_count, samps), out_sha...  0.91 us
    ppermute x3, waiting for transfers between devices, on_device(): mates = [lax.ppermute(a, 'samp', swap) for a in far]  0.84 us
    ppermute x3, starting transfers between devices, on_device(): mates = [lax.ppermute(a, 'samp', swap) for a in far]  0.71 us
    ppermute x1, starting transfers between devices, on_device(): mate_dosage = lax.ppermute(dosage, 'samp', swap)  0.45 us
  transfers between devices with their start and end apart: 9, of which 4 were waited for; matrix products, arithmetic and copies ran while one was open for 0% of the time, Pallas kernels for 7%

profile of v17, /device:TPU:0, one launch (start us, length us, event | category | flops | bytes accessed | tf_op | source)
XLA Modules:
  0.0 14.0 jit_solution(9259371152928596589)
XLA Ops:
  0.0 0.5 %collective-permute-start = (bf16[4,4096]{1,0:T(4,128)(2,1)}, bf16[4,4096]{1,0:T(4,128)(2,1)S(1)}, u32[]{:S(2)}, u32[]{:S(2)}) collective-permute-start(bf16[4,4096]{1,0:T(4,128)(2,1)} %param.4), channel_id=1, source_target_pairs={{0,1},{1,0},{2,3},{3,2},{4,5},{5,4},{6,7},{7,6},{8,9},{9,8},{10,11... | collective-permute-start | bytes 98312 | tf_op jit(solution)/shard_map/ppermute | solution.py:187
  0.5 0.1 collective-permute-start.1
  0.5 0.9 %pick.1 = (bf16[160,128]{1,0:T(8,128)(2,1)S(1)}, bf16[160,128]{1,0:T(8,128)(2,1)S(1)}, bf16[8,128]{1,0:T(8,128)(2,1)S(1)}, s32[2,64]{1,0:T(2,128)S(1)}) custom-call(s32[2,8]{1,0:T(2,128)} %bitcast.13, bf16[128,128]{1,0:T(8,128)(2,1)} %bitcast.12, bf16[2,4]{1,0:T(2,128)(2,1)} %pheno_hbm.1, s32[2,64]{1,0:T(2,128)} %perms_hbm.1), custom_call_target="tpu_custom_call" | custom-call | bytes 163840 | tf_op jit(solution)/shard_map/pick/pallas_call | solution.py:191
  1.4 0.3 %collective-permute-done.1.pheno_ref = bf16[2,4]{1,0:T(2,128)(2,1)S(1)} collective-permute-done((bf16[2,4]{1,0:T(2,128)(2,1)}, bf16[2,4]{1,0:T(2,128)(2,1)S(1)}, u32[]{:S(2)}, u32[]{:S(2)}) %collective-permute-start.1) | collective-permute-done | bytes 48 | tf_op jit(solution)/shard_map/ppermute | solution.py:188
  1.7 0.0 collective-permute-done
  1.7 0.1 %join.1 = (bf16[32,128]{1,0:T(8,128)(2,1)S(1)}, bf16[8,128]{1,0:T(8,128)(2,1)S(1)}, bf16[72,128]{1,0:T(8,128)(2,1)S(1)}, bf16[72,128]{1,0:T(8,128)(2,1)S(1)}, bf...) custom-call(bf16[160,128]{1,0:T(8,128)(2,1)S(1)} %get-tuple-element.15.keep_ref, ...), custom_call_target="tpu_custom_call" | custom-call | tf_op jit(solution)/shard_map/join/pallas_call | solution.py:213
  1.9 2.8 %collective-permute-start.3 = (bf16[72,128]{1,0:T(8,128)(2,1)S(1)}, bf16[72,128]{1,0:T(8,128)(2,1)S(1)}, u32[]{:S(2)}, u32[]{:S(2)}) collective-permute-start(bf16[72,128]{1,0:T(8,128)(2,1)S(1)} %get-tuple-element.22), channel_id=1, source_target_pairs={{0,4},{1,9},{2,6},{3,11},{4,8},{5,13},{6,10},{7,15},{8,12},{9,1},{... | collective-permute-start | bytes 55304 | tf_op jit(solution)/shard_map/ppermute | solution.py:229
  4.7 2.5 %collective-permute-start.4 = (bf16[72,128]{1,0:T(8,128)(2,1)S(1)}, bf16[72,128]{1,0:T(8,128)(2,1)S(1)}, u32[]{:S(2)}, u32[]{:S(2)}) collective-permute-start(bf16[72,128]{1,0:T(8,128)(2,1)S(1)} %get-tuple-element.23), channel_id=1, source_target_pairs={{0,6},{1,11},{2,4},{3,9},{4,10},{5,15},{6,8},{7,13},{8,14},{9,3},{... | collective-permute-start | bytes 55304 | tf_op jit(solution)/shard_map/ppermute | solution.py:229
  7.2 0.5 %collective-permute-start.5 = (bf16[72,128]{1,0:T(8,128)(2,1)S(1)}, bf16[72,128]{1,0:T(8,128)(2,1)S(1)}, u32[]{:S(2)}, u32[]{:S(2)}) collective-permute-start(bf16[72,128]{1,0:T(8,128)(2,1)S(1)} %get-tuple-element.24), channel_id=1, source_target_pairs={{0,2},{1,15},{2,0},{3,13},{4,6},{5,3},{6,4},{7,1},{8,10},{9,7},{10... | collective-permute-start | bytes 55304 | tf_op jit(solution)/shard_map/ppermute | solution.py:229
  7.7 2.2 %collective-permute-start.2 = (bf16[72,128]{1,0:T(8,128)(2,1)S(1)}, bf16[72,128]{1,0:T(8,128)(2,1)S(1)}, u32[]{:S(2)}, u32[]{:S(2)}) collective-permute-start(bf16[72,128]{1,0:T(8,128)(2,1)S(1)} %get-tuple-element.21), channel_id=1, source_target_pairs={{0,12},{1,13},{2,14},{3,15},{4,0},{5,1},{6,2},{7,3},{8,4},{9,5},{1... | collective-permute-start | bytes 55304 | tf_op jit(solution)/shard_map/ppermute | solution.py:229
  10.0 0.0 collective-permute-done.3.refs_0_
  10.0 0.2 %collective-permute-start.6 = (bf16[72,128]{1,0:T(8,128)(2,1)S(1)}, bf16[72,128]{1,0:T(8,128)(2,1)S(1)}, u32[]{:S(2)}, u32[]{:S(2)}) collective-permute-start(bf16[72,128]{1,0:T(8,128)(2,1)S(1)} %collective-permute-done.3.refs_0_), channel_id=1, source_target_pairs={{0,1},{1,0},{2,3},{3,2},{4,5},{5,4},{6,7},{7,6},{8,9},{9,8},{10,11... | collective-permute-start | bytes 55304 | tf_op jit(solution)/shard_map/ppermute | solution.py:231
  10.2 1.0 %collective-permute-done.4.refs_1_ = bf16[72,128]{1,0:T(8,128)(2,1)S(1)} collective-permute-done((bf16[72,128]{1,0:T(8,128)(2,1)S(1)}, bf16[72,128]{1,0:T(8,128)(2,1)S(1)}, u32[]{:S(2)}, u32[]{:S(2)}) %collective-permute-start.4) | collective-permute-done | bytes 18464 | tf_op jit(solution)/shard_map/ppermute | solution.py:229
  11.2 0.0 collective-permute-start.7
  11.2 0.0 collective-permute-done.5.refs_2_
  11.2 0.5 %collective-permute-start.8 = (bf16[72,128]{1,0:T(8,128)(2,1)S(1)}, bf16[72,128]{1,0:T(8,128)(2,1)S(1)}, u32[]{:S(2)}, u32[]{:S(2)}) collective-permute-start(bf16[72,128]{1,0:T(8,128)(2,1)S(1)} %collective-permute-done.5.refs_2_), channel_id=1, source_target_pairs={{0,1},{1,0},{2,3},{3,2},{4,5},{5,4},{6,7},{7,6},{8,9},{9,8},{10,11... | collective-permute-start | bytes 55304 | tf_op jit(solution)/shard_map/ppermute | solution.py:231
  11.7 0.0 collective-permute-done.2.near_ref
  11.7 0.0 collective-permute-done.6.refs_3_
  11.7 0.7 %collective-permute-done.7.refs_4_ = bf16[72,128]{1,0:T(8,128)(2,1)S(1)} collective-permute-done((bf16[72,128]{1,0:T(8,128)(2,1)S(1)}, bf16[72,128]{1,0:T(8,128)(2,1)S(1)}, u32[]{:S(2)}, u32[]{:S(2)}) %collective-permute-start.7) | collective-permute-done | bytes 18464 | tf_op jit(solution)/shard_map/ppermute | solution.py:231
  12.4 0.2 %collective-permute-done.8.refs_5_ = bf16[72,128]{1,0:T(8,128)(2,1)S(1)} collective-permute-done((bf16[72,128]{1,0:T(8,128)(2,1)S(1)}, bf16[72,128]{1,0:T(8,128)(2,1)S(1)}, u32[]{:S(2)}, u32[]{:S(2)}) %collective-permute-start.8) | collective-permute-done | bytes 18464 | tf_op jit(solution)/shard_map/ppermute | solution.py:231
  12.5 1.5 %stat.1 = bf16[1,4,512,256]{3,2,1,0:T(8,128)(2,1)} custom-call(bf16[8,128]{1,0:T(8,128)(2,1)S(1)} %get-tuple-element.19.wave_ref, bf16[160,128]{1,0:T(8,128)(2,1)S(1)} %get-tuple-element.15.keep_ref, bf16[32,128]{1,0:T(8,128)(2,1)S(1)} %get-tuple-element.20.mate_self_ref, bf16[72,128]{1,0:T(8,128)(2,1)S(1)} %collective-permute-done.2.near_ref, ...), custom_call_target="tpu_custom_call" | custom-call | tf_op jit(solution)/shard_map/stat/pallas_call | solution.py:233
Async XLA Ops:
  0.0 1.7 %collective-permute-start = (bf16[4,4096]{1,0:T(4,128)(2,1)}, bf16[4,4096]{1,0:T(4,128)(2,1)S(1)}, u32[]{:S(2)}, u32[]{:S(2)}) collective-permute-start(bf16[4,4096]{1,0:T(4,128)(2,1)} %param.4), channel_id=1, source_target_pairs={{0,1},{1,0},{2,3},{3,2},{4,5},{5,4},{6,7},{7,6},{8,9},{9,8},{10,11... | collective-permute-start | bytes 98312 | tf_op jit(solution)/shard_map/ppermute | solution.py:187
  0.5 1.3 %collective-permute-start.1 = (bf16[2,4]{1,0:T(2,128)(2,1)}, bf16[2,4]{1,0:T(2,128)(2,1)S(1)}, u32[]{:S(2)}, u32[]{:S(2)}) collective-permute-start(bf16[2,4]{1,0:T(2,128)(2,1)} %pheno_hbm.1), channel_id=1, source_target_pairs={{0,1},{1,0},{2,3},{3,2},{4,5},{5,4},{6,7},{7,6},{8,9},{9,8},{10,11... | collective-permute-start | bytes 56 | tf_op jit(solution)/shard_map/ppermute | solution.py:188
  1.9 8.1 %collective-permute-start.3 = (bf16[72,128]{1,0:T(8,128)(2,1)S(1)}, bf16[72,128]{1,0:T(8,128)(2,1)S(1)}, u32[]{:S(2)}, u32[]{:S(2)}) collective-permute-start(bf16[72,128]{1,0:T(8,128)(2,1)S(1)} %get-tuple-element.22), channel_id=1, source_target_pairs={{0,4},{1,9},{2,6},{3,11},{4,8},{5,13},{6,10},{7,15},{8,12},{9,1},{... | collective-permute-start | bytes 55304 | tf_op jit(solution)/shard_map/ppermute | solution.py:229
  4.7 6.5 %collective-permute-start.4 = (bf16[72,128]{1,0:T(8,128)(2,1)S(1)}, bf16[72,128]{1,0:T(8,128)(2,1)S(1)}, u32[]{:S(2)}, u32[]{:S(2)}) collective-permute-start(bf16[72,128]{1,0:T(8,128)(2,1)S(1)} %get-tuple-element.23), channel_id=1, source_target_pairs={{0,6},{1,11},{2,4},{3,9},{4,10},{5,15},{6,8},{7,13},{8,14},{9,3},{... | collective-permute-start | bytes 55304 | tf_op jit(solution)/shard_map/ppermute | solution.py:229
  7.2 4.0 %collective-permute-start.5 = (bf16[72,128]{1,0:T(8,128)(2,1)S(1)}, bf16[72,128]{1,0:T(8,128)(2,1)S(1)}, u32[]{:S(2)}, u32[]{:S(2)}) collective-permute-start(bf16[72,128]{1,0:T(8,128)(2,1)S(1)} %get-tuple-element.24), channel_id=1, source_target_pairs={{0,2},{1,15},{2,0},{3,13},{4,6},{5,3},{6,4},{7,1},{8,10},{9,7},{10... | collective-permute-start | bytes 55304 | tf_op jit(solution)/shard_map/ppermute | solution.py:229
  7.7 4.0 %collective-permute-start.2 = (bf16[72,128]{1,0:T(8,128)(2,1)S(1)}, bf16[72,128]{1,0:T(8,128)(2,1)S(1)}, u32[]{:S(2)}, u32[]{:S(2)}) collective-permute-start(bf16[72,128]{1,0:T(8,128)(2,1)S(1)} %get-tuple-element.21), channel_id=1, source_target_pairs={{0,12},{1,13},{2,14},{3,15},{4,0},{5,1},{6,2},{7,3},{8,4},{9,5},{1... | collective-permute-start | bytes 55304 | tf_op jit(solution)/shard_map/ppermute | solution.py:229
  10.0 1.7 %collective-permute-start.6 = (bf16[72,128]{1,0:T(8,128)(2,1)S(1)}, bf16[72,128]{1,0:T(8,128)(2,1)S(1)}, u32[]{:S(2)}, u32[]{:S(2)}) collective-permute-start(bf16[72,128]{1,0:T(8,128)(2,1)S(1)} %collective-permute-done.3.refs_0_), channel_id=1, source_target_pairs={{0,1},{1,0},{2,3},{3,2},{4,5},{5,4},{6,7},{7,6},{8,9},{9,8},{10,11... | collective-permute-start | bytes 55304 | tf_op jit(solution)/shard_map/ppermute | solution.py:231
  11.2 1.2 %collective-permute-start.7 = (bf16[72,128]{1,0:T(8,128)(2,1)S(1)}, bf16[72,128]{1,0:T(8,128)(2,1)S(1)}, u32[]{:S(2)}, u32[]{:S(2)}) collective-permute-start(bf16[72,128]{1,0:T(8,128)(2,1)S(1)} %collective-permute-done.4.refs_1_), channel_id=1, source_target_pairs={{0,1},{1,0},{2,3},{3,2},{4,5},{5,4},{6,7},{7,6},{8,9},{9,8},{10,11... | collective-permute-start | bytes 55304 | tf_op jit(solution)/shard_map/ppermute | solution.py:231
  11.2 1.4 %collective-permute-start.8 = (bf16[72,128]{1,0:T(8,128)(2,1)S(1)}, bf16[72,128]{1,0:T(8,128)(2,1)S(1)}, u32[]{:S(2)}, u32[]{:S(2)}) collective-permute-start(bf16[72,128]{1,0:T(8,128)(2,1)S(1)} %collective-permute-done.5.refs_2_), channel_id=1, source_target_pairs={{0,1},{1,0},{2,3},{3,2},{4,5},{5,4},{6,7},{7,6},{8,9},{9,8},{10,11... | collective-permute-start | bytes 55304 | tf_op jit(solution)/shard_map/ppermute | solution.py:231

commit v18 on v17

--- a/solution.py
+++ b/solution.py
@@ -151,19 +151,17 @@
         high = products.astype(jnp.bfloat16)
         low = (products - high.astype(jnp.float32)).astype(jnp.bfloat16)
         rights.append(jnp.concatenate([high, low], axis=0))
-    rows = []
-    for geno_a in by_samples(panel_a[:, : TILE // 2]) + by_samples(panel_a[:, TILE // 2 :]):
-        rows.append(jnp.concatenate([geno_a, geno_a], axis=0).astype(jnp.bfloat16).T)
-    left = jnp.concatenate(rows, axis=0)
+    right = jnp.concatenate(rights, axis=1)
     half = out_ref.shape[2]
     copies = []
-    for k in range(0, stats, 2):
-        right = jnp.concatenate(rights[k : k + 2], axis=1)
-        both = jnp.dot(left, right, preferred_element_type=jnp.float32).astype(out_ref.dtype)
-        for j in range(len(rights[k : k + 2])):
-            out_ref[k + j] = both[:, j * half : (j + 1) * half]
-            copies.append(pltpu.make_async_copy(out_ref.at[k + j], out_hbm.at[0, k + j], sems.at[k + j]))
-            copies[-1].start()
+    for q, geno_a in enumerate(by_samples(panel_a[:, : TILE // 2]) + by_samples(panel_a[:, TILE // 2 :])):
+        left = jnp.concatenate([geno_a, geno_a], axis=0).astype(jnp.bfloat16).T
+        piece = slice(q * LANES, (q + 1) * LANES)
+        for k in range(stats):
+            part = jnp.dot(left, right[:, k * half : (k + 1) * half], preferred_element_type=jnp.float32)
+            out_ref[k, piece, :] = part.astype(out_ref.dtype)
+        copies.append(pltpu.make_async_copy(out_ref.at[:, piece], out_hbm.at[0, :, piece], sems.at[q]))
+        copies[-1].start()
     for copy in copies:
         copy.wait()
 
@@ -238,7 +236,7 @@
         scratch_shapes=[
             pltpu.VMEM((pair_count * samps, BLOCK, LANES), dosage.dtype),
             pltpu.VMEM((stats, PANEL, half), jnp.bfloat16),
-            pltpu.SemaphoreType.DMA((stats,)),
+            pltpu.SemaphoreType.DMA((PANEL // LANES,)),
         ],
         compiler_params=pltpu.CompilerParams(vmem_limit_bytes=48 * 1024 * 1024),
         name="stat",

time: 14.2 us -> 14.1 us (level)
  no operation moved by 1% of the time
where the time goes in v18:
time: 14.1 us; the launch traced here: 13.9 us
  starting transfers between devices  9.33 us (66%)
  Pallas kernels  2.48 us (18%)
  waiting for transfers between devices  2.11 us (15%)
    ppermute x4, starting transfers between devices, on_device(): arrived.append(lax.ppermute(message, AXES, route))  8.12 us
    pallas_call x1, Pallas kernels, on_device(): pl.pallas_call(functools.partial(stat_kernel, pair_count, samps), out_sha...  1.42 us
    ppermute x4, waiting for transfers between devices, on_device(): arrived.append(lax.ppermute(message, AXES, route))  1 us
    pallas_call x1, Pallas kernels, on_device(): pl.pallas_call(functools.partial(pick_kernel, pair_count, samps), out_sha...  0.91 us
    ppermute x3, waiting for transfers between devices, on_device(): mates = [lax.ppermute(a, 'samp', swap) for a in far]  0.84 us
    ppermute x3, starting transfers between devices, on_device(): mates = [lax.ppermute(a, 'samp', swap) for a in far]  0.71 us
    ppermute x1, starting transfers between devices, on_device(): mate_dosage = lax.ppermute(dosage, 'samp', swap)  0.45 us
  transfers between devices with their start and end apart: 9, of which 4 were waited for; matrix products, arithmetic and copies ran while one was open for 0% of the time, Pallas kernels for 7%

profile of v18, /device:TPU:0, one launch (start us, length us, event | category | flops | bytes accessed | tf_op | source)
XLA Modules:
  0.0 13.9 jit_solution(10444815883958616100)
XLA Ops:
  0.0 0.5 %collective-permute-start = (bf16[4,4096]{1,0:T(4,128)(2,1)}, bf16[4,4096]{1,0:T(4,128)(2,1)S(1)}, u32[]{:S(2)}, u32[]{:S(2)}) collective-permute-start(bf16[4,4096]{1,0:T(4,128)(2,1)} %param.4), channel_id=1, source_target_pairs={{0,1},{1,0},{2,3},{3,2},{4,5},{5,4},{6,7},{7,6},{8,9},{9,8},{10,11... | collective-permute-start | bytes 98312 | tf_op jit(solution)/shard_map/ppermute | solution.py:185
  0.5 0.1 collective-permute-start.1
  0.5 0.9 %pick.1 = (bf16[160,128]{1,0:T(8,128)(2,1)S(1)}, bf16[160,128]{1,0:T(8,128)(2,1)S(1)}, bf16[8,128]{1,0:T(8,128)(2,1)S(1)}, s32[2,64]{1,0:T(2,128)S(1)}) custom-call(s32[2,8]{1,0:T(2,128)} %bitcast.13, bf16[128,128]{1,0:T(8,128)(2,1)} %bitcast.12, bf16[2,4]{1,0:T(2,128)(2,1)} %pheno_hbm.1, s32[2,64]{1,0:T(2,128)} %perms_hbm.1), custom_call_target="tpu_custom_call" | custom-call | bytes 163840 | tf_op jit(solution)/shard_map/pick/pallas_call | solution.py:189
  1.4 0.3 %collective-permute-done.1.pheno_ref = bf16[2,4]{1,0:T(2,128)(2,1)S(1)} collective-permute-done((bf16[2,4]{1,0:T(2,128)(2,1)}, bf16[2,4]{1,0:T(2,128)(2,1)S(1)}, u32[]{:S(2)}, u32[]{:S(2)}) %collective-permute-start.1) | collective-permute-done | bytes 48 | tf_op jit(solution)/shard_map/ppermute | solution.py:186
  1.7 0.0 collective-permute-done
  1.7 0.1 %join.1 = (bf16[32,128]{1,0:T(8,128)(2,1)S(1)}, bf16[8,128]{1,0:T(8,128)(2,1)S(1)}, bf16[72,128]{1,0:T(8,128)(2,1)S(1)}, bf16[72,128]{1,0:T(8,128)(2,1)S(1)}, bf...) custom-call(bf16[160,128]{1,0:T(8,128)(2,1)S(1)} %get-tuple-element.15.keep_ref, ...), custom_call_target="tpu_custom_call" | custom-call | tf_op jit(solution)/shard_map/join/pallas_call | solution.py:211
  1.9 2.8 %collective-permute-start.3 = (bf16[72,128]{1,0:T(8,128)(2,1)S(1)}, bf16[72,128]{1,0:T(8,128)(2,1)S(1)}, u32[]{:S(2)}, u32[]{:S(2)}) collective-permute-start(bf16[72,128]{1,0:T(8,128)(2,1)S(1)} %get-tuple-element.22), channel_id=1, source_target_pairs={{0,4},{1,9},{2,6},{3,11},{4,8},{5,13},{6,10},{7,15},{8,12},{9,1},{... | collective-permute-start | bytes 55304 | tf_op jit(solution)/shard_map/ppermute | solution.py:227
  4.7 2.5 %collective-permute-start.4 = (bf16[72,128]{1,0:T(8,128)(2,1)S(1)}, bf16[72,128]{1,0:T(8,128)(2,1)S(1)}, u32[]{:S(2)}, u32[]{:S(2)}) collective-permute-start(bf16[72,128]{1,0:T(8,128)(2,1)S(1)} %get-tuple-element.23), channel_id=1, source_target_pairs={{0,6},{1,11},{2,4},{3,9},{4,10},{5,15},{6,8},{7,13},{8,14},{9,3},{... | collective-permute-start | bytes 55304 | tf_op jit(solution)/shard_map/ppermute | solution.py:227
  7.2 0.5 %collective-permute-start.5 = (bf16[72,128]{1,0:T(8,128)(2,1)S(1)}, bf16[72,128]{1,0:T(8,128)(2,1)S(1)}, u32[]{:S(2)}, u32[]{:S(2)}) collective-permute-start(bf16[72,128]{1,0:T(8,128)(2,1)S(1)} %get-tuple-element.24), channel_id=1, source_target_pairs={{0,2},{1,15},{2,0},{3,13},{4,6},{5,3},{6,4},{7,1},{8,10},{9,7},{10... | collective-permute-start | bytes 55304 | tf_op jit(solution)/shard_map/ppermute | solution.py:227
  7.7 2.2 %collective-permute-start.2 = (bf16[72,128]{1,0:T(8,128)(2,1)S(1)}, bf16[72,128]{1,0:T(8,128)(2,1)S(1)}, u32[]{:S(2)}, u32[]{:S(2)}) collective-permute-start(bf16[72,128]{1,0:T(8,128)(2,1)S(1)} %get-tuple-element.21), channel_id=1, source_target_pairs={{0,12},{1,13},{2,14},{3,15},{4,0},{5,1},{6,2},{7,3},{8,4},{9,5},{1... | collective-permute-start | bytes 55304 | tf_op jit(solution)/shard_map/ppermute | solution.py:227
  10.0 0.0 collective-permute-done.3.refs_0_
  10.0 0.2 %collective-permute-start.6 = (bf16[72,128]{1,0:T(8,128)(2,1)S(1)}, bf16[72,128]{1,0:T(8,128)(2,1)S(1)}, u32[]{:S(2)}, u32[]{:S(2)}) collective-permute-start(bf16[72,128]{1,0:T(8,128)(2,1)S(1)} %collective-permute-done.3.refs_0_), channel_id=1, source_target_pairs={{0,1},{1,0},{2,3},{3,2},{4,5},{5,4},{6,7},{7,6},{8,9},{9,8},{10,11... | collective-permute-start | bytes 55304 | tf_op jit(solution)/shard_map/ppermute | solution.py:229
  10.2 1.0 %collective-permute-done.4.refs_1_ = bf16[72,128]{1,0:T(8,128)(2,1)S(1)} collective-permute-done((bf16[72,128]{1,0:T(8,128)(2,1)S(1)}, bf16[72,128]{1,0:T(8,128)(2,1)S(1)}, u32[]{:S(2)}, u32[]{:S(2)}) %collective-permute-start.4) | collective-permute-done | bytes 18464 | tf_op jit(solution)/shard_map/ppermute | solution.py:227
  11.2 0.0 collective-permute-start.7
  11.2 0.0 collective-permute-done.5.refs_2_
  11.2 0.5 %collective-permute-start.8 = (bf16[72,128]{1,0:T(8,128)(2,1)S(1)}, bf16[72,128]{1,0:T(8,128)(2,1)S(1)}, u32[]{:S(2)}, u32[]{:S(2)}) collective-permute-start(bf16[72,128]{1,0:T(8,128)(2,1)S(1)} %collective-permute-done.5.refs_2_), channel_id=1, source_target_pairs={{0,1},{1,0},{2,3},{3,2},{4,5},{5,4},{6,7},{7,6},{8,9},{9,8},{10,11... | collective-permute-start | bytes 55304 | tf_op jit(solution)/shard_map/ppermute | solution.py:229
  11.7 0.0 collective-permute-done.2.near_ref
  11.7 0.0 collective-permute-done.6.refs_3_
  11.7 0.7 %collective-permute-done.7.refs_4_ = bf16[72,128]{1,0:T(8,128)(2,1)S(1)} collective-permute-done((bf16[72,128]{1,0:T(8,128)(2,1)S(1)}, bf16[72,128]{1,0:T(8,128)(2,1)S(1)}, u32[]{:S(2)}, u32[]{:S(2)}) %collective-permute-start.7) | collective-permute-done | bytes 18464 | tf_op jit(solution)/shard_map/ppermute | solution.py:229
  12.4 0.2 %collective-permute-done.8.refs_5_ = bf16[72,128]{1,0:T(8,128)(2,1)S(1)} collective-permute-done((bf16[72,128]{1,0:T(8,128)(2,1)S(1)}, bf16[72,128]{1,0:T(8,128)(2,1)S(1)}, u32[]{:S(2)}, u32[]{:S(2)}) %collective-permute-start.8) | collective-permute-done | bytes 18464 | tf_op jit(solution)/shard_map/ppermute | solution.py:229
  12.5 1.4 %stat.1 = bf16[1,4,512,256]{3,2,1,0:T(8,128)(2,1)} custom-call(bf16[8,128]{1,0:T(8,128)(2,1)S(1)} %get-tuple-element.19.wave_ref, bf16[160,128]{1,0:T(8,128)(2,1)S(1)} %get-tuple-element.15.keep_ref, bf16[32,128]{1,0:T(8,128)(2,1)S(1)} %get-tuple-element.20.mate_self_ref, bf16[72,128]{1,0:T(8,128)(2,1)S(1)} %collective-permute-done.2.near_ref, ...), custom_call_target="tpu_custom_call" | custom-call | tf_op jit(solution)/shard_map/stat/pallas_call | solution.py:231
Async XLA Ops:
  0.0 1.7 %collective-permute-start = (bf16[4,4096]{1,0:T(4,128)(2,1)}, bf16[4,4096]{1,0:T(4,128)(2,1)S(1)}, u32[]{:S(2)}, u32[]{:S(2)}) collective-permute-start(bf16[4,4096]{1,0:T(4,128)(2,1)} %param.4), channel_id=1, source_target_pairs={{0,1},{1,0},{2,3},{3,2},{4,5},{5,4},{6,7},{7,6},{8,9},{9,8},{10,11... | collective-permute-start | bytes 98312 | tf_op jit(solution)/shard_map/ppermute | solution.py:185
  0.5 1.3 %collective-permute-start.1 = (bf16[2,4]{1,0:T(2,128)(2,1)}, bf16[2,4]{1,0:T(2,128)(2,1)S(1)}, u32[]{:S(2)}, u32[]{:S(2)}) collective-permute-start(bf16[2,4]{1,0:T(2,128)(2,1)} %pheno_hbm.1), channel_id=1, source_target_pairs={{0,1},{1,0},{2,3},{3,2},{4,5},{5,4},{6,7},{7,6},{8,9},{9,8},{10,11... | collective-permute-start | bytes 56 | tf_op jit(solution)/shard_map/ppermute | solution.py:186
  1.9 8.1 %collective-permute-start.3 = (bf16[72,128]{1,0:T(8,128)(2,1)S(1)}, bf16[72,128]{1,0:T(8,128)(2,1)S(1)}, u32[]{:S(2)}, u32[]{:S(2)}) collective-permute-start(bf16[72,128]{1,0:T(8,128)(2,1)S(1)} %get-tuple-element.22), channel_id=1, source_target_pairs={{0,4},{1,9},{2,6},{3,11},{4,8},{5,13},{6,10},{7,15},{8,12},{9,1},{... | collective-permute-start | bytes 55304 | tf_op jit(solution)/shard_map/ppermute | solution.py:227
  4.7 6.5 %collective-permute-start.4 = (bf16[72,128]{1,0:T(8,128)(2,1)S(1)}, bf16[72,128]{1,0:T(8,128)(2,1)S(1)}, u32[]{:S(2)}, u32[]{:S(2)}) collective-permute-start(bf16[72,128]{1,0:T(8,128)(2,1)S(1)} %get-tuple-element.23), channel_id=1, source_target_pairs={{0,6},{1,11},{2,4},{3,9},{4,10},{5,15},{6,8},{7,13},{8,14},{9,3},{... | collective-permute-start | bytes 55304 | tf_op jit(solution)/shard_map/ppermute | solution.py:227
  7.2 4.0 %collective-permute-start.5 = (bf16[72,128]{1,0:T(8,128)(2,1)S(1)}, bf16[72,128]{1,0:T(8,128)(2,1)S(1)}, u32[]{:S(2)}, u32[]{:S(2)}) collective-permute-start(bf16[72,128]{1,0:T(8,128)(2,1)S(1)} %get-tuple-element.24), channel_id=1, source_target_pairs={{0,2},{1,15},{2,0},{3,13},{4,6},{5,3},{6,4},{7,1},{8,10},{9,7},{10... | collective-permute-start | bytes 55304 | tf_op jit(solution)/shard_map/ppermute | solution.py:227
  7.7 4.0 %collective-permute-start.2 = (bf16[72,128]{1,0:T(8,128)(2,1)S(1)}, bf16[72,128]{1,0:T(8,128)(2,1)S(1)}, u32[]{:S(2)}, u32[]{:S(2)}) collective-permute-start(bf16[72,128]{1,0:T(8,128)(2,1)S(1)} %get-tuple-element.21), channel_id=1, source_target_pairs={{0,12},{1,13},{2,14},{3,15},{4,0},{5,1},{6,2},{7,3},{8,4},{9,5},{1... | collective-permute-start | bytes 55304 | tf_op jit(solution)/shard_map/ppermute | solution.py:227
  10.0 1.7 %collective-permute-start.6 = (bf16[72,128]{1,0:T(8,128)(2,1)S(1)}, bf16[72,128]{1,0:T(8,128)(2,1)S(1)}, u32[]{:S(2)}, u32[]{:S(2)}) collective-permute-start(bf16[72,128]{1,0:T(8,128)(2,1)S(1)} %collective-permute-done.3.refs_0_), channel_id=1, source_target_pairs={{0,1},{1,0},{2,3},{3,2},{4,5},{5,4},{6,7},{7,6},{8,9},{9,8},{10,11... | collective-permute-start | bytes 55304 | tf_op jit(solution)/shard_map/ppermute | solution.py:229
  11.2 1.2 %collective-permute-start.7 = (bf16[72,128]{1,0:T(8,128)(2,1)S(1)}, bf16[72,128]{1,0:T(8,128)(2,1)S(1)}, u32[]{:S(2)}, u32[]{:S(2)}) collective-permute-start(bf16[72,128]{1,0:T(8,128)(2,1)S(1)} %collective-permute-done.4.refs_1_), channel_id=1, source_target_pairs={{0,1},{1,0},{2,3},{3,2},{4,5},{5,4},{6,7},{7,6},{8,9},{9,8},{10,11... | collective-permute-start | bytes 55304 | tf_op jit(solution)/shard_map/ppermute | solution.py:229
  11.2 1.4 %collective-permute-start.8 = (bf16[72,128]{1,0:T(8,128)(2,1)S(1)}, bf16[72,128]{1,0:T(8,128)(2,1)S(1)}, u32[]{:S(2)}, u32[]{:S(2)}) collective-permute-start(bf16[72,128]{1,0:T(8,128)(2,1)S(1)} %collective-permute-done.5.refs_2_), channel_id=1, source_target_pairs={{0,1},{1,0},{2,3},{3,2},{4,5},{5,4},{6,7},{7,6},{8,9},{9,8},{10,11... | collective-permute-start | bytes 55304 | tf_op jit(solution)/shard_map/ppermute | solution.py:229

commit v19 on v18

--- a/solution.py
+++ b/solution.py
@@ -18,9 +18,7 @@
     shared = pair_count - 2
     rest = [e for e in range(1, pair_count) if e != shared]
     mine = rest[: len(rest) // 2] if core == 0 else rest[len(rest) // 2 :]
-    if core == 0:
-        mine = mine[1:] + mine[:1]
-    return mine + [shared, 0]
+    return mine[1:] + mine[:1] + [shared, 0]
 
 
 def shifted(pair, offset, pair_count, sign=1):

time: 14.1 us -> 14.1 us (level)
  no operation moved by 1% of the time
where the time goes in v19:
time: 14.1 us; the launch traced here: 13.9 us
  starting transfers between devices  9.33 us (66%)
  Pallas kernels  2.48 us (18%)
  waiting for transfers between devices  2.1 us (15%)
    ppermute x4, starting transfers between devices, on_device(): arrived.append(lax.ppermute(message, AXES, route))  8.12 us
    pallas_call x1, Pallas kernels, on_device(): pl.pallas_call(functools.partial(stat_kernel, pair_count, samps), out_sha...  1.43 us
    ppermute x4, waiting for transfers between devices, on_device(): arrived.append(lax.ppermute(message, AXES, route))  0.98 us
    pallas_call x1, Pallas kernels, on_device(): pl.pallas_call(functools.partial(pick_kernel, pair_count, samps), out_sha...  0.91 us
    ppermute x3, waiting for transfers between devices, on_device(): mates = [lax.ppermute(a, 'samp', swap) for a in far]  0.84 us
    ppermute x3, starting transfers between devices, on_device(): mates = [lax.ppermute(a, 'samp', swap) for a in far]  0.71 us
    ppermute x1, starting transfers between devices, on_device(): mate_dosage = lax.ppermute(dosage, 'samp', swap)  0.45 us
  transfers between devices with their start and end apart: 9, of which 4 were waited for; matrix products, arithmetic and copies ran while one was open for 0% of the time, Pallas kernels for 7%

profile of v19, /device:TPU:0, one launch (start us, length us, event | category | flops | bytes accessed | tf_op | source)
XLA Modules:
  0.0 13.9 jit_solution(8427150067578854782)
XLA Ops:
  0.0 0.5 %collective-permute-start = (bf16[4,4096]{1,0:T(4,128)(2,1)}, bf16[4,4096]{1,0:T(4,128)(2,1)S(1)}, u32[]{:S(2)}, u32[]{:S(2)}) collective-permute-start(bf16[4,4096]{1,0:T(4,128)(2,1)} %param.4), channel_id=1, source_target_pairs={{0,1},{1,0},{2,3},{3,2},{4,5},{5,4},{6,7},{7,6},{8,9},{9,8},{10,11... | collective-permute-start | bytes 98312 | tf_op jit(solution)/shard_map/ppermute | solution.py:183
  0.5 0.1 collective-permute-start.1
  0.5 0.9 %pick.1 = (bf16[160,128]{1,0:T(8,128)(2,1)S(1)}, bf16[160,128]{1,0:T(8,128)(2,1)S(1)}, bf16[8,128]{1,0:T(8,128)(2,1)S(1)}, s32[2,64]{1,0:T(2,128)S(1)}) custom-call(s32[2,8]{1,0:T(2,128)} %bitcast.13, bf16[128,128]{1,0:T(8,128)(2,1)} %bitcast.12, bf16[2,4]{1,0:T(2,128)(2,1)} %pheno_hbm.1, s32[2,64]{1,0:T(2,128)} %perms_hbm.1), custom_call_target="tpu_custom_call" | custom-call | bytes 163840 | tf_op jit(solution)/shard_map/pick/pallas_call | solution.py:187
  1.4 0.3 %collective-permute-done.1.pheno_ref = bf16[2,4]{1,0:T(2,128)(2,1)S(1)} collective-permute-done((bf16[2,4]{1,0:T(2,128)(2,1)}, bf16[2,4]{1,0:T(2,128)(2,1)S(1)}, u32[]{:S(2)}, u32[]{:S(2)}) %collective-permute-start.1) | collective-permute-done | bytes 48 | tf_op jit(solution)/shard_map/ppermute | solution.py:184
  1.7 0.0 collective-permute-done
  1.7 0.1 %join.1 = (bf16[32,128]{1,0:T(8,128)(2,1)S(1)}, bf16[8,128]{1,0:T(8,128)(2,1)S(1)}, bf16[72,128]{1,0:T(8,128)(2,1)S(1)}, bf16[72,128]{1,0:T(8,128)(2,1)S(1)}, bf...) custom-call(bf16[160,128]{1,0:T(8,128)(2,1)S(1)} %get-tuple-element.15.keep_ref, ...), custom_call_target="tpu_custom_call" | custom-call | tf_op jit(solution)/shard_map/join/pallas_call | solution.py:209
  1.9 2.8 %collective-permute-start.3 = (bf16[72,128]{1,0:T(8,128)(2,1)S(1)}, bf16[72,128]{1,0:T(8,128)(2,1)S(1)}, u32[]{:S(2)}, u32[]{:S(2)}) collective-permute-start(bf16[72,128]{1,0:T(8,128)(2,1)S(1)} %get-tuple-element.22), channel_id=1, source_target_pairs={{0,4},{1,11},{2,6},{3,9},{4,8},{5,15},{6,10},{7,13},{8,12},{9,3},{... | collective-permute-start | bytes 55304 | tf_op jit(solution)/shard_map/ppermute | solution.py:225
  4.7 2.5 %collective-permute-start.4 = (bf16[72,128]{1,0:T(8,128)(2,1)S(1)}, bf16[72,128]{1,0:T(8,128)(2,1)S(1)}, u32[]{:S(2)}, u32[]{:S(2)}) collective-permute-start(bf16[72,128]{1,0:T(8,128)(2,1)S(1)} %get-tuple-element.23), channel_id=1, source_target_pairs={{0,6},{1,15},{2,4},{3,13},{4,10},{5,3},{6,8},{7,1},{8,14},{9,7},{1... | collective-permute-start | bytes 55304 | tf_op jit(solution)/shard_map/ppermute | solution.py:225
  7.2 0.5 %collective-permute-start.5 = (bf16[72,128]{1,0:T(8,128)(2,1)S(1)}, bf16[72,128]{1,0:T(8,128)(2,1)S(1)}, u32[]{:S(2)}, u32[]{:S(2)}) collective-permute-start(bf16[72,128]{1,0:T(8,128)(2,1)S(1)} %get-tuple-element.24), channel_id=1, source_target_pairs={{0,2},{1,9},{2,0},{3,11},{4,6},{5,13},{6,4},{7,15},{8,10},{9,1},{1... | collective-permute-start | bytes 55304 | tf_op jit(solution)/shard_map/ppermute | solution.py:225
  7.7 2.2 %collective-permute-start.2 = (bf16[72,128]{1,0:T(8,128)(2,1)S(1)}, bf16[72,128]{1,0:T(8,128)(2,1)S(1)}, u32[]{:S(2)}, u32[]{:S(2)}) collective-permute-start(bf16[72,128]{1,0:T(8,128)(2,1)S(1)} %get-tuple-element.21), channel_id=1, source_target_pairs={{0,12},{1,13},{2,14},{3,15},{4,0},{5,1},{6,2},{7,3},{8,4},{9,5},{1... | collective-permute-start | bytes 55304 | tf_op jit(solution)/shard_map/ppermute | solution.py:225
  10.0 0.0 collective-permute-done.3.refs_0_
  10.0 0.2 %collective-permute-start.6 = (bf16[72,128]{1,0:T(8,128)(2,1)S(1)}, bf16[72,128]{1,0:T(8,128)(2,1)S(1)}, u32[]{:S(2)}, u32[]{:S(2)}) collective-permute-start(bf16[72,128]{1,0:T(8,128)(2,1)S(1)} %collective-permute-done.3.refs_0_), channel_id=1, source_target_pairs={{0,1},{1,0},{2,3},{3,2},{4,5},{5,4},{6,7},{7,6},{8,9},{9,8},{10,11... | collective-permute-start | bytes 55304 | tf_op jit(solution)/shard_map/ppermute | solution.py:227
  10.2 1.0 %collective-permute-done.4.refs_1_ = bf16[72,128]{1,0:T(8,128)(2,1)S(1)} collective-permute-done((bf16[72,128]{1,0:T(8,128)(2,1)S(1)}, bf16[72,128]{1,0:T(8,128)(2,1)S(1)}, u32[]{:S(2)}, u32[]{:S(2)}) %collective-permute-start.4) | collective-permute-done | bytes 18464 | tf_op jit(solution)/shard_map/ppermute | solution.py:225
  11.2 0.0 collective-permute-start.7
  11.2 0.0 collective-permute-done.5.refs_2_
  11.2 0.5 %collective-permute-start.8 = (bf16[72,128]{1,0:T(8,128)(2,1)S(1)}, bf16[72,128]{1,0:T(8,128)(2,1)S(1)}, u32[]{:S(2)}, u32[]{:S(2)}) collective-permute-start(bf16[72,128]{1,0:T(8,128)(2,1)S(1)} %collective-permute-done.5.refs_2_), channel_id=1, source_target_pairs={{0,1},{1,0},{2,3},{3,2},{4,5},{5,4},{6,7},{7,6},{8,9},{9,8},{10,11... | collective-permute-start | bytes 55304 | tf_op jit(solution)/shard_map/ppermute | solution.py:227
  11.7 0.0 collective-permute-done.2.near_ref
  11.7 0.0 collective-permute-done.6.refs_3_
  11.7 0.7 %collective-permute-done.7.refs_4_ = bf16[72,128]{1,0:T(8,128)(2,1)S(1)} collective-permute-done((bf16[72,128]{1,0:T(8,128)(2,1)S(1)}, bf16[72,128]{1,0:T(8,128)(2,1)S(1)}, u32[]{:S(2)}, u32[]{:S(2)}) %collective-permute-start.7) | collective-permute-done | bytes 18464 | tf_op jit(solution)/shard_map/ppermute | solution.py:227
  12.3 0.2 %collective-permute-done.8.refs_5_ = bf16[72,128]{1,0:T(8,128)(2,1)S(1)} collective-permute-done((bf16[72,128]{1,0:T(8,128)(2,1)S(1)}, bf16[72,128]{1,0:T(8,128)(2,1)S(1)}, u32[]{:S(2)}, u32[]{:S(2)}) %collective-permute-start.8) | collective-permute-done | bytes 18464 | tf_op jit(solution)/shard_map/ppermute | solution.py:227
  12.5 1.4 %stat.1 = bf16[1,4,512,256]{3,2,1,0:T(8,128)(2,1)} custom-call(bf16[8,128]{1,0:T(8,128)(2,1)S(1)} %get-tuple-element.19.wave_ref, bf16[160,128]{1,0:T(8,128)(2,1)S(1)} %get-tuple-element.15.keep_ref, bf16[32,128]{1,0:T(8,128)(2,1)S(1)} %get-tuple-element.20.mate_self_ref, bf16[72,128]{1,0:T(8,128)(2,1)S(1)} %collective-permute-done.2.near_ref, ...), custom_call_target="tpu_custom_call" | custom-call | tf_op jit(solution)/shard_map/stat/pallas_call | solution.py:229
Async XLA Ops:
  0.0 1.7 %collective-permute-start = (bf16[4,4096]{1,0:T(4,128)(2,1)}, bf16[4,4096]{1,0:T(4,128)(2,1)S(1)}, u32[]{:S(2)}, u32[]{:S(2)}) collective-permute-start(bf16[4,4096]{1,0:T(4,128)(2,1)} %param.4), channel_id=1, source_target_pairs={{0,1},{1,0},{2,3},{3,2},{4,5},{5,4},{6,7},{7,6},{8,9},{9,8},{10,11... | collective-permute-start | bytes 98312 | tf_op jit(solution)/shard_map/ppermute | solution.py:183
  0.5 1.3 %collective-permute-start.1 = (bf16[2,4]{1,0:T(2,128)(2,1)}, bf16[2,4]{1,0:T(2,128)(2,1)S(1)}, u32[]{:S(2)}, u32[]{:S(2)}) collective-permute-start(bf16[2,4]{1,0:T(2,128)(2,1)} %pheno_hbm.1), channel_id=1, source_target_pairs={{0,1},{1,0},{2,3},{3,2},{4,5},{5,4},{6,7},{7,6},{8,9},{9,8},{10,11... | collective-permute-start | bytes 56 | tf_op jit(solution)/shard_map/ppermute | solution.py:184
  1.9 8.1 %collective-permute-start.3 = (bf16[72,128]{1,0:T(8,128)(2,1)S(1)}, bf16[72,128]{1,0:T(8,128)(2,1)S(1)}, u32[]{:S(2)}, u32[]{:S(2)}) collective-permute-start(bf16[72,128]{1,0:T(8,128)(2,1)S(1)} %get-tuple-element.22), channel_id=1, source_target_pairs={{0,4},{1,11},{2,6},{3,9},{4,8},{5,15},{6,10},{7,13},{8,12},{9,3},{... | collective-permute-start | bytes 55304 | tf_op jit(solution)/shard_map/ppermute | solution.py:225
  4.7 6.5 %collective-permute-start.4 = (bf16[72,128]{1,0:T(8,128)(2,1)S(1)}, bf16[72,128]{1,0:T(8,128)(2,1)S(1)}, u32[]{:S(2)}, u32[]{:S(2)}) collective-permute-start(bf16[72,128]{1,0:T(8,128)(2,1)S(1)} %get-tuple-element.23), channel_id=1, source_target_pairs={{0,6},{1,15},{2,4},{3,13},{4,10},{5,3},{6,8},{7,1},{8,14},{9,7},{1... | collective-permute-start | bytes 55304 | tf_op jit(solution)/shard_map/ppermute | solution.py:225
  7.2 4.0 %collective-permute-start.5 = (bf16[72,128]{1,0:T(8,128)(2,1)S(1)}, bf16[72,128]{1,0:T(8,128)(2,1)S(1)}, u32[]{:S(2)}, u32[]{:S(2)}) collective-permute-start(bf16[72,128]{1,0:T(8,128)(2,1)S(1)} %get-tuple-element.24), channel_id=1, source_target_pairs={{0,2},{1,9},{2,0},{3,11},{4,6},{5,13},{6,4},{7,15},{8,10},{9,1},{1... | collective-permute-start | bytes 55304 | tf_op jit(solution)/shard_map/ppermute | solution.py:225
  7.7 3.9 %collective-permute-start.2 = (bf16[72,128]{1,0:T(8,128)(2,1)S(1)}, bf16[72,128]{1,0:T(8,128)(2,1)S(1)}, u32[]{:S(2)}, u32[]{:S(2)}) collective-permute-start(bf16[72,128]{1,0:T(8,128)(2,1)S(1)} %get-tuple-element.21), channel_id=1, source_target_pairs={{0,12},{1,13},{2,14},{3,15},{4,0},{5,1},{6,2},{7,3},{8,4},{9,5},{1... | collective-permute-start | bytes 55304 | tf_op jit(solution)/shard_map/ppermute | solution.py:225
  10.0 1.7 %collective-permute-start.6 = (bf16[72,128]{1,0:T(8,128)(2,1)S(1)}, bf16[72,128]{1,0:T(8,128)(2,1)S(1)}, u32[]{:S(2)}, u32[]{:S(2)}) collective-permute-start(bf16[72,128]{1,0:T(8,128)(2,1)S(1)} %collective-permute-done.3.refs_0_), channel_id=1, source_target_pairs={{0,1},{1,0},{2,3},{3,2},{4,5},{5,4},{6,7},{7,6},{8,9},{9,8},{10,11... | collective-permute-start | bytes 55304 | tf_op jit(solution)/shard_map/ppermute | solution.py:227
  11.2 1.2 %collective-permute-start.7 = (bf16[72,128]{1,0:T(8,128)(2,1)S(1)}, bf16[72,128]{1,0:T(8,128)(2,1)S(1)}, u32[]{:S(2)}, u32[]{:S(2)}) collective-permute-start(bf16[72,128]{1,0:T(8,128)(2,1)S(1)} %collective-permute-done.4.refs_1_), channel_id=1, source_target_pairs={{0,1},{1,0},{2,3},{3,2},{4,5},{5,4},{6,7},{7,6},{8,9},{9,8},{10,11... | collective-permute-start | bytes 55304 | tf_op jit(solution)/shard_map/ppermute | solution.py:227
  11.2 1.4 %collective-permute-start.8 = (bf16[72,128]{1,0:T(8,128)(2,1)S(1)}, bf16[72,128]{1,0:T(8,128)(2,1)S(1)}, u32[]{:S(2)}, u32[]{:S(2)}) collective-permute-start(bf16[72,128]{1,0:T(8,128)(2,1)S(1)} %collective-permute-done.5.refs_2_), channel_id=1, source_target_pairs={{0,1},{1,0},{2,3},{3,2},{4,5},{5,4},{6,7},{7,6},{8,9},{9,8},{10,11... | collective-permute-start | bytes 55304 | tf_op jit(solution)/shard_map/ppermute | solution.py:227

commit v20 on v19

--- a/solution.py
+++ b/solution.py
@@ -15,10 +15,7 @@
 
 
 def offsets(pair_count, core):
-    shared = pair_count - 2
-    rest = [e for e in range(1, pair_count) if e != shared]
-    mine = rest[: len(rest) // 2] if core == 0 else rest[len(rest) // 2 :]
-    return mine[1:] + mine[:1] + [shared, 0]
+    return [e for e in range(2, pair_count) if e % 2 == core] + [1, 0]
 
 
 def shifted(pair, offset, pair_count, sign=1):

time: 14.1 us -> 14 us (level)
  waiting for transfers between devices: 2.1 us -> 1.65 us
  starting transfers between devices: 9.33 us -> 9.67 us
    ppermute x3, waiting for transfers between devices: 0.84 us -> 0.01 us  [on_device(): mates = [lax.ppermute(a, 'samp', swap) for a in far]]
    ppermute x4, waiting for transfers between devices: 0.98 us -> 1.36 us  [on_device(): arrived.append(lax.ppermute(message, AXES, route))]
    ppermute x3, starting transfers between devices: 0.71 us -> 0.9 us  [on_device(): mates = [lax.ppermute(a, 'samp', swap) for a in far]]
    ppermute x4, starting transfers between devices: 8.12 us -> 8.26 us  [on_device(): arrived.append(lax.ppermute(message, AXES, route))]
  transfers between devices with their start and end apart: 9 -> 9, of which waited for: 4 -> 3; matrix products, arithmetic and copies ran while one was open for 0% -> 0% of each run, Pallas kernels for 7% -> 7%
where the time goes in v20:
time: 14 us; the launch traced here: 13.8 us
  starting transfers between devices  9.67 us (69%)
  Pallas kernels  2.49 us (18%)
  waiting for transfers between devices  1.65 us (12%)
    ppermute x4, starting transfers between devices, on_device(): arrived.append(lax.ppermute(message, AXES, route))  8.26 us
    pallas_call x1, Pallas kernels, on_device(): pl.pallas_call(functools.partial(stat_kernel, pair_count, samps), out_sha...  1.43 us
    ppermute x4, waiting for transfers between devices, on_device(): arrived.append(lax.ppermute(message, AXES, route))  1.36 us
    pallas_call x1, Pallas kernels, on_device(): pl.pallas_call(functools.partial(pick_kernel, pair_count, samps), out_sha...  0.91 us
    ppermute x3, starting transfers between devices, on_device(): mates = [lax.ppermute(a, 'samp', swap) for a in far]  0.9 us
    ppermute x1, starting transfers between devices, on_device(): mate_dosage = lax.ppermute(dosage, 'samp', swap)  0.45 us
  transfers between devices with their start and end apart: 9, of which 3 were waited for; matrix products, arithmetic and copies ran while one was open for 0% of the time, Pallas kernels for 7%

profile of v20, /device:TPU:0, one launch (start us, length us, event | category | flops | bytes accessed | tf_op | source)
XLA Modules:
  0.0 13.8 jit_solution(10964413449057529918)
XLA Ops:
  0.0 0.5 %collective-permute-start = (bf16[4,4096]{1,0:T(4,128)(2,1)}, bf16[4,4096]{1,0:T(4,128)(2,1)S(1)}, u32[]{:S(2)}, u32[]{:S(2)}) collective-permute-start(bf16[4,4096]{1,0:T(4,128)(2,1)} %param.4), channel_id=1, source_target_pairs={{0,1},{1,0},{2,3},{3,2},{4,5},{5,4},{6,7},{7,6},{8,9},{9,8},{10,11... | collective-permute-start | bytes 98312 | tf_op jit(solution)/shard_map/ppermute | solution.py:180
  0.5 0.1 collective-permute-start.1
  0.5 0.9 %pick.1 = (bf16[160,128]{1,0:T(8,128)(2,1)S(1)}, bf16[160,128]{1,0:T(8,128)(2,1)S(1)}, bf16[8,128]{1,0:T(8,128)(2,1)S(1)}, s32[2,64]{1,0:T(2,128)S(1)}) custom-call(s32[2,8]{1,0:T(2,128)} %bitcast.13, bf16[128,128]{1,0:T(8,128)(2,1)} %bitcast.12, bf16[2,4]{1,0:T(2,128)(2,1)} %pheno_hbm.1, s32[2,64]{1,0:T(2,128)} %perms_hbm.1), custom_call_target="tpu_custom_call" | custom-call | bytes 163840 | tf_op jit(solution)/shard_map/pick/pallas_call | solution.py:184
  1.4 0.3 %collective-permute-done.1.pheno_ref = bf16[2,4]{1,0:T(2,128)(2,1)S(1)} collective-permute-done((bf16[2,4]{1,0:T(2,128)(2,1)}, bf16[2,4]{1,0:T(2,128)(2,1)S(1)}, u32[]{:S(2)}, u32[]{:S(2)}) %collective-permute-start.1) | collective-permute-done | bytes 48 | tf_op jit(solution)/shard_map/ppermute | solution.py:181
  1.7 0.0 collective-permute-done
  1.7 0.1 %join.1 = (bf16[32,128]{1,0:T(8,128)(2,1)S(1)}, bf16[8,128]{1,0:T(8,128)(2,1)S(1)}, bf16[72,128]{1,0:T(8,128)(2,1)S(1)}, bf16[72,128]{1,0:T(8,128)(2,1)S(1)}, bf...) custom-call(bf16[160,128]{1,0:T(8,128)(2,1)S(1)} %get-tuple-element.15.keep_ref, ...), custom_call_target="tpu_custom_call" | custom-call | tf_op jit(solution)/shard_map/join/pallas_call | solution.py:206
  1.9 2.8 %collective-permute-start.3 = (bf16[72,128]{1,0:T(8,128)(2,1)S(1)}, bf16[72,128]{1,0:T(8,128)(2,1)S(1)}, u32[]{:S(2)}, u32[]{:S(2)}) collective-permute-start(bf16[72,128]{1,0:T(8,128)(2,1)S(1)} %get-tuple-element.22), channel_id=1, source_target_pairs={{0,4},{1,7},{2,6},{3,5},{4,8},{5,11},{6,10},{7,9},{8,12},{9,15},{1... | collective-permute-start | bytes 55304 | tf_op jit(solution)/shard_map/ppermute | solution.py:222
  4.7 2.6 %collective-permute-start.4 = (bf16[72,128]{1,0:T(8,128)(2,1)S(1)}, bf16[72,128]{1,0:T(8,128)(2,1)S(1)}, u32[]{:S(2)}, u32[]{:S(2)}) collective-permute-start(bf16[72,128]{1,0:T(8,128)(2,1)S(1)} %get-tuple-element.23), channel_id=1, source_target_pairs={{0,8},{1,11},{2,10},{3,9},{4,12},{5,15},{6,14},{7,13},{8,0},{9,3},... | collective-permute-start | bytes 55304 | tf_op jit(solution)/shard_map/ppermute | solution.py:222
  7.3 1.3 %collective-permute-start.5 = (bf16[72,128]{1,0:T(8,128)(2,1)S(1)}, bf16[72,128]{1,0:T(8,128)(2,1)S(1)}, u32[]{:S(2)}, u32[]{:S(2)}) collective-permute-start(bf16[72,128]{1,0:T(8,128)(2,1)S(1)} %get-tuple-element.24), channel_id=1, source_target_pairs={{0,12},{1,15},{2,14},{3,13},{4,0},{5,3},{6,2},{7,1},{8,4},{9,7},{1... | collective-permute-start | bytes 55304 | tf_op jit(solution)/shard_map/ppermute | solution.py:222
  8.6 1.5 %collective-permute-start.2 = (bf16[72,128]{1,0:T(8,128)(2,1)S(1)}, bf16[72,128]{1,0:T(8,128)(2,1)S(1)}, u32[]{:S(2)}, u32[]{:S(2)}) collective-permute-start(bf16[72,128]{1,0:T(8,128)(2,1)S(1)} %get-tuple-element.21), channel_id=1, source_target_pairs={{0,2},{1,3},{2,0},{3,1},{4,6},{5,7},{6,4},{7,5},{8,10},{9,11},{10,... | collective-permute-start | bytes 55304 | tf_op jit(solution)/shard_map/ppermute | solution.py:222
  10.1 0.0 collective-permute-done.3.refs_0_
  10.1 0.1 collective-permute-start.6
  10.2 0.0 collective-permute-done.4.refs_1_
  10.2 0.5 %collective-permute-start.7 = (bf16[72,128]{1,0:T(8,128)(2,1)S(1)}, bf16[72,128]{1,0:T(8,128)(2,1)S(1)}, u32[]{:S(2)}, u32[]{:S(2)}) collective-permute-start(bf16[72,128]{1,0:T(8,128)(2,1)S(1)} %collective-permute-done.4.refs_1_), channel_id=1, source_target_pairs={{0,1},{1,0},{2,3},{3,2},{4,5},{5,4},{6,7},{7,6},{8,9},{9,8},{10,11... | collective-permute-start | bytes 55304 | tf_op jit(solution)/shard_map/ppermute | solution.py:224
  10.6 0.4 %collective-permute-done.5.refs_2_ = bf16[72,128]{1,0:T(8,128)(2,1)S(1)} collective-permute-done((bf16[72,128]{1,0:T(8,128)(2,1)S(1)}, bf16[72,128]{1,0:T(8,128)(2,1)S(1)}, u32[]{:S(2)}, u32[]{:S(2)}) %collective-permute-start.5) | collective-permute-done | bytes 18464 | tf_op jit(solution)/shard_map/ppermute | solution.py:222
  11.0 0.4 %collective-permute-start.8 = (bf16[72,128]{1,0:T(8,128)(2,1)S(1)}, bf16[72,128]{1,0:T(8,128)(2,1)S(1)}, u32[]{:S(2)}, u32[]{:S(2)}) collective-permute-start(bf16[72,128]{1,0:T(8,128)(2,1)S(1)} %collective-permute-done.5.refs_2_), channel_id=1, source_target_pairs={{0,1},{1,0},{2,3},{3,2},{4,5},{5,4},{6,7},{7,6},{8,9},{9,8},{10,11... | collective-permute-start | bytes 55304 | tf_op jit(solution)/shard_map/ppermute | solution.py:224
  11.4 1.0 %collective-permute-done.2.near_ref = bf16[72,128]{1,0:T(8,128)(2,1)S(1)} collective-permute-done((bf16[72,128]{1,0:T(8,128)(2,1)S(1)}, bf16[72,128]{1,0:T(8,128)(2,1)S(1)}, u32[]{:S(2)}, u32[]{:S(2)}) %collective-permute-start.2) | collective-permute-done | bytes 18464 | tf_op jit(solution)/shard_map/ppermute | solution.py:222
  12.4 0.0 collective-permute-done.6.refs_3_
  12.4 0.0 collective-permute-done.7.refs_4_
  12.4 0.0 collective-permute-done.8.refs_5_
  12.4 1.4 %stat.1 = bf16[1,4,512,256]{3,2,1,0:T(8,128)(2,1)} custom-call(bf16[8,128]{1,0:T(8,128)(2,1)S(1)} %get-tuple-element.19.wave_ref, bf16[160,128]{1,0:T(8,128)(2,1)S(1)} %get-tuple-element.15.keep_ref, bf16[32,128]{1,0:T(8,128)(2,1)S(1)} %get-tuple-element.20.mate_self_ref, bf16[72,128]{1,0:T(8,128)(2,1)S(1)} %collective-permute-done.2.near_ref, ...), custom_call_target="tpu_custom_call" | custom-call | tf_op jit(solution)/shard_map/stat/pallas_call | solution.py:226
Async XLA Ops:
  0.0 1.7 %collective-permute-start = (bf16[4,4096]{1,0:T(4,128)(2,1)}, bf16[4,4096]{1,0:T(4,128)(2,1)S(1)}, u32[]{:S(2)}, u32[]{:S(2)}) collective-permute-start(bf16[4,4096]{1,0:T(4,128)(2,1)} %param.4), channel_id=1, source_target_pairs={{0,1},{1,0},{2,3},{3,2},{4,5},{5,4},{6,7},{7,6},{8,9},{9,8},{10,11... | collective-permute-start | bytes 98312 | tf_op jit(solution)/shard_map/ppermute | solution.py:180
  0.5 1.3 %collective-permute-start.1 = (bf16[2,4]{1,0:T(2,128)(2,1)}, bf16[2,4]{1,0:T(2,128)(2,1)S(1)}, u32[]{:S(2)}, u32[]{:S(2)}) collective-permute-start(bf16[2,4]{1,0:T(2,128)(2,1)} %pheno_hbm.1), channel_id=1, source_target_pairs={{0,1},{1,0},{2,3},{3,2},{4,5},{5,4},{6,7},{7,6},{8,9},{9,8},{10,11... | collective-permute-start | bytes 56 | tf_op jit(solution)/shard_map/ppermute | solution.py:181
  1.9 8.3 %collective-permute-start.3 = (bf16[72,128]{1,0:T(8,128)(2,1)S(1)}, bf16[72,128]{1,0:T(8,128)(2,1)S(1)}, u32[]{:S(2)}, u32[]{:S(2)}) collective-permute-start(bf16[72,128]{1,0:T(8,128)(2,1)S(1)} %get-tuple-element.22), channel_id=1, source_target_pairs={{0,4},{1,7},{2,6},{3,5},{4,8},{5,11},{6,10},{7,9},{8,12},{9,15},{1... | collective-permute-start | bytes 55304 | tf_op jit(solution)/shard_map/ppermute | solution.py:222
  4.7 5.5 %collective-permute-start.4 = (bf16[72,128]{1,0:T(8,128)(2,1)S(1)}, bf16[72,128]{1,0:T(8,128)(2,1)S(1)}, u32[]{:S(2)}, u32[]{:S(2)}) collective-permute-start(bf16[72,128]{1,0:T(8,128)(2,1)S(1)} %get-tuple-element.23), channel_id=1, source_target_pairs={{0,8},{1,11},{2,10},{3,9},{4,12},{5,15},{6,14},{7,13},{8,0},{9,3},... | collective-permute-start | bytes 55304 | tf_op jit(solution)/shard_map/ppermute | solution.py:222
  7.3 3.8 %collective-permute-start.5 = (bf16[72,128]{1,0:T(8,128)(2,1)S(1)}, bf16[72,128]{1,0:T(8,128)(2,1)S(1)}, u32[]{:S(2)}, u32[]{:S(2)}) collective-permute-start(bf16[72,128]{1,0:T(8,128)(2,1)S(1)} %get-tuple-element.24), channel_id=1, source_target_pairs={{0,12},{1,15},{2,14},{3,13},{4,0},{5,3},{6,2},{7,1},{8,4},{9,7},{1... | collective-permute-start | bytes 55304 | tf_op jit(solution)/shard_map/ppermute | solution.py:222
  8.6 3.8 %collective-permute-start.2 = (bf16[72,128]{1,0:T(8,128)(2,1)S(1)}, bf16[72,128]{1,0:T(8,128)(2,1)S(1)}, u32[]{:S(2)}, u32[]{:S(2)}) collective-permute-start(bf16[72,128]{1,0:T(8,128)(2,1)S(1)} %get-tuple-element.21), channel_id=1, source_target_pairs={{0,2},{1,3},{2,0},{3,1},{4,6},{5,7},{6,4},{7,5},{8,10},{9,11},{10,... | collective-permute-start | bytes 55304 | tf_op jit(solution)/shard_map/ppermute | solution.py:222
  10.1 2.3 %collective-permute-start.6 = (bf16[72,128]{1,0:T(8,128)(2,1)S(1)}, bf16[72,128]{1,0:T(8,128)(2,1)S(1)}, u32[]{:S(2)}, u32[]{:S(2)}) collective-permute-start(bf16[72,128]{1,0:T(8,128)(2,1)S(1)} %collective-permute-done.3.refs_0_), channel_id=1, source_target_pairs={{0,1},{1,0},{2,3},{3,2},{4,5},{5,4},{6,7},{7,6},{8,9},{9,8},{10,11... | collective-permute-start | bytes 55304 | tf_op jit(solution)/shard_map/ppermute | solution.py:224
  10.2 2.2 %collective-permute-start.7 = (bf16[72,128]{1,0:T(8,128)(2,1)S(1)}, bf16[72,128]{1,0:T(8,128)(2,1)S(1)}, u32[]{:S(2)}, u32[]{:S(2)}) collective-permute-start(bf16[72,128]{1,0:T(8,128)(2,1)S(1)} %collective-permute-done.4.refs_1_), channel_id=1, source_target_pairs={{0,1},{1,0},{2,3},{3,2},{4,5},{5,4},{6,7},{7,6},{8,9},{9,8},{10,11... | collective-permute-start | bytes 55304 | tf_op jit(solution)/shard_map/ppermute | solution.py:224
  11.0 1.4 %collective-permute-start.8 = (bf16[72,128]{1,0:T(8,128)(2,1)S(1)}, bf16[72,128]{1,0:T(8,128)(2,1)S(1)}, u32[]{:S(2)}, u32[]{:S(2)}) collective-permute-start(bf16[72,128]{1,0:T(8,128)(2,1)S(1)} %collective-permute-done.5.refs_2_), channel_id=1, source_target_pairs={{0,1},{1,0},{2,3},{3,2},{4,5},{5,4},{6,7},{7,6},{8,9},{9,8},{10,11... | collective-permute-start | bytes 55304 | tf_op jit(solution)/shard_map/ppermute | solution.py:224

commit v21 on v20

--- a/solution.py
+++ b/solution.py
@@ -155,8 +155,8 @@
         for k in range(stats):
             part = jnp.dot(left, right[:, k * half : (k + 1) * half], preferred_element_type=jnp.float32)
             out_ref[k, piece, :] = part.astype(out_ref.dtype)
-        copies.append(pltpu.make_async_copy(out_ref.at[:, piece], out_hbm.at[0, :, piece], sems.at[q]))
-        copies[-1].start()
+            copies.append(pltpu.make_async_copy(out_ref.at[k, piece], out_hbm.at[0, k, piece], sems.at[q, k]))
+            copies[-1].start()
     for copy in copies:
         copy.wait()
 
@@ -231,7 +231,7 @@
         scratch_shapes=[
             pltpu.VMEM((pair_count * samps, BLOCK, LANES), dosage.dtype),
             pltpu.VMEM((stats, PANEL, half), jnp.bfloat16),
-            pltpu.SemaphoreType.DMA((PANEL // LANES,)),
+            pltpu.SemaphoreType.DMA((PANEL // LANES, stats)),
         ],
         compiler_params=pltpu.CompilerParams(vmem_limit_bytes=48 * 1024 * 1024),
         name="stat",

time: 14 us -> 14.1 us (level)
  no operation moved by 1% of the time
where the time goes in v21:
time: 14.1 us; the launch traced here: 13.9 us
  starting transfers between devices  9.67 us (69%)
  Pallas kernels  2.54 us (18%)
  waiting for transfers between devices  1.65 us (12%)
    ppermute x4, starting transfers between devices, on_device(): arrived.append(lax.ppermute(message, AXES, route))  8.26 us
    pallas_call x1, Pallas kernels, on_device(): pl.pallas_call(functools.partial(stat_kernel, pair_count, samps), out_sha...  1.49 us
    ppermute x4, waiting for transfers between devices, on_device(): arrived.append(lax.ppermute(message, AXES, route))  1.36 us
    pallas_call x1, Pallas kernels, on_device(): pl.pallas_call(functools.partial(pick_kernel, pair_count, samps), out_sha...  0.91 us
    ppermute x3, starting transfers between devices, on_device(): mates = [lax.ppermute(a, 'samp', swap) for a in far]  0.9 us
    ppermute x1, starting transfers between devices, on_device(): mate_dosage = lax.ppermute(dosage, 'samp', swap)  0.45 us
  transfers between devices with their start and end apart: 9, of which 3 were waited for; matrix products, arithmetic and copies ran while one was open for 0% of the time, Pallas kernels for 7%

profile of v21, /device:TPU:0, one launch (start us, length us, event | category | flops | bytes accessed | tf_op | source)
XLA Modules:
  0.0 13.9 jit_solution(3868924987536406888)
XLA Ops:
  0.0 0.5 %collective-permute-start = (bf16[4,4096]{1,0:T(4,128)(2,1)}, bf16[4,4096]{1,0:T(4,128)(2,1)S(1)}, u32[]{:S(2)}, u32[]{:S(2)}) collective-permute-start(bf16[4,4096]{1,0:T(4,128)(2,1)} %param.4), channel_id=1, source_target_pairs={{0,1},{1,0},{2,3},{3,2},{4,5},{5,4},{6,7},{7,6},{8,9},{9,8},{10,11... | collective-permute-start | bytes 98312 | tf_op jit(solution)/shard_map/ppermute | solution.py:180
  0.5 0.1 collective-permute-start.1
  0.5 0.9 %pick.1 = (bf16[160,128]{1,0:T(8,128)(2,1)S(1)}, bf16[160,128]{1,0:T(8,128)(2,1)S(1)}, bf16[8,128]{1,0:T(8,128)(2,1)S(1)}, s32[2,64]{1,0:T(2,128)S(1)}) custom-call(s32[2,8]{1,0:T(2,128)} %bitcast.13, bf16[128,128]{1,0:T(8,128)(2,1)} %bitcast.12, bf16[2,4]{1,0:T(2,128)(2,1)} %pheno_hbm.1, s32[2,64]{1,0:T(2,128)} %perms_hbm.1), custom_call_target="tpu_custom_call" | custom-call | bytes 163840 | tf_op jit(solution)/shard_map/pick/pallas_call | solution.py:184
  1.4 0.3 %collective-permute-done.1.pheno_ref = bf16[2,4]{1,0:T(2,128)(2,1)S(1)} collective-permute-done((bf16[2,4]{1,0:T(2,128)(2,1)}, bf16[2,4]{1,0:T(2,128)(2,1)S(1)}, u32[]{:S(2)}, u32[]{:S(2)}) %collective-permute-start.1) | collective-permute-done | bytes 48 | tf_op jit(solution)/shard_map/ppermute | solution.py:181
  1.7 0.0 collective-permute-done
  1.7 0.1 %join.1 = (bf16[32,128]{1,0:T(8,128)(2,1)S(1)}, bf16[8,128]{1,0:T(8,128)(2,1)S(1)}, bf16[72,128]{1,0:T(8,128)(2,1)S(1)}, bf16[72,128]{1,0:T(8,128)(2,1)S(1)}, bf...) custom-call(bf16[160,128]{1,0:T(8,128)(2,1)S(1)} %get-tuple-element.15.keep_ref, ...), custom_call_target="tpu_custom_call" | custom-call | tf_op jit(solution)/shard_map/join/pallas_call | solution.py:206
  1.9 2.8 %collective-permute-start.3 = (bf16[72,128]{1,0:T(8,128)(2,1)S(1)}, bf16[72,128]{1,0:T(8,128)(2,1)S(1)}, u32[]{:S(2)}, u32[]{:S(2)}) collective-permute-start(bf16[72,128]{1,0:T(8,128)(2,1)S(1)} %get-tuple-element.22), channel_id=1, source_target_pairs={{0,4},{1,7},{2,6},{3,5},{4,8},{5,11},{6,10},{7,9},{8,12},{9,15},{1... | collective-permute-start | bytes 55304 | tf_op jit(solution)/shard_map/ppermute | solution.py:222
  4.7 2.6 %collective-permute-start.4 = (bf16[72,128]{1,0:T(8,128)(2,1)S(1)}, bf16[72,128]{1,0:T(8,128)(2,1)S(1)}, u32[]{:S(2)}, u32[]{:S(2)}) collective-permute-start(bf16[72,128]{1,0:T(8,128)(2,1)S(1)} %get-tuple-element.23), channel_id=1, source_target_pairs={{0,8},{1,11},{2,10},{3,9},{4,12},{5,15},{6,14},{7,13},{8,0},{9,3},... | collective-permute-start | bytes 55304 | tf_op jit(solution)/shard_map/ppermute | solution.py:222
  7.3 1.3 %collective-permute-start.5 = (bf16[72,128]{1,0:T(8,128)(2,1)S(1)}, bf16[72,128]{1,0:T(8,128)(2,1)S(1)}, u32[]{:S(2)}, u32[]{:S(2)}) collective-permute-start(bf16[72,128]{1,0:T(8,128)(2,1)S(1)} %get-tuple-element.24), channel_id=1, source_target_pairs={{0,12},{1,15},{2,14},{3,13},{4,0},{5,3},{6,2},{7,1},{8,4},{9,7},{1... | collective-permute-start | bytes 55304 | tf_op jit(solution)/shard_map/ppermute | solution.py:222
  8.6 1.5 %collective-permute-start.2 = (bf16[72,128]{1,0:T(8,128)(2,1)S(1)}, bf16[72,128]{1,0:T(8,128)(2,1)S(1)}, u32[]{:S(2)}, u32[]{:S(2)}) collective-permute-start(bf16[72,128]{1,0:T(8,128)(2,1)S(1)} %get-tuple-element.21), channel_id=1, source_target_pairs={{0,2},{1,3},{2,0},{3,1},{4,6},{5,7},{6,4},{7,5},{8,10},{9,11},{10,... | collective-permute-start | bytes 55304 | tf_op jit(solution)/shard_map/ppermute | solution.py:222
  10.1 0.0 collective-permute-done.3.refs_0_
  10.1 0.1 collective-permute-start.6
  10.2 0.0 collective-permute-done.4.refs_1_
  10.2 0.5 %collective-permute-start.7 = (bf16[72,128]{1,0:T(8,128)(2,1)S(1)}, bf16[72,128]{1,0:T(8,128)(2,1)S(1)}, u32[]{:S(2)}, u32[]{:S(2)}) collective-permute-start(bf16[72,128]{1,0:T(8,128)(2,1)S(1)} %collective-permute-done.4.refs_1_), channel_id=1, source_target_pairs={{0,1},{1,0},{2,3},{3,2},{4,5},{5,4},{6,7},{7,6},{8,9},{9,8},{10,11... | collective-permute-start | bytes 55304 | tf_op jit(solution)/shard_map/ppermute | solution.py:224
  10.6 0.4 %collective-permute-done.5.refs_2_ = bf16[72,128]{1,0:T(8,128)(2,1)S(1)} collective-permute-done((bf16[72,128]{1,0:T(8,128)(2,1)S(1)}, bf16[72,128]{1,0:T(8,128)(2,1)S(1)}, u32[]{:S(2)}, u32[]{:S(2)}) %collective-permute-start.5) | collective-permute-done | bytes 18464 | tf_op jit(solution)/shard_map/ppermute | solution.py:222
  11.0 0.4 %collective-permute-start.8 = (bf16[72,128]{1,0:T(8,128)(2,1)S(1)}, bf16[72,128]{1,0:T(8,128)(2,1)S(1)}, u32[]{:S(2)}, u32[]{:S(2)}) collective-permute-start(bf16[72,128]{1,0:T(8,128)(2,1)S(1)} %collective-permute-done.5.refs_2_), channel_id=1, source_target_pairs={{0,1},{1,0},{2,3},{3,2},{4,5},{5,4},{6,7},{7,6},{8,9},{9,8},{10,11... | collective-permute-start | bytes 55304 | tf_op jit(solution)/shard_map/ppermute | solution.py:224
  11.4 1.0 %collective-permute-done.2.near_ref = bf16[72,128]{1,0:T(8,128)(2,1)S(1)} collective-permute-done((bf16[72,128]{1,0:T(8,128)(2,1)S(1)}, bf16[72,128]{1,0:T(8,128)(2,1)S(1)}, u32[]{:S(2)}, u32[]{:S(2)}) %collective-permute-start.2) | collective-permute-done | bytes 18464 | tf_op jit(solution)/shard_map/ppermute | solution.py:222
  12.4 0.0 collective-permute-done.6.refs_3_
  12.4 0.0 collective-permute-done.7.refs_4_
  12.4 0.0 collective-permute-done.8.refs_5_
  12.4 1.5 %stat.1 = bf16[1,4,512,256]{3,2,1,0:T(8,128)(2,1)} custom-call(bf16[8,128]{1,0:T(8,128)(2,1)S(1)} %get-tuple-element.19.wave_ref, bf16[160,128]{1,0:T(8,128)(2,1)S(1)} %get-tuple-element.15.keep_ref, bf16[32,128]{1,0:T(8,128)(2,1)S(1)} %get-tuple-element.20.mate_self_ref, bf16[72,128]{1,0:T(8,128)(2,1)S(1)} %collective-permute-done.2.near_ref, ...), custom_call_target="tpu_custom_call" | custom-call | tf_op jit(solution)/shard_map/stat/pallas_call | solution.py:226
Async XLA Ops:
  0.0 1.7 %collective-permute-start = (bf16[4,4096]{1,0:T(4,128)(2,1)}, bf16[4,4096]{1,0:T(4,128)(2,1)S(1)}, u32[]{:S(2)}, u32[]{:S(2)}) collective-permute-start(bf16[4,4096]{1,0:T(4,128)(2,1)} %param.4), channel_id=1, source_target_pairs={{0,1},{1,0},{2,3},{3,2},{4,5},{5,4},{6,7},{7,6},{8,9},{9,8},{10,11... | collective-permute-start | bytes 98312 | tf_op jit(solution)/shard_map/ppermute | solution.py:180
  0.5 1.3 %collective-permute-start.1 = (bf16[2,4]{1,0:T(2,128)(2,1)}, bf16[2,4]{1,0:T(2,128)(2,1)S(1)}, u32[]{:S(2)}, u32[]{:S(2)}) collective-permute-start(bf16[2,4]{1,0:T(2,128)(2,1)} %pheno_hbm.1), channel_id=1, source_target_pairs={{0,1},{1,0},{2,3},{3,2},{4,5},{5,4},{6,7},{7,6},{8,9},{9,8},{10,11... | collective-permute-start | bytes 56 | tf_op jit(solution)/shard_map/ppermute | solution.py:181
  1.9 8.3 %collective-permute-start.3 = (bf16[72,128]{1,0:T(8,128)(2,1)S(1)}, bf16[72,128]{1,0:T(8,128)(2,1)S(1)}, u32[]{:S(2)}, u32[]{:S(2)}) collective-permute-start(bf16[72,128]{1,0:T(8,128)(2,1)S(1)} %get-tuple-element.22), channel_id=1, source_target_pairs={{0,4},{1,7},{2,6},{3,5},{4,8},{5,11},{6,10},{7,9},{8,12},{9,15},{1... | collective-permute-start | bytes 55304 | tf_op jit(solution)/shard_map/ppermute | solution.py:222
  4.7 5.5 %collective-permute-start.4 = (bf16[72,128]{1,0:T(8,128)(2,1)S(1)}, bf16[72,128]{1,0:T(8,128)(2,1)S(1)}, u32[]{:S(2)}, u32[]{:S(2)}) collective-permute-start(bf16[72,128]{1,0:T(8,128)(2,1)S(1)} %get-tuple-element.23), channel_id=1, source_target_pairs={{0,8},{1,11},{2,10},{3,9},{4,12},{5,15},{6,14},{7,13},{8,0},{9,3},... | collective-permute-start | bytes 55304 | tf_op jit(solution)/shard_map/ppermute | solution.py:222
  7.3 3.8 %collective-permute-start.5 = (bf16[72,128]{1,0:T(8,128)(2,1)S(1)}, bf16[72,128]{1,0:T(8,128)(2,1)S(1)}, u32[]{:S(2)}, u32[]{:S(2)}) collective-permute-start(bf16[72,128]{1,0:T(8,128)(2,1)S(1)} %get-tuple-element.24), channel_id=1, source_target_pairs={{0,12},{1,15},{2,14},{3,13},{4,0},{5,3},{6,2},{7,1},{8,4},{9,7},{1... | collective-permute-start | bytes 55304 | tf_op jit(solution)/shard_map/ppermute | solution.py:222
  8.6 3.8 %collective-permute-start.2 = (bf16[72,128]{1,0:T(8,128)(2,1)S(1)}, bf16[72,128]{1,0:T(8,128)(2,1)S(1)}, u32[]{:S(2)}, u32[]{:S(2)}) collective-permute-start(bf16[72,128]{1,0:T(8,128)(2,1)S(1)} %get-tuple-element.21), channel_id=1, source_target_pairs={{0,2},{1,3},{2,0},{3,1},{4,6},{5,7},{6,4},{7,5},{8,10},{9,11},{10,... | collective-permute-start | bytes 55304 | tf_op jit(solution)/shard_map/ppermute | solution.py:222
  10.1 2.3 %collective-permute-start.6 = (bf16[72,128]{1,0:T(8,128)(2,1)S(1)}, bf16[72,128]{1,0:T(8,128)(2,1)S(1)}, u32[]{:S(2)}, u32[]{:S(2)}) collective-permute-start(bf16[72,128]{1,0:T(8,128)(2,1)S(1)} %collective-permute-done.3.refs_0_), channel_id=1, source_target_pairs={{0,1},{1,0},{2,3},{3,2},{4,5},{5,4},{6,7},{7,6},{8,9},{9,8},{10,11... | collective-permute-start | bytes 55304 | tf_op jit(solution)/shard_map/ppermute | solution.py:224
  10.2 2.2 %collective-permute-start.7 = (bf16[72,128]{1,0:T(8,128)(2,1)S(1)}, bf16[72,128]{1,0:T(8,128)(2,1)S(1)}, u32[]{:S(2)}, u32[]{:S(2)}) collective-permute-start(bf16[72,128]{1,0:T(8,128)(2,1)S(1)} %collective-permute-done.4.refs_1_), channel_id=1, source_target_pairs={{0,1},{1,0},{2,3},{3,2},{4,5},{5,4},{6,7},{7,6},{8,9},{9,8},{10,11... | collective-permute-start | bytes 55304 | tf_op jit(solution)/shard_map/ppermute | solution.py:224
  11.0 1.4 %collective-permute-start.8 = (bf16[72,128]{1,0:T(8,128)(2,1)S(1)}, bf16[72,128]{1,0:T(8,128)(2,1)S(1)}, u32[]{:S(2)}, u32[]{:S(2)}) collective-permute-start(bf16[72,128]{1,0:T(8,128)(2,1)S(1)} %collective-permute-done.5.refs_2_), channel_id=1, source_target_pairs={{0,1},{1,0},{2,3},{3,2},{4,5},{5,4},{6,7},{7,6},{8,9},{9,8},{10,11... | collective-permute-start | bytes 55304 | tf_op jit(solution)/shard_map/ppermute | solution.py:224

commit v22 on v21

--- a/solution.py
+++ b/solution.py
@@ -155,7 +155,9 @@
         for k in range(stats):
             part = jnp.dot(left, right[:, k * half : (k + 1) * half], preferred_element_type=jnp.float32)
             out_ref[k, piece, :] = part.astype(out_ref.dtype)
-            copies.append(pltpu.make_async_copy(out_ref.at[k, piece], out_hbm.at[0, k, piece], sems.at[q, k]))
+        if q % 2 == 1:
+            done = slice((q - 1) * LANES, (q + 1) * LANES)
+            copies.append(pltpu.make_async_copy(out_ref.at[:, done], out_hbm.at[0, :, done], sems.at[q // 2]))
             copies[-1].start()
     for copy in copies:
         copy.wait()
@@ -231,7 +233,7 @@
         scratch_shapes=[
             pltpu.VMEM((pair_count * samps, BLOCK, LANES), dosage.dtype),
             pltpu.VMEM((stats, PANEL, half), jnp.bfloat16),
-            pltpu.SemaphoreType.DMA((PANEL // LANES, stats)),
+            pltpu.SemaphoreType.DMA((PANEL // LANES // 2,)),
         ],
         compiler_params=pltpu.CompilerParams(vmem_limit_bytes=48 * 1024 * 1024),
         name="stat",

time: 14.1 us -> 14.1 us (level)
  no operation moved by 1% of the time
where the time goes in v22:
time: 14.1 us; the launch traced here: 13.9 us
  starting transfers between devices  9.67 us (69%)
  Pallas kernels  2.54 us (18%)
  waiting for transfers between devices  1.65 us (12%)
    ppermute x4, starting transfers between devices, on_device(): arrived.append(lax.ppermute(message, AXES, route))  8.26 us
    pallas_call x1, Pallas kernels, on_device(): pl.pallas_call(functools.partial(stat_kernel, pair_count, samps), out_sha...  1.49 us
    ppermute x4, waiting for transfers between devices, on_device(): arrived.append(lax.ppermute(message, AXES, route))  1.36 us
    pallas_call x1, Pallas kernels, on_device(): pl.pallas_call(functools.partial(pick_kernel, pair_count, samps), out_sha...  0.91 us
    ppermute x3, starting transfers between devices, on_device(): mates = [lax.ppermute(a, 'samp', swap) for a in far]  0.9 us
    ppermute x1, starting transfers between devices, on_device(): mate_dosage = lax.ppermute(dosage, 'samp', swap)  0.45 us
  transfers between devices with their start and end apart: 9, of which 3 were waited for; matrix products, arithmetic and copies ran while one was open for 0% of the time, Pallas kernels for 7%

profile of v22, /device:TPU:0, one launch (start us, length us, event | category | flops | bytes accessed | tf_op | source)
XLA Modules:
  0.0 13.9 jit_solution(9629619739468676944)
XLA Ops:
  0.0 0.5 %collective-permute-start = (bf16[4,4096]{1,0:T(4,128)(2,1)}, bf16[4,4096]{1,0:T(4,128)(2,1)S(1)}, u32[]{:S(2)}, u32[]{:S(2)}) collective-permute-start(bf16[4,4096]{1,0:T(4,128)(2,1)} %param.4), channel_id=1, source_target_pairs={{0,1},{1,0},{2,3},{3,2},{4,5},{5,4},{6,7},{7,6},{8,9},{9,8},{10,11... | collective-permute-start | bytes 98312 | tf_op jit(solution)/shard_map/ppermute | solution.py:182
  0.5 0.1 collective-permute-start.1
  0.5 0.9 %pick.1 = (bf16[160,128]{1,0:T(8,128)(2,1)S(1)}, bf16[160,128]{1,0:T(8,128)(2,1)S(1)}, bf16[8,128]{1,0:T(8,128)(2,1)S(1)}, s32[2,64]{1,0:T(2,128)S(1)}) custom-call(s32[2,8]{1,0:T(2,128)} %bitcast.13, bf16[128,128]{1,0:T(8,128)(2,1)} %bitcast.12, bf16[2,4]{1,0:T(2,128)(2,1)} %pheno_hbm.1, s32[2,64]{1,0:T(2,128)} %perms_hbm.1), custom_call_target="tpu_custom_call" | custom-call | bytes 163840 | tf_op jit(solution)/shard_map/pick/pallas_call | solution.py:186
  1.4 0.3 %collective-permute-done.1.pheno_ref = bf16[2,4]{1,0:T(2,128)(2,1)S(1)} collective-permute-done((bf16[2,4]{1,0:T(2,128)(2,1)}, bf16[2,4]{1,0:T(2,128)(2,1)S(1)}, u32[]{:S(2)}, u32[]{:S(2)}) %collective-permute-start.1) | collective-permute-done | bytes 48 | tf_op jit(solution)/shard_map/ppermute | solution.py:183
  1.7 0.0 collective-permute-done
  1.7 0.1 %join.1 = (bf16[32,128]{1,0:T(8,128)(2,1)S(1)}, bf16[8,128]{1,0:T(8,128)(2,1)S(1)}, bf16[72,128]{1,0:T(8,128)(2,1)S(1)}, bf16[72,128]{1,0:T(8,128)(2,1)S(1)}, bf...) custom-call(bf16[160,128]{1,0:T(8,128)(2,1)S(1)} %get-tuple-element.15.keep_ref, ...), custom_call_target="tpu_custom_call" | custom-call | tf_op jit(solution)/shard_map/join/pallas_call | solution.py:208
  1.9 2.8 %collective-permute-start.3 = (bf16[72,128]{1,0:T(8,128)(2,1)S(1)}, bf16[72,128]{1,0:T(8,128)(2,1)S(1)}, u32[]{:S(2)}, u32[]{:S(2)}) collective-permute-start(bf16[72,128]{1,0:T(8,128)(2,1)S(1)} %get-tuple-element.22), channel_id=1, source_target_pairs={{0,4},{1,7},{2,6},{3,5},{4,8},{5,11},{6,10},{7,9},{8,12},{9,15},{1... | collective-permute-start | bytes 55304 | tf_op jit(solution)/shard_map/ppermute | solution.py:224
  4.7 2.6 %collective-permute-start.4 = (bf16[72,128]{1,0:T(8,128)(2,1)S(1)}, bf16[72,128]{1,0:T(8,128)(2,1)S(1)}, u32[]{:S(2)}, u32[]{:S(2)}) collective-permute-start(bf16[72,128]{1,0:T(8,128)(2,1)S(1)} %get-tuple-element.23), channel_id=1, source_target_pairs={{0,8},{1,11},{2,10},{3,9},{4,12},{5,15},{6,14},{7,13},{8,0},{9,3},... | collective-permute-start | bytes 55304 | tf_op jit(solution)/shard_map/ppermute | solution.py:224
  7.3 1.3 %collective-permute-start.5 = (bf16[72,128]{1,0:T(8,128)(2,1)S(1)}, bf16[72,128]{1,0:T(8,128)(2,1)S(1)}, u32[]{:S(2)}, u32[]{:S(2)}) collective-permute-start(bf16[72,128]{1,0:T(8,128)(2,1)S(1)} %get-tuple-element.24), channel_id=1, source_target_pairs={{0,12},{1,15},{2,14},{3,13},{4,0},{5,3},{6,2},{7,1},{8,4},{9,7},{1... | collective-permute-start | bytes 55304 | tf_op jit(solution)/shard_map/ppermute | solution.py:224
  8.6 1.5 %collective-permute-start.2 = (bf16[72,128]{1,0:T(8,128)(2,1)S(1)}, bf16[72,128]{1,0:T(8,128)(2,1)S(1)}, u32[]{:S(2)}, u32[]{:S(2)}) collective-permute-start(bf16[72,128]{1,0:T(8,128)(2,1)S(1)} %get-tuple-element.21), channel_id=1, source_target_pairs={{0,2},{1,3},{2,0},{3,1},{4,6},{5,7},{6,4},{7,5},{8,10},{9,11},{10,... | collective-permute-start | bytes 55304 | tf_op jit(solution)/shard_map/ppermute | solution.py:224
  10.1 0.0 collective-permute-done.3.refs_0_
  10.1 0.1 collective-permute-start.6
  10.2 0.0 collective-permute-done.4.refs_1_
  10.2 0.5 %collective-permute-start.7 = (bf16[72,128]{1,0:T(8,128)(2,1)S(1)}, bf16[72,128]{1,0:T(8,128)(2,1)S(1)}, u32[]{:S(2)}, u32[]{:S(2)}) collective-permute-start(bf16[72,128]{1,0:T(8,128)(2,1)S(1)} %collective-permute-done.4.refs_1_), channel_id=1, source_target_pairs={{0,1},{1,0},{2,3},{3,2},{4,5},{5,4},{6,7},{7,6},{8,9},{9,8},{10,11... | collective-permute-start | bytes 55304 | tf_op jit(solution)/shard_map/ppermute | solution.py:226
  10.6 0.4 %collective-permute-done.5.refs_2_ = bf16[72,128]{1,0:T(8,128)(2,1)S(1)} collective-permute-done((bf16[72,128]{1,0:T(8,128)(2,1)S(1)}, bf16[72,128]{1,0:T(8,128)(2,1)S(1)}, u32[]{:S(2)}, u32[]{:S(2)}) %collective-permute-start.5) | collective-permute-done | bytes 18464 | tf_op jit(solution)/shard_map/ppermute | solution.py:224
  11.0 0.4 %collective-permute-start.8 = (bf16[72,128]{1,0:T(8,128)(2,1)S(1)}, bf16[72,128]{1,0:T(8,128)(2,1)S(1)}, u32[]{:S(2)}, u32[]{:S(2)}) collective-permute-start(bf16[72,128]{1,0:T(8,128)(2,1)S(1)} %collective-permute-done.5.refs_2_), channel_id=1, source_target_pairs={{0,1},{1,0},{2,3},{3,2},{4,5},{5,4},{6,7},{7,6},{8,9},{9,8},{10,11... | collective-permute-start | bytes 55304 | tf_op jit(solution)/shard_map/ppermute | solution.py:226
  11.4 1.0 %collective-permute-done.2.near_ref = bf16[72,128]{1,0:T(8,128)(2,1)S(1)} collective-permute-done((bf16[72,128]{1,0:T(8,128)(2,1)S(1)}, bf16[72,128]{1,0:T(8,128)(2,1)S(1)}, u32[]{:S(2)}, u32[]{:S(2)}) %collective-permute-start.2) | collective-permute-done | bytes 18464 | tf_op jit(solution)/shard_map/ppermute | solution.py:224
  12.4 0.0 collective-permute-done.6.refs_3_
  12.4 0.0 collective-permute-done.7.refs_4_
  12.4 0.0 collective-permute-done.8.refs_5_
  12.4 1.5 %stat.1 = bf16[1,4,512,256]{3,2,1,0:T(8,128)(2,1)} custom-call(bf16[8,128]{1,0:T(8,128)(2,1)S(1)} %get-tuple-element.19.wave_ref, bf16[160,128]{1,0:T(8,128)(2,1)S(1)} %get-tuple-element.15.keep_ref, bf16[32,128]{1,0:T(8,128)(2,1)S(1)} %get-tuple-element.20.mate_self_ref, bf16[72,128]{1,0:T(8,128)(2,1)S(1)} %collective-permute-done.2.near_ref, ...), custom_call_target="tpu_custom_call" | custom-call | tf_op jit(solution)/shard_map/stat/pallas_call | solution.py:228
Async XLA Ops:
  0.0 1.7 %collective-permute-start = (bf16[4,4096]{1,0:T(4,128)(2,1)}, bf16[4,4096]{1,0:T(4,128)(2,1)S(1)}, u32[]{:S(2)}, u32[]{:S(2)}) collective-permute-start(bf16[4,4096]{1,0:T(4,128)(2,1)} %param.4), channel_id=1, source_target_pairs={{0,1},{1,0},{2,3},{3,2},{4,5},{5,4},{6,7},{7,6},{8,9},{9,8},{10,11... | collective-permute-start | bytes 98312 | tf_op jit(solution)/shard_map/ppermute | solution.py:182
  0.5 1.3 %collective-permute-start.1 = (bf16[2,4]{1,0:T(2,128)(2,1)}, bf16[2,4]{1,0:T(2,128)(2,1)S(1)}, u32[]{:S(2)}, u32[]{:S(2)}) collective-permute-start(bf16[2,4]{1,0:T(2,128)(2,1)} %pheno_hbm.1), channel_id=1, source_target_pairs={{0,1},{1,0},{2,3},{3,2},{4,5},{5,4},{6,7},{7,6},{8,9},{9,8},{10,11... | collective-permute-start | bytes 56 | tf_op jit(solution)/shard_map/ppermute | solution.py:183
  1.9 8.3 %collective-permute-start.3 = (bf16[72,128]{1,0:T(8,128)(2,1)S(1)}, bf16[72,128]{1,0:T(8,128)(2,1)S(1)}, u32[]{:S(2)}, u32[]{:S(2)}) collective-permute-start(bf16[72,128]{1,0:T(8,128)(2,1)S(1)} %get-tuple-element.22), channel_id=1, source_target_pairs={{0,4},{1,7},{2,6},{3,5},{4,8},{5,11},{6,10},{7,9},{8,12},{9,15},{1... | collective-permute-start | bytes 55304 | tf_op jit(solution)/shard_map/ppermute | solution.py:224
  4.7 5.5 %collective-permute-start.4 = (bf16[72,128]{1,0:T(8,128)(2,1)S(1)}, bf16[72,128]{1,0:T(8,128)(2,1)S(1)}, u32[]{:S(2)}, u32[]{:S(2)}) collective-permute-start(bf16[72,128]{1,0:T(8,128)(2,1)S(1)} %get-tuple-element.23), channel_id=1, source_target_pairs={{0,8},{1,11},{2,10},{3,9},{4,12},{5,15},{6,14},{7,13},{8,0},{9,3},... | collective-permute-start | bytes 55304 | tf_op jit(solution)/shard_map/ppermute | solution.py:224
  7.3 3.8 %collective-permute-start.5 = (bf16[72,128]{1,0:T(8,128)(2,1)S(1)}, bf16[72,128]{1,0:T(8,128)(2,1)S(1)}, u32[]{:S(2)}, u32[]{:S(2)}) collective-permute-start(bf16[72,128]{1,0:T(8,128)(2,1)S(1)} %get-tuple-element.24), channel_id=1, source_target_pairs={{0,12},{1,15},{2,14},{3,13},{4,0},{5,3},{6,2},{7,1},{8,4},{9,7},{1... | collective-permute-start | bytes 55304 | tf_op jit(solution)/shard_map/ppermute | solution.py:224
  8.6 3.8 %collective-permute-start.2 = (bf16[72,128]{1,0:T(8,128)(2,1)S(1)}, bf16[72,128]{1,0:T(8,128)(2,1)S(1)}, u32[]{:S(2)}, u32[]{:S(2)}) collective-permute-start(bf16[72,128]{1,0:T(8,128)(2,1)S(1)} %get-tuple-element.21), channel_id=1, source_target_pairs={{0,2},{1,3},{2,0},{3,1},{4,6},{5,7},{6,4},{7,5},{8,10},{9,11},{10,... | collective-permute-start | bytes 55304 | tf_op jit(solution)/shard_map/ppermute | solution.py:224
  10.1 2.3 %collective-permute-start.6 = (bf16[72,128]{1,0:T(8,128)(2,1)S(1)}, bf16[72,128]{1,0:T(8,128)(2,1)S(1)}, u32[]{:S(2)}, u32[]{:S(2)}) collective-permute-start(bf16[72,128]{1,0:T(8,128)(2,1)S(1)} %collective-permute-done.3.refs_0_), channel_id=1, source_target_pairs={{0,1},{1,0},{2,3},{3,2},{4,5},{5,4},{6,7},{7,6},{8,9},{9,8},{10,11... | collective-permute-start | bytes 55304 | tf_op jit(solution)/shard_map/ppermute | solution.py:226
  10.2 2.2 %collective-permute-start.7 = (bf16[72,128]{1,0:T(8,128)(2,1)S(1)}, bf16[72,128]{1,0:T(8,128)(2,1)S(1)}, u32[]{:S(2)}, u32[]{:S(2)}) collective-permute-start(bf16[72,128]{1,0:T(8,128)(2,1)S(1)} %collective-permute-done.4.refs_1_), channel_id=1, source_target_pairs={{0,1},{1,0},{2,3},{3,2},{4,5},{5,4},{6,7},{7,6},{8,9},{9,8},{10,11... | collective-permute-start | bytes 55304 | tf_op jit(solution)/shard_map/ppermute | solution.py:226
  11.0 1.4 %collective-permute-start.8 = (bf16[72,128]{1,0:T(8,128)(2,1)S(1)}, bf16[72,128]{1,0:T(8,128)(2,1)S(1)}, u32[]{:S(2)}, u32[]{:S(2)}) collective-permute-start(bf16[72,128]{1,0:T(8,128)(2,1)S(1)} %collective-permute-done.5.refs_2_), channel_id=1, source_target_pairs={{0,1},{1,0},{2,3},{3,2},{4,5},{5,4},{6,7},{7,6},{8,9},{9,8},{10,11... | collective-permute-start | bytes 55304 | tf_op jit(solution)/shard_map/ppermute | solution.py:226

commit v23 on v20

--- a/solution.py
+++ b/solution.py
@@ -49,7 +49,7 @@
 def pick_kernel(
     pair_count, samps, pairs_hbm, grid_hbm, pheno_hbm, perms_hbm, keep_ref, pick_ref, wave_ref, perms_ref, pairs_ref, grid_ref, pheno_ref, sems
 ):
-    fetched = ((pairs_hbm, pairs_ref), (grid_hbm, grid_ref), (pheno_hbm, pheno_ref), (perms_hbm, perms_ref))
+    fetched = ((grid_hbm, grid_ref), (pairs_hbm, pairs_ref), (pheno_hbm, pheno_ref), (perms_hbm, perms_ref))
     copies = [pltpu.make_async_copy(source, target, sems.at[i]) for i, (source, target) in enumerate(fetched)]
     for copy in copies:
         copy.start()

time: 14 us -> 14.1 us (level)
  no operation moved by 1% of the time
where the time goes in v23:
time: 14.1 us; the launch traced here: 13.9 us
  starting transfers between devices  9.67 us (69%)
  Pallas kernels  2.55 us (18%)
  waiting for transfers between devices  1.64 us (12%)
    ppermute x4, starting transfers between devices, on_device(): arrived.append(lax.ppermute(message, AXES, route))  8.31 us
    pallas_call x1, Pallas kernels, on_device(): pl.pallas_call(functools.partial(stat_kernel, pair_count, samps), out_sha...  1.43 us
    ppermute x4, waiting for transfers between devices, on_device(): arrived.append(lax.ppermute(message, AXES, route))  1.42 us
    pallas_call x1, Pallas kernels, on_device(): pl.pallas_call(functools.partial(pick_kernel, pair_count, samps), out_sha...  0.98 us
    ppermute x3, starting transfers between devices, on_device(): mates = [lax.ppermute(a, 'samp', swap) for a in far]  0.85 us
    ppermute x1, starting transfers between devices, on_device(): mate_dosage = lax.ppermute(dosage, 'samp', swap)  0.45 us
  transfers between devices with their start and end apart: 9, of which 3 were waited for; matrix products, arithmetic and copies ran while one was open for 0% of the time, Pallas kernels for 7%

profile of v23, /device:TPU:0, one launch (start us, length us, event | category | flops | bytes accessed | tf_op | source)
XLA Modules:
  0.0 13.9 jit_solution(1343583047734025775)
XLA Ops:
  0.0 0.5 %collective-permute-start = (bf16[4,4096]{1,0:T(4,128)(2,1)}, bf16[4,4096]{1,0:T(4,128)(2,1)S(1)}, u32[]{:S(2)}, u32[]{:S(2)}) collective-permute-start(bf16[4,4096]{1,0:T(4,128)(2,1)} %param.4), channel_id=1, source_target_pairs={{0,1},{1,0},{2,3},{3,2},{4,5},{5,4},{6,7},{7,6},{8,9},{9,8},{10,11... | collective-permute-start | bytes 98312 | tf_op jit(solution)/shard_map/ppermute | solution.py:180
  0.5 0.1 collective-permute-start.1
  0.5 1.0 %pick.1 = (bf16[160,128]{1,0:T(8,128)(2,1)S(1)}, bf16[160,128]{1,0:T(8,128)(2,1)S(1)}, bf16[8,128]{1,0:T(8,128)(2,1)S(1)}, s32[2,64]{1,0:T(2,128)S(1)}) custom-call(s32[2,8]{1,0:T(2,128)} %bitcast.13, bf16[128,128]{1,0:T(8,128)(2,1)} %bitcast.12, bf16[2,4]{1,0:T(2,128)(2,1)} %pheno_hbm.1, s32[2,64]{1,0:T(2,128)} %perms_hbm.1), custom_call_target="tpu_custom_call" | custom-call | bytes 163840 | tf_op jit(solution)/shard_map/pick/pallas_call | solution.py:184
  1.5 0.2 %collective-permute-done.1.pheno_ref = bf16[2,4]{1,0:T(2,128)(2,1)S(1)} collective-permute-done((bf16[2,4]{1,0:T(2,128)(2,1)}, bf16[2,4]{1,0:T(2,128)(2,1)S(1)}, u32[]{:S(2)}, u32[]{:S(2)}) %collective-permute-start.1) | collective-permute-done | bytes 48 | tf_op jit(solution)/shard_map/ppermute | solution.py:181
  1.7 0.0 collective-permute-done
  1.7 0.1 %join.1 = (bf16[32,128]{1,0:T(8,128)(2,1)S(1)}, bf16[8,128]{1,0:T(8,128)(2,1)S(1)}, bf16[72,128]{1,0:T(8,128)(2,1)S(1)}, bf16[72,128]{1,0:T(8,128)(2,1)S(1)}, bf...) custom-call(bf16[160,128]{1,0:T(8,128)(2,1)S(1)} %get-tuple-element.15.keep_ref, ...), custom_call_target="tpu_custom_call" | custom-call | tf_op jit(solution)/shard_map/join/pallas_call | solution.py:206
  1.9 2.9 %collective-permute-start.3 = (bf16[72,128]{1,0:T(8,128)(2,1)S(1)}, bf16[72,128]{1,0:T(8,128)(2,1)S(1)}, u32[]{:S(2)}, u32[]{:S(2)}) collective-permute-start(bf16[72,128]{1,0:T(8,128)(2,1)S(1)} %get-tuple-element.22), channel_id=1, source_target_pairs={{0,4},{1,7},{2,6},{3,5},{4,8},{5,11},{6,10},{7,9},{8,12},{9,15},{1... | collective-permute-start | bytes 55304 | tf_op jit(solution)/shard_map/ppermute | solution.py:222
  4.7 2.6 %collective-permute-start.4 = (bf16[72,128]{1,0:T(8,128)(2,1)S(1)}, bf16[72,128]{1,0:T(8,128)(2,1)S(1)}, u32[]{:S(2)}, u32[]{:S(2)}) collective-permute-start(bf16[72,128]{1,0:T(8,128)(2,1)S(1)} %get-tuple-element.23), channel_id=1, source_target_pairs={{0,8},{1,11},{2,10},{3,9},{4,12},{5,15},{6,14},{7,13},{8,0},{9,3},... | collective-permute-start | bytes 55304 | tf_op jit(solution)/shard_map/ppermute | solution.py:222
  7.3 1.3 %collective-permute-start.5 = (bf16[72,128]{1,0:T(8,128)(2,1)S(1)}, bf16[72,128]{1,0:T(8,128)(2,1)S(1)}, u32[]{:S(2)}, u32[]{:S(2)}) collective-permute-start(bf16[72,128]{1,0:T(8,128)(2,1)S(1)} %get-tuple-element.24), channel_id=1, source_target_pairs={{0,12},{1,15},{2,14},{3,13},{4,0},{5,3},{6,2},{7,1},{8,4},{9,7},{1... | collective-permute-start | bytes 55304 | tf_op jit(solution)/shard_map/ppermute | solution.py:222
  8.7 1.5 %collective-permute-start.2 = (bf16[72,128]{1,0:T(8,128)(2,1)S(1)}, bf16[72,128]{1,0:T(8,128)(2,1)S(1)}, u32[]{:S(2)}, u32[]{:S(2)}) collective-permute-start(bf16[72,128]{1,0:T(8,128)(2,1)S(1)} %get-tuple-element.21), channel_id=1, source_target_pairs={{0,2},{1,3},{2,0},{3,1},{4,6},{5,7},{6,4},{7,5},{8,10},{9,11},{10,... | collective-permute-start | bytes 55304 | tf_op jit(solution)/shard_map/ppermute | solution.py:222
  10.2 0.0 collective-permute-done.3.refs_0_
  10.2 0.0 collective-permute-start.6
  10.2 0.0 collective-permute-done.4.refs_1_
  10.2 0.5 %collective-permute-start.7 = (bf16[72,128]{1,0:T(8,128)(2,1)S(1)}, bf16[72,128]{1,0:T(8,128)(2,1)S(1)}, u32[]{:S(2)}, u32[]{:S(2)}) collective-permute-start(bf16[72,128]{1,0:T(8,128)(2,1)S(1)} %collective-permute-done.4.refs_1_), channel_id=1, source_target_pairs={{0,1},{1,0},{2,3},{3,2},{4,5},{5,4},{6,7},{7,6},{8,9},{9,8},{10,11... | collective-permute-start | bytes 55304 | tf_op jit(solution)/shard_map/ppermute | solution.py:224
  10.7 0.4 %collective-permute-done.5.refs_2_ = bf16[72,128]{1,0:T(8,128)(2,1)S(1)} collective-permute-done((bf16[72,128]{1,0:T(8,128)(2,1)S(1)}, bf16[72,128]{1,0:T(8,128)(2,1)S(1)}, u32[]{:S(2)}, u32[]{:S(2)}) %collective-permute-start.5) | collective-permute-done | bytes 18464 | tf_op jit(solution)/shard_map/ppermute | solution.py:222
  11.1 0.3 %collective-permute-start.8 = (bf16[72,128]{1,0:T(8,128)(2,1)S(1)}, bf16[72,128]{1,0:T(8,128)(2,1)S(1)}, u32[]{:S(2)}, u32[]{:S(2)}) collective-permute-start(bf16[72,128]{1,0:T(8,128)(2,1)S(1)} %collective-permute-done.5.refs_2_), channel_id=1, source_target_pairs={{0,1},{1,0},{2,3},{3,2},{4,5},{5,4},{6,7},{7,6},{8,9},{9,8},{10,11... | collective-permute-start | bytes 55304 | tf_op jit(solution)/shard_map/ppermute | solution.py:224
  11.4 1.0 %collective-permute-done.2.near_ref = bf16[72,128]{1,0:T(8,128)(2,1)S(1)} collective-permute-done((bf16[72,128]{1,0:T(8,128)(2,1)S(1)}, bf16[72,128]{1,0:T(8,128)(2,1)S(1)}, u32[]{:S(2)}, u32[]{:S(2)}) %collective-permute-start.2) | collective-permute-done | bytes 18464 | tf_op jit(solution)/shard_map/ppermute | solution.py:222
  12.4 0.0 collective-permute-done.6.refs_3_
  12.4 0.0 collective-permute-done.7.refs_4_
  12.4 0.0 collective-permute-done.8.refs_5_
  12.5 1.4 %stat.1 = bf16[1,4,512,256]{3,2,1,0:T(8,128)(2,1)} custom-call(bf16[8,128]{1,0:T(8,128)(2,1)S(1)} %get-tuple-element.19.wave_ref, bf16[160,128]{1,0:T(8,128)(2,1)S(1)} %get-tuple-element.15.keep_ref, bf16[32,128]{1,0:T(8,128)(2,1)S(1)} %get-tuple-element.20.mate_self_ref, bf16[72,128]{1,0:T(8,128)(2,1)S(1)} %collective-permute-done.2.near_ref, ...), custom_call_target="tpu_custom_call" | custom-call | tf_op jit(solution)/shard_map/stat/pallas_call | solution.py:226
Async XLA Ops:
  0.0 1.7 %collective-permute-start = (bf16[4,4096]{1,0:T(4,128)(2,1)}, bf16[4,4096]{1,0:T(4,128)(2,1)S(1)}, u32[]{:S(2)}, u32[]{:S(2)}) collective-permute-start(bf16[4,4096]{1,0:T(4,128)(2,1)} %param.4), channel_id=1, source_target_pairs={{0,1},{1,0},{2,3},{3,2},{4,5},{5,4},{6,7},{7,6},{8,9},{9,8},{10,11... | collective-permute-start | bytes 98312 | tf_op jit(solution)/shard_map/ppermute | solution.py:180
  0.5 1.3 %collective-permute-start.1 = (bf16[2,4]{1,0:T(2,128)(2,1)}, bf16[2,4]{1,0:T(2,128)(2,1)S(1)}, u32[]{:S(2)}, u32[]{:S(2)}) collective-permute-start(bf16[2,4]{1,0:T(2,128)(2,1)} %pheno_hbm.1), channel_id=1, source_target_pairs={{0,1},{1,0},{2,3},{3,2},{4,5},{5,4},{6,7},{7,6},{8,9},{9,8},{10,11... | collective-permute-start | bytes 56 | tf_op jit(solution)/shard_map/ppermute | solution.py:181
  1.9 8.3 %collective-permute-start.3 = (bf16[72,128]{1,0:T(8,128)(2,1)S(1)}, bf16[72,128]{1,0:T(8,128)(2,1)S(1)}, u32[]{:S(2)}, u32[]{:S(2)}) collective-permute-start(bf16[72,128]{1,0:T(8,128)(2,1)S(1)} %get-tuple-element.22), channel_id=1, source_target_pairs={{0,4},{1,7},{2,6},{3,5},{4,8},{5,11},{6,10},{7,9},{8,12},{9,15},{1... | collective-permute-start | bytes 55304 | tf_op jit(solution)/shard_map/ppermute | solution.py:222
  4.7 5.4 %collective-permute-start.4 = (bf16[72,128]{1,0:T(8,128)(2,1)S(1)}, bf16[72,128]{1,0:T(8,128)(2,1)S(1)}, u32[]{:S(2)}, u32[]{:S(2)}) collective-permute-start(bf16[72,128]{1,0:T(8,128)(2,1)S(1)} %get-tuple-element.23), channel_id=1, source_target_pairs={{0,8},{1,11},{2,10},{3,9},{4,12},{5,15},{6,14},{7,13},{8,0},{9,3},... | collective-permute-start | bytes 55304 | tf_op jit(solution)/shard_map/ppermute | solution.py:222
  7.3 3.8 %collective-permute-start.5 = (bf16[72,128]{1,0:T(8,128)(2,1)S(1)}, bf16[72,128]{1,0:T(8,128)(2,1)S(1)}, u32[]{:S(2)}, u32[]{:S(2)}) collective-permute-start(bf16[72,128]{1,0:T(8,128)(2,1)S(1)} %get-tuple-element.24), channel_id=1, source_target_pairs={{0,12},{1,15},{2,14},{3,13},{4,0},{5,3},{6,2},{7,1},{8,4},{9,7},{1... | collective-permute-start | bytes 55304 | tf_op jit(solution)/shard_map/ppermute | solution.py:222
  8.7 3.8 %collective-permute-start.2 = (bf16[72,128]{1,0:T(8,128)(2,1)S(1)}, bf16[72,128]{1,0:T(8,128)(2,1)S(1)}, u32[]{:S(2)}, u32[]{:S(2)}) collective-permute-start(bf16[72,128]{1,0:T(8,128)(2,1)S(1)} %get-tuple-element.21), channel_id=1, source_target_pairs={{0,2},{1,3},{2,0},{3,1},{4,6},{5,7},{6,4},{7,5},{8,10},{9,11},{10,... | collective-permute-start | bytes 55304 | tf_op jit(solution)/shard_map/ppermute | solution.py:222
  10.2 2.3 %collective-permute-start.6 = (bf16[72,128]{1,0:T(8,128)(2,1)S(1)}, bf16[72,128]{1,0:T(8,128)(2,1)S(1)}, u32[]{:S(2)}, u32[]{:S(2)}) collective-permute-start(bf16[72,128]{1,0:T(8,128)(2,1)S(1)} %collective-permute-done.3.refs_0_), channel_id=1, source_target_pairs={{0,1},{1,0},{2,3},{3,2},{4,5},{5,4},{6,7},{7,6},{8,9},{9,8},{10,11... | collective-permute-start | bytes 55304 | tf_op jit(solution)/shard_map/ppermute | solution.py:224
  10.2 2.3 %collective-permute-start.7 = (bf16[72,128]{1,0:T(8,128)(2,1)S(1)}, bf16[72,128]{1,0:T(8,128)(2,1)S(1)}, u32[]{:S(2)}, u32[]{:S(2)}) collective-permute-start(bf16[72,128]{1,0:T(8,128)(2,1)S(1)} %collective-permute-done.4.refs_1_), channel_id=1, source_target_pairs={{0,1},{1,0},{2,3},{3,2},{4,5},{5,4},{6,7},{7,6},{8,9},{9,8},{10,11... | collective-permute-start | bytes 55304 | tf_op jit(solution)/shard_map/ppermute | solution.py:224
  11.1 1.4 %collective-permute-start.8 = (bf16[72,128]{1,0:T(8,128)(2,1)S(1)}, bf16[72,128]{1,0:T(8,128)(2,1)S(1)}, u32[]{:S(2)}, u32[]{:S(2)}) collective-permute-start(bf16[72,128]{1,0:T(8,128)(2,1)S(1)} %collective-permute-done.5.refs_2_), channel_id=1, source_target_pairs={{0,1},{1,0},{2,3},{3,2},{4,5},{5,4},{6,7},{7,6},{8,9},{9,8},{10,11... | collective-permute-start | bytes 55304 | tf_op jit(solution)/shard_map/ppermute | solution.py:224
